TPU v7x, 32 devices: a whole 2x2x4 slice. The times are simulated.
32 devices in a mesh: dp: 16 (over z, y, core), mp: 2 (over x).
Axes of the slice: x: 2, y: 2, z: 4, core: 2. Of those that a mesh axis runs over, the one named last changes fastest.
Arguments:
- latents: bfloat16 [16, 5, 16, 16, 1024], P('dp', None, 'mp'), may hold values from -6 to 6
- cotangent: bfloat16 [16, 5, 16, 16, 1024], P('dp', None, 'mp'), may hold values from -6 to 6
- frame_counts: int32 [16], P('dp'), may hold values from 2 to 5
- band_ids: int32 [16], replicated, may hold values from 0 to 31
- class_ids: int32 [16], replicated, may hold values from 0 to 100
- time_table: bfloat16 [32, 1024], replicated, may hold values from -6 to 6
- class_table: bfloat16 [101, 1024], replicated, may hold values from -6 to 6
- ada_weight: bfloat16 [2, 1024, 6144], P(None, None, ('dp', 'mp')), may hold values from -0.1875 to 0.1875, as said below
- ada_bias: bfloat16 [2, 6144], P(None, ('dp', 'mp')), may hold values from -3 to 3
- qkv_weight: bfloat16 [2, 1024, 3, 1024], P(None, 'dp', None, 'mp'), may hold values from -0.1875 to 0.1875
- out_weight: bfloat16 [2, 1024, 1024], P(None, 'mp', 'dp'), may hold values from -0.75 to 0.75
- up_weight: bfloat16 [2, 1024, 4096], P(None, 'dp', 'mp'), may hold values from -0.1875 to 0.1875
- down_weight: bfloat16 [2, 4096, 1024], P(None, 'mp', 'dp'), may hold values from -0.09375 to 0.09375
- spatial_bias: bfloat16 [16, 961], P('mp'), may hold values from -3 to 3
- joint_bias: bfloat16 [16, 2025], P('mp'), may hold values from -3 to 3
Outputs:
- mixed_output: float32 [16, 5, 16, 16, 1024], P('dp', None, 'mp')
- grad_latents: float32 [16, 5, 16, 16, 1024], P('dp', None, 'mp')
- grad_time_table: float32 [32, 1024], replicated
- grad_class_table: float32 [101, 1024], replicated
- grad_ada_weight: float32 [2, 1024, 6144], P(None, None, ('dp', 'mp'))
- grad_ada_bias: float32 [2, 6144], P(None, ('dp', 'mp'))
- grad_qkv_weight: float32 [2, 1024, 3, 1024], P(None, 'dp', None, 'mp')
- grad_out_weight: float32 [2, 1024, 1024], P(None, 'mp', 'dp')
- grad_up_weight: float32 [2, 1024, 4096], P(None, 'dp', 'mp')
- grad_down_weight: float32 [2, 4096, 1024], P(None, 'mp', 'dp')
- grad_spatial_bias: float32 [16, 961], P('mp')
- grad_joint_bias: float32 [16, 2025], P('mp')
Inputs may be any that keep to these rules, and one draw needn't show every extreme that they name: `ada_weight`: entries of the modulation map, of mean zero.
All inputs are finite; a program needn't handle non-finite values.
Results may differ from a plain program's by a relative error of at most 0.034.
Values may be sent and summed in bfloat16 or wider, within the bound.
No kernel may reach another device: no remote copies, remote signals or barrier semaphores. Data moves between devices by JAX's collectives and lax.ppermute only.
A program may use at most 320 MiB of HBM per device.

v0:
```python
import jax
import jax.numpy as jnp
import numpy as np
from jax import lax
from jax.sharding import PartitionSpec as P

HEAD_DIM = 64
CLASSES = 101
BANDS = 32
FRAMES = 5
WIN_S = 16
WIN_T = 8


epsilon = 1e-06
masked_score = -1e30


def spatial_table():
    places = np.arange(WIN_S * WIN_S)
    row_at = places // WIN_S
    col_at = places % WIN_S
    row_rel = row_at[:, None] - row_at[None, :] + WIN_S - 1
    col_rel = col_at[:, None] - col_at[None, :] + WIN_S - 1
    return (row_rel * (2 * WIN_S - 1) + col_rel).astype(np.int32)


def joint_table():
    places = np.arange(FRAMES * WIN_T * WIN_T)
    time_at = places // (WIN_T * WIN_T)
    row_at = places // WIN_T % WIN_T
    col_at = places % WIN_T
    time_rel = time_at[:, None] - time_at[None, :] + FRAMES - 1
    row_rel = row_at[:, None] - row_at[None, :] + WIN_T - 1
    col_rel = col_at[:, None] - col_at[None, :] + WIN_T - 1
    return ((time_rel * (2 * WIN_T - 1) + row_rel) * (2 * WIN_T - 1) + col_rel).astype(np.int32)


def to_windows(values, window, is_joint):
    clip_count, frames, side_cells, channels = (
        values.shape[0],
        values.shape[1],
        values.shape[2],
        values.shape[4],
    )
    per_side = side_cells // window
    if is_joint:
        shaped = values.reshape(clip_count, frames, per_side, window, per_side, window, channels)
        shaped = shaped.transpose(0, 2, 4, 1, 3, 5, 6)
        return shaped.reshape(clip_count * per_side * per_side, frames * window * window, channels)
    shaped = values.reshape(clip_count, frames, per_side, window, per_side, window, channels)
    shaped = shaped.transpose(0, 1, 2, 4, 3, 5, 6)
    return shaped.reshape(clip_count * frames * per_side * per_side, window * window, channels)


def from_windows(values, clip_count, frames, side_cells, window, is_joint):
    per_side = side_cells // window
    channels = values.shape[-1]
    if is_joint:
        shaped = values.reshape(clip_count, per_side, per_side, frames, window, window, channels)
        shaped = shaped.transpose(0, 3, 1, 4, 2, 5, 6)
    else:
        shaped = values.reshape(clip_count, frames, per_side, per_side, window, window, channels)
        shaped = shaped.transpose(0, 1, 2, 4, 3, 5, 6)
    return shaped.reshape(clip_count, frames, side_cells, side_cells, channels)


def normalize(values):
    center = values - jnp.mean(values, axis=-1, keepdims=True)
    spread = jnp.mean(center * center, axis=-1, keepdims=True)
    inverse = lax.rsqrt(spread + epsilon)
    return (center * inverse, inverse)


def norm_back(grad_normed, normed, inverse):
    first_mean = jnp.mean(grad_normed, axis=-1, keepdims=True)
    second_mean = jnp.mean(grad_normed * normed, axis=-1, keepdims=True)
    return inverse * (grad_normed - first_mean - normed * second_mean)


def exact_gelu(values):
    return jax.nn.gelu(values, approximate=False)


def gather_rows(values):
    return lax.all_gather(values, "mp", axis=2, tiled=True)


def sum_rows(values):
    return lax.psum_scatter(
        values.astype(jnp.bfloat16), "mp", scatter_dimension=2, tiled=True
    ).astype(jnp.float32)


def gather_grads(values):
    return lax.all_gather(values, "mp", axis=2, tiled=True)


def input_sums(values):
    return lax.psum_scatter(
        values.astype(jnp.bfloat16), "mp", scatter_dimension=2, tiled=True
    ).astype(jnp.float32)


def inputs_again(moved):
    return lax.all_gather(moved, "mp", axis=2, tiled=True)


def attention_scores(query_part, key_part, bias_matrix, key_valid):
    scores = (
        jnp.einsum("nqhe,nkhe->nhqk", query_part, key_part, preferred_element_type=jnp.float32)
        * HEAD_DIM ** (-0.5)
        + bias_matrix[None]
    )
    if key_valid is not None:
        scores = jnp.where(key_valid[:, None, None, :] > 0, scores, masked_score)
    return scores


def local(
    latents,
    cotangent,
    frame_counts,
    band_ids,
    class_ids,
    time_table,
    class_table,
    ada_weight,
    ada_bias,
    qkv_weight,
    out_weight,
    up_weight,
    down_weight,
    spatial_bias,
    joint_bias,
):
    clip_count = latents.shape[0]
    frames = latents.shape[1]
    side_cells = latents.shape[3]
    model_width = latents.shape[4]
    heads_local = spatial_bias.shape[0]
    local_width = heads_local * HEAD_DIM
    dp_count = lax.axis_size("dp")
    mp_count = lax.axis_size("mp")
    col_width = ada_weight.shape[2]
    band_hot = (band_ids[:, None] == jnp.arange(BANDS)[None, :]).astype(jnp.bfloat16)
    class_hot = (class_ids[:, None] == jnp.arange(CLASSES)[None, :]).astype(jnp.bfloat16)
    condition = jnp.dot(band_hot, time_table, preferred_element_type=jnp.float32) + jnp.dot(
        class_hot, class_table, preferred_element_type=jnp.float32
    )
    activity_low = jax.nn.silu(condition).astype(jnp.bfloat16)
    ada_cols, ada_bias_cols = (
        lax.all_gather(ada_weight, "mp", axis=2, tiled=True),
        lax.all_gather(ada_bias, "mp", axis=1, tiled=True),
    )
    mod_part = jnp.einsum(
        "cd,bde->bce", activity_low, ada_cols, preferred_element_type=jnp.float32
    ) + ada_bias_cols[:, None, :].astype(jnp.float32)
    modulation = lax.all_gather(mod_part, "dp", axis=2, tiled=True)
    first_clip = lax.axis_index("dp") * clip_count
    own_mod = lax.dynamic_slice_in_dim(modulation, first_clip, clip_count, 1).reshape(
        2, clip_count, 6, model_width
    )
    frame_valid = (jnp.arange(frames)[None, :] < frame_counts[:, None]).astype(jnp.float32)
    frame_mask = frame_valid[:, :, None, None, None]
    key_frames = np.arange(frames * WIN_T * WIN_T) // (WIN_T * WIN_T)
    joint_cells = key_frames.shape[0]
    per_side = side_cells // WIN_T
    key_valid = frame_valid[:, key_frames]
    key_valid = jnp.broadcast_to(
        key_valid[:, None, :], (clip_count, per_side * per_side, joint_cells)
    ).reshape(clip_count * per_side * per_side, joint_cells)
    w_qkv, w_out, w_up, w_down = (
        lax.all_gather(qkv_weight, "dp", axis=1, tiled=True),
        lax.all_gather(out_weight, "dp", axis=2, tiled=True),
        lax.all_gather(up_weight, "dp", axis=1, tiled=True),
        lax.all_gather(down_weight, "dp", axis=2, tiled=True),
    )
    spatial_index = spatial_table()
    joint_index = joint_table()
    spatial_matrix = spatial_bias.astype(jnp.float32)[:, spatial_index]
    joint_matrix = joint_bias.astype(jnp.float32)[:, joint_index]
    current = latents.astype(jnp.float32)
    stored = []
    for which_block in range(2):
        is_joint = which_block == 1
        window = WIN_T if is_joint else WIN_S
        bias_matrix = joint_matrix if is_joint else spatial_matrix
        mask_keys = key_valid if is_joint else None
        block_mod = own_mod[which_block][:, :, None, None, None, :]
        normed_one, inverse_one = normalize(current)
        moved_one = (normed_one * (1.0 + block_mod[:, 1]) + block_mod[:, 0]).astype(jnp.bfloat16)
        gathered_one = gather_rows(moved_one)
        projected = jnp.einsum(
            "cfyxd,dkh->cfyxkh",
            gathered_one,
            w_qkv[which_block],
            preferred_element_type=jnp.float32,
        ).astype(jnp.bfloat16)
        windows = to_windows(
            projected.reshape(clip_count, frames, side_cells, side_cells, 3 * local_width),
            window,
            is_joint,
        )
        windows = windows.reshape(windows.shape[0], windows.shape[1], 3, heads_local, HEAD_DIM)
        scores = attention_scores(windows[:, :, 0], windows[:, :, 1], bias_matrix, mask_keys)
        row_max = jnp.max(scores, axis=-1, keepdims=True)
        log_total = row_max + jnp.log(jnp.sum(jnp.exp(scores - row_max), axis=-1, keepdims=True))
        probs_low = jnp.exp(scores - log_total).astype(jnp.bfloat16)
        mixed_win = jnp.einsum(
            "nhqk,nkhe->nqhe", probs_low, windows[:, :, 2], preferred_element_type=jnp.float32
        ).astype(jnp.bfloat16)
        mixed_rows = from_windows(
            mixed_win.reshape(mixed_win.shape[0], mixed_win.shape[1], local_width),
            clip_count,
            frames,
            side_cells,
            window,
            is_joint,
        )
        branch_one = sum_rows(
            jnp.einsum(
                "cfyxk,kd->cfyxd",
                mixed_rows,
                w_out[which_block],
                preferred_element_type=jnp.float32,
            )
        )
        after_attn = current + frame_mask * block_mod[:, 2] * branch_one
        normed_two, inverse_two = normalize(after_attn)
        moved_two = (normed_two * (1.0 + block_mod[:, 4]) + block_mod[:, 3]).astype(jnp.bfloat16)
        gathered_two = gather_rows(moved_two)
        hidden = jnp.einsum(
            "cfyxd,dk->cfyxk", gathered_two, w_up[which_block], preferred_element_type=jnp.float32
        )
        activated = exact_gelu(hidden).astype(jnp.bfloat16)
        branch_two = sum_rows(
            jnp.einsum(
                "cfyxk,kd->cfyxd",
                activated,
                w_down[which_block],
                preferred_element_type=jnp.float32,
            )
        )
        current = after_attn + frame_mask * block_mod[:, 5] * branch_two
        stored.append(
            (
                normed_one,
                inverse_one,
                moved_one,
                gathered_one,
                windows,
                log_total,
                mixed_rows,
                branch_one,
                normed_two,
                inverse_two,
                moved_two,
                gathered_two,
                hidden,
                activated,
                branch_two,
            )
        )
    grad_state = cotangent.astype(jnp.float32)
    mod_grads = []
    qkv_grads = []
    out_grads = []
    up_grads = []
    down_grads = []
    table_parts = []
    for which_block in (1, 0):
        is_joint = which_block == 1
        window = WIN_T if is_joint else WIN_S
        bias_matrix = joint_matrix if is_joint else spatial_matrix
        mask_keys = key_valid if is_joint else None
        block_mod = own_mod[which_block][:, :, None, None, None, :]
        (
            normed_one,
            inverse_one,
            moved_one,
            gathered_one,
            windows,
            log_total,
            mixed_rows,
            branch_one,
            normed_two,
            inverse_two,
            moved_two,
            gathered_two,
            hidden,
            activated,
            branch_two,
        ) = stored[which_block]
        grad_gate_two = jnp.sum(frame_mask * grad_state * branch_two, axis=(1, 2, 3))
        grad_rows = gather_grads((frame_mask * block_mod[:, 5] * grad_state).astype(jnp.bfloat16))
        down_grads.append(
            jnp.einsum("cfyxk,cfyxd->kd", activated, grad_rows, preferred_element_type=jnp.float32)
        )
        grad_act = jnp.einsum(
            "cfyxd,kd->cfyxk", grad_rows, w_down[which_block], preferred_element_type=jnp.float32
        )
        grad_hidden = jax.vjp(exact_gelu, hidden)[1](grad_act)[0].astype(jnp.bfloat16)
        inputs_two = inputs_again(moved_two)
        up_grads.append(
            jnp.einsum(
                "cfyxd,cfyxk->dk", inputs_two, grad_hidden, preferred_element_type=jnp.float32
            )
        )
        grad_moved = input_sums(
            jnp.einsum(
                "cfyxk,dk->cfyxd",
                grad_hidden,
                w_up[which_block],
                preferred_element_type=jnp.float32,
            )
        )
        grad_shift_two = jnp.sum(grad_moved, axis=(1, 2, 3))
        grad_scale_two = jnp.sum(grad_moved * normed_two, axis=(1, 2, 3))
        grad_state = grad_state + norm_back(
            grad_moved * (1.0 + block_mod[:, 4]), normed_two, inverse_two
        )
        grad_gate_one = jnp.sum(frame_mask * grad_state * branch_one, axis=(1, 2, 3))
        grad_rows = gather_grads((frame_mask * block_mod[:, 2] * grad_state).astype(jnp.bfloat16))
        out_grads.append(
            jnp.einsum("cfyxk,cfyxd->kd", mixed_rows, grad_rows, preferred_element_type=jnp.float32)
        )
        grad_mixed = jnp.einsum(
            "cfyxd,kd->cfyxk", grad_rows, w_out[which_block], preferred_element_type=jnp.float32
        ).astype(jnp.bfloat16)
        grad_win = to_windows(grad_mixed, window, is_joint)
        grad_win = grad_win.reshape(grad_win.shape[0], grad_win.shape[1], heads_local, HEAD_DIM)
        query_part = windows[:, :, 0]
        key_part = windows[:, :, 1]
        value_part = windows[:, :, 2]
        probs_full = jnp.exp(
            attention_scores(query_part, key_part, bias_matrix, mask_keys) - log_total
        )
        grad_value = jnp.einsum(
            "nhqk,nqhe->nkhe",
            probs_full.astype(jnp.bfloat16),
            grad_win,
            preferred_element_type=jnp.float32,
        ).astype(jnp.bfloat16)
        grad_probs = jnp.einsum(
            "nqhe,nkhe->nhqk", grad_win, value_part, preferred_element_type=jnp.float32
        )
        row_dot = jnp.sum(probs_full * grad_probs, axis=-1, keepdims=True)
        grad_scores = (probs_full * (grad_probs - row_dot)).astype(jnp.bfloat16)
        bias_sum = jnp.sum(grad_scores.astype(jnp.float32), axis=0)
        if is_joint:
            table_parts.append(
                jnp.zeros((heads_local, joint_bias.shape[1]), jnp.float32)
                .at[:, joint_index]
                .add(bias_sum)
            )
        else:
            table_parts.append(
                jnp.zeros((heads_local, spatial_bias.shape[1]), jnp.float32)
                .at[:, spatial_index]
                .add(bias_sum)
            )
        grad_query = (
            jnp.einsum("nhqk,nkhe->nqhe", grad_scores, key_part, preferred_element_type=jnp.float32)
            * HEAD_DIM ** (-0.5)
        ).astype(jnp.bfloat16)
        grad_key = (
            jnp.einsum(
                "nhqk,nqhe->nkhe", grad_scores, query_part, preferred_element_type=jnp.float32
            )
            * HEAD_DIM ** (-0.5)
        ).astype(jnp.bfloat16)
        stacked = jnp.stack([grad_query, grad_key, grad_value], axis=2).reshape(
            grad_query.shape[0], grad_query.shape[1], 3 * local_width
        )
        grad_projected = from_windows(
            stacked, clip_count, frames, side_cells, window, is_joint
        ).reshape(clip_count, frames, side_cells, side_cells, 3, local_width)
        inputs_one = inputs_again(moved_one)
        qkv_grads.append(
            jnp.einsum(
                "cfyxd,cfyxkh->dkh", inputs_one, grad_projected, preferred_element_type=jnp.float32
            )
        )
        grad_moved = input_sums(
            jnp.einsum(
                "cfyxkh,dkh->cfyxd",
                grad_projected,
                w_qkv[which_block],
                preferred_element_type=jnp.float32,
            )
        )
        grad_shift_one = jnp.sum(grad_moved, axis=(1, 2, 3))
        grad_scale_one = jnp.sum(grad_moved * normed_one, axis=(1, 2, 3))
        grad_state = grad_state + norm_back(
            grad_moved * (1.0 + block_mod[:, 1]), normed_one, inverse_one
        )
        mod_grads.append(
            jnp.stack(
                [
                    grad_shift_one,
                    grad_scale_one,
                    grad_gate_one,
                    grad_shift_two,
                    grad_scale_two,
                    grad_gate_two,
                ],
                axis=1,
            )
        )
    grad_mod = jnp.stack(mod_grads[::-1], axis=0).reshape(2, clip_count, 6 * model_width)
    ordered = (
        grad_mod.reshape(2, clip_count, dp_count, mp_count, col_width)
        .transpose(0, 1, 3, 2, 4)
        .reshape(2, clip_count, 6 * model_width)
    )
    summed_cols = lax.psum_scatter(ordered, "mp", scatter_dimension=2, tiled=True)
    grad_mod_cols = lax.all_to_all(summed_cols, "dp", split_axis=2, concat_axis=1, tiled=True)
    grad_ada_weight = jnp.einsum(
        "cd,bce->bde",
        activity_low.astype(jnp.float32),
        grad_mod_cols,
        precision=lax.Precision.HIGHEST,
    )
    grad_ada_bias = jnp.sum(grad_mod_cols, axis=1)
    grad_mod_block = lax.all_gather(grad_mod_cols, "mp", axis=2, tiled=True)
    activity_part = jnp.einsum(
        "bce,bde->cd", grad_mod_block, ada_cols.astype(jnp.float32), precision=lax.Precision.HIGHEST
    )
    grad_activity = lax.psum(activity_part, "dp")
    grad_condition = jax.vjp(jax.nn.silu, condition)[1](grad_activity)[0]
    grad_time = jnp.dot(
        band_hot.astype(jnp.float32).T, grad_condition, precision=lax.Precision.HIGHEST
    )
    grad_class = jnp.dot(
        class_hot.astype(jnp.float32).T, grad_condition, precision=lax.Precision.HIGHEST
    )
    grad_spatial, grad_joint = lax.psum((table_parts[1], table_parts[0]), "dp")
    grad_qkv, grad_out, grad_up, grad_down = (
        lax.psum_scatter(jnp.stack(qkv_grads[::-1], axis=0), "dp", scatter_dimension=1, tiled=True),
        lax.psum_scatter(jnp.stack(out_grads[::-1], axis=0), "dp", scatter_dimension=2, tiled=True),
        lax.psum_scatter(jnp.stack(up_grads[::-1], axis=0), "dp", scatter_dimension=1, tiled=True),
        lax.psum_scatter(
            jnp.stack(down_grads[::-1], axis=0), "dp", scatter_dimension=2, tiled=True
        ),
    )
    return (
        current,
        grad_state,
        grad_time,
        grad_class,
        grad_ada_weight,
        grad_ada_bias,
        grad_qkv,
        grad_out,
        grad_up,
        grad_down,
        grad_spatial,
        grad_joint,
    )


def solution(mesh):
    placed = (
        P("dp", None, "mp", None, None),
        P("dp", None, "mp", None, None),
        P("dp"),
        P(),
        P(),
        P(),
        P(),
        P(None, None, ("dp", "mp")),
        P(None, ("dp", "mp")),
        P(None, "dp", None, "mp"),
        P(None, "mp", "dp"),
        P(None, "dp", "mp"),
        P(None, "mp", "dp"),
        P("mp", None),
        P("mp", None),
    )
    return jax.shard_map(
        local,
        mesh=mesh,
        in_specs=placed,
        out_specs=(
            P("dp", None, "mp", None, None),
            P("dp", None, "mp", None, None),
            P(),
            P(),
            P(None, None, ("dp", "mp")),
            P(None, ("dp", "mp")),
            P(None, "dp", None, "mp"),
            P(None, "mp", "dp"),
            P(None, "dp", "mp"),
            P(None, "mp", "dp"),
            P("mp", None),
            P("mp", None),
        ),
        check_vma=False,
    )
```

profile of v0, /device:TPU:9, one launch (start us, length us, event | category | flops | bytes accessed | tf_op | source)
XLA Modules:
  0.0 3643.1 jit_solution(1151377836664301898)
XLA Ops:
  15.7 22.3 all-gather.15.cloned.1.call-done
  40.0 22.2 all_gather.54
  64.8 215.9 %gather_fusion = f32[65536,8]{1,0:T(8,128)} fusion(f32[8,961]{0,1:T(8,128)S(1)} %copy.250, s32[65536]{0:T(1024)S(1)} %broadcast_clamp_fusion.1), kind=kCustom, calls=%fused_computation | custom fusion | bytes 4456448 | tf_op jit(solution)/shard_map/gather | solution.py:181
  280.8 19.5 copy.251
  322.2 10.7 reshape_reshape_transpose_reshape_reshape.4
  378.2 33.0 reduce-scatter.42.cloned.1.call-done
  416.4 72.3 %all-gather.27.cloned.1.call-done = bf16[2,2048,1024]{1,0,2:T(2,128)(2,1)} async-done(((bf16[2,2048,64]{1,0,2:T(2,128)(2,1)}), bf16[2,2048,1024]{1,0,2:T(2,128)(2,1)}) %all-gather.27.cloned.1.call-update) | async-done | bytes 8388624 | tf_op jit(solution)/shard_map/all_gather | solution.py:177
  488.8 17.2 fusion.209
  505.9 20.1 copy.366
  526.0 38.3 %all-gather.25.cloned.1.call-done = bf16[2,1024,2048]{2,1,0:T(8,128)(2,1)} async-done(((bf16[2,64,2048]{2,1,0:T(8,128)(2,1)}), bf16[2,1024,2048]{2,1,0:T(8,128)(2,1)}) %all-gather.25.cloned.1.call-update) | async-done | bytes 8388624 | tf_op jit(solution)/shard_map/all_gather | solution.py:176
  564.4 39.7 %all-gather.23.cloned.1.call-done = bf16[1,5,16,16,1024]{4,3,2,1,0:T(8,128)(2,1)} async-done(((bf16[1,5,8,16,1024]{4,3,2,1,0:T(8,128)(2,1)}), bf16[1,5,16,16,1024]{4,3,2,1,0:T(8,128)(2,1)}) %all-gather.23.cloned.1.call-update) | async-done | bytes 2621456 | tf_op jit(solution)/shard_map/all_gather | solution.py:86
  604.0 10.5 fusion.17
  614.6 24.9 multiply_convert_fusion.3
  651.5 37.0 %reduce-scatter.44.cloned.1.call-done = bf16[8,81920]{1,0:T(8,128)(2,1)} async-done(((bf16[16,81920]{1,0:T(8,128)(2,1)}), bf16[8,81920]{1,0:T(8,128)(2,1)}) %reduce-scatter.44.cloned.1.call-update) | async-done | bytes 1310736
  695.0 337.0 %gather_fusion.1 = f32[102400,8]{1,0:T(8,128)} fusion(f32[8,2025]{0,1:T(8,128)S(1)} %copy.263, s32[102400]{0:T(1024)S(1)} %broadcast_clamp_fusion), kind=kCustom, calls=%fused_computation.1 | custom fusion | bytes 6963200 | tf_op jit(solution)/shard_map/gather | solution.py:182
  1032.0 33.3 copy.264
  1080.3 10.1 copy.258
  1090.5 11.6 reshape_reshape.17
  1106.7 10.9 reshape_reshape.18
  1135.3 10.0 fusion.215
  1145.3 8.2 exponential_reduce_fusion
  1153.5 9.0 fusion.156
  1177.4 37.7 %reduce-scatter.46.cloned.1.call-done = bf16[8,81920]{1,0:T(8,128)(2,1)} async-done(((bf16[16,81920]{1,0:T(8,128)(2,1)}), bf16[8,81920]{1,0:T(8,128)(2,1)}) %reduce-scatter.46.cloned.1.call-update) | async-done | bytes 1310736
  1222.8 20.2 copy.371
  1243.0 17.4 all-gather.31.cloned.1.call-done
  1260.5 10.5 fusion.18
  1271.0 24.8 multiply_convert_fusion.2
  1307.3 16.1 add_convert_fusion.1
  1323.5 9.1 convert_bitcast_fusion.1
  1335.8 9.1 reduce-scatter.48.cloned.1.call-done
  1348.1 36.6 %reduce-scatter.50.cloned.1.call-done = bf16[8,81920]{1,0:T(8,128)(2,1)} async-done(((bf16[16,81920]{1,0:T(8,128)(2,1)}), bf16[8,81920]{1,0:T(8,128)(2,1)}) %reduce-scatter.50.cloned.1.call-update) | async-done | bytes 1310736
  1392.5 39.1 %all-gather.35.cloned.1.call-done = bf16[1,5,16,16,1024]{4,3,2,1,0:T(8,128)(2,1)} async-done(((bf16[1,5,8,16,1024]{4,3,2,1,0:T(8,128)(2,1)}), bf16[1,5,16,16,1024]{4,3,2,1,0:T(8,128)(2,1)}) %all-gather.35.cloned.1.call-update) | async-done | bytes 2621456 | tf_op jit(solution)/shard_map/all_gather | solution.py:96
  1441.4 8.1 fusion.153
  1449.5 10.3 multiply_reduce_fusion
  1459.8 13.7 convert_reduce_fusion
  1480.3 9.9 copy.276
  1490.2 11.5 reshape_reshape.21
  1506.2 12.1 reshape.742
  1518.3 7.8 fusion.82
  1529.5 37.7 %reduce-scatter.52.cloned.1.call-done = bf16[8,81920]{1,0:T(8,128)(2,1)} async-done(((bf16[16,81920]{1,0:T(8,128)(2,1)}), bf16[8,81920]{1,0:T(8,128)(2,1)}) %reduce-scatter.52.cloned.1.call-update) | async-done | bytes 1310736
  1574.0 39.2 %all-gather.37.cloned.1.call-done = bf16[1,5,16,16,1024]{4,3,2,1,0:T(8,128)(2,1)} async-done(((bf16[1,5,8,16,1024]{4,3,2,1,0:T(8,128)(2,1)}), bf16[1,5,16,16,1024]{4,3,2,1,0:T(8,128)(2,1)}) %all-gather.37.cloned.1.call-update) | async-done | bytes 2621456 | tf_op jit(solution)/shard_map/all_gather | solution.py:96
  1613.2 15.8 add_convert_fusion
  1629.0 9.1 convert_bitcast_fusion
  1641.3 37.7 %reduce-scatter.54.cloned.1.call-done = bf16[8,81920]{1,0:T(8,128)(2,1)} async-done(((bf16[16,81920]{1,0:T(8,128)(2,1)}), bf16[8,81920]{1,0:T(8,128)(2,1)}) %reduce-scatter.54.cloned.1.call-update) | async-done | bytes 1310736
  1691.7 10.4 convolution_bitcast_fusion
  1702.2 31.6 copy.339
  1733.8 543.2 %scatter_custom_fusion.1 = f32[8,2025]{0,1:T(8,128)} fusion(s32[102400]{0:T(1024)} %constant.150, f32[102400,8]{1,0:T(8,128)} %bitcast.535, f32[]{:T(128)} %constant.52.clone.1), kind=kCustom, calls=%fused_computation.259 | custom fusion | flops 819200 | bytes 65312 | tf_op jit(solution)/shard_map/scatter-add | solution.py:355
  2295.2 7.9 fusion.162
  2303.1 8.2 multiply_reduce_fusion.1
  2311.3 9.2 convert_reduce_fusion.1
  2361.2 10.2 pad_maximum_fusion.1
  2371.4 25.5 copy.298
  2408.5 39.1 %reduce-scatter.58.cloned.1.call-done = f32[3072,2]{1,0:T(8,128)} async-done(((f32[6144,2]{1,0:T(8,128)}), f32[3072,2]{1,0:T(8,128)}) %reduce-scatter.58.cloned.1.call-update) | async-done | bytes 24592
  2448.1 16.3 reduce.44
  2487.2 16.2 copy.300
  2503.4 348.3 %scatter_custom_fusion = f32[8,961]{0,1:T(8,128)} fusion(s32[65536]{0:T(1024)} %constant.143, f32[65536,8]{1,0:T(8,128)} %copy.300, f32[]{:T(128)} %constant.52.clone.1), kind=kCustom, calls=%fused_computation.262 | custom fusion | flops 524288 | bytes 31264 | tf_op jit(solution)/shard_map/scatter-add | solution.py:361
  2864.6 8.6 convolution_bitcast_fusion.2
  2873.3 7.7 convolution_bitcast_fusion.3
  2889.1 9.6 fusion.49
  2903.1 9.5 pad_maximum_fusion.2
  2914.5 30.4 all-reduce.7.cloned.1.call-done
  2956.1 359.6 %all-reduce.9.cloned.1.call-done = (f32[16,1024]{1,0:T(8,128)}, f32[2,512,1024]{1,0,2:T(2,128)}, f32[2,2048,1024]{1,0,2:T(2,128)}) async-done(((f32[16,1024]{1,0:T(8,128)}, f32[2,512,1024]{1,0,2:T(2,128)}, f32[2,2048,1024]{1,0,2:T(2,128)}), (f32[16,1024]{1,0:T(8,128)}, f32[2,512,1024]{1,0,2:T(2,128)}, f32[2,2048,1024]{1,0,2:T(2,128)})) %all-reduce.9.cloned.1.call-update) | async-done | bytes 21037072 | tf_op jit(solution)/shard_map/psum | solution.py:430
  3322.5 175.1 %reduce-scatter.40.cloned.1.call-done = f32[2,64,2048]{2,1,0:T(8,128)} async-done(((f32[2,1024,2048]{2,1,0:T(8,128)}), f32[2,64,2048]{2,1,0:T(8,128)}) %reduce-scatter.40.cloned.1.call-update) | async-done | bytes 1048592 | tf_op jit(solution)/shard_map/reduce_scatter | solution.py:442
  3497.6 138.8 %reduce-scatter.38.cloned.1.call-done = f32[2,64,3,512]{3,1,2,0:T(8,128)} async-done(((f32[2,1024,3,512]{3,1,2,0:T(8,128)}), f32[2,64,3,512]{3,1,2,0:T(8,128)}) %reduce-scatter.38.cloned.1.call-update) | async-done | bytes 786448 | tf_op jit(solution)/shard_map/reduce_scatter | solution.py:440
  (486 shorter events, 373.1 us)
Async XLA Ops:
  7.2 30.8 all-gather.15.cloned.1.call-start
  8.0 292.3 %all-gather.21.cloned.1.call-start = ((), (), s32[]{:S(2)}) async-start(), calls=%async_computation.15 | async-start | bytes 2228224 | tf_op jit(solution)/shard_map/all_gather | solution.py:175
  9.7 303.2 %all-gather.17.cloned.1.call-start = ((), (), s32[]{:S(2)}) async-start(), calls=%async_computation.13 | async-start | bytes 3932160 | tf_op jit(solution)/shard_map/all_gather | solution.py:86
  14.8 49.2 %copy-start.67 = (f32[5,8,16]{2,1,0:T(8,128)}, f32[5,8,16]{2,1,0:T(8,128)S(1)}, u32[]{:S(2)}) copy-start(f32[5,8,16]{2,1,0:T(8,128)S(1)} %broadcast_multiply_fusion.15) | copy-start | bytes 7684
  15.3 48.7 %copy-start.75 = (f32[5,8,16]{2,1,0:T(8,128)}, f32[5,8,16]{2,1,0:T(8,128)S(1)}, u32[]{:S(2)}) copy-start(f32[5,8,16]{2,1,0:T(8,128)S(1)} %add_rsqrt_fusion.3) | copy-start | bytes 7684
  15.7 48.3 %copy-start.62 = (f32[16,1024]{1,0:T(8,128)}, f32[16,1024]{1,0:T(8,128)S(1)}, u32[]{:S(2)}) copy-start(f32[16,1024]{1,0:T(8,128)S(1)} %convolution_add_fusion) | copy-start | bytes 196612
  62.3 218.4 %copy-start.87 = (f32[1,1,1,1,1,1024]{5,1,4,3,2,0:T(1,128)}, f32[1,1,1,1,1,1024]{5,1,4,3,2,0:T(1,128)S(1)}, u32[]{:S(2)}) copy-start(f32[1,1,1,1,1,1024]{5,1,4,3,2,0:T(1,128)S(1)} %get-tuple-element.141) | copy-start | bytes 12292
  62.3 352.1 %copy-start.94 = (f32[1,1,1,1,1,1024]{5,1,4,3,2,0:T(1,128)}, f32[1,1,1,1,1,1024]{5,1,4,3,2,0:T(1,128)S(1)}, u32[]{:S(2)}) copy-start(f32[1,1,1,1,1,1024]{5,1,4,3,2,0:T(1,128)S(1)} %get-tuple-element.139) | copy-start | bytes 12292
  64.0 249.0 %all-gather.19.cloned.1.call-start = ((), (), s32[]{:S(2)}) async-start(), calls=%async_computation.14 | async-start | bytes 6684672 | tf_op jit(solution)/shard_map/all_gather | solution.py:174
  64.6 346.6 %reduce-scatter.42.cloned.1.call-start = ((), (), s32[]{:S(2)}) async-start(), calls=%async_computation.27 | async-start | bytes 3932160
  375.0 113.8 %all-gather.27.cloned.1.call-start = ((), (), s32[]{:S(2)}) async-start(), calls=%async_computation.18 | async-start | bytes 8912896 | tf_op jit(solution)/shard_map/all_gather | solution.py:177
  376.4 188.0 %all-gather.25.cloned.1.call-start = ((), (), s32[]{:S(2)}) async-start(), calls=%async_computation.17 | async-start | bytes 8912896 | tf_op jit(solution)/shard_map/all_gather | solution.py:176
  377.1 226.9 %all-gather.23.cloned.1.call-start = ((), (), s32[]{:S(2)}) async-start(), calls=%async_computation.16 | async-start | bytes 3932160 | tf_op jit(solution)/shard_map/all_gather | solution.py:86
  378.0 35.7 copy-start.110
  378.1 314.2 %copy-start.90 = (f32[1,1,1,1,1,1024]{5,1,4,3,2,0:T(1,128)}, f32[1,1,1,1,1,1024]{5,1,4,3,2,0:T(1,128)S(1)}, u32[]{:S(2)}) copy-start(f32[1,1,1,1,1,1024]{5,1,4,3,2,0:T(1,128)S(1)} %get-tuple-element.135) | copy-start | bytes 12292
  378.2 312.6 %copy-start.56 = (f32[5,1024]{1,0:T(8,128)}, f32[5,1024]{1,0:T(8,128)S(1)}, u32[]{:S(2)}) copy-start(f32[5,1024]{1,0:T(8,128)S(1)} %get-tuple-element.146) | copy-start | bytes 61444
  378.2 312.6 %copy-start.82 = (f32[5,1024]{1,0:T(8,128)}, f32[5,1024]{1,0:T(8,128)S(1)}, u32[]{:S(2)}) copy-start(f32[5,1024]{1,0:T(8,128)S(1)} %get-tuple-element.144) | copy-start | bytes 61444
  414.5 91.5 %copy-start.78 = (f32[5,8,16]{2,1,0:T(8,128)}, f32[5,8,16]{2,1,0:T(8,128)S(1)}, u32[]{:S(2)}) copy-start(f32[5,8,16]{2,1,0:T(8,128)S(1)} %add_rsqrt_fusion.2) | copy-start | bytes 7684
  416.4 272.2 %reduce-scatter.44.cloned.1.call-start = ((), (), s32[]{:S(2)}) async-start(), calls=%async_computation.28 | async-start | bytes 3932160
  650.8 422.6 %all-gather.29.cloned.1.call-start = ((), (), s32[]{:S(2)}) async-start(), calls=%async_computation.19 | async-start | bytes 3932160 | tf_op jit(solution)/shard_map/all_gather | solution.py:86
  692.2 339.8 %copy-start.80 = (f32[5,8,16]{2,1,0:T(8,128)}, f32[5,8,16]{2,1,0:T(8,128)S(1)}, u32[]{:S(2)}) copy-start(f32[5,8,16]{2,1,0:T(8,128)S(1)} %add_rsqrt_fusion.1) | copy-start | bytes 7684
  694.9 520.2 %reduce-scatter.46.cloned.1.call-start = ((), (), s32[]{:S(2)}) async-start(), calls=%async_computation.29 | async-start | bytes 3932160
  1032.0 34.0 copy-start.115
  1032.0 37.2 %copy-start.46 = (bf16[1,512,1024]{1,0,2:T(2,128)(2,1)S(1)}, bf16[1,512,1024]{1,0,2:T(2,128)(2,1)}, u32[]{:S(2)}) copy-start(bf16[1,512,1024]{1,0,2:T(2,128)(2,1)} %get-tuple-element.129) | copy-start | bytes 3145732
  1177.3 39.8 %copy-start.10 = (f32[1,5,8,16,1024]{4,3,2,1,0:T(8,128)S(1)}, f32[1,5,8,16,1024]{4,3,2,1,0:T(8,128)}, u32[]{:S(2)}) copy-start(f32[1,5,8,16,1024]{4,3,2,1,0:T(8,128)} %copy-done.9) | copy-start | bytes 7864324
  1177.3 83.1 %all-gather.31.cloned.1.call-start = ((), (), s32[]{:S(2)}) async-start(), calls=%async_computation.20 | async-start | bytes 3932160 | tf_op jit(solution)/shard_map/all_gather | solution.py:86
  1221.3 86.0 %all-gather.33.cloned.1.call-start = ((), (), s32[]{:S(2)}) async-start(), calls=%async_computation.21 | async-start | bytes 3932160 | tf_op jit(solution)/shard_map/all_gather | solution.py:96
  1222.8 122.2 %reduce-scatter.48.cloned.1.call-start = ((), (), s32[]{:S(2)}) async-start(), calls=%async_computation.30 | async-start | bytes 3932160
  1307.2 77.5 %reduce-scatter.50.cloned.1.call-start = ((), (), s32[]{:S(2)}) async-start(), calls=%async_computation.31 | async-start | bytes 3932160
  1335.8 51.1 %copy-start.13 = (f32[1,5,8,16,1024]{4,3,2,1,0:T(8,128)S(1)}, f32[1,5,8,16,1024]{4,3,2,1,0:T(8,128)}, u32[]{:S(2)}) copy-start(f32[1,5,8,16,1024]{4,3,2,1,0:T(8,128)} %copy-done.12) | copy-start | bytes 7864324
  1335.8 95.9 %all-gather.35.cloned.1.call-start = ((), (), s32[]{:S(2)}) async-start(), calls=%async_computation.22 | async-start | bytes 3932160 | tf_op jit(solution)/shard_map/all_gather | solution.py:96
  1392.4 174.8 %reduce-scatter.52.cloned.1.call-start = ((), (), s32[]{:S(2)}) async-start(), calls=%async_computation.32 | async-start | bytes 3932160
  1529.4 40.0 %copy-start.11 = (f32[1,5,8,16,1024]{4,3,2,1,0:T(8,128)S(1)}, f32[1,5,8,16,1024]{4,3,2,1,0:T(8,128)}, u32[]{:S(2)}) copy-start(f32[1,5,8,16,1024]{4,3,2,1,0:T(8,128)} %copy-done.9) | copy-start | bytes 7864324
  1529.4 40.0 %copy-start.73 = (f32[5,8,16]{2,1,0:T(8,128)S(1)}, f32[5,8,16]{2,1,0:T(8,128)}, u32[]{:S(2)}) copy-start(f32[5,8,16]{2,1,0:T(8,128)} %copy-done.72) | copy-start | bytes 7684
  1529.4 40.0 %copy-start.81 = (f32[5,8,16]{2,1,0:T(8,128)S(1)}, f32[5,8,16]{2,1,0:T(8,128)}, u32[]{:S(2)}) copy-start(f32[5,8,16]{2,1,0:T(8,128)} %copy-done.80) | copy-start | bytes 7684
  1529.4 40.0 %copy-start.91 = (f32[1,1,1,1,1,1024]{5,1,4,3,2,0:T(1,128)S(1)}, f32[1,1,1,1,1,1024]{5,1,4,3,2,0:T(1,128)}, u32[]{:S(2)}) copy-start(f32[1,1,1,1,1,1024]{5,1,4,3,2,0:T(1,128)} %copy-done.90) | copy-start | bytes 12292
  1529.5 83.7 %all-gather.37.cloned.1.call-start = ((), (), s32[]{:S(2)}) async-start(), calls=%async_computation.23 | async-start | bytes 3932160 | tf_op jit(solution)/shard_map/all_gather | solution.py:96
  1573.9 105.1 %reduce-scatter.54.cloned.1.call-start = ((), (), s32[]{:S(2)}) async-start(), calls=%async_computation.33 | async-start | bytes 3932160
  1641.2 40.0 %copy-start.4 = (bf16[1,5,8,16,1024]{4,3,2,1,0:T(8,128)(2,1)S(1)}, bf16[1,5,8,16,1024]{4,3,2,1,0:T(8,128)(2,1)}, u32[]{:S(2)}) copy-start(bf16[1,5,8,16,1024]{4,3,2,1,0:T(8,128)(2,1)} %param.23) | copy-start | bytes 3932164
  1641.2 40.0 %copy-start.16 = (bf16[1,8,80,1024]{3,2,1,0:T(8,128)(2,1)S(1)}, bf16[1,8,80,1024]{3,2,1,0:T(8,128)(2,1)}, u32[]{:S(2)}) copy-start(bf16[1,8,80,1024]{3,2,1,0:T(8,128)(2,1)} %copy-done.14) | copy-start | bytes 3932164
  1641.2 40.0 %copy-start.57 = (f32[5,1024]{1,0:T(8,128)S(1)}, f32[5,1024]{1,0:T(8,128)}, u32[]{:S(2)}) copy-start(f32[5,1024]{1,0:T(8,128)} %copy-done.56) | copy-start | bytes 61444
  1641.2 40.0 %copy-start.71 = (f32[5,8,16]{2,1,0:T(8,128)S(1)}, f32[5,8,16]{2,1,0:T(8,128)}, u32[]{:S(2)}) copy-start(f32[5,8,16]{2,1,0:T(8,128)} %copy-done.70) | copy-start | bytes 7684
  1641.2 40.0 %copy-start.79 = (f32[5,8,16]{2,1,0:T(8,128)S(1)}, f32[5,8,16]{2,1,0:T(8,128)}, u32[]{:S(2)}) copy-start(f32[5,8,16]{2,1,0:T(8,128)} %copy-done.78) | copy-start | bytes 7684
  1641.2 40.0 %copy-start.95 = (f32[1,1,1,1,1,1024]{5,1,4,3,2,0:T(1,128)S(1)}, f32[1,1,1,1,1,1024]{5,1,4,3,2,0:T(1,128)}, u32[]{:S(2)}) copy-start(f32[1,1,1,1,1,1024]{5,1,4,3,2,0:T(1,128)} %copy-done.94) | copy-start | bytes 12292
  1641.3 640.4 %all-gather.39.cloned.1.call-start = ((), (), s32[]{:S(2)}) async-start(), calls=%async_computation.24 | async-start | bytes 3932160 | tf_op jit(solution)/shard_map/all_gather | solution.py:96
  1691.7 705.5 %reduce-scatter.56.cloned.1.call-start = ((), (), s32[]{:S(2)}) async-start(), calls=%async_computation.34 | async-start | bytes 3932160
  1702.2 574.8 %copy-start.51 = (bf16[1,5,2,8,2,8,512]{6,5,4,3,2,1,0:T(8,128)(2,1)S(1)}, bf16[1,5,2,8,2,8,512]{6,5,4,3,2,1,0:T(8,128)(2,1)}, u32[]{:S(2)}) copy-start(bf16[1,5,2,8,2,8,512]{6,5,4,3,2,1,0:T(8,128)(2,1)} %copy-done.50) | copy-start | bytes 3932164
  2353.5 94.1 %reduce-scatter.58.cloned.1.call-start = ((), (), s32[]{:S(2)}) async-start(), calls=%async_computation.35 | async-start | bytes 4718592
  2408.5 65.3 %copy-start.45 = (f32[1,512,1024]{2,1,0:T(8,128)S(1)}, f32[1,512,1024]{2,1,0:T(8,128)}, u32[]{:S(2)}) copy-start(f32[1,512,1024]{2,1,0:T(8,128)} %fusion.128) | copy-start | bytes 6291460
  2467.4 384.4 %all-to-all-start = ((f32[16,1,384]{2,1,0:T(1,128)}), f32[16,1,384]{2,1,0:T(1,128)S(1)}, u32[]{:S(2)}, u32[]{:S(2)}) async-start(f32[16,1,384]{2,1,0:T(1,128)} %reshape.873), calls=%async_computation | async-start | bytes 49152 | tf_op jit(solution)/shard_map/all_to_all | solution.py:418
  2473.8 471.1 %all-reduce.7.cloned.1.call-start = ((), (), s32[]{:S(2)}) async-start(), calls=%async_computation.36 | async-start | bytes 3072000 | tf_op jit(solution)/shard_map/psum | solution.py:438
  2503.4 359.7 %copy-start.47 = (bf16[2,1024,384]{1,2,0:T(8,128)(2,1)S(1)}, bf16[2,1024,384]{1,2,0:T(8,128)(2,1)}, u32[]{:S(2)}) copy-start(bf16[2,1024,384]{1,2,0:T(8,128)(2,1)} %all-gather.15.cloned.1.call-done) | copy-start | bytes 4718596
  2851.7 463.9 %all-reduce.9.cloned.1.call-start = ((), (), s32[]{:S(2)}) async-start(), calls=%async_computation.37 | async-start | bytes 42074112 | tf_op jit(solution)/shard_map/psum | solution.py:430
  2864.6 633.0 %reduce-scatter.40.cloned.1.call-start = ((), (), s32[]{:S(2)}) async-start(), calls=%async_computation.26 | async-start | bytes 17825792 | tf_op jit(solution)/shard_map/reduce_scatter | solution.py:442
  2887.4 748.9 %reduce-scatter.38.cloned.1.call-start = ((), (), s32[]{:S(2)}) async-start(), calls=%async_computation.25 | async-start | bytes 13369344 | tf_op jit(solution)/shard_map/reduce_scatter | solution.py:440
  2912.7 36.2 copy-start.86
  2912.7 36.2 copy-start.85
  2912.7 36.2 copy-start.6
  2912.7 36.2 copy-start.69
  2912.7 36.2 copy-start.77
  2912.7 36.2 copy-start.89
  2954.1 366.2 %copy-start.113 = (s32[16]{0:T(128)S(1)}, s32[16]{0:T(128)}, u32[]{:S(2)}) copy-start(s32[16]{0:T(128)} %param.26) | copy-start | bytes 196
  2954.1 682.2 %copy-start.1 = (bf16[101,1024]{1,0:T(8,128)(2,1)S(1)}, bf16[101,1024]{1,0:T(8,128)(2,1)}, u32[]{:S(2)}) copy-start(bf16[101,1024]{1,0:T(8,128)(2,1)} %param.29) | copy-start | bytes 620548
  2956.1 365.2 %copy-start.109 = (s32[16]{0:T(128)S(1)}, s32[16]{0:T(128)}, u32[]{:S(2)}) copy-start(s32[16]{0:T(128)} %param.27) | copy-start | bytes 196
  (92 other events, 911.7 us)
Sparse Core Ops, SparseCore 0:
  9.6 28.3 all-gather.14
  40.8 41.7 all-gather.20
  84.7 38.3 all-gather.16
  125.1 62.3 all-gather.18
  375.1 36.0 reduce-scatter.41
  414.0 74.7 all-gather.26
  491.2 73.1 all-gather.24
  566.6 37.4 all-gather.22
  651.0 37.5 reduce-scatter.43
  695.0 39.0 all-gather.28
  1177.4 37.6 reduce-scatter.45
  1221.4 39.0 all-gather.30
  1262.1 39.0 all-gather.32
  1307.3 37.5 reduce-scatter.47
  1347.0 37.6 reduce-scatter.49
  1392.6 39.0 all-gather.34
  1529.6 37.5 reduce-scatter.51
  1574.1 39.0 all-gather.36
  1641.4 37.5 reduce-scatter.53
  1691.8 39.0 all-gather.38
  2353.6 37.5 reduce-scatter.55
  2404.0 43.5 reduce-scatter.57
  2851.8 93.0 all-reduce.6
  2950.5 365.0 all-reduce.8
  3320.3 177.2 reduce-scatter.39
  3502.1 134.2 reduce-scatter.37
where the time goes:
time: 3660 us; the launch traced here: 3640 us
  waiting for transfers between devices  1240 us (34%)
  other arithmetic  1070 us (29%)
  local copies, waits for them, and re-layouts  1020 us (28%)
  matrix products  260 us (7%)
    scatter-add x1, other arithmetic, local(): table_parts.append(jnp.zeros((heads_local, joint_bias.shape[1]), jnp.floa...  543 us
    gather x2, local copies, waits for them, and re-layouts, local(): joint_matrix = joint_bias.astype(jnp.float32)[:, joint_index]  370 us
    psum x1, waiting for transfers between devices, local(): grad_activity = lax.psum(activity_part, 'dp')  360 us
    scatter-add x1, other arithmetic, local(): table_parts.append(jnp.zeros((heads_local, spatial_bias.shape[1]), jnp.fl...  348 us
    unnamed x35, waiting for transfers between devices  270 us
    gather x2, local copies, waits for them, and re-layouts, local(): spatial_matrix = spatial_bias.astype(jnp.float32)[:, spatial_index]  235 us
    reduce_scatter x1, waiting for transfers between devices, local(): lax.psum_scatter(jnp.stack(up_grads[::-1], axis=0), 'dp', scatter_dimensi...  175 us
    unnamed x306, local copies, waits for them, and re-layouts  154 us
  transfers between devices with their start and end apart: 27, of which 19 were waited for; matrix products, arithmetic and copies ran while one was open for 51% of the time, Pallas kernels for 0%

commit v1 on v0

--- a/solution.py
+++ b/solution.py
@@ -2,6 +2,9 @@
 import jax.numpy as jnp
 import numpy as np
 from jax import lax
+from jax.experimental import pallas as pl
+from jax.experimental.pallas import tpu as pltpu
+from jax.sharding import Mesh
 from jax.sharding import PartitionSpec as P
 
 HEAD_DIM = 64
@@ -460,7 +463,7 @@
     )
 
 
-def solution(mesh):
+def solution_any(mesh):
     placed = (
         P("dp", None, "mp", None, None),
         P("dp", None, "mp", None, None),
@@ -498,3 +501,727 @@
         ),
         check_vma=False,
     )
+
+
+low = jnp.bfloat16
+full = jnp.float32
+HALF_ROOT = 0.7071067811865476
+PHI_AT_ZERO = 0.3989422804014327
+MIB = 1024 * 1024
+
+
+def flip(values, axis):
+    return lax.ppermute(values, axis, [(0, 1), (1, 0)])
+
+
+def z_trade(values, step):
+    return lax.ppermute(values, "z", [(place, place ^ step) for place in range(4)])
+
+
+def swap(values):
+    return lax.ppermute(values, ("c", "x"), [(0, 0), (1, 2), (2, 1), (3, 3)])
+
+
+def params(mib, semantics=None):
+    return pltpu.CompilerParams(vmem_limit_bytes=mib * MIB, dimension_semantics=semantics)
+
+
+def place_kernel(where, own, from_y, from_x, far_lo, far_hi, whole):
+    k = pl.program_id(0)
+    place = where[1] * 2 + where[2]
+    whole[0, place] = own[0]
+    whole[0, place ^ 1] = from_x[0]
+    whole[0, place ^ 2] = from_y[0]
+
+    @pl.when(k < 2)
+    def _():
+        whole[0, place ^ 3] = far_lo[0]
+
+    @pl.when(k >= 2)
+    def _():
+        whole[0, place ^ 3] = far_hi[0]
+
+
+def gather_piece(shard, where):
+    rows, width = shard.shape
+    near = [shard] + [z_trade(shard, k) for k in (1, 2, 3)]
+    own = jnp.stack(near)
+    from_y = flip(own, "y")
+    from_x = flip(own, "x")
+    far_lo = flip(from_y[:2], "x")
+    far_hi = flip(from_x[2:], "y")
+    block = (1, rows, width)
+    whole = pl.pallas_call(
+        place_kernel,
+        grid_spec=pltpu.PrefetchScalarGridSpec(
+            num_scalar_prefetch=1,
+            grid=(4,),
+            in_specs=[pl.BlockSpec(block, lambda k, where: (k, 0, 0))] * 3
+            + [
+                pl.BlockSpec(block, lambda k, where: (jnp.minimum(k, 1), 0, 0)),
+                pl.BlockSpec(block, lambda k, where: (jnp.maximum(k - 2, 0), 0, 0)),
+            ],
+            out_specs=pl.BlockSpec(
+                (1, 4, rows, width), lambda k, where: (where[0] ^ k, 0, 0, 0)
+            ),
+        ),
+        out_shape=jax.ShapeDtypeStruct((4, 4, rows, width), shard.dtype),
+        compiler_params=params(16),
+        cost_estimate=pl.CostEstimate(
+            flops=0, bytes_accessed=2 * 16 * rows * width * 2, transcendentals=0
+        ),
+        name="place_weights",
+    )(where, own, from_y, from_x, far_lo, far_hi)
+    return whole.reshape(16 * rows, width)
+
+
+def scatter_piece(parts, where):
+    own, to_x, to_y, far_lo, far_hi = parts
+    z = where[0]
+    got_x = flip(far_lo, "x")
+    got_y = flip(far_hi, "y")
+    add = lambda a, b: (a.astype(full) + b.astype(full)).astype(low)
+    to_y = jnp.concatenate([add(to_y[:2], got_x), to_y[2:]])
+    to_x = jnp.concatenate([to_x[:2], add(to_x[2:], got_y)])
+    got_y = flip(to_y, "y")
+    got_x = flip(to_x, "x")
+
+    def total(k):
+        pick = lambda a: lax.dynamic_index_in_dim(a, z ^ k, 0, keepdims=False).astype(full)
+        return pick(own) + pick(got_y) + pick(got_x)
+
+    result = total(0)
+    for k in (1, 2, 3):
+        result = result + z_trade(total(k).astype(low), k).astype(full)
+    return swap(result.astype(low)).astype(full)
+
+
+def weight_grad_kernel(where, *refs, pairs, widths):
+    lhs = refs[: 2 * pairs]
+    rhs = refs[2 * pairs : 3 * pairs]
+    own, to_x, to_y, far_lo, far_hi, held = refs[3 * pairs :]
+    z = pl.program_id(0)
+    place = where[1] * 2 + where[2]
+    start = 0
+    for at in range(pairs):
+        first = lhs[2 * at][...].T
+        second = lhs[2 * at + 1][...].T
+        for begin in range(0, widths[at], 512):
+            cols = slice(begin, begin + 512)
+            block = jnp.dot(
+                first, rhs[at][0, :, cols], preferred_element_type=full
+            ) + jnp.dot(second, rhs[at][1, :, cols], preferred_element_type=full)
+            held[:, start + begin : start + begin + 512] = block.astype(low)
+        start += widths[at]
+
+    def part(rel):
+        return held[pl.ds(pl.multiple_of((place ^ rel) * 64, 64), 64), :]
+
+    own[0] = part(0)
+    to_x[0] = part(1)
+    to_y[0] = part(2)
+
+    @pl.when(z < 2)
+    def _():
+        far_lo[0] = part(3)
+
+    @pl.when(z >= 2)
+    def _():
+        far_hi[0] = part(3)
+
+
+def weight_grad(where, *items):
+    pairs = len(items)
+    widths = tuple(item[2].shape[2] for item in items)
+    width = sum(widths)
+    rows, features = items[0][0].shape
+    tile = features // 4
+    quads = jax.ShapeDtypeStruct((4, 64, width), low)
+    twos = jax.ShapeDtypeStruct((2, 64, width), low)
+    lhs_spec = pl.BlockSpec((rows, tile), lambda z: (0, z))
+    return pl.pallas_call(
+        lambda *refs: weight_grad_kernel(*refs, pairs=pairs, widths=widths),
+        grid=(4,),
+        out_shape=[quads, quads, quads, twos, twos],
+        in_specs=[pl.BlockSpec(memory_space=pltpu.SMEM)]
+        + [lhs_spec] * (2 * pairs)
+        + [pl.BlockSpec((2, rows, w), lambda z: (0, 0, 0)) for w in widths],
+        out_specs=[pl.BlockSpec((1, 64, width), lambda z: (z, 0, 0))] * 3
+        + [
+            pl.BlockSpec((1, 64, width), lambda z: (jnp.minimum(z, 1), 0, 0)),
+            pl.BlockSpec((1, 64, width), lambda z: (jnp.maximum(z - 2, 0), 0, 0)),
+        ],
+        scratch_shapes=[pltpu.VMEM((tile, width), low)],
+        compiler_params=params(56),
+        cost_estimate=pl.CostEstimate(
+            flops=4 * rows * features * width,
+            bytes_accessed=4 * rows * (width + features) + 2 * features * width,
+            transcendentals=0,
+        ),
+        name="weight_grad",
+    )(where, *[half for item in items for half in item[:2]], *[item[2] for item in items])
+
+
+def gelu_and_slope(values):
+    bell = jnp.exp(-0.5 * values * values)
+    t = 1.0 / (1.0 + (0.3275911 * HALF_ROOT) * jnp.abs(values))
+    poly = t * (
+        0.254829592
+        + t * (-0.284496736 + t * (1.421413741 + t * (-1.453152027 + t * 1.061405429)))
+    )
+    tail = 0.5 * poly * bell
+    phi = jnp.where(values >= 0, 1.0 - tail, tail)
+    return values * phi, phi + (PHI_AT_ZERO * values) * bell
+
+
+def both_kernel(kind, *refs):
+    weight = refs[2][...]
+    for half in range(2):
+        product = jnp.dot(refs[half][...], weight, preferred_element_type=full)
+        if kind == "gelu":
+            act, slope = gelu_and_slope(product)
+            refs[3][half] = act.astype(low)
+            refs[4][half] = slope.astype(low)
+        elif kind == "slope":
+            refs[4][half] = (product * refs[3][half].astype(full)).astype(low)
+        else:
+            refs[3][half] = product.astype(low)
+
+
+def both_times(kind, own, other, weight, slope=None):
+    rows, depth = own.shape
+    width = weight.shape[1]
+    tile = 256 if kind == "gelu" else 512
+    out_spec = pl.BlockSpec((2, rows, tile), lambda j: (0, 0, j))
+    out = jax.ShapeDtypeStruct((2, rows, width), low)
+    extra = [] if slope is None else [slope]
+    count = 2 if kind == "gelu" else 1
+    return pl.pallas_call(
+        lambda *refs: both_kernel(kind, *refs),
+        grid=(width // tile,),
+        out_shape=[out] * count,
+        in_specs=[pl.BlockSpec((rows, depth), lambda j: (0, 0))] * 2
+        + [pl.BlockSpec((depth, tile), lambda j: (0, j))]
+        + [out_spec] * len(extra),
+        out_specs=[out_spec] * count,
+        compiler_params=params(40),
+        cost_estimate=pl.CostEstimate(
+            flops=4 * rows * depth * width,
+            bytes_accessed=4 * rows * depth + 2 * depth * width + 4 * rows * width * count,
+            transcendentals=0,
+        ),
+        name="both_" + kind,
+    )(own, other, weight, *extra)
+
+
+def one_kernel(values, weight, out):
+    out[...] = lax.dot_general(
+        values[0], weight[...], (((1,), (1,)), ((), ())), preferred_element_type=full
+    ).astype(low)
+
+
+def one_back(values, half, weight):
+    rows, depth = values.shape[1:]
+    width = weight.shape[0]
+    tile = 256
+    return pl.pallas_call(
+        one_kernel,
+        grid=(width // tile,),
+        out_shape=jax.ShapeDtypeStruct((rows, width), low),
+        in_specs=[
+            pl.BlockSpec((1, rows, depth), lambda j: (half, 0, 0)),
+            pl.BlockSpec((tile, depth), lambda j: (j, 0)),
+        ],
+        out_specs=pl.BlockSpec((rows, tile), lambda j: (0, j)),
+        compiler_params=params(40),
+        cost_estimate=pl.CostEstimate(
+            flops=2 * rows * depth * width,
+            bytes_accessed=2 * (rows * depth + depth * width + rows * width),
+            transcendentals=0,
+        ),
+        name="one_back",
+    )(values, weight)
+
+
+def branch_sum(values, weight):
+    away = flip(one_back(values, 1, weight), "c")
+    return one_back(values, 0, weight).astype(full) + away.astype(full)
+
+
+def attend_kernel(count, bias, joined, mixed, probs, *, heads, cells, masked):
+    width = heads * HEAD_DIM
+    values = joined[...].reshape(cells, 3 * width)
+    lead = mixed.shape
+    if masked:
+        column = lax.broadcasted_iota(jnp.int32, (1, cells), 1)
+        shown = column < count[0] * (WIN_T * WIN_T)
+    outs = []
+    for h in range(heads):
+        cols = slice(h * HEAD_DIM, (h + 1) * HEAD_DIM)
+        query = values[:, cols]
+        key = values[:, width + h * HEAD_DIM : width + (h + 1) * HEAD_DIM]
+        value = values[:, 2 * width + h * HEAD_DIM : 2 * width + (h + 1) * HEAD_DIM]
+        scores = lax.dot_general(
+            query, key, (((1,), (1,)), ((), ())), preferred_element_type=full
+        ) * HEAD_DIM ** (-0.5) + bias[h].astype(full)
+        if masked:
+            scores = jnp.where(shown, scores, masked_score)
+        weights = jnp.exp(scores - jnp.max(scores, axis=-1, keepdims=True))
+        share = (weights * (1.0 / jnp.sum(weights, axis=-1, keepdims=True))).astype(low)
+        probs[0, h] = share
+        outs.append(jnp.dot(share, value, preferred_element_type=full).astype(low))
+    mixed[...] = jnp.concatenate(outs, axis=1).reshape(lead)
+
+
+def attend_back_kernel(joined, grad, probs, back, bias_out, total, *, heads, cells, sides):
+    step = pl.program_id(0) * pl.num_programs(1) + pl.program_id(1)
+    width = heads * HEAD_DIM
+    values = joined[...].reshape(cells, 3 * width)
+    grads = grad[...].reshape(cells, width)
+    grads_t = grads.astype(full).T.astype(low)
+    queries_t = values[:, :width].astype(full).T.astype(low)
+    queries, keys_t, values_t = [], [], []
+
+    @pl.when(step == 0)
+    def _():
+        total[...] = jnp.zeros(total.shape, full)
+
+    for h in range(heads):
+        cols = slice(h * HEAD_DIM, (h + 1) * HEAD_DIM)
+        key = values[:, width + h * HEAD_DIM : width + (h + 1) * HEAD_DIM]
+        value = values[:, 2 * width + h * HEAD_DIM : 2 * width + (h + 1) * HEAD_DIM]
+        share = probs[0, h]
+        values_t.append(jnp.dot(grads_t[cols], share, preferred_element_type=full).astype(low))
+        grad_share = lax.dot_general(
+            grads[:, cols], value, (((1,), (1,)), ((), ())), preferred_element_type=full
+        )
+        share_full = share.astype(full)
+        product = share_full * grad_share
+        row_dot = jnp.sum(product, axis=-1, keepdims=True)
+        grad_scores = (product - share_full * row_dot).astype(low)
+
+        total[h] += grad_scores.astype(full)
+        queries.append(
+            (jnp.dot(grad_scores, key, preferred_element_type=full) * HEAD_DIM ** (-0.5)).astype(
+                low
+            )
+        )
+        keys_t.append(
+            (
+                jnp.dot(queries_t[cols], grad_scores, preferred_element_type=full)
+                * HEAD_DIM ** (-0.5)
+            ).astype(low)
+        )
+    key_grads = jnp.concatenate(keys_t, axis=0).astype(full).T.astype(low)
+    value_grads = jnp.concatenate(values_t, axis=0).astype(full).T.astype(low)
+    back[...] = jnp.concatenate(queries + [key_grads, value_grads], axis=1).reshape(back.shape)
+
+    @pl.when(step == pl.num_programs(0) * pl.num_programs(1) - 1)
+    def _():
+        for h in range(heads):
+            for place, spots in enumerate(sides):
+                part = None
+                for row, col in spots:
+                    block = total[h, row * 64 : row * 64 + 64, :][:, col * 64 : col * 64 + 64]
+                    part = block if part is None else part + block
+                bias_out[h, place] = part
+
+
+def spatial_sides():
+    sides = [[] for _ in range(9)]
+    for row in range(4):
+        for col in range(4):
+            place = (row // 2 - col // 2 + 1) * 3 + (row % 2 - col % 2 + 1)
+            sides[place].append((row, col))
+    return sides
+
+
+def joint_sides():
+    sides = [[] for _ in range(2 * FRAMES - 1)]
+    for row in range(FRAMES):
+        for col in range(FRAMES):
+            sides[row - col + FRAMES - 1].append((row, col))
+    return sides
+
+
+def window_specs(is_joint, frames, width):
+    if is_joint:
+        shape, at = (1, frames, 1, 64, width), lambda i, j: (i, 0, j, 0, 0)
+    else:
+        shape, at = (2, 1, 2, 64, width), lambda i, j: (0, j, 0, 0, 0)
+    return pl.BlockSpec(shape, at)
+
+
+def attend(count, bias, joined, is_joint):
+    frames = joined.shape[1]
+    heads, cells = bias.shape[0], bias.shape[1]
+    width = heads * HEAD_DIM
+    grid = (2, 2) if is_joint else (1, frames)
+    number = grid[0] * grid[1]
+    fetch = lambda i, j: (i * grid[1] + j, 0, 0, 0)
+    return pl.pallas_call(
+        lambda *refs: attend_kernel(*refs, heads=heads, cells=cells, masked=is_joint),
+        grid=grid,
+        out_shape=[
+            jax.ShapeDtypeStruct(joined.shape[:4] + (width,), low),
+            jax.ShapeDtypeStruct((number, heads, cells, cells), low),
+        ],
+        in_specs=[
+            pl.BlockSpec(memory_space=pltpu.SMEM),
+            pl.BlockSpec(bias.shape, lambda i, j: (0, 0, 0)),
+            window_specs(is_joint, frames, 3 * width),
+        ],
+        out_specs=[
+            window_specs(is_joint, frames, width),
+            pl.BlockSpec((1, heads, cells, cells), fetch),
+        ],
+        compiler_params=params(48),
+        cost_estimate=pl.CostEstimate(
+            flops=16 * number * heads * cells * cells * HEAD_DIM,
+            bytes_accessed=2 * number * heads * cells * cells,
+            transcendentals=number * heads * cells * cells,
+        ),
+        name="attend_joint" if is_joint else "attend_spatial",
+    )(count, bias, joined)
+
+
+def attend_back(joined, grad, probs, is_joint):
+    frames = joined.shape[1]
+    number, heads, cells, _ = probs.shape
+    width = heads * HEAD_DIM
+    grid = (2, 2) if is_joint else (1, frames)
+    fetch = lambda i, j: (i * grid[1] + j, 0, 0, 0)
+    return pl.pallas_call(
+        lambda *refs: attend_back_kernel(
+            *refs, heads=heads, cells=cells, sides=joint_sides() if is_joint else spatial_sides()
+        ),
+        grid=grid,
+        out_shape=[
+            jax.ShapeDtypeStruct(joined.shape, low),
+            jax.ShapeDtypeStruct((heads, 9, 64, 64), full),
+        ],
+        in_specs=[
+            window_specs(is_joint, frames, 3 * width),
+            window_specs(is_joint, frames, width),
+            pl.BlockSpec((1, heads, cells, cells), fetch),
+        ],
+        out_specs=[
+            window_specs(is_joint, frames, 3 * width),
+            pl.BlockSpec((heads, 9, 64, 64), lambda i, j: (0, 0, 0, 0)),
+        ],
+        scratch_shapes=[pltpu.VMEM((heads, cells, cells), full)],
+        compiler_params=params(56),
+        cost_estimate=pl.CostEstimate(
+            flops=32 * number * heads * cells * cells * HEAD_DIM,
+            bytes_accessed=2 * number * heads * cells * cells,
+            transcendentals=number * heads * cells * cells,
+        ),
+        name="attend_back_joint" if is_joint else "attend_back_spatial",
+    )(joined, grad, probs)
+
+
+def offset_hot():
+    places = np.arange(WIN_T * WIN_T)
+    rows = places[:, None] // WIN_T - places[None, :] // WIN_T + WIN_T - 1
+    cols = places[:, None] % WIN_T - places[None, :] % WIN_T + WIN_T - 1
+    spots = (rows * (2 * WIN_T - 1) + cols).reshape(-1).astype(np.int32)
+    return jnp.arange((2 * WIN_T - 1) ** 2, dtype=jnp.int32)[:, None] == jnp.asarray(spots)[None]
+
+
+def fast_local(
+    latents,
+    cotangent,
+    frame_counts,
+    band_ids,
+    class_ids,
+    time_table,
+    class_table,
+    ada_weight,
+    ada_bias,
+    qkv_weight,
+    out_weight,
+    up_weight,
+    down_weight,
+    spatial_bias,
+    joint_bias,
+):
+    frames = latents.shape[1]
+    model_width = latents.shape[4]
+    heads = spatial_bias.shape[0]
+    width = heads * HEAD_DIM
+    col_width = ada_weight.shape[2]
+    rows = frames * 128
+    z, y, c, x = (lax.axis_index(name) for name in ("z", "y", "c", "x"))
+    where = jnp.stack([z, y, x]).astype(jnp.int32)
+
+    count = swap(frame_counts.astype(full)).astype(jnp.int32)
+
+    def rearranged(values):
+        shaped = values.reshape(frames, 8, 2, 8, model_width).transpose(0, 2, 1, 3, 4)
+        return shaped.reshape(rows, model_width)
+
+    qkv_rows = qkv_weight.reshape(2, -1, 3 * width)
+    out_rows = out_weight.transpose(0, 2, 1)
+    down_rows = down_weight.transpose(0, 2, 1)
+    weights = []
+    for k in range(2):
+        weights.append(
+            [
+                gather_piece(swap(shard), where)
+                for shard in (qkv_rows[k], out_rows[k], up_weight[k], down_rows[k])
+            ]
+        )
+
+    band_hot = (band_ids[:, None] == jnp.arange(BANDS)[None, :]).astype(low)
+    class_hot = (class_ids[:, None] == jnp.arange(CLASSES)[None, :]).astype(low)
+    condition = jnp.dot(band_hot, time_table, preferred_element_type=full) + jnp.dot(
+        class_hot, class_table, preferred_element_type=full
+    )
+    activity = jax.nn.silu(condition).astype(low)
+    mod_part = jnp.einsum(
+        "cd,bde->cbe", activity, ada_weight, preferred_element_type=full
+    ) + ada_bias[None].astype(full)
+    mine = lax.all_to_all(mod_part, ("z", "y", "x"), split_axis=0, concat_axis=0, tiled=True)
+    theirs = flip(mine, "c")
+    pair = jnp.where(c == 0, jnp.stack([mine, theirs]), jnp.stack([theirs, mine]))
+    own_mod = (
+        pair.reshape(2, 8, 2, 2, col_width)
+        .transpose(3, 1, 0, 2, 4)
+        .reshape(2, 6, 1, 1, model_width)
+    )
+
+    hot = offset_hot()
+    wide = 2 * WIN_T - 1
+    square = spatial_bias.reshape(heads, 2 * WIN_S - 1, 2 * WIN_S - 1)
+    spatial_parts = jnp.stack(
+        [
+            square[:, 8 * a : 8 * a + wide, 8 * b : 8 * b + wide].reshape(heads, -1)
+            for a in range(3)
+            for b in range(3)
+        ],
+        axis=1,
+    )
+    parts = swap(jnp.concatenate([spatial_parts, joint_bias.reshape(heads, 9, -1)]))
+    blocks = jnp.dot(
+        parts.reshape(heads * 18, wide * wide), hot.astype(low), preferred_element_type=full
+    ).astype(low)
+    blocks = blocks.reshape(2, heads, 9, 64, 64)
+    near = blocks[0].reshape(heads, 3, 3, 64, 64)
+    near = jnp.where(c == 0, near, near[:, ::-1])
+    spatial_matrix = jnp.concatenate(
+        [
+            jnp.concatenate(
+                [
+                    near[:, row // 2 - col // 2 + 1, row % 2 - col % 2 + 1]
+                    for col in range(4)
+                ],
+                axis=2,
+            )
+            for row in range(4)
+        ],
+        axis=1,
+    )
+    joint_matrix = jnp.concatenate(
+        [
+            jnp.concatenate(
+                [blocks[1][:, row - col + FRAMES - 1] for col in range(FRAMES)], axis=2
+            )
+            for row in range(FRAMES)
+        ],
+        axis=1,
+    )
+
+    mask = (jnp.arange(frames) < count[0]).astype(full)[:, None, None]
+    tall = lambda values: values.reshape(frames, 128, model_width)
+    flat = lambda values: values.reshape(rows, model_width)
+    windowed = lambda values: values.reshape(2, frames, 2, 64, values.shape[-1])
+    current = tall(rearranged(swap(latents))).astype(full)
+    stored = []
+    for k in range(2):
+        w_qkv, w_out, w_up, w_down = weights[k]
+        mod = own_mod[k]
+        normed_one, inverse_one = normalize(current)
+        moved_one = flat((normed_one * (1.0 + mod[1]) + mod[0]).astype(low))
+        other_one = flip(moved_one, "c")
+        (joined,) = both_times("plain", moved_one, other_one, w_qkv)
+        joined = windowed(joined)
+        mixed, probs = attend(count, joint_matrix if k else spatial_matrix, joined, k == 1)
+        mixed = mixed.reshape(2, rows, width)
+        branch_one = tall(branch_sum(mixed, w_out))
+        after_attn = current + mask * mod[2] * branch_one
+        normed_two, inverse_two = normalize(after_attn)
+        moved_two = flat((normed_two * (1.0 + mod[4]) + mod[3]).astype(low))
+        other_two = flip(moved_two, "c")
+        act, slope = both_times("gelu", moved_two, other_two, w_up)
+        branch_two = tall(branch_sum(act, w_down))
+        current = after_attn + mask * mod[5] * branch_two
+        stored.append(
+            (
+                normed_one,
+                inverse_one,
+                moved_one,
+                other_one,
+                joined,
+                probs,
+                mixed,
+                branch_one,
+                normed_two,
+                inverse_two,
+                moved_two,
+                other_two,
+                act,
+                slope,
+                branch_two,
+            )
+        )
+
+    def restored(values):
+        sent = swap(values.reshape(rows, model_width).astype(low)).astype(full)
+        shaped = sent.reshape(frames, 2, 8, 8, model_width).transpose(0, 2, 1, 3, 4)
+        return shaped.reshape(1, frames, 8, 16, model_width)
+
+    output = restored(current)
+    state = tall(rearranged(swap(cotangent))).astype(full)
+    summed = lambda values: jnp.sum(values, axis=(0, 1))
+    mod_grads = [None, None]
+    grads = [None, None]
+    bias_blocks = [None, None]
+    for k in (1, 0):
+        w_qkv, w_out, w_up, w_down = weights[k]
+        mod = own_mod[k]
+        (
+            normed_one,
+            inverse_one,
+            moved_one,
+            other_one,
+            joined,
+            probs,
+            mixed,
+            branch_one,
+            normed_two,
+            inverse_two,
+            moved_two,
+            other_two,
+            act,
+            slope,
+            branch_two,
+        ) = stored[k]
+        gate_two = summed(mask * state * branch_two)
+        grad_own = flat((mask * mod[5] * state).astype(low))
+        grad_other = flip(grad_own, "c")
+        (grad_hidden,) = both_times("slope", grad_own, grad_other, w_down, slope)
+        down_parts = weight_grad(where, (grad_own, grad_other, act))
+        grad_down = scatter_piece(down_parts, where)
+        grad_moved = tall(branch_sum(grad_hidden, w_up))
+        up_parts = weight_grad(where, (moved_two, other_two, grad_hidden))
+        grad_up = scatter_piece(up_parts, where)
+        shift_two = summed(grad_moved)
+        scale_two = summed(grad_moved * normed_two)
+        state = state + norm_back(grad_moved * (1.0 + mod[4]), normed_two, inverse_two)
+        gate_one = summed(mask * state * branch_one)
+        grad_own = flat((mask * mod[2] * state).astype(low))
+        grad_other = flip(grad_own, "c")
+        (grad_mixed,) = both_times("plain", grad_own, grad_other, w_out)
+        back, bias_blocks[k] = attend_back(joined, windowed(grad_mixed), probs, k == 1)
+        back = back.reshape(2, rows, 3 * width)
+        out_parts = weight_grad(where, (grad_own, grad_other, mixed))
+        grad_out = scatter_piece(out_parts, where)
+        grad_moved = tall(branch_sum(back, w_qkv))
+        qkv_parts = weight_grad(where, (moved_one, other_one, back))
+        grad_qkv = scatter_piece(qkv_parts, where)
+        shift_one = summed(grad_moved)
+        scale_one = summed(grad_moved * normed_one)
+        state = state + norm_back(grad_moved * (1.0 + mod[1]), normed_one, inverse_one)
+        mod_grads[k] = jnp.stack([shift_one, scale_one, gate_one, shift_two, scale_two, gate_two])
+        grads[k] = (grad_qkv, grad_out, grad_up, grad_down)
+
+    grad_latents = restored(state)
+    exact = lax.Precision.HIGHEST
+
+    near = bias_blocks[0].reshape(heads, 3, 3, 64, 64)
+    near = jnp.where(c == 0, near, near[:, ::-1]).reshape(heads, 9, 64, 64)
+    tables = jnp.dot(
+        jnp.stack([near, bias_blocks[1]]).reshape(heads * 18, 64 * 64),
+        hot.astype(full).T,
+        precision=exact,
+    )
+    for name in ("x", "y"):
+        tables = tables + flip(tables, name)
+    for step in (1, 2):
+        tables = tables + z_trade(tables, step)
+    tables = swap(tables).reshape(2, heads, 9, wide, wide)
+    grad_joint = tables[1].reshape(heads, 9 * wide * wide)
+    near = tables[0].reshape(heads, 3, 3, wide, wide)
+    long = 2 * WIN_S - 1
+    grad_spatial = 0.0
+    for a in range(3):
+        for b in range(3):
+            grad_spatial = grad_spatial + jnp.pad(
+                near[:, a, b],
+                ((0, 0), (8 * a, long - wide - 8 * a), (8 * b, long - wide - 8 * b)),
+            )
+    grad_spatial = grad_spatial.reshape(heads, long * long)
+
+    grad_mod = jnp.stack(mod_grads).reshape(2, 6 * model_width)
+    grad_mod = grad_mod + flip(grad_mod, "c")
+    ordered = grad_mod.reshape(2, 8, 2, 2, col_width).transpose(2, 1, 3, 0, 4)
+    ordered = lax.dynamic_index_in_dim(ordered, c, 0, keepdims=False)
+    cols = lax.all_to_all(
+        ordered.reshape(16, 2, col_width),
+        ("z", "y", "x"),
+        split_axis=0,
+        concat_axis=0,
+        tiled=True,
+    )
+    grad_ada_weight = jnp.einsum("cd,cbe->bde", activity.astype(full), cols, precision=exact)
+    grad_ada_bias = jnp.sum(cols, axis=0)
+    grad_activity = jnp.einsum("cbe,bde->cd", cols, ada_weight.astype(full), precision=exact)
+    for name in ("c", "x", "y"):
+        grad_activity = grad_activity + flip(grad_activity, name)
+    for step in (1, 2):
+        grad_activity = grad_activity + z_trade(grad_activity, step)
+    grad_condition = jax.vjp(jax.nn.silu, condition)[1](grad_activity)[0]
+    grad_time = jnp.dot(band_hot.astype(full).T, grad_condition, precision=exact)
+    grad_class = jnp.dot(class_hot.astype(full).T, grad_condition, precision=exact)
+
+    stack = lambda at: jnp.stack([grads[0][at], grads[1][at]])
+    return (
+        output,
+        grad_latents,
+        grad_time,
+        grad_class,
+        grad_ada_weight,
+        grad_ada_bias,
+        stack(0).reshape(2, -1, 3, width),
+        stack(1).transpose(0, 2, 1),
+        stack(2),
+        stack(3).transpose(0, 2, 1),
+        grad_spatial,
+        grad_joint,
+    )
+
+
+def solution(mesh):
+    if mesh.shape["dp"] != 16 or mesh.shape["mp"] != 2:
+        return solution_any(mesh)
+    fine = Mesh(mesh.devices.reshape(4, 2, 2, 2), ("z", "y", "c", "x"))
+    dp, mp = ("z", "y", "c"), "x"
+    both = dp + (mp,)
+    tokens = P(dp, None, mp, None, None)
+    weight_specs = (
+        P(None, None, both),
+        P(None, both),
+        P(None, dp, None, mp),
+        P(None, mp, dp),
+        P(None, dp, mp),
+        P(None, mp, dp),
+        P(mp, None),
+        P(mp, None),
+    )
+    return jax.shard_map(
+        fast_local,
+        mesh=fine,
+        in_specs=(tokens, tokens, P(dp), P(), P(), P(), P()) + weight_specs,
+        out_specs=(tokens, tokens, P(), P()) + weight_specs,
+        check_vma=False,
+    )

time: 3660 us -> 1190 us (0.33)
  other arithmetic: 1070 us -> 127 us
  waiting for transfers between devices: 1240 us -> 330 us
  local copies, waits for them, and re-layouts: 1020 us -> 138 us
  Pallas kernels: 0 us -> 295 us
  starting transfers between devices: 8.05 us -> 263 us
  matrix products: 260 us -> 11.5 us
    scatter-add x2 -> x0, other arithmetic: 892 us -> none  [the longest x1 543 us: local(): table_parts.append(jnp.zeros((heads_local, joint_bias.shape[1]), jnp.floa...]
    gather x5 -> x0, local copies, waits for them, and re-layouts: 606 us -> none  [the longest x2 370 us: local(): joint_matrix = joint_bias.astype(jnp.float32)[:, joint_index]]
    psum x2 -> x0, waiting for transfers between devices: 390 us -> none  [the longest x1 360 us: local(): grad_activity = lax.psum(activity_part, 'dp')]
    ppermute x0 -> x162, waiting for transfers between devices: none -> 318 us  [the longest x87 166 us: flip(): return lax.ppermute(values, axis, [(0, 1), (1, 0)])]
    reduce_scatter x2 -> x0, waiting for transfers between devices: 314 us -> none  [the longest x1 175 us: local(): lax.psum_scatter(jnp.stack(up_grads[::-1], axis=0), 'dp', scatter_dimensi...]
    pallas_call x0 -> x44, Pallas kernels: none -> 295 us  [the longest x8 76.8 us: weight_grad(): pl.pallas_call(lambda *refs: weight_grad_kernel(*refs, pairs=pairs, width...]
    unnamed x35 -> x0, waiting for transfers between devices: 270 us -> none
    all_gather x13 -> x0, waiting for transfers between devices: 268 us -> none  [the longest x4 78.3 us: gather_grads(): return lax.all_gather(values, 'mp', axis=2, tiled=True)]
  transfers between devices with their start and end apart: 27 -> 164, of which waited for: 19 -> 50; matrix products, arithmetic and copies ran while one was open for 51% -> 18% of each run, Pallas kernels for 0% -> 18%
where the time goes in v1:
time: 1190 us; the launch traced here: 1170 us
  waiting for transfers between devices  330 us (28%)
  Pallas kernels  295 us (25%)
  starting transfers between devices  263 us (22%)
  local copies, waits for them, and re-layouts  138 us (12%)
  other arithmetic  127 us (11%)
    ppermute x87, waiting for transfers between devices, flip(): return lax.ppermute(values, axis, [(0, 1), (1, 0)])  166 us
    ppermute x52, waiting for transfers between devices, z_trade(): lax.ppermute(values, 'z', [(place, place ^ step) for place in range(4)])  114 us
    ppermute x87, starting transfers between devices, flip(): return lax.ppermute(values, axis, [(0, 1), (1, 0)])  101 us
    ppermute x23, starting transfers between devices, swap(): return lax.ppermute(values, ('c', 'x'), [(0, 0), (1, 2), (2, 1), (3, 3)])  86.1 us
    pallas_call x8, Pallas kernels, weight_grad(): pl.pallas_call(lambda *refs: weight_grad_kernel(*refs, pairs=pairs, width...  76.8 us
    pallas_call x8, Pallas kernels, both_times(): pl.pallas_call(lambda *refs: both_kernel(kind, *refs), grid=(width // til...  73.9 us
    ppermute x52, starting transfers between devices, z_trade(): lax.ppermute(values, 'z', [(place, place ^ step) for place in range(4)])  66.6 us
    unnamed x359, local copies, waits for them, and re-layouts  61.6 us
  transfers between devices with their start and end apart: 164, of which 50 were waited for; matrix products, arithmetic and copies ran while one was open for 18% of the time, Pallas kernels for 18%

profile of v1, /device:TPU:9, one launch (start us, length us, event | category | flops | bytes accessed | tf_op | source)
XLA Modules:
  0.0 1170.9 jit_solution(4388905868478750372)
XLA Ops:
  1.4 4.4 collective-permute-start.1
  10.3 5.7 all-to-all-start
  17.6 3.9 collective-permute-start.13
  41.8 3.9 collective-permute-start.7
  46.3 11.1 collective-permute-done.8
  84.9 6.2 collective-permute-done.18.from_x
  95.9 5.4 collective-permute-start.31
  105.6 7.7 both_plain.4
  115.3 15.3 %attend_spatial.1 = (bf16[2,5,2,64,512]{4,3,2,1,0:T(8,128)(2,1)S(1)}, bf16[5,8,256,256]{3,2,1,0:T(8,128)(2,1)}) custom-call(s32[1]{0:T(128)} %convert_element_type.981.refs_0_, bf16[8,256,256]{2,1,0:T(8,128)(2,1)S(1)} %maximum_maximum_fusion.refs_1_, bf16[2,5,2,64,1536]{4,3,2,1,0:T(8,128)(2,1)} %bitcast.489), custom_call_target="tpu_custom_call" | custom-call | flops 2684354560 | bytes 5242880 | tf_op jit(solution)/shard_map/attend_spatial/pallas_call | solution.py:862
  145.4 13.6 %collective-permute-done.34 = bf16[64,2048]{1,0:T(8,128)(2,1)} collective-permute-done((bf16[64,2048]{1,0:T(8,128)(2,1)}, bf16[64,2048]{1,0:T(8,128)(2,1)}, u32[]{:S(2)}, u32[]{:S(2)}) %collective-permute-start.34) | collective-permute-done | bytes 262176 | tf_op jit(solution)/shard_map/ppermute | solution.py:518
  159.0 16.2 %collective-permute-done.33 = bf16[64,2048]{1,0:T(8,128)(2,1)} collective-permute-done((bf16[64,2048]{1,0:T(8,128)(2,1)}, bf16[64,2048]{1,0:T(8,128)(2,1)}, u32[]{:S(2)}, u32[]{:S(2)}) %collective-permute-start.33) | collective-permute-done | bytes 262176 | tf_op jit(solution)/shard_map/ppermute | solution.py:518
  201.3 4.5 add_convert_fusion.3
  210.0 16.4 %collective-permute-done.28.from_x = bf16[4,64,2048]{2,1,0:T(8,128)(2,1)} collective-permute-done((bf16[4,64,2048]{2,1,0:T(8,128)(2,1)}, bf16[4,64,2048]{2,1,0:T(8,128)(2,1)}, u32[]{:S(2)}, u32[]{:S(2)}) %collective-permute-start.28) | collective-permute-done | bytes 1048608 | tf_op jit(solution)/shard_map/ppermute | solution.py:514
  232.3 7.3 collective-permute-done.38.far_hi
  242.9 8.0 collective-permute-done.30.far_hi
  254.2 16.8 %both_gelu.2 = (bf16[2,640,2048]{2,1,0:T(8,128)(2,1)S(1)}, bf16[2,640,2048]{2,1,0:T(8,128)(2,1)}) custom-call(bf16[640,1024]{1,0:T(8,128)(2,1)S(1)} %get-tuple-element.171.refs_0_.refs_1_, bf16[640,1024]{1,0:T(8,128)(2,1)S(1)} %collective-permute-done.22.refs_1_.refs_2_, bf16[1024,2048]{1,0:T(8,128)(2,1)S(1)} %bitcast.451), custom_call_target="tpu_custom_call" | custom-call | flops 5368709120 | bytes 17301504 | tf_op jit(solution)/shard_map/both_gelu/pallas_call | solution.py:699
  279.7 4.1 collective-permute-done.41
  296.6 4.5 add_convert_fusion.2
  308.4 14.7 %collective-permute-done.49 = bf16[64,512]{1,0:T(8,128)(2,1)} collective-permute-done((bf16[64,512]{1,0:T(8,128)(2,1)S(1)}, bf16[64,512]{1,0:T(8,128)(2,1)}, u32[]{:S(2)}, u32[]{:S(2)}) %collective-permute-start.49) | collective-permute-done | bytes 65568 | tf_op jit(solution)/shard_map/ppermute | solution.py:522
  366.8 7.9 both_plain.5
  376.7 17.2 %attend_joint.1 = (bf16[2,5,2,64,512]{4,3,2,1,0:T(8,128)(2,1)S(1)}, bf16[4,8,320,320]{3,2,1,0:T(8,128)(2,1)}) custom-call(s32[1]{0:T(128)} %convert_element_type.981.refs_0_, bf16[8,320,320]{2,1,0:T(8,128)(2,1)S(1)} %copy-done.53, bf16[2,5,2,64,1536]{4,3,2,1,0:T(8,128)(2,1)} %bitcast.491), custom_call_target="tpu_custom_call" | custom-call | flops 3355443200 | bytes 6553600 | tf_op jit(solution)/shard_map/attend_joint/pallas_call | solution.py:862
  395.5 4.8 collective-permute-start.57
  412.3 19.4 %collective-permute-done.70 = bf16[64,2048]{1,0:T(8,128)(2,1)S(1)} collective-permute-done((bf16[64,2048]{1,0:T(8,128)(2,1)S(1)}, bf16[64,2048]{1,0:T(8,128)(2,1)S(1)}, u32[]{:S(2)}, u32[]{:S(2)}) %collective-permute-start.70) | collective-permute-done | bytes 262176 | tf_op jit(solution)/shard_map/ppermute | solution.py:518
  431.7 7.5 collective-permute-done.69
  445.8 3.8 collective-permute-start.72
  456.3 4.9 add_convert_fusion.1
  461.2 28.5 %collective-permute-done.72.from_x = bf16[4,64,2048]{2,1,0:T(8,128)(2,1)} collective-permute-done((bf16[4,64,2048]{2,1,0:T(8,128)(2,1)}, bf16[4,64,2048]{2,1,0:T(8,128)(2,1)}, u32[]{:S(2)}, u32[]{:S(2)}) %collective-permute-start.72) | collective-permute-done | bytes 1048608 | tf_op jit(solution)/shard_map/ppermute | solution.py:514
  509.9 6.3 collective-permute-done.73.far_lo
  520.7 6.8 collective-permute-done.65.far_lo
  531.1 19.8 %both_gelu.3 = (bf16[2,640,2048]{2,1,0:T(8,128)(2,1)S(1)}, bf16[2,640,2048]{2,1,0:T(8,128)(2,1)}) custom-call(bf16[640,1024]{1,0:T(8,128)(2,1)} %get-tuple-element.165.refs_0_.refs_1_, bf16[640,1024]{1,0:T(8,128)(2,1)} %collective-permute-done.58.refs_1_.refs_2_, bf16[1024,2048]{1,0:T(8,128)(2,1)S(1)} %bitcast.460), custom_call_target="tpu_custom_call" | custom-call | flops 5368709120 | bytes 17301504 | tf_op jit(solution)/shard_map/both_gelu/pallas_call | solution.py:699
  553.2 8.9 both_slope.2.values.refs_3_
  571.8 11.5 weight_grad.13
  596.5 11.6 weight_grad.15
  619.1 3.9 one_back.25
  640.4 5.1 fusion.6
  646.9 8.8 collective-permute-done.136
  660.8 17.4 %collective-permute-done.152 = bf16[4,64,2048]{2,1,0:T(8,128)(2,1)} collective-permute-done((bf16[4,64,2048]{2,1,0:T(8,128)(2,1)S(1)}, bf16[4,64,2048]{2,1,0:T(8,128)(2,1)}, u32[]{:S(2)}, u32[]{:S(2)}) %collective-permute-start.152) | collective-permute-done | bytes 1048608 | tf_op jit(solution)/shard_map/ppermute | solution.py:514
  695.6 10.1 collective-permute-done.155
  705.7 5.8 collective-permute-done.154
  714.4 5.8 weight_grad.11
  725.6 21.7 %attend_back_joint.1 = (bf16[2,5,2,64,1536]{4,3,2,1,0:T(8,128)(2,1)}, f32[8,9,64,64]{3,2,1,0:T(8,128)}) custom-call(bf16[2,5,2,64,1536]{4,3,2,1,0:T(8,128)(2,1)} %bitcast.492, bf16[2,5,2,64,512]{4,3,2,1,0:T(8,128)(2,1)} %bitcast.487, bf16[4,8,320,320]{3,2,1,0:T(8,128)(2,1)} %get-tuple-element.69.refs_2_), custom_call_target="tpu_custom_call" | custom-call | flops 6710886400 | bytes 6553600 | tf_op jit(solution)/shard_map/attend_back_joint/pallas_call | solution.py:894
  752.4 9.4 weight_grad.9
  776.0 7.0 collective-permute-done.101
  792.0 13.4 %collective-permute-done.104 = bf16[4,64,1536]{2,1,0:T(8,128)(2,1)S(1)} collective-permute-done((bf16[4,64,1536]{2,1,0:T(8,128)(2,1)S(1)}, bf16[4,64,1536]{2,1,0:T(8,128)(2,1)S(1)}, u32[]{:S(2)}, u32[]{:S(2)}) %collective-permute-start.104) | collective-permute-done | bytes 786464 | tf_op jit(solution)/shard_map/ppermute | solution.py:514
  815.1 8.9 collective-permute-done.106
  824.9 11.8 %weight_grad.14 = (bf16[4,64,2048]{2,1,0:T(8,128)(2,1)}, bf16[4,64,2048]{2,1,0:T(8,128)(2,1)}, bf16[4,64,2048]{2,1,0:T(8,128)(2,1)}, bf16[2,64,2048]{2,1,0:T(8,128)(2,1)}, bf16[2,64,2048]{2,1,0:T(8,128)(2,1)}) custom-call(s32[3]{0:T(128)} %copy-done.54, bf16[640,1024]{1,0:T(8,128)(2,1)} %copy-done.48, ...), custom_call_target="tpu_custom_call" | custom-call | flops 5368709120 | bytes 12058624 | tf_op jit(solution)/shard_map/weight_grad/pallas_call | solution.py:642
  845.1 8.5 both_slope.3.values.refs_3_
  855.9 11.7 weight_grad.12
  879.6 3.9 one_back.28
  894.3 15.7 %collective-permute-done.144 = bf16[4,64,2048]{2,1,0:T(8,128)(2,1)S(1)} collective-permute-done((bf16[4,64,2048]{2,1,0:T(8,128)(2,1)S(1)}, bf16[4,64,2048]{2,1,0:T(8,128)(2,1)S(1)}, u32[]{:S(2)}, u32[]{:S(2)}) %collective-permute-start.144) | collective-permute-done | bytes 1048608 | tf_op jit(solution)/shard_map/ppermute | solution.py:514
  918.9 5.8 multiply_reduce_fusion.3
  925.0 7.6 collective-permute-done.128
  946.6 6.8 collective-permute-start.156
  954.4 6.7 collective-permute-done.131
  961.1 9.4 collective-permute-start.108
  996.6 20.5 %attend_back_spatial.1 = (bf16[2,5,2,64,1536]{4,3,2,1,0:T(8,128)(2,1)}, f32[8,9,64,64]{3,2,1,0:T(8,128)}) custom-call(bf16[2,5,2,64,1536]{4,3,2,1,0:T(8,128)(2,1)} %bitcast.490, bf16[2,5,2,64,512]{4,3,2,1,0:T(8,128)(2,1)} %bitcast.488, bf16[5,8,256,256]{3,2,1,0:T(8,128)(2,1)} %get-tuple-element.72.refs_2_), custom_call_target="tpu_custom_call" | custom-call | flops 5368709120 | bytes 5242880 | tf_op jit(solution)/shard_map/attend_back_spatial/pallas_call | solution.py:894
  1030.4 5.5 weight_grad.10
  1040.7 9.5 weight_grad.8
  1076.9 6.8 collective-permute-start.116
  1083.8 4.3 collective-permute-start.161
  1089.1 7.6 collective-permute-done.116
  1114.5 3.9 all-to-all-start.1
  1118.3 12.8 %all-to-all-done.1 = f32[16,2,192]{2,1,0:T(2,128)S(1)} async-done(((f32[16,2,192]{2,1,0:T(2,128)}), f32[16,2,192]{2,1,0:T(2,128)S(1)}, u32[]{:S(2)}, u32[]{:S(2)}) %all-to-all-start.1) | async-done | bytes 24608 | tf_op jit(solution)/shard_map/all_to_all | solution.py:1169
  1152.3 7.4 collective-permute-done.100
  (902 shorter events, 553.3 us)
Async XLA Ops:
  1.4 31.7 %collective-permute-start.1 = (f32[1]{0:T(128)}, f32[1]{0:T(128)}, u32[]{:S(2)}, u32[]{:S(2)}) collective-permute-start(f32[1]{0:T(128)} %convert_element_type.980), channel_id=1, source_target_pairs={{0,0},{1,2},{2,1},{3,3},{4,4},{5,6},{6,5},{7,7},{8,8},{9,10},{10,9... | collective-permute-start | bytes 20 | tf_op jit(solution)/shard_map/ppermute | solution.py:522
  30.3 33.7 %collective-permute-start = (bf16[1,5,8,16,1024]{4,3,2,1,0:T(8,128)(2,1)}, bf16[1,5,8,16,1024]{4,3,2,1,0:T(8,128)(2,1)}, u32[]{:S(2)}, u32[]{:S(2)}) collective-permute-start(bf16[1,5,8,16,1024]{4,3,2,1,0:T(8,128)(2,1)} %param.16), channel_id=1, source_target_pairs={{0,0},{1,2},{2,1},{3,3},{4,4},{5,6},{6,5},{7,7},{8,8},{9,10},{10,9... | collective-permute-start | bytes 3932168 | tf_op jit(solution)/shard_map/ppermute | solution.py:522
  39.4 34.4 %collective-permute-start.16 = (bf16[64,512]{1,0:T(8,128)(2,1)}, bf16[64,512]{1,0:T(8,128)(2,1)}, u32[]{:S(2)}, u32[]{:S(2)}) collective-permute-start(bf16[64,512]{1,0:T(8,128)(2,1)} %collective-permute-done.13), channel_id=1, source_target_pairs={{0,24},{8,16},{16,8},{24,0},{1,25},{9,17},{17,9},{25,1},{2,26},{10... | collective-permute-start | bytes 196616 | tf_op jit(solution)/shard_map/ppermute | solution.py:518
  63.6 28.9 %collective-permute-start.10 = (bf16[4,64,1536]{2,1,0:T(8,128)(2,1)S(1)}, bf16[4,64,1536]{2,1,0:T(8,128)(2,1)S(1)}, u32[]{:S(2)}, u32[]{:S(2)}) collective-permute-start(bf16[4,64,1536]{2,1,0:T(8,128)(2,1)S(1)} %pad_maximum_fusion.13.own), channel_id=1, source_target_pairs={{0,1},{1,0},{2,3},{3,2},{4,5},{5,4},{6,7},{7,6},{8,9},{9,8},{10,11... | collective-permute-start | bytes 2359304 | tf_op jit(solution)/shard_map/ppermute | solution.py:514
  64.0 29.8 %collective-permute-start.9 = (bf16[4,64,1536]{2,1,0:T(8,128)(2,1)S(1)}, bf16[4,64,1536]{2,1,0:T(8,128)(2,1)S(1)}, u32[]{:S(2)}, u32[]{:S(2)}) collective-permute-start(bf16[4,64,1536]{2,1,0:T(8,128)(2,1)S(1)} %pad_maximum_fusion.13.own), channel_id=1, source_target_pairs={{0,4},{4,0},{1,5},{5,1},{2,6},{6,2},{3,7},{7,3},{8,12},{12,8},{9,1... | collective-permute-start | bytes 2359304 | tf_op jit(solution)/shard_map/ppermute | solution.py:514
  73.8 31.8 %collective-permute-start.4 = (bf16[640,1024]{1,0:T(8,128)(2,1)}, bf16[640,1024]{1,0:T(8,128)(2,1)}, u32[]{:S(2)}, u32[]{:S(2)}) collective-permute-start(bf16[640,1024]{1,0:T(8,128)(2,1)} %add_convert_fusion.4.refs_0_.refs_1_), channel_id=1, source_target_pairs={{0,2},{2,0},{1,3},{3,1},{4,6},{6,4},{5,7},{7,5},{8,10},{10,8},{9,1... | collective-permute-start | bytes 3932168 | tf_op jit(solution)/shard_map/ppermute | solution.py:514
  95.9 43.4 %collective-permute-start.31 = (bf16[64,2048]{1,0:T(8,128)(2,1)S(1)}, bf16[64,2048]{1,0:T(8,128)(2,1)}, u32[]{:S(2)}, u32[]{:S(2)}) collective-permute-start(bf16[64,2048]{1,0:T(8,128)(2,1)S(1)} %copy-done.130), channel_id=1, source_target_pairs={{0,0},{1,2},{2,1},{3,3},{4,4},{5,6},{6,5},{7,7},{8,8},{9,10},{10,9... | collective-permute-start | bytes 786440 | tf_op jit(solution)/shard_map/ppermute | solution.py:522
  133.2 61.8 %collective-permute-start.21 = (bf16[640,1024]{1,0:T(8,128)(2,1)}, bf16[640,1024]{1,0:T(8,128)(2,1)}, u32[]{:S(2)}, u32[]{:S(2)}) collective-permute-start(bf16[640,1024]{1,0:T(8,128)(2,1)} %one_back.17), channel_id=1, source_target_pairs={{0,2},{2,0},{1,3},{3,1},{4,6},{6,4},{5,7},{7,5},{8,10},{10,8},{9,1... | collective-permute-start | bytes 3932168 | tf_op jit(solution)/shard_map/ppermute | solution.py:514
  140.8 34.4 %collective-permute-start.33 = (bf16[64,2048]{1,0:T(8,128)(2,1)}, bf16[64,2048]{1,0:T(8,128)(2,1)}, u32[]{:S(2)}, u32[]{:S(2)}) collective-permute-start(bf16[64,2048]{1,0:T(8,128)(2,1)} %collective-permute-done.31), channel_id=1, source_target_pairs={{0,16},{8,24},{16,0},{24,8},{1,17},{9,25},{17,1},{25,9},{2,18},{10... | collective-permute-start | bytes 786440 | tf_op jit(solution)/shard_map/ppermute | solution.py:518
  141.3 36.4 %collective-permute-start.32 = (bf16[64,2048]{1,0:T(8,128)(2,1)}, bf16[64,2048]{1,0:T(8,128)(2,1)S(1)}, u32[]{:S(2)}, u32[]{:S(2)}) collective-permute-start(bf16[64,2048]{1,0:T(8,128)(2,1)} %collective-permute-done.31), channel_id=1, source_target_pairs={{0,8},{8,0},{16,24},{24,16},{1,9},{9,1},{17,25},{25,17},{2,10},{10... | collective-permute-start | bytes 786440 | tf_op jit(solution)/shard_map/ppermute | solution.py:518
  144.0 37.3 %collective-permute-start.26 = (bf16[64,2048]{1,0:T(8,128)(2,1)}, bf16[64,2048]{1,0:T(8,128)(2,1)S(1)}, u32[]{:S(2)}, u32[]{:S(2)}) collective-permute-start(bf16[64,2048]{1,0:T(8,128)(2,1)} %collective-permute-done.23), channel_id=1, source_target_pairs={{0,24},{8,16},{16,8},{24,0},{1,25},{9,17},{17,9},{25,1},{2,26},{10... | collective-permute-start | bytes 786440 | tf_op jit(solution)/shard_map/ppermute | solution.py:518
  159.0 27.5 %collective-permute-start.25 = (bf16[64,2048]{1,0:T(8,128)(2,1)}, bf16[64,2048]{1,0:T(8,128)(2,1)S(1)}, u32[]{:S(2)}, u32[]{:S(2)}) collective-permute-start(bf16[64,2048]{1,0:T(8,128)(2,1)} %collective-permute-done.23), channel_id=1, source_target_pairs={{0,16},{8,24},{16,0},{24,8},{1,17},{9,25},{17,1},{25,9},{2,18},{10... | collective-permute-start | bytes 786440 | tf_op jit(solution)/shard_map/ppermute | solution.py:518
  179.9 27.1 %collective-permute-start.36 = (bf16[4,64,2048]{2,1,0:T(8,128)(2,1)}, bf16[4,64,2048]{2,1,0:T(8,128)(2,1)}, u32[]{:S(2)}, u32[]{:S(2)}) collective-permute-start(bf16[4,64,2048]{2,1,0:T(8,128)(2,1)} %pad_maximum_fusion.2.own), channel_id=1, source_target_pairs={{0,1},{1,0},{2,3},{3,2},{4,5},{5,4},{6,7},{7,6},{8,9},{9,8},{10,11... | collective-permute-start | bytes 3145736 | tf_op jit(solution)/shard_map/ppermute | solution.py:514
  181.3 26.9 %collective-permute-start.35 = (bf16[4,64,2048]{2,1,0:T(8,128)(2,1)}, bf16[4,64,2048]{2,1,0:T(8,128)(2,1)}, u32[]{:S(2)}, u32[]{:S(2)}) collective-permute-start(bf16[4,64,2048]{2,1,0:T(8,128)(2,1)} %pad_maximum_fusion.2.own), channel_id=1, source_target_pairs={{0,4},{4,0},{1,5},{5,1},{2,6},{6,2},{3,7},{7,3},{8,12},{12,8},{9,1... | collective-permute-start | bytes 3145736 | tf_op jit(solution)/shard_map/ppermute | solution.py:514
  189.6 36.7 %collective-permute-start.28 = (bf16[4,64,2048]{2,1,0:T(8,128)(2,1)}, bf16[4,64,2048]{2,1,0:T(8,128)(2,1)}, u32[]{:S(2)}, u32[]{:S(2)}) collective-permute-start(bf16[4,64,2048]{2,1,0:T(8,128)(2,1)} %pad_maximum_fusion.1.own), channel_id=1, source_target_pairs={{0,1},{1,0},{2,3},{3,2},{4,5},{5,4},{6,7},{7,6},{8,9},{9,8},{10,11... | collective-permute-start | bytes 3145736 | tf_op jit(solution)/shard_map/ppermute | solution.py:514
  191.9 37.7 %collective-permute-start.27 = (bf16[4,64,2048]{2,1,0:T(8,128)(2,1)}, bf16[4,64,2048]{2,1,0:T(8,128)(2,1)}, u32[]{:S(2)}, u32[]{:S(2)}) collective-permute-start(bf16[4,64,2048]{2,1,0:T(8,128)(2,1)} %pad_maximum_fusion.1.own), channel_id=1, source_target_pairs={{0,4},{4,0},{1,5},{5,1},{2,6},{6,2},{3,7},{7,3},{8,12},{12,8},{9,1... | collective-permute-start | bytes 3145736 | tf_op jit(solution)/shard_map/ppermute | solution.py:514
  205.8 48.4 %collective-permute-start.22 = (bf16[640,1024]{1,0:T(8,128)(2,1)S(1)}, bf16[640,1024]{1,0:T(8,128)(2,1)S(1)}, u32[]{:S(2)}, u32[]{:S(2)}) collective-permute-start(bf16[640,1024]{1,0:T(8,128)(2,1)S(1)} %get-tuple-element.171.refs_0_.refs_1_), channel_id=1, source_target_pairs={{0,2},{2,0},{1,3},{3,1},{4,6},{6,4},{5,7},{7,5},{8,10},{10,8},{9,1... | collective-permute-start | bytes 3932168 | tf_op jit(solution)/shard_map/ppermute | solution.py:514
  208.1 31.5 %collective-permute-start.38 = (bf16[2,64,2048]{2,1,0:T(8,128)(2,1)S(1)}, bf16[2,64,2048]{2,1,0:T(8,128)(2,1)S(1)}, u32[]{:S(2)}, u32[]{:S(2)}) collective-permute-start(bf16[2,64,2048]{2,1,0:T(8,128)(2,1)S(1)} %slice.540), channel_id=1, source_target_pairs={{0,4},{4,0},{1,5},{5,1},{2,6},{6,2},{3,7},{7,3},{8,12},{12,8},{9,1... | collective-permute-start | bytes 1572872 | tf_op jit(solution)/shard_map/ppermute | solution.py:514
  209.3 30.4 %collective-permute-start.37 = (bf16[2,64,2048]{2,1,0:T(8,128)(2,1)S(1)}, bf16[2,64,2048]{2,1,0:T(8,128)(2,1)S(1)}, u32[]{:S(2)}, u32[]{:S(2)}) collective-permute-start(bf16[2,64,2048]{2,1,0:T(8,128)(2,1)S(1)} %slice.539), channel_id=1, source_target_pairs={{0,1},{1,0},{2,3},{3,2},{4,5},{5,4},{6,7},{7,6},{8,9},{9,8},{10,11... | collective-permute-start | bytes 1572872 | tf_op jit(solution)/shard_map/ppermute | solution.py:514
  301.2 65.6 %collective-permute-start.40 = (bf16[640,1024]{1,0:T(8,128)(2,1)}, bf16[640,1024]{1,0:T(8,128)(2,1)}, u32[]{:S(2)}, u32[]{:S(2)}) collective-permute-start(bf16[640,1024]{1,0:T(8,128)(2,1)} %get-tuple-element.167.refs_0_.refs_1_), channel_id=1, source_target_pairs={{0,2},{2,0},{1,3},{3,1},{4,6},{6,4},{5,7},{7,5},{8,10},{10,8},{9,1... | collective-permute-start | bytes 3932168 | tf_op jit(solution)/shard_map/ppermute | solution.py:514
  302.5 36.4 %collective-permute-start.46 = (bf16[4,64,1536]{2,1,0:T(8,128)(2,1)S(1)}, bf16[4,64,1536]{2,1,0:T(8,128)(2,1)}, u32[]{:S(2)}, u32[]{:S(2)}) collective-permute-start(bf16[4,64,1536]{2,1,0:T(8,128)(2,1)S(1)} %pad_maximum_fusion.14.own), channel_id=1, source_target_pairs={{0,1},{1,0},{2,3},{3,2},{4,5},{5,4},{6,7},{7,6},{8,9},{9,8},{10,11... | collective-permute-start | bytes 2359304 | tf_op jit(solution)/shard_map/ppermute | solution.py:514
  304.2 36.5 %collective-permute-start.45 = (bf16[4,64,1536]{2,1,0:T(8,128)(2,1)S(1)}, bf16[4,64,1536]{2,1,0:T(8,128)(2,1)}, u32[]{:S(2)}, u32[]{:S(2)}) collective-permute-start(bf16[4,64,1536]{2,1,0:T(8,128)(2,1)S(1)} %pad_maximum_fusion.14.own), channel_id=1, source_target_pairs={{0,4},{4,0},{1,5},{5,1},{2,6},{6,2},{3,7},{7,3},{8,12},{12,8},{9,1... | collective-permute-start | bytes 2359304 | tf_op jit(solution)/shard_map/ppermute | solution.py:514
  395.5 57.5 %collective-permute-start.57 = (bf16[640,1024]{1,0:T(8,128)(2,1)S(1)}, bf16[640,1024]{1,0:T(8,128)(2,1)S(1)}, u32[]{:S(2)}, u32[]{:S(2)}) collective-permute-start(bf16[640,1024]{1,0:T(8,128)(2,1)S(1)} %one_back.21), channel_id=1, source_target_pairs={{0,2},{2,0},{1,3},{3,1},{4,6},{6,4},{5,7},{7,5},{8,10},{10,8},{9,1... | collective-permute-start | bytes 3932168 | tf_op jit(solution)/shard_map/ppermute | solution.py:514
  409.4 29.8 %collective-permute-start.69 = (bf16[64,2048]{1,0:T(8,128)(2,1)S(1)}, bf16[64,2048]{1,0:T(8,128)(2,1)S(1)}, u32[]{:S(2)}, u32[]{:S(2)}) collective-permute-start(bf16[64,2048]{1,0:T(8,128)(2,1)S(1)} %collective-permute-done.67), channel_id=1, source_target_pairs={{0,16},{8,24},{16,0},{24,8},{1,17},{9,25},{17,1},{25,9},{2,18},{10... | collective-permute-start | bytes 786440 | tf_op jit(solution)/shard_map/ppermute | solution.py:518
  411.3 30.0 %collective-permute-start.68 = (bf16[64,2048]{1,0:T(8,128)(2,1)S(1)}, bf16[64,2048]{1,0:T(8,128)(2,1)S(1)}, u32[]{:S(2)}, u32[]{:S(2)}) collective-permute-start(bf16[64,2048]{1,0:T(8,128)(2,1)S(1)} %collective-permute-done.67), channel_id=1, source_target_pairs={{0,8},{8,0},{16,24},{24,16},{1,9},{9,1},{17,25},{25,17},{2,10},{10... | collective-permute-start | bytes 786440 | tf_op jit(solution)/shard_map/ppermute | solution.py:518
  411.3 34.4 %collective-permute-start.62 = (bf16[64,2048]{1,0:T(8,128)(2,1)S(1)}, bf16[64,2048]{1,0:T(8,128)(2,1)S(1)}, u32[]{:S(2)}, u32[]{:S(2)}) collective-permute-start(bf16[64,2048]{1,0:T(8,128)(2,1)S(1)} %collective-permute-done.59), channel_id=1, source_target_pairs={{0,24},{8,16},{16,8},{24,0},{1,25},{9,17},{17,9},{25,1},{2,26},{10... | collective-permute-start | bytes 786440 | tf_op jit(solution)/shard_map/ppermute | solution.py:518
  441.3 53.1 %collective-permute-start.77 = (bf16[1,5,8,16,1024]{4,3,2,1,0:T(8,128)(2,1)}, bf16[1,5,8,16,1024]{4,3,2,1,0:T(8,128)(2,1)}, u32[]{:S(2)}, u32[]{:S(2)}) collective-permute-start(bf16[1,5,8,16,1024]{4,3,2,1,0:T(8,128)(2,1)} %param.17), channel_id=1, source_target_pairs={{0,0},{1,2},{2,1},{3,3},{4,4},{5,6},{6,5},{7,7},{8,8},{9,10},{10,9... | collective-permute-start | bytes 3932168 | tf_op jit(solution)/shard_map/ppermute | solution.py:522
  445.8 44.0 %collective-permute-start.72 = (bf16[4,64,2048]{2,1,0:T(8,128)(2,1)}, bf16[4,64,2048]{2,1,0:T(8,128)(2,1)}, u32[]{:S(2)}, u32[]{:S(2)}) collective-permute-start(bf16[4,64,2048]{2,1,0:T(8,128)(2,1)} %pad_maximum_fusion.4.own), channel_id=1, source_target_pairs={{0,1},{1,0},{2,3},{3,2},{4,5},{5,4},{6,7},{7,6},{8,9},{9,8},{10,11... | collective-permute-start | bytes 3145736 | tf_op jit(solution)/shard_map/ppermute | solution.py:514
  449.6 48.8 %collective-permute-start.71 = (bf16[4,64,2048]{2,1,0:T(8,128)(2,1)}, bf16[4,64,2048]{2,1,0:T(8,128)(2,1)}, u32[]{:S(2)}, u32[]{:S(2)}) collective-permute-start(bf16[4,64,2048]{2,1,0:T(8,128)(2,1)} %pad_maximum_fusion.4.own), channel_id=1, source_target_pairs={{0,4},{4,0},{1,5},{5,1},{2,6},{6,2},{3,7},{7,3},{8,12},{12,8},{9,1... | collective-permute-start | bytes 3145736 | tf_op jit(solution)/shard_map/ppermute | solution.py:514
  451.1 52.1 %collective-permute-start.64 = (bf16[4,64,2048]{2,1,0:T(8,128)(2,1)}, bf16[4,64,2048]{2,1,0:T(8,128)(2,1)}, u32[]{:S(2)}, u32[]{:S(2)}) collective-permute-start(bf16[4,64,2048]{2,1,0:T(8,128)(2,1)} %pad_maximum_fusion.3.own), channel_id=1, source_target_pairs={{0,1},{1,0},{2,3},{3,2},{4,5},{5,4},{6,7},{7,6},{8,9},{9,8},{10,11... | collective-permute-start | bytes 3145736 | tf_op jit(solution)/shard_map/ppermute | solution.py:514
  453.0 54.2 %collective-permute-start.63 = (bf16[4,64,2048]{2,1,0:T(8,128)(2,1)}, bf16[4,64,2048]{2,1,0:T(8,128)(2,1)}, u32[]{:S(2)}, u32[]{:S(2)}) collective-permute-start(bf16[4,64,2048]{2,1,0:T(8,128)(2,1)} %pad_maximum_fusion.3.own), channel_id=1, source_target_pairs={{0,4},{4,0},{1,5},{5,1},{2,6},{6,2},{3,7},{7,3},{8,12},{12,8},{9,1... | collective-permute-start | bytes 3145736 | tf_op jit(solution)/shard_map/ppermute | solution.py:514
  489.7 41.4 %collective-permute-start.58 = (bf16[640,1024]{1,0:T(8,128)(2,1)}, bf16[640,1024]{1,0:T(8,128)(2,1)}, u32[]{:S(2)}, u32[]{:S(2)}) collective-permute-start(bf16[640,1024]{1,0:T(8,128)(2,1)} %get-tuple-element.165.refs_0_.refs_1_), channel_id=1, source_target_pairs={{0,2},{2,0},{1,3},{3,1},{4,6},{6,4},{5,7},{7,5},{8,10},{10,8},{9,1... | collective-permute-start | bytes 3932168 | tf_op jit(solution)/shard_map/ppermute | solution.py:514
  498.4 54.8 %collective-permute-start.78 = (bf16[640,1024]{1,0:T(8,128)(2,1)}, bf16[640,1024]{1,0:T(8,128)(2,1)}, u32[]{:S(2)}, u32[]{:S(2)}) collective-permute-start(bf16[640,1024]{1,0:T(8,128)(2,1)} %fusion.9.refs_0_.refs_1_), channel_id=1, source_target_pairs={{0,2},{2,0},{1,3},{3,1},{4,6},{6,4},{5,7},{7,5},{8,10},{10,8},{9,1... | collective-permute-start | bytes 3932168 | tf_op jit(solution)/shard_map/ppermute | solution.py:514
  587.1 44.0 %collective-permute-start.133 = (bf16[2,64,2048]{2,1,0:T(8,128)(2,1)}, bf16[2,64,2048]{2,1,0:T(8,128)(2,1)}, u32[]{:S(2)}, u32[]{:S(2)}) collective-permute-start(bf16[2,64,2048]{2,1,0:T(8,128)(2,1)} %get-tuple-element.101), channel_id=1, source_target_pairs={{0,1},{1,0},{2,3},{3,2},{4,5},{5,4},{6,7},{7,6},{8,9},{9,8},{10,11... | collective-permute-start | bytes 1572872 | tf_op jit(solution)/shard_map/ppermute | solution.py:514
  589.3 39.9 %collective-permute-start.135 = (bf16[2,64,2048]{2,1,0:T(8,128)(2,1)}, bf16[2,64,2048]{2,1,0:T(8,128)(2,1)}, u32[]{:S(2)}, u32[]{:S(2)}) collective-permute-start(bf16[2,64,2048]{2,1,0:T(8,128)(2,1)} %get-tuple-element.103), channel_id=1, source_target_pairs={{0,4},{4,0},{1,5},{5,1},{2,6},{6,2},{3,7},{7,3},{8,12},{12,8},{9,1... | collective-permute-start | bytes 1572872 | tf_op jit(solution)/shard_map/ppermute | solution.py:514
  610.3 25.1 %collective-permute-start.149 = (bf16[2,64,2048]{2,1,0:T(8,128)(2,1)}, bf16[2,64,2048]{2,1,0:T(8,128)(2,1)}, u32[]{:S(2)}, u32[]{:S(2)}) collective-permute-start(bf16[2,64,2048]{2,1,0:T(8,128)(2,1)} %get-tuple-element.111), channel_id=1, source_target_pairs={{0,1},{1,0},{2,3},{3,2},{4,5},{5,4},{6,7},{7,6},{8,9},{9,8},{10,11... | collective-permute-start | bytes 1572872 | tf_op jit(solution)/shard_map/ppermute | solution.py:514
  611.9 28.5 %collective-permute-start.75 = (bf16[640,1024]{1,0:T(8,128)(2,1)}, bf16[640,1024]{1,0:T(8,128)(2,1)}, u32[]{:S(2)}, u32[]{:S(2)}) collective-permute-start(bf16[640,1024]{1,0:T(8,128)(2,1)} %copy-done.50), channel_id=1, source_target_pairs={{0,2},{2,0},{1,3},{3,1},{4,6},{6,4},{5,7},{7,5},{8,10},{10,8},{9,1... | collective-permute-start | bytes 3932168 | tf_op jit(solution)/shard_map/ppermute | solution.py:514
  635.4 42.8 %collective-permute-start.152 = (bf16[4,64,2048]{2,1,0:T(8,128)(2,1)S(1)}, bf16[4,64,2048]{2,1,0:T(8,128)(2,1)}, u32[]{:S(2)}, u32[]{:S(2)}) collective-permute-start(bf16[4,64,2048]{2,1,0:T(8,128)(2,1)S(1)} %pad_maximum_fusion.12), channel_id=1, source_target_pairs={{0,1},{1,0},{2,3},{3,2},{4,5},{5,4},{6,7},{7,6},{8,9},{9,8},{10,11... | collective-permute-start | bytes 3145736 | tf_op jit(solution)/shard_map/ppermute | solution.py:514
  637.0 43.5 %collective-permute-start.150 = (bf16[4,64,2048]{2,1,0:T(8,128)(2,1)S(1)}, bf16[4,64,2048]{2,1,0:T(8,128)(2,1)S(1)}, u32[]{:S(2)}, u32[]{:S(2)}) collective-permute-start(bf16[4,64,2048]{2,1,0:T(8,128)(2,1)S(1)} %pad_maximum_fusion.11), channel_id=1, source_target_pairs={{0,4},{4,0},{1,5},{5,1},{2,6},{6,2},{3,7},{7,3},{8,12},{12,8},{9,1... | collective-permute-start | bytes 3145736 | tf_op jit(solution)/shard_map/ppermute | solution.py:514
  645.5 67.9 %collective-permute-start.80 = (bf16[640,1024]{1,0:T(8,128)(2,1)S(1)}, bf16[640,1024]{1,0:T(8,128)(2,1)S(1)}, u32[]{:S(2)}, u32[]{:S(2)}) collective-permute-start(bf16[640,1024]{1,0:T(8,128)(2,1)S(1)} %get-tuple-element.163.refs_0_.refs_1_), channel_id=1, source_target_pairs={{0,2},{2,0},{1,3},{3,1},{4,6},{6,4},{5,7},{7,5},{8,10},{10,8},{9,1... | collective-permute-start | bytes 3932168 | tf_op jit(solution)/shard_map/ppermute | solution.py:514
  659.7 25.8 %collective-permute-start.137 = (bf16[64,2048]{1,0:T(8,128)(2,1)S(1)}, bf16[64,2048]{1,0:T(8,128)(2,1)S(1)}, u32[]{:S(2)}, u32[]{:S(2)}) collective-permute-start(bf16[64,2048]{1,0:T(8,128)(2,1)S(1)} %get-tuple-element.184), channel_id=1, source_target_pairs={{0,8},{8,0},{16,24},{24,16},{1,9},{9,1},{17,25},{25,17},{2,10},{10... | collective-permute-start | bytes 786440 | tf_op jit(solution)/shard_map/ppermute | solution.py:518
  659.8 26.9 %collective-permute-start.139 = (bf16[64,2048]{1,0:T(8,128)(2,1)S(1)}, bf16[64,2048]{1,0:T(8,128)(2,1)S(1)}, u32[]{:S(2)}, u32[]{:S(2)}) collective-permute-start(bf16[64,2048]{1,0:T(8,128)(2,1)S(1)} %get-tuple-element.185), channel_id=1, source_target_pairs={{0,24},{8,16},{16,8},{24,0},{1,25},{9,17},{17,9},{25,1},{2,26},{10... | collective-permute-start | bytes 786440 | tf_op jit(solution)/shard_map/ppermute | solution.py:518
  680.6 127.5 %collective-permute-start.76 = (bf16[640,1024]{1,0:T(8,128)(2,1)}, bf16[640,1024]{1,0:T(8,128)(2,1)}, u32[]{:S(2)}, u32[]{:S(2)}) collective-permute-start(bf16[640,1024]{1,0:T(8,128)(2,1)} %get-tuple-element.187), channel_id=1, source_target_pairs={{0,0},{1,2},{2,1},{3,3},{4,4},{5,6},{6,5},{7,7},{8,8},{9,10},{10,9... | collective-permute-start | bytes 3932168 | tf_op jit(solution)/shard_map/ppermute | solution.py:522
  720.3 51.5 %collective-permute-start.119 = (bf16[2,64,512]{2,1,0:T(8,128)(2,1)}, bf16[2,64,512]{2,1,0:T(8,128)(2,1)S(1)}, u32[]{:S(2)}, u32[]{:S(2)}) collective-permute-start(bf16[2,64,512]{2,1,0:T(8,128)(2,1)} %get-tuple-element.93), channel_id=1, source_target_pairs={{0,4},{4,0},{1,5},{5,1},{2,6},{6,2},{3,7},{7,3},{8,12},{12,8},{9,1... | collective-permute-start | bytes 393224 | tf_op jit(solution)/shard_map/ppermute | solution.py:514
  773.3 35.5 %collective-permute-start.120 = (bf16[4,64,512]{2,1,0:T(8,128)(2,1)S(1)}, bf16[4,64,512]{2,1,0:T(8,128)(2,1)S(1)}, u32[]{:S(2)}, u32[]{:S(2)}) collective-permute-start(bf16[4,64,512]{2,1,0:T(8,128)(2,1)S(1)} %pad_maximum_fusion.24), channel_id=1, source_target_pairs={{0,1},{1,0},{2,3},{3,2},{4,5},{5,4},{6,7},{7,6},{8,9},{9,8},{10,11... | collective-permute-start | bytes 786440 | tf_op jit(solution)/shard_map/ppermute | solution.py:514
  790.1 34.8 %collective-permute-start.82 = (bf16[640,1024]{1,0:T(8,128)(2,1)S(1)}, bf16[640,1024]{1,0:T(8,128)(2,1)}, u32[]{:S(2)}, u32[]{:S(2)}) collective-permute-start(bf16[640,1024]{1,0:T(8,128)(2,1)S(1)} %get-tuple-element.161.refs_0_.refs_1_), channel_id=1, source_target_pairs={{0,2},{2,0},{1,3},{3,1},{4,6},{6,4},{5,7},{7,5},{8,10},{10,8},{9,1... | collective-permute-start | bytes 3932168 | tf_op jit(solution)/shard_map/ppermute | solution.py:514
  840.4 46.2 %collective-permute-start.141 = (bf16[2,64,2048]{2,1,0:T(8,128)(2,1)}, bf16[2,64,2048]{2,1,0:T(8,128)(2,1)}, u32[]{:S(2)}, u32[]{:S(2)}) collective-permute-start(bf16[2,64,2048]{2,1,0:T(8,128)(2,1)} %get-tuple-element.106), channel_id=1, source_target_pairs={{0,1},{1,0},{2,3},{3,2},{4,5},{5,4},{6,7},{7,6},{8,9},{9,8},{10,11... | collective-permute-start | bytes 1572872 | tf_op jit(solution)/shard_map/ppermute | solution.py:514
  842.2 41.2 %collective-permute-start.143 = (bf16[2,64,2048]{2,1,0:T(8,128)(2,1)}, bf16[2,64,2048]{2,1,0:T(8,128)(2,1)}, u32[]{:S(2)}, u32[]{:S(2)}) collective-permute-start(bf16[2,64,2048]{2,1,0:T(8,128)(2,1)} %get-tuple-element.108), channel_id=1, source_target_pairs={{0,4},{4,0},{1,5},{5,1},{2,6},{6,2},{3,7},{7,3},{8,12},{12,8},{9,1... | collective-permute-start | bytes 1572872 | tf_op jit(solution)/shard_map/ppermute | solution.py:514
  884.9 25.2 %collective-permute-start.144 = (bf16[4,64,2048]{2,1,0:T(8,128)(2,1)S(1)}, bf16[4,64,2048]{2,1,0:T(8,128)(2,1)S(1)}, u32[]{:S(2)}, u32[]{:S(2)}) collective-permute-start(bf16[4,64,2048]{2,1,0:T(8,128)(2,1)S(1)} %pad_maximum_fusion.10), channel_id=1, source_target_pairs={{0,1},{1,0},{2,3},{3,2},{4,5},{5,4},{6,7},{7,6},{8,9},{9,8},{10,11... | collective-permute-start | bytes 3145736 | tf_op jit(solution)/shard_map/ppermute | solution.py:514
  889.7 42.9 %collective-permute-start.128 = (bf16[4,64,2048]{2,1,0:T(8,128)(2,1)S(1)}, bf16[4,64,2048]{2,1,0:T(8,128)(2,1)}, u32[]{:S(2)}, u32[]{:S(2)}) collective-permute-start(bf16[4,64,2048]{2,1,0:T(8,128)(2,1)S(1)} %pad_maximum_fusion.6), channel_id=1, source_target_pairs={{0,1},{1,0},{2,3},{3,2},{4,5},{5,4},{6,7},{7,6},{8,9},{9,8},{10,11... | collective-permute-start | bytes 3145736 | tf_op jit(solution)/shard_map/ppermute | solution.py:514
  891.5 44.1 %collective-permute-start.126 = (bf16[4,64,2048]{2,1,0:T(8,128)(2,1)S(1)}, bf16[4,64,2048]{2,1,0:T(8,128)(2,1)S(1)}, u32[]{:S(2)}, u32[]{:S(2)}) collective-permute-start(bf16[4,64,2048]{2,1,0:T(8,128)(2,1)S(1)} %pad_maximum_fusion.5), channel_id=1, source_target_pairs={{0,4},{4,0},{1,5},{5,1},{2,6},{6,2},{3,7},{7,3},{8,12},{12,8},{9,1... | collective-permute-start | bytes 3145736 | tf_op jit(solution)/shard_map/ppermute | solution.py:514
  913.7 26.1 %collective-permute-start.145 = (bf16[64,2048]{1,0:T(8,128)(2,1)}, bf16[64,2048]{1,0:T(8,128)(2,1)}, u32[]{:S(2)}, u32[]{:S(2)}) collective-permute-start(bf16[64,2048]{1,0:T(8,128)(2,1)} %get-tuple-element.175), channel_id=1, source_target_pairs={{0,8},{8,0},{16,24},{24,16},{1,9},{9,1},{17,25},{25,17},{2,10},{10... | collective-permute-start | bytes 786440 | tf_op jit(solution)/shard_map/ppermute | solution.py:518
  916.7 25.5 %collective-permute-start.147 = (bf16[64,2048]{1,0:T(8,128)(2,1)}, bf16[64,2048]{1,0:T(8,128)(2,1)}, u32[]{:S(2)}, u32[]{:S(2)}) collective-permute-start(bf16[64,2048]{1,0:T(8,128)(2,1)} %get-tuple-element.176), channel_id=1, source_target_pairs={{0,24},{8,16},{16,8},{24,0},{1,25},{9,17},{17,9},{25,1},{2,26},{10... | collective-permute-start | bytes 786440 | tf_op jit(solution)/shard_map/ppermute | solution.py:518
  917.1 26.2 %collective-permute-start.146 = (bf16[64,2048]{1,0:T(8,128)(2,1)S(1)}, bf16[64,2048]{1,0:T(8,128)(2,1)}, u32[]{:S(2)}, u32[]{:S(2)}) collective-permute-start(bf16[64,2048]{1,0:T(8,128)(2,1)S(1)} %get-tuple-element.177), channel_id=1, source_target_pairs={{0,16},{8,24},{16,0},{24,8},{1,17},{9,25},{17,1},{25,9},{2,18},{10... | collective-permute-start | bytes 786440 | tf_op jit(solution)/shard_map/ppermute | solution.py:518
  937.6 55.1 %collective-permute-start.84 = (bf16[640,1024]{1,0:T(8,128)(2,1)S(1)}, bf16[640,1024]{1,0:T(8,128)(2,1)}, u32[]{:S(2)}, u32[]{:S(2)}) collective-permute-start(bf16[640,1024]{1,0:T(8,128)(2,1)S(1)} %fusion.2.refs_0_.refs_1_), channel_id=1, source_target_pairs={{0,2},{2,0},{1,3},{3,1},{4,6},{6,4},{5,7},{7,5},{8,10},{10,8},{9,1... | collective-permute-start | bytes 3932168 | tf_op jit(solution)/shard_map/ppermute | solution.py:514
  943.3 27.3 %collective-permute-start.130 = (bf16[64,2048]{1,0:T(8,128)(2,1)S(1)}, bf16[64,2048]{1,0:T(8,128)(2,1)S(1)}, u32[]{:S(2)}, u32[]{:S(2)}) collective-permute-start(bf16[64,2048]{1,0:T(8,128)(2,1)S(1)} %get-tuple-element.183), channel_id=1, source_target_pairs={{0,16},{8,24},{16,0},{24,8},{1,17},{9,25},{17,1},{25,9},{2,18},{10... | collective-permute-start | bytes 786440 | tf_op jit(solution)/shard_map/ppermute | solution.py:518
  946.6 40.0 %collective-permute-start.156 = (bf16[64,2048]{1,0:T(8,128)(2,1)}, bf16[64,2048]{1,0:T(8,128)(2,1)}, u32[]{:S(2)}, u32[]{:S(2)}) collective-permute-start(bf16[64,2048]{1,0:T(8,128)(2,1)} %fusion.32), channel_id=1, source_target_pairs={{0,0},{1,2},{2,1},{3,3},{4,4},{5,6},{6,5},{7,7},{8,8},{9,10},{10,9... | collective-permute-start | bytes 786440 | tf_op jit(solution)/shard_map/ppermute | solution.py:522
  986.6 102.5 %collective-permute-start.124 = (bf16[64,512]{1,0:T(8,128)(2,1)S(1)}, bf16[64,512]{1,0:T(8,128)(2,1)}, u32[]{:S(2)}, u32[]{:S(2)}) collective-permute-start(bf16[64,512]{1,0:T(8,128)(2,1)S(1)} %fusion.68), channel_id=1, source_target_pairs={{0,0},{1,2},{2,1},{3,3},{4,4},{5,6},{6,5},{7,7},{8,8},{9,10},{10,9... | collective-permute-start | bytes 196616 | tf_op jit(solution)/shard_map/ppermute | solution.py:522
  1065.6 36.7 %collective-permute-start.85 = (bf16[640,1024]{1,0:T(8,128)(2,1)S(1)}, bf16[640,1024]{1,0:T(8,128)(2,1)}, u32[]{:S(2)}, u32[]{:S(2)}) collective-permute-start(bf16[640,1024]{1,0:T(8,128)(2,1)S(1)} %one_back.31), channel_id=1, source_target_pairs={{0,2},{2,0},{1,3},{3,1},{4,6},{6,4},{5,7},{7,5},{8,10},{10,8},{9,1... | collective-permute-start | bytes 3932168 | tf_op jit(solution)/shard_map/ppermute | solution.py:514
  1076.2 29.9 %collective-permute-start.96 = (bf16[4,64,1536]{2,1,0:T(8,128)(2,1)}, bf16[4,64,1536]{2,1,0:T(8,128)(2,1)}, u32[]{:S(2)}, u32[]{:S(2)}) collective-permute-start(bf16[4,64,1536]{2,1,0:T(8,128)(2,1)} %pad_maximum_fusion.16), channel_id=1, source_target_pairs={{0,1},{1,0},{2,3},{3,2},{4,5},{5,4},{6,7},{7,6},{8,9},{9,8},{10,11... | collective-permute-start | bytes 2359304 | tf_op jit(solution)/shard_map/ppermute | solution.py:514
  1109.4 33.1 %collective-permute-start.97 = (bf16[64,1536]{1,0:T(8,128)(2,1)}, bf16[64,1536]{1,0:T(8,128)(2,1)}, u32[]{:S(2)}, u32[]{:S(2)}) collective-permute-start(bf16[64,1536]{1,0:T(8,128)(2,1)} %get-tuple-element.188), channel_id=1, source_target_pairs={{0,8},{8,0},{16,24},{24,16},{1,9},{9,1},{17,25},{25,17},{2,10},{10... | collective-permute-start | bytes 589832 | tf_op jit(solution)/shard_map/ppermute | solution.py:518
  1111.5 31.0 %collective-permute-start.99 = (bf16[64,1536]{1,0:T(8,128)(2,1)}, bf16[64,1536]{1,0:T(8,128)(2,1)}, u32[]{:S(2)}, u32[]{:S(2)}) collective-permute-start(bf16[64,1536]{1,0:T(8,128)(2,1)} %get-tuple-element.189), channel_id=1, source_target_pairs={{0,24},{8,16},{16,8},{24,0},{1,25},{9,17},{17,9},{25,1},{2,26},{10... | collective-permute-start | bytes 589832 | tf_op jit(solution)/shard_map/ppermute | solution.py:518
  1112.4 30.1 %collective-permute-start.98 = (bf16[64,1536]{1,0:T(8,128)(2,1)}, bf16[64,1536]{1,0:T(8,128)(2,1)}, u32[]{:S(2)}, u32[]{:S(2)}) collective-permute-start(bf16[64,1536]{1,0:T(8,128)(2,1)} %get-tuple-element.190), channel_id=1, source_target_pairs={{0,16},{8,24},{16,0},{24,8},{1,17},{9,25},{17,1},{25,9},{2,18},{10... | collective-permute-start | bytes 589832 | tf_op jit(solution)/shard_map/ppermute | solution.py:518
  1138.6 30.3 %collective-permute-start.86 = (bf16[640,1024]{1,0:T(8,128)(2,1)S(1)}, bf16[640,1024]{1,0:T(8,128)(2,1)S(1)}, u32[]{:S(2)}, u32[]{:S(2)}) collective-permute-start(bf16[640,1024]{1,0:T(8,128)(2,1)S(1)} %add_convert_fusion), channel_id=1, source_target_pairs={{0,0},{1,2},{2,1},{3,3},{4,4},{5,6},{6,5},{7,7},{8,8},{9,10},{10,9... | collective-permute-start | bytes 3932168 | tf_op jit(solution)/shard_map/ppermute | solution.py:522
  (271 other events, 4351.1 us)

commit v2 on v0

--- a/solution.py
+++ b/solution.py
@@ -2,6 +2,9 @@
 import jax.numpy as jnp
 import numpy as np
 from jax import lax
+from jax.experimental import pallas as pl
+from jax.experimental.pallas import tpu as pltpu
+from jax.sharding import Mesh
 from jax.sharding import PartitionSpec as P
 
 HEAD_DIM = 64
@@ -460,7 +463,7 @@
     )
 
 
-def solution(mesh):
+def solution_any(mesh):
     placed = (
         P("dp", None, "mp", None, None),
         P("dp", None, "mp", None, None),
@@ -498,3 +501,1133 @@
         ),
         check_vma=False,
     )
+
+
+low = jnp.bfloat16
+full = jnp.float32
+HALF_ROOT = 0.7071067811865476
+PHI_AT_ZERO = 0.3989422804014327
+MIB = 1024 * 1024
+
+
+def flip(values, axis):
+    return lax.ppermute(values, axis, [(0, 1), (1, 0)])
+
+
+def z_trade(values, step):
+    return lax.ppermute(values, "z", [(place, place ^ step) for place in range(4)])
+
+
+def swap(values):
+    return lax.ppermute(values, ("c", "x"), [(0, 0), (1, 2), (2, 1), (3, 3)])
+
+
+def shape_of(dims, dtype=low):
+    return jax.ShapeDtypeStruct(tuple(dims), dtype)
+
+
+def whole(array):
+    zeros = (0,) * len(array.shape)
+    return pl.BlockSpec(tuple(array.shape), lambda *at: zeros)
+
+
+class Chain:
+    def __init__(self, info):
+        self.info = info
+        self.last = []
+        self.pending = []
+
+    def wait(self, *values):
+        self.pending += values
+
+    def run(self, name, kernel, args, in_specs, outs, out_specs, grid=(1,), scratch=(), mib=48, waits=()):
+        count = len(args)
+        unread = self.last + self.pending + list(waits)
+        self.pending = []
+        held = len(unread)
+
+        def body(*refs):
+            kernel(*refs[: 1 + count], *refs[1 + count + held :])
+
+        results = pl.pallas_call(
+            body,
+            grid_spec=pltpu.PrefetchScalarGridSpec(
+                num_scalar_prefetch=1,
+                grid=grid,
+                in_specs=list(in_specs) + [pl.BlockSpec(memory_space=pl.ANY)] * held,
+                out_specs=list(out_specs),
+                scratch_shapes=list(scratch),
+            ),
+            out_shape=list(outs),
+            compiler_params=pltpu.CompilerParams(vmem_limit_bytes=mib * MIB),
+            cost_estimate=pl.CostEstimate(flops=1, bytes_accessed=1, transcendentals=0),
+            name=name,
+        )(self.info, *args, *unread)
+        self.last = [results[0]]
+        return results
+
+
+def cut_kernel(info, packed, *outs):
+    start = 0
+    for out in outs:
+        width = out.shape[1]
+        out[...] = packed[:, start : start + width]
+        start += width
+
+
+PIECE = 2048
+PIECE_TILE = 512
+
+
+def tile_spec(count, rows=64):
+    return pl.BlockSpec((count, rows, PIECE_TILE), lambda j, info: (0, 0, j))
+
+
+def flat_spec(rows=64):
+    return pl.BlockSpec((rows, PIECE_TILE), lambda j, info: (0, j))
+
+
+class Gather:
+    def __init__(self, chain, shards):
+        self.chain = chain
+        self.shards = shards
+        self.near = {}
+        self.sent = {}
+        self.got = {}
+        self.step_at = 0
+
+    def over_z(self, at):
+        self.near[at] = [z_trade(self.shards[at], k) for k in (1, 2, 3)]
+
+    def step(self):
+        at = self.step_at
+        self.step_at += 1
+        own = at < len(self.shards)
+        far = at > 0
+        args, specs = [], []
+        if own:
+            args += [self.shards[at]] + self.near[at]
+            specs += [flat_spec()] * 4
+        start = 0
+        if far:
+            got_x, got_y = self.got[at - 1]
+            start = got_x.shape[0] - 4
+            args += [got_x, got_y]
+            specs += [tile_spec(got_x.shape[0])] * 2
+
+        def kernel(info, *refs):
+            to_x, to_y = refs[-2:]
+            if own:
+                for k in range(4):
+                    to_x[(2 if far else 0) + k] = refs[k][...]
+                    to_y[(2 if far else 0) + k] = refs[k][...]
+            if far:
+                from_x, from_y = refs[-4:-2]
+                to_x[0:2] = from_y[start : start + 2]
+                to_y[0:2] = from_x[start + 2 : start + 4]
+
+        count = (2 if far else 0) + (4 if own else 0)
+        outs = [shape_of((count, 64, PIECE))] * 2
+        to_x, to_y = self.chain.run(
+            "gather_step",
+            kernel,
+            args,
+            specs,
+            outs,
+            [tile_spec(count)] * 2,
+            grid=(PIECE // PIECE_TILE,),
+        )
+        self.sent[at] = to_x
+        self.got[at] = (flip(to_x, "x"), flip(to_y, "y"))
+
+    def place(self, at, widths):
+        def kernel(info, own, from_x, from_y, far_lo, far_hi, *outs):
+            k = pl.program_id(0)
+            place = info[1] * 2 + info[2]
+
+            def put(rel, block):
+                start = 0
+                for out in outs:
+                    width = out.shape[3]
+                    out[0, place ^ rel] = block[0, :, start : start + width]
+                    start += width
+
+            put(0, own)
+            put(1, from_x)
+            put(2, from_y)
+
+            @pl.when(k < 2)
+            def _():
+                put(3, far_lo)
+
+            @pl.when(k >= 2)
+            def _():
+                put(3, far_hi)
+
+        got_x, got_y = self.got[at]
+        start = got_x.shape[0] - 4
+        block = (1, 64, PIECE)
+        quad = pl.BlockSpec(block, lambda k, info: (k + start, 0, 0))
+        results = self.chain.run(
+            "place_weights",
+            kernel,
+            [self.sent[at], got_x, got_y, *self.got[at + 1]],
+            [
+                quad,
+                quad,
+                quad,
+                pl.BlockSpec(block, lambda k, info: (jnp.minimum(k, 1), 0, 0)),
+                pl.BlockSpec(block, lambda k, info: (jnp.maximum(k - 2, 0), 0, 0)),
+            ],
+            [shape_of((4, 4, 64, w)) for w in widths],
+            [pl.BlockSpec((1, 4, 64, w), lambda k, info: (info[0] ^ k, 0, 0, 0)) for w in widths],
+            grid=(4,),
+        )
+        return [a.reshape(16 * 64, a.shape[3]) for a in results]
+
+
+def weight_grad_kernel(info, *refs, pairs, widths):
+    lhs = refs[: 4 * pairs]
+    rhs = refs[4 * pairs : 5 * pairs]
+    near, to_x, to_y, far_lo, far_hi, held = refs[5 * pairs :]
+    z = pl.program_id(0)
+    place = info[1] * 2 + info[2]
+    start = 0
+    for at in range(pairs):
+        halves = []
+        for half in range(2):
+            spot = 4 * at + 2 * half
+            halves.append(jnp.concatenate([lhs[spot][...].T, lhs[spot + 1][...].T], axis=1))
+        for begin in range(0, widths[at], 512):
+            cols = slice(begin, begin + 512)
+            block = jnp.dot(
+                halves[0], rhs[at][0, :, cols], preferred_element_type=full
+            ) + jnp.dot(halves[1], rhs[at][1, :, cols], preferred_element_type=full)
+            held[:, start + begin : start + begin + 512] = block.astype(low)
+        start += widths[at]
+
+    def part(rel):
+        return held[pl.ds(pl.multiple_of((place ^ rel) * 64, 64), 64), :]
+
+    near[0] = part(0)
+    to_x[0] = part(1)
+    to_y[0] = part(2)
+
+    @pl.when(z < 2)
+    def _():
+        far_lo[0] = part(3)
+
+    @pl.when(z >= 2)
+    def _():
+        far_hi[0] = part(3)
+
+
+class Scatter:
+    def __init__(self, chain):
+        self.chain = chain
+        self.parts = []
+        self.got = None
+        self.held = None
+        self.done = []
+        self.step_at = 0
+
+    def weight_grad(self, *items):
+        pairs = len(items)
+        widths = tuple(item[2].shape[2] for item in items)
+        rows, features = items[0][0][0].shape
+        tile = features // 4
+        quads = shape_of((4, 64, PIECE))
+        twos = shape_of((2, 64, PIECE))
+        lhs_spec = pl.BlockSpec((rows, tile), lambda z, info: (0, z))
+        block = (1, 64, PIECE)
+        self.parts.append(
+            self.chain.run(
+                "weight_grad",
+                lambda *refs: weight_grad_kernel(*refs, pairs=pairs, widths=widths),
+                [part for item in items for pair in item[:2] for part in pair]
+                + [item[2] for item in items],
+                [lhs_spec] * (4 * pairs)
+                + [pl.BlockSpec((2, 2 * rows, w), lambda z, info: (0, 0, 0)) for w in widths],
+                [quads, quads, quads, twos, twos],
+                [pl.BlockSpec(block, lambda z, info: (z, 0, 0))] * 3
+                + [
+                    pl.BlockSpec(block, lambda z, info: (jnp.minimum(z, 1), 0, 0)),
+                    pl.BlockSpec(block, lambda z, info: (jnp.maximum(z - 2, 0), 0, 0)),
+                ],
+                grid=(4,),
+                scratch=[pltpu.VMEM((tile, PIECE), low)],
+                mib=56,
+            )
+        )
+        if len(self.parts) == 1:
+            self.got = (flip(self.parts[0][3], "x"), flip(self.parts[0][4], "y"))
+
+    def step(self, total):
+        at = self.step_at
+        self.step_at += 1
+        far = at + 1 < total
+        mid = at < total
+        near = 0 <= at - 1 < total
+        last = 0 <= at - 2 < total
+        args, specs = [], []
+
+        def put(array, spec):
+            args.append(array)
+            specs.append(spec)
+            return len(args) - 1
+
+        names = {}
+        if far:
+            names["far_lo"] = put(self.parts[at + 1][3], tile_spec(2))
+            names["far_hi"] = put(self.parts[at + 1][4], tile_spec(2))
+        if mid:
+            names["to_x"] = put(self.parts[at][1], tile_spec(4))
+            names["to_y"] = put(self.parts[at][2], tile_spec(4))
+        if near:
+            names["near"] = put(self.parts[at - 1][0], tile_spec(4))
+        if mid or near:
+            count = self.got[0].shape[0]
+            names["got_x"] = put(self.got[0], tile_spec(count))
+            names["got_y"] = put(self.got[1], tile_spec(count))
+        if last:
+            for k in range(4):
+                names["held%d" % k] = put(self.held[k], flat_spec())
+        outs, out_specs = [], []
+        sent = (2 if far else 0) + (4 if mid else 0)
+        if mid:
+            outs += [shape_of((sent, 64, PIECE))] * 2
+            out_specs += [tile_spec(sent)] * 2
+        if near:
+            outs += [shape_of((64, PIECE), full)] + [shape_of((64, PIECE))] * 3
+            out_specs += [flat_spec()] * 4
+        if last:
+            outs.append(shape_of((64, PIECE)))
+            out_specs.append(flat_spec())
+        number = len(args)
+
+        def kernel(info, *refs):
+            out = list(refs[number:])
+            get = {name: refs[spot] for name, spot in names.items()}
+            if mid:
+                out_x, out_y = out[:2]
+                del out[:2]
+                start = 0
+                if far:
+                    out_x[0:2] = get["far_lo"][...]
+                    out_y[0:2] = get["far_hi"][...]
+                    start = 2
+                for k in range(4):
+                    part_x = get["to_x"][k]
+                    part_y = get["to_y"][k]
+                    if k < 2:
+                        part_y = (part_y.astype(full) + get["got_x"][k].astype(full)).astype(low)
+                    else:
+                        part_x = (
+                            part_x.astype(full) + get["got_y"][k - 2].astype(full)
+                        ).astype(low)
+                    out_x[start + k] = part_x
+                    out_y[start + k] = part_y
+            if near:
+                start = get["got_x"].shape[0] - 4
+                for k in range(4):
+                    spot = info[0] ^ k
+                    value = get["near"][spot].astype(full)
+                    value = value + get["got_x"][start + spot].astype(full)
+                    value = value + get["got_y"][start + spot].astype(full)
+                    out[k][...] = value.astype(out[k].dtype)
+                del out[:4]
+            if last:
+                value = get["held0"][...]
+                for k in (1, 2, 3):
+                    value = value + get["held%d" % k][...].astype(full)
+                out[0][...] = value.astype(low)
+
+        results = list(
+            self.chain.run(
+                "scatter_step", kernel, args, specs, outs, out_specs, grid=(PIECE // PIECE_TILE,)
+            )
+        )
+        if mid:
+            self.got = (flip(results[0], "x"), flip(results[1], "y"))
+            del results[:2]
+        if near:
+            self.held = [results[0]] + [z_trade(results[k], k) for k in (1, 2, 3)]
+            del results[:4]
+        if last:
+            self.done.append(results[0])
+
+
+def add_all(chain, *values):
+    def kernel(info, *refs):
+        total = refs[0][...]
+        for other in refs[1:-1]:
+            total = total + other[...]
+        refs[-1][...] = total
+
+    out = shape_of(values[0].shape, full)
+    (result,) = chain.run(
+        "add_all", kernel, list(values), [whole(a) for a in values], [out], [whole(out)]
+    )
+    return result
+
+
+def join_pieces(chain, pieces):
+    def kernel(info, *refs):
+        for at, piece in enumerate(refs[:-1]):
+            refs[-1][:, at * PIECE : (at + 1) * PIECE] = piece[...]
+
+    out = shape_of((64, PIECE * len(pieces)))
+    (result,) = chain.run(
+        "join_pieces", kernel, pieces, [whole(a) for a in pieces], [out], [whole(out)]
+    )
+    return result
+
+
+def gelu_and_slope(values):
+    bell = jnp.exp(-0.5 * values * values)
+    t = 1.0 / (1.0 + (0.3275911 * HALF_ROOT) * jnp.abs(values))
+    poly = t * (
+        0.254829592
+        + t * (-0.284496736 + t * (1.421413741 + t * (-1.453152027 + t * 1.061405429)))
+    )
+    tail = 0.5 * poly * bell
+    phi = jnp.where(values >= 0, 1.0 - tail, tail)
+    return values * phi, phi + (PHI_AT_ZERO * values) * bell
+
+
+ROW_TILE = 320
+
+
+def flip_rows(pair):
+    return tuple(flip(part, "c") for part in pair)
+
+
+def both_kernel(info, *refs, kind):
+    weight = refs[4][...]
+    for part in range(4):
+        half = part // 2
+        rows = slice(part % 2 * ROW_TILE, (part % 2 + 1) * ROW_TILE)
+        product = jnp.dot(refs[part][...], weight, preferred_element_type=full)
+        if kind == "gelu":
+            act, slope = gelu_and_slope(product)
+            refs[5][half, rows] = act.astype(low)
+            refs[6][half, rows] = slope.astype(low)
+        elif kind == "slope":
+            refs[6][half, rows] = (product * refs[5][half, rows].astype(full)).astype(low)
+        else:
+            refs[5][half, rows] = product.astype(low)
+
+
+def both_times(chain, kind, own, other, weight, slope=None, waits=()):
+    depth = weight.shape[0]
+    rows = 2 * ROW_TILE
+    width = weight.shape[1]
+    tile = 256 if kind == "gelu" else 512
+    out_spec = pl.BlockSpec((2, rows, tile), lambda j, info: (0, 0, j))
+    extra = [] if slope is None else [slope]
+    count = 2 if kind == "gelu" else 1
+    return chain.run(
+        "both_" + kind,
+        lambda *refs: both_kernel(*refs, kind=kind),
+        [*own, *other, weight] + extra,
+        [whole(part) for part in (*own, *other)]
+        + [pl.BlockSpec((depth, tile), lambda j, info: (0, j))]
+        + [out_spec] * len(extra),
+        [shape_of((2, rows, width))] * count,
+        [out_spec] * count,
+        grid=(width // tile,),
+        waits=waits,
+    )
+
+
+def times_back(values, weight):
+    return lax.dot_general(
+        values, weight, (((1,), (1,)), ((), ())), preferred_element_type=full
+    ).astype(low)
+
+
+def other_rows(chain, values, weight):
+    rows, depth = values.shape[1:]
+    width = weight.shape[0]
+    tile = 256
+
+    def kernel(info, rows_in, weight_in, first, second):
+        result = times_back(rows_in[0], weight_in[...])
+        first[...] = result[:ROW_TILE]
+        second[...] = result[ROW_TILE:]
+
+    half = pl.BlockSpec((ROW_TILE, tile), lambda j, info: (0, j))
+    results = chain.run(
+        "other_rows",
+        kernel,
+        [values, weight],
+        [
+            pl.BlockSpec((1, rows, depth), lambda j, info: (1, 0, 0)),
+            pl.BlockSpec((tile, depth), lambda j, info: (j, 0)),
+        ],
+        [shape_of((ROW_TILE, width))] * 2,
+        [half] * 2,
+        grid=(width // tile,),
+    )
+    return flip_rows(results)
+
+
+def put_half(pair, values):
+    @pl.when(pl.program_id(0) == 0)
+    def _():
+        pair[0][...] = values
+
+    @pl.when(pl.program_id(0) == 1)
+    def _():
+        pair[1][...] = values
+
+
+def get_half(pair):
+    return jnp.where(pl.program_id(0) == 0, pair[0][...].astype(full), pair[1][...].astype(full))
+
+
+def shown_rows(info):
+    first = pl.program_id(0) * ROW_TILE
+    row = first + lax.broadcasted_iota(jnp.int32, (ROW_TILE, 1), 0)
+    return (row < info[3] * 128).astype(full)
+
+
+def norm_and_move(values, shift, scale):
+    center = values - jnp.mean(values, axis=-1, keepdims=True)
+    spread = jnp.mean(center * center, axis=-1, keepdims=True)
+    inverse = lax.rsqrt(spread + epsilon)
+    normed = center * inverse
+    return normed.astype(low), inverse, (normed * (1.0 + scale) + shift).astype(low)
+
+
+def row_specs(model_width):
+    tall = pl.BlockSpec((ROW_TILE, model_width), lambda i, info: (i, 0))
+    thin = pl.BlockSpec((ROW_TILE, 1), lambda i, info: (i, 0))
+    return tall, thin
+
+
+def first_norm(chain, current, rows_of):
+    rows, model_width = current.shape
+    tall, thin = row_specs(model_width)
+
+    def kernel(info, values, given, normed, inverse, *moved):
+        normed[...], inverse[...], result = norm_and_move(
+            values[...].astype(full), given[0:1], given[1:2]
+        )
+        put_half(moved, result)
+
+    half = shape_of((ROW_TILE, model_width))
+    normed, inverse, *moved = chain.run(
+        "first_norm",
+        kernel,
+        [current, rows_of],
+        [tall, whole(rows_of)],
+        [shape_of(current.shape), shape_of((rows, 1), full), half, half],
+        [tall, thin, whole(half), whole(half)],
+        grid=(rows // ROW_TILE,),
+    )
+    return normed, inverse, moved
+
+
+def forward_step(chain, values, weight, away, current, rows_of, last, waits=()):
+    rows, model_width = current.shape
+    depth = values.shape[2]
+    tall, thin = row_specs(model_width)
+
+    def kernel(info, own, weight_in, first, second, current_in, given, after, branch_out, *rest):
+        branch = times_back(own[0], weight_in[...]).astype(full) + get_half((first, second))
+        total = current_in[...].astype(full) + shown_rows(info) * given[0:1] * branch
+        after[...] = total.astype(after.dtype)
+        branch_out[...] = branch.astype(low)
+        if not last:
+            normed, inverse, *moved = rest
+            normed[...], inverse[...], result = norm_and_move(total, given[1:2], given[2:3])
+            put_half(moved, result)
+
+    outs = [shape_of(current.shape, low if last else full), shape_of(current.shape)]
+    specs = [tall, tall]
+    if not last:
+        half = shape_of((ROW_TILE, model_width))
+        outs += [shape_of(current.shape), shape_of((rows, 1), full), half, half]
+        specs += [tall, thin, whole(half), whole(half)]
+    results = chain.run(
+        "forward_step",
+        kernel,
+        [values, weight, *away, current, rows_of],
+        [
+            pl.BlockSpec((1, ROW_TILE, depth), lambda i, info: (0, i, 0)),
+            whole(weight),
+            whole(away[0]),
+            whole(away[1]),
+            tall,
+            whole(rows_of),
+        ],
+        outs,
+        specs,
+        grid=(rows // ROW_TILE,),
+        waits=waits,
+    )
+    return results if last else (*results[:4], results[4:])
+
+
+def add_rows(out, at, values):
+    total = jnp.sum(values, axis=0, keepdims=True)
+
+    @pl.when(pl.program_id(0) == 0)
+    def _():
+        out[at : at + 1] = total
+
+    @pl.when(pl.program_id(0) > 0)
+    def _():
+        out[at : at + 1] += total
+
+
+def first_back(chain, state, branch, gate):
+    rows, model_width = state.shape
+    tall, _ = row_specs(model_width)
+
+    def kernel(info, state_in, branch_in, gate_in, first, second, sums):
+        values = state_in[...].astype(full) * shown_rows(info)
+        put_half((first, second), (values * gate_in[...]).astype(low))
+        add_rows(sums, 0, values * branch_in[...].astype(full))
+
+    sums = shape_of((8, model_width), full)
+    half = shape_of((ROW_TILE, model_width))
+    first, second, sums = chain.run(
+        "first_back",
+        kernel,
+        [state, branch, gate],
+        [tall, tall, whole(gate)],
+        [half, half, sums],
+        [whole(half), whole(half), whole(sums)],
+        grid=(rows // ROW_TILE,),
+    )
+    return (first, second), sums
+
+
+def backward_step(chain, values, weight, away, normed, inverse, state, rows_of, branch):
+    rows, model_width = state.shape
+    depth = values.shape[2]
+    tall, thin = row_specs(model_width)
+    last = branch is None
+
+    def kernel(
+        info, own, weight_in, first, second, normed_in, inverse_in, state_in, given, *rest
+    ):
+        grad = times_back(own[0], weight_in[...]).astype(full) + get_half((first, second))
+        normal = normed_in[...].astype(full)
+        moved = grad * (1.0 + given[0:1])
+        first_mean = jnp.mean(moved, axis=-1, keepdims=True)
+        second_mean = jnp.mean(moved * normal, axis=-1, keepdims=True)
+        total = state_in[...].astype(full) + inverse_in[...] * (
+            moved - first_mean - normal * second_mean
+        )
+        if last:
+            state_out, sums = rest
+        else:
+            branch_in, state_out, sums, *sent = rest
+        state_out[...] = total.astype(state_out.dtype)
+        add_rows(sums, 0, grad)
+        add_rows(sums, 1, grad * normal)
+        if not last:
+            shown = total * shown_rows(info)
+            put_half(sent, (shown * given[1:2]).astype(low))
+            add_rows(sums, 2, shown * branch_in[...].astype(full))
+
+    sums = shape_of((8, model_width), full)
+    outs = [shape_of(state.shape, low if last else full), sums]
+    specs = [tall, whole(sums)]
+    if not last:
+        half = shape_of((ROW_TILE, model_width))
+        outs += [half, half]
+        specs += [whole(half)] * 2
+    extra = [] if last else [branch]
+    results = chain.run(
+        "backward_step",
+        kernel,
+        [values, weight, *away, normed, inverse, state, rows_of] + extra,
+        [
+            pl.BlockSpec((1, ROW_TILE, depth), lambda i, info: (0, i, 0)),
+            whole(weight),
+            whole(away[0]),
+            whole(away[1]),
+            tall,
+            thin,
+            tall,
+            whole(rows_of),
+        ]
+        + [tall] * len(extra),
+        outs,
+        specs,
+        grid=(rows // ROW_TILE,),
+    )
+    return results if last else (*results[:2], results[2:])
+
+
+def attend_kernel(info, blocks, joined, mixed, probs, bias, *, heads, cells, masked, sides):
+    width = heads * HEAD_DIM
+
+    @pl.when((pl.program_id(0) == 0) & (pl.program_id(1) == 0))
+    def _():
+        for h in range(heads):
+            for place, spots in enumerate(sides):
+                block = blocks[h, place]
+                for row, col in spots:
+                    bias[h, row * 64 : row * 64 + 64, col * 64 : col * 64 + 64] = block
+
+    values = joined[...].reshape(cells, 3 * width)
+    lead = mixed.shape
+    if masked:
+        column = lax.broadcasted_iota(jnp.int32, (1, cells), 1)
+        shown = column < info[3] * (WIN_T * WIN_T)
+    outs = []
+    for h in range(heads):
+        cols = slice(h * HEAD_DIM, (h + 1) * HEAD_DIM)
+        query = values[:, cols]
+        key = values[:, width + h * HEAD_DIM : width + (h + 1) * HEAD_DIM]
+        value = values[:, 2 * width + h * HEAD_DIM : 2 * width + (h + 1) * HEAD_DIM]
+        scores = lax.dot_general(
+            query, key, (((1,), (1,)), ((), ())), preferred_element_type=full
+        ) * HEAD_DIM ** (-0.5) + bias[h].astype(full)
+        if masked:
+            scores = jnp.where(shown, scores, masked_score)
+        weights = jnp.exp(scores - jnp.max(scores, axis=-1, keepdims=True))
+        share = (weights * (1.0 / jnp.sum(weights, axis=-1, keepdims=True))).astype(low)
+        probs[0, h] = share
+        outs.append(jnp.dot(share, value, preferred_element_type=full).astype(low))
+    mixed[...] = jnp.concatenate(outs, axis=1).reshape(lead)
+
+
+def attend_back_kernel(info, joined, grad, probs, back, bias_out, total, *, heads, cells, sides):
+    step = pl.program_id(0) * pl.num_programs(1) + pl.program_id(1)
+    width = heads * HEAD_DIM
+    values = joined[...].reshape(cells, 3 * width)
+    grads = grad[...].reshape(cells, width)
+    grads_t = grads.astype(full).T.astype(low)
+    queries_t = values[:, :width].astype(full).T.astype(low)
+    queries, keys_t, values_t = [], [], []
+
+    @pl.when(step == 0)
+    def _():
+        total[...] = jnp.zeros(total.shape, full)
+
+    for h in range(heads):
+        cols = slice(h * HEAD_DIM, (h + 1) * HEAD_DIM)
+        key = values[:, width + h * HEAD_DIM : width + (h + 1) * HEAD_DIM]
+        value = values[:, 2 * width + h * HEAD_DIM : 2 * width + (h + 1) * HEAD_DIM]
+        share = probs[0, h]
+        values_t.append(jnp.dot(grads_t[cols], share, preferred_element_type=full).astype(low))
+        grad_share = lax.dot_general(
+            grads[:, cols], value, (((1,), (1,)), ((), ())), preferred_element_type=full
+        )
+        share_full = share.astype(full)
+        product = share_full * grad_share
+        row_dot = jnp.sum(product, axis=-1, keepdims=True)
+        grad_scores = (product - share_full * row_dot).astype(low)
+        total[h] += grad_scores.astype(full)
+        queries.append(
+            (jnp.dot(grad_scores, key, preferred_element_type=full) * HEAD_DIM ** (-0.5)).astype(
+                low
+            )
+        )
+        keys_t.append(
+            (
+                jnp.dot(queries_t[cols], grad_scores, preferred_element_type=full)
+                * HEAD_DIM ** (-0.5)
+            ).astype(low)
+        )
+    key_grads = jnp.concatenate(keys_t, axis=0).astype(full).T.astype(low)
+    value_grads = jnp.concatenate(values_t, axis=0).astype(full).T.astype(low)
+    back[...] = jnp.concatenate(queries + [key_grads, value_grads], axis=1).reshape(back.shape)
+
+    @pl.when(step == pl.num_programs(0) * pl.num_programs(1) - 1)
+    def _():
+        for h in range(heads):
+            for place, spots in enumerate(sides):
+                part = None
+                for row, col in spots:
+                    block = total[h, row * 64 : row * 64 + 64, :][:, col * 64 : col * 64 + 64]
+                    part = block if part is None else part + block
+                bias_out[h, place] = part
+
+
+def spatial_sides():
+    sides = [[] for _ in range(9)]
+    for row in range(4):
+        for col in range(4):
+            place = (row // 2 - col // 2 + 1) * 3 + (row % 2 - col % 2 + 1)
+            sides[place].append((row, col))
+    return sides
+
+
+def joint_sides():
+    sides = [[] for _ in range(2 * FRAMES - 1)]
+    for row in range(FRAMES):
+        for col in range(FRAMES):
+            sides[row - col + FRAMES - 1].append((row, col))
+    return sides
+
+
+def window_specs(is_joint, frames, width):
+    if is_joint:
+        shape, at = (1, frames, 1, 64, width), lambda i, j, info: (i, 0, j, 0, 0)
+    else:
+        shape, at = (2, 1, 2, 64, width), lambda i, j, info: (0, j, 0, 0, 0)
+    return pl.BlockSpec(shape, at)
+
+
+def attend(chain, blocks, joined, is_joint):
+    frames = joined.shape[1]
+    heads = blocks.shape[0]
+    width = heads * HEAD_DIM
+    grid = (2, 2) if is_joint else (1, frames)
+    cells = 64 * frames if is_joint else 256
+    number = grid[0] * grid[1]
+    sides = joint_sides() if is_joint else spatial_sides()
+    fetch = lambda i, j, info: (i * grid[1] + j, 0, 0, 0)
+    return chain.run(
+        "attend_joint" if is_joint else "attend_spatial",
+        lambda *refs: attend_kernel(
+            *refs, heads=heads, cells=cells, masked=is_joint, sides=sides
+        ),
+        [blocks, joined],
+        [whole(blocks), window_specs(is_joint, frames, 3 * width)],
+        [shape_of(joined.shape[:4] + (width,)), shape_of((number, heads, cells, cells))],
+        [window_specs(is_joint, frames, width), pl.BlockSpec((1, heads, cells, cells), fetch)],
+        grid=grid,
+        scratch=[pltpu.VMEM((heads, cells, cells), low)],
+    )
+
+
+def attend_back(chain, joined, grad, probs, is_joint):
+    frames = joined.shape[1]
+    number, heads, cells, _ = probs.shape
+    width = heads * HEAD_DIM
+    grid = (2, 2) if is_joint else (1, frames)
+    sides = joint_sides() if is_joint else spatial_sides()
+    fetch = lambda i, j, info: (i * grid[1] + j, 0, 0, 0)
+    sums = shape_of((heads, 9, 64, 64), full)
+    return chain.run(
+        "attend_back_joint" if is_joint else "attend_back_spatial",
+        lambda *refs: attend_back_kernel(*refs, heads=heads, cells=cells, sides=sides),
+        [joined, grad, probs],
+        [
+            window_specs(is_joint, frames, 3 * width),
+            window_specs(is_joint, frames, width),
+            pl.BlockSpec((1, heads, cells, cells), fetch),
+        ],
+        [shape_of(joined.shape), sums],
+        [window_specs(is_joint, frames, 3 * width), whole(sums)],
+        grid=grid,
+        scratch=[pltpu.VMEM((heads, cells, cells), full)],
+        mib=56,
+    )
+
+
+def offset_hot():
+    places = np.arange(WIN_T * WIN_T)
+    rows = places[:, None] // WIN_T - places[None, :] // WIN_T + WIN_T - 1
+    cols = places[:, None] % WIN_T - places[None, :] % WIN_T + WIN_T - 1
+    spots = (rows * (2 * WIN_T - 1) + cols).reshape(-1).astype(np.int32)
+    return jnp.arange((2 * WIN_T - 1) ** 2, dtype=jnp.int32)[:, None] == jnp.asarray(spots)[None]
+
+
+def fast_local(
+    latents,
+    cotangent,
+    frame_counts,
+    band_ids,
+    class_ids,
+    time_table,
+    class_table,
+    ada_weight,
+    ada_bias,
+    qkv_weight,
+    out_weight,
+    up_weight,
+    down_weight,
+    spatial_bias,
+    joint_bias,
+):
+    frames = latents.shape[1]
+    model_width = latents.shape[4]
+    heads = spatial_bias.shape[0]
+    width = heads * HEAD_DIM
+    hidden = up_weight.shape[2]
+    col_width = ada_weight.shape[2]
+    rows = frames * 128
+    z, y, c, x = (lax.axis_index(name) for name in ("z", "y", "c", "x"))
+    count = swap(frame_counts.astype(full)).astype(jnp.int32)
+    chain = Chain(jnp.concatenate([jnp.stack([z, y, x]).astype(jnp.int32), count]))
+
+    def rearranged(values):
+        shaped = values.reshape(frames, 8, 2, 8, model_width).transpose(0, 2, 1, 3, 4)
+        return shaped.reshape(rows, model_width)
+
+    qkv_rows = qkv_weight.reshape(2, -1, 3 * width)
+    out_rows = out_weight.transpose(0, 2, 1)
+    down_rows = down_weight.transpose(0, 2, 1)
+    first_shard = swap(jnp.concatenate([qkv_rows[0], out_rows[0]], axis=1))
+    traded_latents = swap(latents)
+    packed = swap(
+        jnp.concatenate(
+            [up_weight[0], down_rows[0], qkv_rows[1], out_rows[1], up_weight[1], down_rows[1]],
+            axis=1,
+        )
+    )
+
+    band_hot = (band_ids[:, None] == jnp.arange(BANDS)[None, :]).astype(low)
+    class_hot = (class_ids[:, None] == jnp.arange(CLASSES)[None, :]).astype(low)
+    condition = jnp.dot(band_hot, time_table, preferred_element_type=full) + jnp.dot(
+        class_hot, class_table, preferred_element_type=full
+    )
+    activity = jax.nn.silu(condition).astype(low)
+    everyone = ("z", "y", "c", "x")
+    mod_part = jnp.einsum(
+        "cd,bde->cbe", activity, ada_weight, preferred_element_type=full
+    ) + ada_bias[None].astype(full)
+    mod_part = jnp.broadcast_to(
+        mod_part.reshape(8, 1, 2, 2, col_width), (8, 2, 2, 2, col_width)
+    ).reshape(32, 2, col_width)
+    own_mod = lax.all_to_all(mod_part, everyone, split_axis=0, concat_axis=0, tiled=True)
+    own_mod = own_mod.transpose(1, 0, 2).reshape(2, 6, model_width)
+    rows_of = lambda *items: jnp.stack([own_mod[k, at] for k, at in items])
+
+    hot = offset_hot()
+    wide = 2 * WIN_T - 1
+    square = spatial_bias.reshape(heads, 2 * WIN_S - 1, 2 * WIN_S - 1)
+    spatial_parts = jnp.stack(
+        [
+            square[:, 8 * a : 8 * a + wide, 8 * b : 8 * b + wide].reshape(heads, -1)
+            for a in range(3)
+            for b in range(3)
+        ],
+        axis=1,
+    )
+    parts = swap(jnp.concatenate([spatial_parts, joint_bias.reshape(heads, 9, -1)]))
+    blocks = jnp.dot(
+        parts.reshape(heads * 18, wide * wide), hot.astype(low), preferred_element_type=full
+    ).astype(low)
+    blocks = blocks.reshape(2, heads, 9, 64, 64)
+    near = blocks[0].reshape(heads, 3, 3, 64, 64)
+    near = jnp.where(c == 0, near, near[:, ::-1])
+    bias_blocks = [near.reshape(heads, 9, 64, 64), blocks[1]]
+
+    windowed = lambda values: values.reshape(2, frames, 2, 64, values.shape[-1])
+
+    latent_rows = rearranged(traded_latents)
+    cuts = [shape_of((64, PIECE))] * 5
+    shards = chain.run(
+        "cut_shards", cut_kernel, [packed], [whole(packed)], cuts, [whole(a) for a in cuts]
+    )
+    gather = Gather(chain, [first_shard] + list(shards))
+    gather.over_z(0)
+    gather.step()
+    gather.over_z(1)
+    normed_0, inverse_0, moved_0 = first_norm(chain, latent_rows, rows_of((0, 0), (0, 1)))
+    other_0 = flip_rows(moved_0)
+    gather.step()
+    gather.over_z(2)
+    gather.step()
+    gather.over_z(3)
+    qkv_0, out_0 = gather.place(0, [3 * width, width])
+    (joined_0,) = both_times(chain, "plain", moved_0, other_0, qkv_0)
+    joined_0 = windowed(joined_0)
+    mixed_0, probs_0 = attend(chain, bias_blocks[0], joined_0, False)
+    mixed_0 = mixed_0.reshape(2, rows, width)
+    away = other_rows(chain, mixed_0, out_0)
+    gather.step()
+    gather.over_z(4)
+    (up_0,) = gather.place(1, [hidden])
+    after_0, branch_one_0, normed_1, inverse_1, moved_1 = forward_step(
+        chain, mixed_0, out_0, away, latent_rows, rows_of((0, 2), (0, 3), (0, 4)), False
+    )
+    other_1 = flip_rows(moved_1)
+    act_0, slope_0 = both_times(chain, "gelu", moved_1, other_1, up_0)
+    gather.step()
+    gather.over_z(5)
+    (down_0,) = gather.place(2, [hidden])
+    away = other_rows(chain, act_0, down_0)
+    current_1, branch_two_0, normed_2, inverse_2, moved_2 = forward_step(
+        chain, act_0, down_0, away, after_0, rows_of((0, 5), (1, 0), (1, 1)), False
+    )
+    other_2 = flip_rows(moved_2)
+
+    gather.step()
+    qkv_1, out_1 = gather.place(3, [3 * width, width])
+    (joined_1,) = both_times(chain, "plain", moved_2, other_2, qkv_1)
+    joined_1 = windowed(joined_1)
+    mixed_1, probs_1 = attend(chain, bias_blocks[1], joined_1, True)
+    mixed_1 = mixed_1.reshape(2, rows, width)
+    away = other_rows(chain, mixed_1, out_1)
+    gather.step()
+    (up_1,) = gather.place(4, [hidden])
+    after_1, branch_one_1, normed_3, inverse_3, moved_3 = forward_step(
+        chain, mixed_1, out_1, away, current_1, rows_of((1, 2), (1, 3), (1, 4)), False
+    )
+    other_3 = flip_rows(moved_3)
+    traded_cotangent = swap(cotangent)
+    act_1, slope_1 = both_times(chain, "gelu", moved_3, other_3, up_1)
+    (down_1,) = gather.place(5, [hidden])
+    away = other_rows(chain, act_1, down_1)
+    final, branch_two_1 = forward_step(
+        chain, act_1, down_1, away, after_1, rows_of((1, 5)), True
+    )
+
+    def restored(sent):
+        shaped = sent.reshape(frames, 2, 8, 8, model_width).transpose(0, 2, 1, 3, 4)
+        return shaped.astype(full).reshape(1, frames, 8, 16, model_width)
+
+    traded_final = swap(final)
+
+    state = rearranged(traded_cotangent)
+    own_g, sums_a = first_back(chain, state, branch_two_1, rows_of((1, 5)))
+    other_g = flip_rows(own_g)
+    scatter = Scatter(chain)
+    (hidden_g,) = both_times(chain, "slope", own_g, other_g, down_1, slope_1)
+    away = other_rows(chain, hidden_g, up_1)
+    scatter.weight_grad((own_g, other_g, act_1))
+    state, sums_b, own_g = backward_step(
+        chain, hidden_g, up_1, away, normed_3, inverse_3, state, rows_of((1, 4), (1, 2)), branch_one_1
+    )
+    other_g = flip_rows(own_g)
+    scatter.weight_grad((moved_3, other_3, hidden_g))
+    chain.wait(traded_final)
+    scatter.step(6)
+    (mixed_g,) = both_times(chain, "plain", own_g, other_g, out_1)
+    back, joint_sums = attend_back(chain, joined_1, windowed(mixed_g), probs_1, True)
+    back = back.reshape(2, rows, 3 * width)
+    away = other_rows(chain, back, qkv_1)
+    scatter.weight_grad((moved_2, other_2, back), (own_g, other_g, mixed_1))
+    scatter.step(6)
+    state, sums_c, own_g = backward_step(
+        chain, back, qkv_1, away, normed_2, inverse_2, state, rows_of((1, 1), (0, 5)), branch_two_0
+    )
+    other_g = flip_rows(own_g)
+
+    (hidden_g,) = both_times(chain, "slope", own_g, other_g, down_0, slope_0)
+    away = other_rows(chain, hidden_g, up_0)
+    scatter.weight_grad((own_g, other_g, act_0))
+    scatter.step(6)
+    state, sums_d, own_g = backward_step(
+        chain, hidden_g, up_0, away, normed_1, inverse_1, state, rows_of((0, 4), (0, 2)), branch_one_0
+    )
+    other_g = flip_rows(own_g)
+    scatter.weight_grad((moved_1, other_1, hidden_g))
+    (mixed_g,) = both_times(chain, "plain", own_g, other_g, out_0)
+    scatter.step(6)
+    back, spatial_sums = attend_back(chain, joined_0, windowed(mixed_g), probs_0, False)
+    back = back.reshape(2, rows, 3 * width)
+    away = other_rows(chain, back, qkv_0)
+    scatter.weight_grad((moved_0, other_0, back), (own_g, other_g, mixed_0))
+    scatter.step(6)
+    state, sums_e = backward_step(
+        chain, back, qkv_0, away, normed_0, inverse_0, state, rows_of((0, 1)), None
+    )
+    traded_state = swap(state)
+    output = restored(traded_final)
+
+    exact = lax.Precision.HIGHEST
+    grad_mod = jnp.stack(
+        [
+            sums_e[0], sums_e[1], sums_d[2], sums_d[0], sums_d[1], sums_c[2],
+            sums_c[0], sums_c[1], sums_b[2], sums_b[0], sums_b[1], sums_a[0],
+        ]
+    )
+    ordered = grad_mod.reshape(2, 32, col_width).transpose(1, 0, 2)
+    cols = lax.all_to_all(ordered, everyone, split_axis=0, concat_axis=0, tiled=True)
+    cols = cols.reshape(8, 2, 2, 2, col_width)
+    cols = (cols[:, 0] + cols[:, 1]).reshape(16, 2, col_width)
+    grad_ada_weight = jnp.einsum("cd,cbe->bde", activity.astype(full), cols, precision=exact)
+    grad_ada_bias = jnp.sum(cols, axis=0)
+    grad_activity = jnp.einsum("cbe,bde->cd", cols, ada_weight.astype(full), precision=exact)
+    grad_activity = grad_activity + flip(grad_activity, "c")
+
+    near = spatial_sums.reshape(heads, 3, 3, 64, 64)
+    near = jnp.where(c == 0, near, near[:, ::-1]).reshape(heads, 9, 64, 64)
+    tables = jnp.dot(
+        jnp.stack([near, joint_sums]).reshape(heads * 18, 64 * 64),
+        hot.astype(full).T,
+        precision=exact,
+    )
+
+    scatter.step(6)
+    shared = add_all(chain, grad_activity)
+    shared_tables = add_all(chain, tables)
+    scatter.step(6)
+    sent = flip(shared, "x"), flip(shared_tables, "x")
+    shared = add_all(chain, shared, sent[0])
+    shared_tables = add_all(chain, shared_tables, sent[1])
+    sent = flip(shared, "y"), flip(shared_tables, "y")
+    early = swap(join_pieces(chain, scatter.done))
+    shared = add_all(chain, shared, sent[0])
+    shared_tables = add_all(chain, shared_tables, sent[1])
+    sent = [[z_trade(values, k) for k in (1, 2, 3)] for values in (shared, shared_tables)]
+    scatter.step(6)
+    late = swap(scatter.done[5]).astype(full)
+    grad_activity = add_all(chain, shared, *sent[0])
+    tables = add_all(chain, shared_tables, *sent[1])
+    grad_latents = restored(traded_state)
+    early = early.astype(full)
+    piece = lambda at: early[:, at * PIECE : (at + 1) * PIECE]
+    grad_down = jnp.stack([piece(3).T, piece(0).T])
+    grad_up = jnp.stack([piece(4), piece(1)])
+    grad_qkv = jnp.stack([late[:, : 3 * width], piece(2)[:, : 3 * width]])
+    grad_out = jnp.stack([late[:, 3 * width :].T, piece(2)[:, 3 * width :].T])
+
+    tables = jnp.where(c == x, tables, flip(tables, "c")).reshape(2, heads, 9, wide, wide)
+    grad_joint = tables[1].reshape(heads, 9 * wide * wide)
+    near = tables[0].reshape(heads, 3, 3, wide, wide)
+    long = 2 * WIN_S - 1
+    grad_spatial = 0.0
+    for a in range(3):
+        for b in range(3):
+            grad_spatial = grad_spatial + jnp.pad(
+                near[:, a, b],
+                ((0, 0), (8 * a, long - wide - 8 * a), (8 * b, long - wide - 8 * b)),
+            )
+    grad_spatial = grad_spatial.reshape(heads, long * long)
+    grad_condition = jax.vjp(jax.nn.silu, condition)[1](grad_activity)[0]
+    grad_time = jnp.dot(band_hot.astype(full).T, grad_condition, precision=exact)
+    grad_class = jnp.dot(class_hot.astype(full).T, grad_condition, precision=exact)
+
+    return (
+        output,
+        grad_latents,
+        grad_time,
+        grad_class,
+        grad_ada_weight,
+        grad_ada_bias,
+        grad_qkv.reshape(2, -1, 3, width),
+        grad_out,
+        grad_up,
+        grad_down,
+        grad_spatial,
+        grad_joint,
+    )
+
+
+def solution(mesh):
+    if mesh.shape["dp"] != 16 or mesh.shape["mp"] != 2:
+        return solution_any(mesh)
+    fine = Mesh(mesh.devices.reshape(4, 2, 2, 2), ("z", "y", "c", "x"))
+    dp, mp = ("z", "y", "c"), "x"
+    both = dp + (mp,)
+    tokens = P(dp, None, mp, None, None)
+    weight_specs = (
+        P(None, None, both),
+        P(None, both),
+        P(None, dp, None, mp),
+        P(None, mp, dp),
+        P(None, dp, mp),
+        P(None, mp, dp),
+        P(mp, None),
+        P(mp, None),
+    )
+    return jax.shard_map(
+        fast_local,
+        mesh=fine,
+        in_specs=(tokens, tokens, P(dp), P(), P(), P(), P()) + weight_specs,
+        out_specs=(tokens, tokens, P(), P()) + weight_specs,
+        check_vma=False,
+    )

time: 3660 us -> 934 us (0.26)
  waiting for transfers between devices: 1240 us -> 130 us
  other arithmetic: 1070 us -> 24.9 us
  local copies, waits for them, and re-layouts: 1020 us -> 104 us
  Pallas kernels: 0 us -> 448 us
  matrix products: 260 us -> 11.7 us
  starting transfers between devices: 8.05 us -> 172 us
    scatter-add x2 -> x0, other arithmetic: 892 us -> none  [the longest x1 543 us: local(): table_parts.append(jnp.zeros((heads_local, joint_bias.shape[1]), jnp.floa...]
    gather x5 -> x0, local copies, waits for them, and re-layouts: 606 us -> none  [the longest x2 370 us: local(): joint_matrix = joint_bias.astype(jnp.float32)[:, joint_index]]
    pallas_call x0 -> x67, Pallas kernels: none -> 448 us  [run(): pl.pallas_call(body, grid_spec=pltpu.PrefetchScalarGridSpec(num_scalar_pr...]
    psum x2 -> x0, waiting for transfers between devices: 390 us -> none  [the longest x1 360 us: local(): grad_activity = lax.psum(activity_part, 'dp')]
    reduce_scatter x2 -> x0, waiting for transfers between devices: 314 us -> none  [the longest x1 175 us: local(): lax.psum_scatter(jnp.stack(up_grads[::-1], axis=0), 'dp', scatter_dimensi...]
    unnamed x35 -> x0, waiting for transfers between devices: 270 us -> none
    all_gather x13 -> x0, waiting for transfers between devices: 268 us -> none  [the longest x4 78.3 us: gather_grads(): return lax.all_gather(values, 'mp', axis=2, tiled=True)]
    dot_general x43 -> x9, matrix products: 260 us -> 11.7 us  [the longest x1 4.77 us: fast_local(): jnp.dot(jnp.stack([near, joint_sums]).reshape(heads * 18, 64 * 64), hot.a...]
  transfers between devices with their start and end apart: 27 -> 119, of which waited for: 19 -> 26; matrix products, arithmetic and copies ran while one was open for 51% -> 8% of each run, Pallas kernels for 0% -> 44%
where the time goes in v2:
time: 934 us; the launch traced here: 920 us
  Pallas kernels  448 us (48%)
  starting transfers between devices  172 us (18%)
  waiting for transfers between devices  130 us (14%)
  local copies, waits for them, and re-layouts  104 us (11%)
  blocking collectives  25.2 us (3%)
  other arithmetic  24.9 us (3%)
  matrix products  11.7 us (1%)
    pallas_call x67, Pallas kernels, run(): pl.pallas_call(body, grid_spec=pltpu.PrefetchScalarGridSpec(num_scalar_pr...  448 us
    ppermute x42, waiting for transfers between devices, z_trade(): lax.ppermute(values, 'z', [(place, place ^ step) for place in range(4)])  77.1 us
    unnamed x392, local copies, waits for them, and re-layouts  68.8 us
    ppermute x10, starting transfers between devices, swap(): return lax.ppermute(values, ('c', 'x'), [(0, 0), (1, 2), (2, 1), (3, 3)])  68 us
    ppermute x42, starting transfers between devices, z_trade(): lax.ppermute(values, 'z', [(place, place ^ step) for place in range(4)])  52.4 us
    ppermute x66, starting transfers between devices, flip(): return lax.ppermute(values, axis, [(0, 1), (1, 0)])  48.6 us
    ppermute x10, waiting for transfers between devices, swap(): return lax.ppermute(values, ('c', 'x'), [(0, 0), (1, 2), (2, 1), (3, 3)])  30.1 us
    all_to_all x1, blocking collectives, fast_local(): lax.all_to_all(mod_part, everyone, split_axis=0, concat_axis=0, tiled=True)  25.2 us
  transfers between devices with their start and end apart: 119, of which 26 were waited for; matrix products, arithmetic and copies ran while one was open for 8% of the time, Pallas kernels for 44%

profile of v2, /device:TPU:9, one launch (start us, length us, event | category | flops | bytes accessed | tf_op | source)
XLA Modules:
  0.0 920.3 jit_solution(4595869689582230818)
XLA Ops:
  16.7 25.0 %collective-permute-start = (f32[1]{0:T(128)}, f32[1]{0:T(128)}, u32[]{:S(2)}, u32[]{:S(2)}) collective-permute-start(f32[1]{0:T(128)} %convert_element_type.62), channel_id=1, source_target_pairs={{0,0},{1,2},{2,1},{3,3},{4,4},{5,6},{6,5},{7,7},{8,8},{9,10},{10,9... | collective-permute-start | bytes 20 | tf_op jit(solution)/shard_map/ppermute | solution.py:522
  59.3 25.2 %all_to_all.10 = f32[32,2,192]{2,1,0:T(2,128)S(1)} all-to-all(f32[32,2,192]{2,1,0:T(2,128)S(1)} %bitcast.234), channel_id=1, replica_groups=mesh['z'=4,'y'=2,'c'=2,'x'=2] {'z','y','c','x'}, dimensions={0} | all-to-all | bytes 98304 | tf_op jit(solution)/shard_map/all_to_all | solution.py:1392
  94.5 9.0 collective-permute-done.14.refs_4_
  133.5 7.0 collective-permute-done.18.refs_3_
  140.5 5.9 collective-permute-done.16.refs_6_.refs_5_.refs_3_
  148.5 4.9 gather_step.9
  154.5 6.2 collective-permute-start.1
  160.7 30.1 %collective-permute-done.1 = bf16[16,9,225]{2,0,1:T(8,128)(2,1)S(1)} collective-permute-done((bf16[16,9,225]{2,0,1:T(8,128)(2,1)S(1)}, bf16[16,9,225]{2,0,1:T(8,128)(2,1)S(1)}, u32[]{:S(2)}, u32[]{:S(2)}) %collective-permute-start.1) | collective-permute-done | bytes 64832 | tf_op jit(solution)/shard_map/ppermute | solution.py:522
  206.5 4.7 place_weights.6
  213.0 6.5 both_plain.4.refs_3_
  219.6 16.6 %attend_spatial.1 = (bf16[2,5,2,64,512]{4,3,2,1,0:T(8,128)(2,1)S(1)}, bf16[5,8,256,256]{3,2,1,0:T(8,128)(2,1)}) custom-call(s32[4]{0:T(128)S(1)} %pad_add_fusion.1.refs_0_, bf16[8,9,64,64]{3,2,1,0:T(8,128)(2,1)S(1)} %bitcast.210, bf16[2,5,2,64,1536]{4,3,2,1,0:T(8,128)(2,1)} %bitcast.211, bf16[2,640,1536]{2,1,0:T(8,128)(2,1)} %both_plain.4.refs_3_), custom_call_target="tpu_custom_call" | custom-call | flops 1 | bytes 1 | tf_op jit(solution)/shard_map/attend_spatial/pallas_call | solution.py:552
  239.9 4.7 gather_step.10
  245.8 5.0 place_weights.7.refs_7_
  250.9 5.5 forward_step.4
  264.4 17.6 %both_gelu.2 = (bf16[2,640,2048]{2,1,0:T(8,128)(2,1)}, bf16[2,640,2048]{2,1,0:T(8,128)(2,1)}) custom-call(s32[4]{0:T(128)S(1)} %pad_add_fusion.1.refs_0_, bf16[320,1024]{1,0:T(8,128)(2,1)S(1)} %get-tuple-element.193.refs_1_, bf16[320,1024]{1,0:T(8,128)(2,1)S(1)} %get-tuple-element.194.refs_2_, bf16[320,1024]{1,0:T(8,128)(2,1)S(1)} %collective-permute-done.27.refs_3_, ...), custom_call_target="tpu_custom_call" | custom-call | flops 1 | bytes 1 | tf_op jit(solution)/shard_map/both_gelu/pallas_call | solution.py:552
  289.5 5.3 place_weights.8.refs_3_
  296.9 6.0 other_rows.9
  309.2 10.2 %forward_step.5 = (f32[640,1024]{1,0:T(8,128)}, bf16[640,1024]{1,0:T(8,128)(2,1)S(1)}, bf16[640,1024]{1,0:T(8,128)(2,1)}, f32[640,1]{1,0:T(8,128)S(1)}, bf16[320...) custom-call(s32[4]{0:T(128)S(1)} %pad_add_fusion.1.refs_0_, ...), custom_call_target="tpu_custom_call" | custom-call | flops 1 | bytes 1 | tf_op jit(solution)/shard_map/forward_step/pallas_call | solution.py:552
  328.0 4.7 gather_step.12
  348.1 8.1 both_plain.5.refs_3_
  356.2 18.4 %attend_joint.1 = (bf16[2,5,2,64,512]{4,3,2,1,0:T(8,128)(2,1)S(1)}, bf16[4,8,320,320]{3,2,1,0:T(8,128)(2,1)}) custom-call(s32[4]{0:T(128)S(1)} %pad_add_fusion.1.refs_0_, bf16[8,9,64,64]{3,2,1,0:T(8,128)(2,1)S(1)} %copy-done.37, bf16[2,5,2,64,1536]{4,3,2,1,0:T(8,128)(2,1)} %bitcast.213, bf16[2,640,1536]{2,1,0:T(8,128)(2,1)} %both_plain.5.refs_3_), custom_call_target="tpu_custom_call" | custom-call | flops 1 | bytes 1 | tf_op jit(solution)/shard_map/attend_joint/pallas_call | solution.py:552
  381.8 4.6 place_weights.10.refs_7_
  386.4 5.6 forward_step.6
  400.8 17.7 %both_gelu.3 = (bf16[2,640,2048]{2,1,0:T(8,128)(2,1)}, bf16[2,640,2048]{2,1,0:T(8,128)(2,1)}) custom-call(s32[4]{0:T(128)S(1)} %pad_add_fusion.1.refs_0_, bf16[320,1024]{1,0:T(8,128)(2,1)S(1)} %get-tuple-element.215.refs_1_, bf16[320,1024]{1,0:T(8,128)(2,1)S(1)} %get-tuple-element.216.refs_2_, bf16[320,1024]{1,0:T(8,128)(2,1)S(1)} %collective-permute-done.47.refs_3_, ...), custom_call_target="tpu_custom_call" | custom-call | flops 1 | bytes 1 | tf_op jit(solution)/shard_map/both_gelu/pallas_call | solution.py:552
  418.5 5.4 collective-permute-done.49.refs_4_
  424.0 5.0 place_weights.11.refs_3_
  431.2 6.0 other_rows.11
  441.3 8.0 forward_step.7
  454.4 11.0 %both_slope.2.refs_1_.refs_3_.refs_5_ = bf16[2,640,2048]{2,1,0:T(8,128)(2,1)} custom-call(s32[4]{0:T(128)S(1)} %pad_add_fusion.1.refs_0_, bf16[320,1024]{1,0:T(8,128)(2,1)S(1)} %get-tuple-element.224.refs_1_.refs_7_, bf16[320,1024]{1,0:T(8,128)(2,1)S(1)} %get-tuple-element.225.refs_2_, bf16[320,1024]{1,0:T(8,128)(2,1)S(1)} %collective-permute-done.55.refs_3_, ...), custom_call_target="tpu_custom_call" | custom-call | flops 1 | bytes 1 | tf_op jit(solution)/shard_map/both_slope/pallas_call | solution.py:552
  465.4 6.6 other_rows.12
  472.0 8.9 collective-permute-start.58
  481.0 13.9 %weight_grad.6 = (bf16[4,64,2048]{2,1,0:T(8,128)(2,1)}, bf16[4,64,2048]{2,1,0:T(8,128)(2,1)}, bf16[4,64,2048]{2,1,0:T(8,128)(2,1)}, bf16[2,64,2048]{2,1,0:T(8,128)(2,1)}, bf16[2,64,2048]{2,1,0:T(8,128)(2,1)}) custom-call(s32[4]{0:T(128)} %copy-done.78, bf16[320,1024]{1,0:T(8,128)(2,1)} %copy-done.34, bf16[320,1024]{1,0:T(8,128)(2,1)} %copy-done.75, ...), custom_call_target="tpu_custom_call" | custom-call | flops 1 | bytes 1 | tf_op jit(solution)/shard_map/weight_grad/pallas_call | solution.py:552
  497.2 10.6 %backward_step.4 = (f32[640,1024]{1,0:T(8,128)}, f32[8,1024]{1,0:T(8,128)S(1)}, bf16[320,1024]{1,0:T(8,128)(2,1)S(1)}, bf16[320,1024]{1,0:T(8,128)(2,1)S(1)}) custom-call(s32[4]{0:T(128)S(1)} %copy-done.79, bf16[2,640,2048]{2,1,0:T(8,128)(2,1)} %both_slope.2.refs_1_.refs_3_.refs_5_, bf16[1024,2048]{1,0:T(8,128)(2,1)} %bitcast.178, ...), custom_call_target="tpu_custom_call" | custom-call | flops 1 | bytes 1 | tf_op jit(solution)/shard_map/backward_step/pallas_call | solution.py:552
  507.8 14.1 %weight_grad.7 = (bf16[4,64,2048]{2,1,0:T(8,128)(2,1)}, bf16[4,64,2048]{2,1,0:T(8,128)(2,1)}, bf16[4,64,2048]{2,1,0:T(8,128)(2,1)}, bf16[2,64,2048]{2,1,0:T(8,128)(2,1)}, bf16[2,64,2048]{2,1,0:T(8,128)(2,1)}) custom-call(s32[4]{0:T(128)} %copy-done.78, bf16[320,1024]{1,0:T(8,128)(2,1)} %copy-done.67, bf16[320,1024]{1,0:T(8,128)(2,1)} %copy-done.68, ...), custom_call_target="tpu_custom_call" | custom-call | flops 1 | bytes 1 | tf_op jit(solution)/shard_map/weight_grad/pallas_call | solution.py:552
  537.3 22.7 %attend_back_joint.1 = (bf16[2,5,2,64,1536]{4,3,2,1,0:T(8,128)(2,1)}, f32[8,9,64,64]{3,2,1,0:T(8,128)}) custom-call(s32[4]{0:T(128)} %copy-done.78, bf16[2,5,2,64,1536]{4,3,2,1,0:T(8,128)(2,1)} %bitcast.214, bf16[2,5,2,64,512]{4,3,2,1,0:T(8,128)(2,1)} %bitcast.203, bf16[4,8,320,320]{3,2,1,0:T(8,128)(2,1)} %get-tuple-element.244.refs_3_, ...), custom_call_target="tpu_custom_call" | custom-call | flops 1 | bytes 1 | tf_op jit(solution)/shard_map/attend_back_joint/pallas_call | solution.py:552
  560.0 5.7 other_rows.13
  566.5 14.1 %weight_grad.8 = (bf16[4,64,2048]{2,1,0:T(8,128)(2,1)}, bf16[4,64,2048]{2,1,0:T(8,128)(2,1)}, bf16[4,64,2048]{2,1,0:T(8,128)(2,1)}, bf16[2,64,2048]{2,1,0:T(8,128)(2,1)}, bf16[2,64,2048]{2,1,0:T(8,128)(2,1)}) custom-call(s32[4]{0:T(128)} %copy-done.78, bf16[320,1024]{1,0:T(8,128)(2,1)} %get-tuple-element.202.refs_1_, ...), custom_call_target="tpu_custom_call" | custom-call | flops 1 | bytes 1 | tf_op jit(solution)/shard_map/weight_grad/pallas_call | solution.py:552
  582.8 5.4 scatter_step.9
  589.3 9.4 %backward_step.5 = (f32[640,1024]{1,0:T(8,128)}, f32[8,1024]{1,0:T(8,128)S(1)}, bf16[320,1024]{1,0:T(8,128)(2,1)S(1)}, bf16[320,1024]{1,0:T(8,128)(2,1)S(1)}) custom-call(s32[4]{0:T(128)S(1)} %copy-done.82, bf16[2,640,1536]{2,1,0:T(8,128)(2,1)} %bitcast.220, bf16[1024,1536]{1,0:T(8,128)(2,1)} %bitcast.189, ...), custom_call_target="tpu_custom_call" | custom-call | flops 1 | bytes 1 | tf_op jit(solution)/shard_map/backward_step/pallas_call | solution.py:552
  607.4 10.5 %both_slope.3.refs_1_.refs_3_.refs_5_ = bf16[2,640,2048]{2,1,0:T(8,128)(2,1)} custom-call(s32[4]{0:T(128)S(1)} %copy-done.82, bf16[320,1024]{1,0:T(8,128)(2,1)S(1)} %get-tuple-element.258.refs_1_, bf16[320,1024]{1,0:T(8,128)(2,1)S(1)} %get-tuple-element.259.refs_2_, bf16[320,1024]{1,0:T(8,128)(2,1)S(1)} %collective-permute-done.67.refs_3_, ...), custom_call_target="tpu_custom_call" | custom-call | flops 1 | bytes 1 | tf_op jit(solution)/shard_map/both_slope/pallas_call | solution.py:552
  618.0 6.0 other_rows.14
  625.7 14.1 %weight_grad.9 = (bf16[4,64,2048]{2,1,0:T(8,128)(2,1)}, bf16[4,64,2048]{2,1,0:T(8,128)(2,1)}, bf16[4,64,2048]{2,1,0:T(8,128)(2,1)}, bf16[2,64,2048]{2,1,0:T(8,128)(2,1)}, bf16[2,64,2048]{2,1,0:T(8,128)(2,1)}) custom-call(s32[4]{0:T(128)} %copy-done.78, bf16[320,1024]{1,0:T(8,128)(2,1)} %copy-done.55, bf16[320,1024]{1,0:T(8,128)(2,1)} %copy-done.56, ...), custom_call_target="tpu_custom_call" | custom-call | flops 1 | bytes 1 | tf_op jit(solution)/shard_map/weight_grad/pallas_call | solution.py:552
  643.0 5.7 scatter_step.10
  650.8 10.3 %backward_step.6 = (f32[640,1024]{1,0:T(8,128)}, f32[8,1024]{1,0:T(8,128)S(1)}, bf16[320,1024]{1,0:T(8,128)(2,1)S(1)}, bf16[320,1024]{1,0:T(8,128)(2,1)S(1)}) custom-call(s32[4]{0:T(128)S(1)} %copy-done.83, bf16[2,640,2048]{2,1,0:T(8,128)(2,1)} %both_slope.3.refs_1_.refs_3_.refs_5_, bf16[1024,2048]{1,0:T(8,128)(2,1)} %bitcast.175, ...), custom_call_target="tpu_custom_call" | custom-call | flops 1 | bytes 1 | tf_op jit(solution)/shard_map/backward_step/pallas_call | solution.py:552
  666.1 13.9 %weight_grad.10 = (bf16[4,64,2048]{2,1,0:T(8,128)(2,1)}, bf16[4,64,2048]{2,1,0:T(8,128)(2,1)}, bf16[4,64,2048]{2,1,0:T(8,128)(2,1)}, bf16[2,64,2048]{2,1,0:T(8,128)(2,1)}, bf16[2,64,2048]{2,1,0:T(8,128)(2,1)}) custom-call(s32[4]{0:T(128)} %copy-done.78, bf16[320,1024]{1,0:T(8,128)(2,1)} %copy-done.63, bf16[320,1024]{1,0:T(8,128)(2,1)} %copy-done.64, ...), custom_call_target="tpu_custom_call" | custom-call | flops 1 | bytes 1 | tf_op jit(solution)/shard_map/weight_grad/pallas_call | solution.py:552
  684.4 4.9 collective-permute-done.82.refs_11_
  689.3 5.3 scatter_step.11
  699.0 21.0 %attend_back_spatial.1 = (bf16[2,5,2,64,1536]{4,3,2,1,0:T(8,128)(2,1)}, f32[8,9,64,64]{3,2,1,0:T(8,128)}) custom-call(s32[4]{0:T(128)} %copy-done.78, bf16[2,5,2,64,1536]{4,3,2,1,0:T(8,128)(2,1)} %bitcast.212, bf16[2,5,2,64,512]{4,3,2,1,0:T(8,128)(2,1)} %bitcast.202, bf16[5,8,256,256]{3,2,1,0:T(8,128)(2,1)} %get-tuple-element.282.refs_3_, ...), custom_call_target="tpu_custom_call" | custom-call | flops 1 | bytes 1 | tf_op jit(solution)/shard_map/attend_back_spatial/pallas_call | solution.py:552
  720.0 5.3 other_rows.15
  726.1 14.1 %weight_grad.11 = (bf16[4,64,2048]{2,1,0:T(8,128)(2,1)}, bf16[4,64,2048]{2,1,0:T(8,128)(2,1)}, bf16[4,64,2048]{2,1,0:T(8,128)(2,1)}, bf16[2,64,2048]{2,1,0:T(8,128)(2,1)}, bf16[2,64,2048]{2,1,0:T(8,128)(2,1)}) custom-call(s32[4]{0:T(128)} %copy-done.78, bf16[320,1024]{1,0:T(8,128)(2,1)} %copy-done.47, bf16[320,1024]{1,0:T(8,128)(2,1)} %copy-done.49, ...), custom_call_target="tpu_custom_call" | custom-call | flops 1 | bytes 1 | tf_op jit(solution)/shard_map/weight_grad/pallas_call | solution.py:552
  742.5 5.3 scatter_step.12
  759.2 7.4 backward_step.7
  773.8 4.6 reverse_select_fusion
  778.4 4.8 collective-permute-done.94.refs_7_
  787.1 10.1 %collective-permute-done.96.refs_9_ = bf16[64,2048]{1,0:T(8,128)(2,1)S(1)} collective-permute-done((bf16[64,2048]{1,0:T(8,128)(2,1)}, bf16[64,2048]{1,0:T(8,128)(2,1)S(1)}, u32[]{:S(2)}, u32[]{:S(2)}) %collective-permute-start.96) | collective-permute-done | bytes 262176 | tf_op jit(solution)/shard_map/ppermute | solution.py:518
  797.2 5.1 scatter_step.13
  811.2 5.5 pad_maximum_fusion
  816.7 5.3 reshape.199
  825.0 4.8 fusion.refs_1_
  831.8 9.8 %collective-permute-done.101.refs_6_ = bf16[64,2048]{1,0:T(8,128)(2,1)} collective-permute-done((bf16[64,2048]{1,0:T(8,128)(2,1)}, bf16[64,2048]{1,0:T(8,128)(2,1)}, u32[]{:S(2)}, u32[]{:S(2)}) %collective-permute-start.101) | collective-permute-done | bytes 262176 | tf_op jit(solution)/shard_map/ppermute | solution.py:518
  841.8 6.7 collective-permute-done.102.refs_7_
  870.7 9.9 %collective-permute-done.109.refs_3_ = bf16[64,2048]{1,0:T(8,128)(2,1)S(1)} collective-permute-done((bf16[64,2048]{1,0:T(8,128)(2,1)S(1)}, bf16[64,2048]{1,0:T(8,128)(2,1)S(1)}, u32[]{:S(2)}, u32[]{:S(2)}) %collective-permute-start.109) | collective-permute-done | bytes 262176 | tf_op jit(solution)/shard_map/ppermute | solution.py:518
  880.5 6.6 collective-permute-start.113
  892.9 10.3 %collective-permute-start.112 = (bf16[64,2048]{1,0:T(8,128)(2,1)S(1)}, bf16[64,2048]{1,0:T(8,128)(2,1)S(1)}, u32[]{:S(2)}, u32[]{:S(2)}) collective-permute-start(bf16[64,2048]{1,0:T(8,128)(2,1)S(1)} %scatter_step.15.refs_5_), channel_id=1, source_target_pairs={{0,0},{1,2},{2,1},{3,3},{4,4},{5,6},{6,5},{7,7},{8,8},{9,10},{10,9... | collective-permute-start | bytes 786440 | tf_op jit(solution)/shard_map/ppermute | solution.py:522
  (724 shorter events, 308.0 us)
Async XLA Ops:
  6.3 39.6 %collective-permute-start.7 = (bf16[64,10240]{1,0:T(8,128)(2,1)}, bf16[64,10240]{1,0:T(8,128)(2,1)S(1)}, u32[]{:S(2)}, u32[]{:S(2)}) collective-permute-start(bf16[64,10240]{1,0:T(8,128)(2,1)} %fusion.3), channel_id=1, source_target_pairs={{0,0},{1,2},{2,1},{3,3},{4,4},{5,6},{6,5},{7,7},{8,8},{9,10},{10,9... | collective-permute-start | bytes 3932168 | tf_op jit(solution)/shard_map/ppermute | solution.py:522
  10.3 31.4 %collective-permute-start.3 = (bf16[64,2048]{1,0:T(8,128)(2,1)S(1)}, bf16[64,2048]{1,0:T(8,128)(2,1)S(1)}, u32[]{:S(2)}, u32[]{:S(2)}) collective-permute-start(bf16[64,2048]{1,0:T(8,128)(2,1)S(1)} %pad_maximum_fusion.4), channel_id=1, source_target_pairs={{0,0},{1,2},{2,1},{3,3},{4,4},{5,6},{6,5},{7,7},{8,8},{9,10},{10,9... | collective-permute-start | bytes 786440 | tf_op jit(solution)/shard_map/ppermute | solution.py:522
  12.4 76.1 %collective-permute-start.2 = (bf16[1,5,8,16,1024]{4,3,2,1,0:T(8,128)(2,1)}, bf16[1,5,8,16,1024]{4,3,2,1,0:T(8,128)(2,1)}, u32[]{:S(2)}, u32[]{:S(2)}) collective-permute-start(bf16[1,5,8,16,1024]{4,3,2,1,0:T(8,128)(2,1)} %param.16), channel_id=1, source_target_pairs={{0,0},{1,2},{2,1},{3,3},{4,4},{5,6},{6,5},{7,7},{8,8},{9,10},{10,9... | collective-permute-start | bytes 3932168 | tf_op jit(solution)/shard_map/ppermute | solution.py:522
  16.7 27.3 %collective-permute-start = (f32[1]{0:T(128)}, f32[1]{0:T(128)}, u32[]{:S(2)}, u32[]{:S(2)}) collective-permute-start(f32[1]{0:T(128)} %convert_element_type.62), channel_id=1, source_target_pairs={{0,0},{1,2},{2,1},{3,3},{4,4},{5,6},{6,5},{7,7},{8,8},{9,10},{10,9... | collective-permute-start | bytes 20 | tf_op jit(solution)/shard_map/ppermute | solution.py:522
  57.2 50.0 %collective-permute-start.11 = (bf16[4,64,2048]{2,1,0:T(8,128)(2,1)}, bf16[4,64,2048]{2,1,0:T(8,128)(2,1)S(1)}, u32[]{:S(2)}, u32[]{:S(2)}) collective-permute-start(bf16[4,64,2048]{2,1,0:T(8,128)(2,1)} %get-tuple-element.179), channel_id=1, source_target_pairs={{0,4},{4,0},{1,5},{5,1},{2,6},{6,2},{3,7},{7,3},{8,12},{12,8},{9,1... | collective-permute-start | bytes 3145736 | tf_op jit(solution)/shard_map/ppermute | solution.py:514
  58.5 48.8 %collective-permute-start.10 = (bf16[4,64,2048]{2,1,0:T(8,128)(2,1)}, bf16[4,64,2048]{2,1,0:T(8,128)(2,1)S(1)}, u32[]{:S(2)}, u32[]{:S(2)}) collective-permute-start(bf16[4,64,2048]{2,1,0:T(8,128)(2,1)} %get-tuple-element.176.refs_3_.refs_1_), channel_id=1, source_target_pairs={{0,1},{1,0},{2,3},{3,2},{4,5},{5,4},{6,7},{7,6},{8,9},{9,8},{10,11... | collective-permute-start | bytes 3145736 | tf_op jit(solution)/shard_map/ppermute | solution.py:514
  84.8 22.4 %collective-permute-start.13 = (bf16[64,2048]{1,0:T(8,128)(2,1)}, bf16[64,2048]{1,0:T(8,128)(2,1)S(1)}, u32[]{:S(2)}, u32[]{:S(2)}) collective-permute-start(bf16[64,2048]{1,0:T(8,128)(2,1)} %get-tuple-element.175.refs_5_.refs_1_), channel_id=1, source_target_pairs={{0,16},{8,24},{16,0},{24,8},{1,17},{9,25},{17,1},{25,9},{2,18},{10... | collective-permute-start | bytes 786440 | tf_op jit(solution)/shard_map/ppermute | solution.py:518
  111.4 35.0 %collective-permute-start.16 = (bf16[6,64,2048]{2,1,0:T(8,128)(2,1)}, bf16[6,64,2048]{2,1,0:T(8,128)(2,1)S(1)}, u32[]{:S(2)}, u32[]{:S(2)}) collective-permute-start(bf16[6,64,2048]{2,1,0:T(8,128)(2,1)} %get-tuple-element.182), channel_id=1, source_target_pairs={{0,4},{4,0},{1,5},{5,1},{2,6},{6,2},{3,7},{7,3},{8,12},{12,8},{9,1... | collective-permute-start | bytes 4718600 | tf_op jit(solution)/shard_map/ppermute | solution.py:514
  112.1 34.3 %collective-permute-start.15 = (bf16[6,64,2048]{2,1,0:T(8,128)(2,1)}, bf16[6,64,2048]{2,1,0:T(8,128)(2,1)}, u32[]{:S(2)}, u32[]{:S(2)}) collective-permute-start(bf16[6,64,2048]{2,1,0:T(8,128)(2,1)} %get-tuple-element.181.refs_7_.refs_1_), channel_id=1, source_target_pairs={{0,1},{1,0},{2,3},{3,2},{4,5},{5,4},{6,7},{7,6},{8,9},{9,8},{10,11... | collective-permute-start | bytes 4718600 | tf_op jit(solution)/shard_map/ppermute | solution.py:514
  119.9 20.6 %collective-permute-start.18 = (bf16[64,2048]{1,0:T(8,128)(2,1)}, bf16[64,2048]{1,0:T(8,128)(2,1)S(1)}, u32[]{:S(2)}, u32[]{:S(2)}) collective-permute-start(bf16[64,2048]{1,0:T(8,128)(2,1)} %copy-done.148), channel_id=1, source_target_pairs={{0,16},{8,24},{16,0},{24,8},{1,17},{9,25},{17,1},{25,9},{2,18},{10... | collective-permute-start | bytes 786440 | tf_op jit(solution)/shard_map/ppermute | solution.py:518
  153.4 86.5 %collective-permute-start.23 = (bf16[6,64,2048]{2,1,0:T(8,128)(2,1)}, bf16[6,64,2048]{2,1,0:T(8,128)(2,1)}, u32[]{:S(2)}, u32[]{:S(2)}) collective-permute-start(bf16[6,64,2048]{2,1,0:T(8,128)(2,1)} %get-tuple-element.190), channel_id=1, source_target_pairs={{0,4},{4,0},{1,5},{5,1},{2,6},{6,2},{3,7},{7,3},{8,12},{12,8},{9,1... | collective-permute-start | bytes 4718600 | tf_op jit(solution)/shard_map/ppermute | solution.py:514
  153.7 86.2 %collective-permute-start.22 = (bf16[6,64,2048]{2,1,0:T(8,128)(2,1)}, bf16[6,64,2048]{2,1,0:T(8,128)(2,1)}, u32[]{:S(2)}, u32[]{:S(2)}) collective-permute-start(bf16[6,64,2048]{2,1,0:T(8,128)(2,1)} %get-tuple-element.184.refs_6_.refs_1_), channel_id=1, source_target_pairs={{0,1},{1,0},{2,3},{3,2},{4,5},{5,4},{6,7},{7,6},{8,9},{9,8},{10,11... | collective-permute-start | bytes 4718600 | tf_op jit(solution)/shard_map/ppermute | solution.py:514
  154.5 36.3 %collective-permute-start.1 = (bf16[16,9,225]{2,0,1:T(8,128)(2,1)S(1)}, bf16[16,9,225]{2,0,1:T(8,128)(2,1)S(1)}, u32[]{:S(2)}, u32[]{:S(2)}) collective-permute-start(bf16[16,9,225]{2,0,1:T(8,128)(2,1)S(1)} %pad_maximum_fusion.6), channel_id=1, source_target_pairs={{0,0},{1,2},{2,1},{3,3},{4,4},{5,6},{6,5},{7,7},{8,8},{9,10},{10,9... | collective-permute-start | bytes 194408 | tf_op jit(solution)/shard_map/ppermute | solution.py:522
  197.4 41.7 %collective-permute-start.26 = (bf16[64,2048]{1,0:T(8,128)(2,1)}, bf16[64,2048]{1,0:T(8,128)(2,1)S(1)}, u32[]{:S(2)}, u32[]{:S(2)}) collective-permute-start(bf16[64,2048]{1,0:T(8,128)(2,1)} %copy-done.144), channel_id=1, source_target_pairs={{0,24},{8,16},{16,8},{24,0},{1,25},{9,17},{17,9},{25,1},{2,26},{10... | collective-permute-start | bytes 786440 | tf_op jit(solution)/shard_map/ppermute | solution.py:518
  199.6 40.2 %collective-permute-start.25 = (bf16[64,2048]{1,0:T(8,128)(2,1)}, bf16[64,2048]{1,0:T(8,128)(2,1)S(1)}, u32[]{:S(2)}, u32[]{:S(2)}) collective-permute-start(bf16[64,2048]{1,0:T(8,128)(2,1)} %copy-done.144), channel_id=1, source_target_pairs={{0,16},{8,24},{16,0},{24,8},{1,17},{9,25},{17,1},{25,9},{2,18},{10... | collective-permute-start | bytes 786440 | tf_op jit(solution)/shard_map/ppermute | solution.py:518
  204.3 35.6 %collective-permute-start.24 = (bf16[64,2048]{1,0:T(8,128)(2,1)}, bf16[64,2048]{1,0:T(8,128)(2,1)S(1)}, u32[]{:S(2)}, u32[]{:S(2)}) collective-permute-start(bf16[64,2048]{1,0:T(8,128)(2,1)} %copy-done.144), channel_id=1, source_target_pairs={{0,8},{8,0},{16,24},{24,16},{1,9},{9,1},{17,25},{25,17},{2,10},{10... | collective-permute-start | bytes 786440 | tf_op jit(solution)/shard_map/ppermute | solution.py:518
  244.6 37.4 %collective-permute-start.30 = (bf16[6,64,2048]{2,1,0:T(8,128)(2,1)}, bf16[6,64,2048]{2,1,0:T(8,128)(2,1)S(1)}, u32[]{:S(2)}, u32[]{:S(2)}) collective-permute-start(bf16[6,64,2048]{2,1,0:T(8,128)(2,1)} %get-tuple-element.197), channel_id=1, source_target_pairs={{0,4},{4,0},{1,5},{5,1},{2,6},{6,2},{3,7},{7,3},{8,12},{12,8},{9,1... | collective-permute-start | bytes 4718600 | tf_op jit(solution)/shard_map/ppermute | solution.py:514
  245.8 36.3 %collective-permute-start.29 = (bf16[6,64,2048]{2,1,0:T(8,128)(2,1)S(1)}, bf16[6,64,2048]{2,1,0:T(8,128)(2,1)S(1)}, u32[]{:S(2)}, u32[]{:S(2)}) collective-permute-start(bf16[6,64,2048]{2,1,0:T(8,128)(2,1)S(1)} %get-tuple-element.192.refs_6_.refs_1_), channel_id=1, source_target_pairs={{0,1},{1,0},{2,3},{3,2},{4,5},{5,4},{6,7},{7,6},{8,9},{9,8},{10,11... | collective-permute-start | bytes 4718600 | tf_op jit(solution)/shard_map/ppermute | solution.py:514
  258.3 23.7 %collective-permute-start.33 = (bf16[64,2048]{1,0:T(8,128)(2,1)S(1)}, bf16[64,2048]{1,0:T(8,128)(2,1)S(1)}, u32[]{:S(2)}, u32[]{:S(2)}) collective-permute-start(bf16[64,2048]{1,0:T(8,128)(2,1)S(1)} %copy-done.141), channel_id=1, source_target_pairs={{0,24},{8,16},{16,8},{24,0},{1,25},{9,17},{17,9},{25,1},{2,26},{10... | collective-permute-start | bytes 786440 | tf_op jit(solution)/shard_map/ppermute | solution.py:518
  260.0 22.0 %collective-permute-start.32 = (bf16[64,2048]{1,0:T(8,128)(2,1)S(1)}, bf16[64,2048]{1,0:T(8,128)(2,1)S(1)}, u32[]{:S(2)}, u32[]{:S(2)}) collective-permute-start(bf16[64,2048]{1,0:T(8,128)(2,1)S(1)} %copy-done.141), channel_id=1, source_target_pairs={{0,16},{8,24},{16,0},{24,8},{1,17},{9,25},{17,1},{25,9},{2,18},{10... | collective-permute-start | bytes 786440 | tf_op jit(solution)/shard_map/ppermute | solution.py:518
  287.6 39.3 %collective-permute-start.39 = (bf16[6,64,2048]{2,1,0:T(8,128)(2,1)}, bf16[6,64,2048]{2,1,0:T(8,128)(2,1)S(1)}, u32[]{:S(2)}, u32[]{:S(2)}) collective-permute-start(bf16[6,64,2048]{2,1,0:T(8,128)(2,1)} %get-tuple-element.204), channel_id=1, source_target_pairs={{0,4},{4,0},{1,5},{5,1},{2,6},{6,2},{3,7},{7,3},{8,12},{12,8},{9,1... | collective-permute-start | bytes 4718600 | tf_op jit(solution)/shard_map/ppermute | solution.py:514
  288.3 38.6 %collective-permute-start.38 = (bf16[6,64,2048]{2,1,0:T(8,128)(2,1)S(1)}, bf16[6,64,2048]{2,1,0:T(8,128)(2,1)S(1)}, u32[]{:S(2)}, u32[]{:S(2)}) collective-permute-start(bf16[6,64,2048]{2,1,0:T(8,128)(2,1)S(1)} %get-tuple-element.199.refs_6_.refs_1_), channel_id=1, source_target_pairs={{0,1},{1,0},{2,3},{3,2},{4,5},{5,4},{6,7},{7,6},{8,9},{9,8},{10,11... | collective-permute-start | bytes 4718600 | tf_op jit(solution)/shard_map/ppermute | solution.py:514
  306.0 20.8 %collective-permute-start.41 = (bf16[64,2048]{1,0:T(8,128)(2,1)S(1)}, bf16[64,2048]{1,0:T(8,128)(2,1)S(1)}, u32[]{:S(2)}, u32[]{:S(2)}) collective-permute-start(bf16[64,2048]{1,0:T(8,128)(2,1)S(1)} %copy-done.137), channel_id=1, source_target_pairs={{0,16},{8,24},{16,0},{24,8},{1,17},{9,25},{17,1},{25,9},{2,18},{10... | collective-permute-start | bytes 786440 | tf_op jit(solution)/shard_map/ppermute | solution.py:518
  332.7 45.6 %collective-permute-start.46 = (bf16[6,64,2048]{2,1,0:T(8,128)(2,1)}, bf16[6,64,2048]{2,1,0:T(8,128)(2,1)}, u32[]{:S(2)}, u32[]{:S(2)}) collective-permute-start(bf16[6,64,2048]{2,1,0:T(8,128)(2,1)} %get-tuple-element.213), channel_id=1, source_target_pairs={{0,4},{4,0},{1,5},{5,1},{2,6},{6,2},{3,7},{7,3},{8,12},{12,8},{9,1... | collective-permute-start | bytes 4718600 | tf_op jit(solution)/shard_map/ppermute | solution.py:514
  333.9 44.4 %collective-permute-start.45 = (bf16[6,64,2048]{2,1,0:T(8,128)(2,1)}, bf16[6,64,2048]{2,1,0:T(8,128)(2,1)}, u32[]{:S(2)}, u32[]{:S(2)}) collective-permute-start(bf16[6,64,2048]{2,1,0:T(8,128)(2,1)} %get-tuple-element.207.refs_6_.refs_1_), channel_id=1, source_target_pairs={{0,1},{1,0},{2,3},{3,2},{4,5},{5,4},{6,7},{7,6},{8,9},{9,8},{10,11... | collective-permute-start | bytes 4718600 | tf_op jit(solution)/shard_map/ppermute | solution.py:514
  394.3 44.4 %collective-permute-start.54 = (bf16[1,5,8,16,1024]{4,3,2,1,0:T(8,128)(2,1)S(1)}, bf16[1,5,8,16,1024]{4,3,2,1,0:T(8,128)(2,1)S(1)}, u32[]{:S(2)}, u32[]{:S(2)}) collective-permute-start(bf16[1,5,8,16,1024]{4,3,2,1,0:T(8,128)(2,1)S(1)} %copy-done.187), channel_id=1, source_target_pairs={{0,0},{1,2},{2,1},{3,3},{4,4},{5,6},{6,5},{7,7},{8,8},{9,10},{10,9... | collective-permute-start | bytes 3932168 | tf_op jit(solution)/shard_map/ppermute | solution.py:522
  398.5 25.4 %collective-permute-start.49 = (bf16[2,64,2048]{2,1,0:T(8,128)(2,1)S(1)}, bf16[2,64,2048]{2,1,0:T(8,128)(2,1)S(1)}, u32[]{:S(2)}, u32[]{:S(2)}) collective-permute-start(bf16[2,64,2048]{2,1,0:T(8,128)(2,1)S(1)} %get-tuple-element.214.refs_6_), channel_id=1, source_target_pairs={{0,1},{1,0},{2,3},{3,2},{4,5},{5,4},{6,7},{7,6},{8,9},{9,8},{10,11... | collective-permute-start | bytes 1572872 | tf_op jit(solution)/shard_map/ppermute | solution.py:514
  451.6 70.3 %collective-permute-start.53 = (bf16[640,1024]{1,0:T(8,128)(2,1)}, bf16[640,1024]{1,0:T(8,128)(2,1)}, u32[]{:S(2)}, u32[]{:S(2)}) collective-permute-start(bf16[640,1024]{1,0:T(8,128)(2,1)} %get-tuple-element.222.refs_4_), channel_id=1, source_target_pairs={{0,0},{1,2},{2,1},{3,3},{4,4},{5,6},{6,5},{7,7},{8,8},{9,10},{10,9... | collective-permute-start | bytes 3932168 | tf_op jit(solution)/shard_map/ppermute | solution.py:522
  472.0 23.9 %collective-permute-start.58 = (bf16[320,1024]{1,0:T(8,128)(2,1)}, bf16[320,1024]{1,0:T(8,128)(2,1)S(1)}, u32[]{:S(2)}, u32[]{:S(2)}) collective-permute-start(bf16[320,1024]{1,0:T(8,128)(2,1)} %get-tuple-element.228), channel_id=1, source_target_pairs={{0,2},{2,0},{1,3},{3,1},{4,6},{6,4},{5,7},{7,5},{8,10},{10,8},{9,1... | collective-permute-start | bytes 1966088 | tf_op jit(solution)/shard_map/ppermute | solution.py:514
  494.9 27.0 %collective-permute-start.61 = (bf16[2,64,2048]{2,1,0:T(8,128)(2,1)}, bf16[2,64,2048]{2,1,0:T(8,128)(2,1)S(1)}, u32[]{:S(2)}, u32[]{:S(2)}) collective-permute-start(bf16[2,64,2048]{2,1,0:T(8,128)(2,1)} %get-tuple-element.240), channel_id=1, source_target_pairs={{0,1},{1,0},{2,3},{3,2},{4,5},{5,4},{6,7},{7,6},{8,9},{9,8},{10,11... | collective-permute-start | bytes 1572872 | tf_op jit(solution)/shard_map/ppermute | solution.py:514
  495.6 26.3 %collective-permute-start.62 = (bf16[2,64,2048]{2,1,0:T(8,128)(2,1)}, bf16[2,64,2048]{2,1,0:T(8,128)(2,1)S(1)}, u32[]{:S(2)}, u32[]{:S(2)}) collective-permute-start(bf16[2,64,2048]{2,1,0:T(8,128)(2,1)} %get-tuple-element.241), channel_id=1, source_target_pairs={{0,4},{4,0},{1,5},{5,1},{2,6},{6,2},{3,7},{7,3},{8,12},{12,8},{9,1... | collective-permute-start | bytes 1572872 | tf_op jit(solution)/shard_map/ppermute | solution.py:514
  528.2 52.5 %collective-permute-start.66 = (bf16[6,64,2048]{2,1,0:T(8,128)(2,1)}, bf16[6,64,2048]{2,1,0:T(8,128)(2,1)}, u32[]{:S(2)}, u32[]{:S(2)}) collective-permute-start(bf16[6,64,2048]{2,1,0:T(8,128)(2,1)} %get-tuple-element.255), channel_id=1, source_target_pairs={{0,4},{4,0},{1,5},{5,1},{2,6},{6,2},{3,7},{7,3},{8,12},{12,8},{9,1... | collective-permute-start | bytes 4718600 | tf_op jit(solution)/shard_map/ppermute | solution.py:514
  529.3 51.3 %collective-permute-start.65 = (bf16[6,64,2048]{2,1,0:T(8,128)(2,1)}, bf16[6,64,2048]{2,1,0:T(8,128)(2,1)}, u32[]{:S(2)}, u32[]{:S(2)}) collective-permute-start(bf16[6,64,2048]{2,1,0:T(8,128)(2,1)} %get-tuple-element.243.refs_6_), channel_id=1, source_target_pairs={{0,1},{1,0},{2,3},{3,2},{4,5},{5,4},{6,7},{7,6},{8,9},{9,8},{10,11... | collective-permute-start | bytes 4718600 | tf_op jit(solution)/shard_map/ppermute | solution.py:514
  565.7 23.6 %collective-permute-start.64 = (bf16[320,1024]{1,0:T(8,128)(2,1)}, bf16[320,1024]{1,0:T(8,128)(2,1)S(1)}, u32[]{:S(2)}, u32[]{:S(2)}) collective-permute-start(bf16[320,1024]{1,0:T(8,128)(2,1)} %get-tuple-element.247), channel_id=1, source_target_pairs={{0,2},{2,0},{1,3},{3,1},{4,6},{6,4},{5,7},{7,5},{8,10},{10,8},{9,1... | collective-permute-start | bytes 1966088 | tf_op jit(solution)/shard_map/ppermute | solution.py:514
  566.1 23.1 %collective-permute-start.63 = (bf16[320,1024]{1,0:T(8,128)(2,1)S(1)}, bf16[320,1024]{1,0:T(8,128)(2,1)S(1)}, u32[]{:S(2)}, u32[]{:S(2)}) collective-permute-start(bf16[320,1024]{1,0:T(8,128)(2,1)S(1)} %get-tuple-element.246.refs_11_), channel_id=1, source_target_pairs={{0,2},{2,0},{1,3},{3,1},{4,6},{6,4},{5,7},{7,5},{8,10},{10,8},{9,1... | collective-permute-start | bytes 1966088 | tf_op jit(solution)/shard_map/ppermute | solution.py:514
  588.2 52.6 %collective-permute-start.72 = (bf16[6,64,2048]{2,1,0:T(8,128)(2,1)}, bf16[6,64,2048]{2,1,0:T(8,128)(2,1)}, u32[]{:S(2)}, u32[]{:S(2)}) collective-permute-start(bf16[6,64,2048]{2,1,0:T(8,128)(2,1)} %get-tuple-element.271), channel_id=1, source_target_pairs={{0,4},{4,0},{1,5},{5,1},{2,6},{6,2},{3,7},{7,3},{8,12},{12,8},{9,1... | collective-permute-start | bytes 4718600 | tf_op jit(solution)/shard_map/ppermute | solution.py:514
  588.8 52.1 %collective-permute-start.71 = (bf16[6,64,2048]{2,1,0:T(8,128)(2,1)}, bf16[6,64,2048]{2,1,0:T(8,128)(2,1)}, u32[]{:S(2)}, u32[]{:S(2)}) collective-permute-start(bf16[6,64,2048]{2,1,0:T(8,128)(2,1)} %get-tuple-element.257.refs_10_), channel_id=1, source_target_pairs={{0,1},{1,0},{2,3},{3,2},{4,5},{5,4},{6,7},{7,6},{8,9},{9,8},{10,11... | collective-permute-start | bytes 4718600 | tf_op jit(solution)/shard_map/ppermute | solution.py:514
  599.7 40.0 %collective-permute-start.73 = (bf16[64,2048]{1,0:T(8,128)(2,1)}, bf16[64,2048]{1,0:T(8,128)(2,1)}, u32[]{:S(2)}, u32[]{:S(2)}) collective-permute-start(bf16[64,2048]{1,0:T(8,128)(2,1)} %get-tuple-element.273), channel_id=1, source_target_pairs={{0,8},{8,0},{16,24},{24,16},{1,9},{9,1},{17,25},{25,17},{2,10},{10... | collective-permute-start | bytes 786440 | tf_op jit(solution)/shard_map/ppermute | solution.py:518
  602.8 37.9 %collective-permute-start.74 = (bf16[64,2048]{1,0:T(8,128)(2,1)}, bf16[64,2048]{1,0:T(8,128)(2,1)}, u32[]{:S(2)}, u32[]{:S(2)}) collective-permute-start(bf16[64,2048]{1,0:T(8,128)(2,1)} %get-tuple-element.274), channel_id=1, source_target_pairs={{0,16},{8,24},{16,0},{24,8},{1,17},{9,25},{17,1},{25,9},{2,18},{10... | collective-permute-start | bytes 786440 | tf_op jit(solution)/shard_map/ppermute | solution.py:518
  604.6 36.3 %collective-permute-start.75 = (bf16[64,2048]{1,0:T(8,128)(2,1)}, bf16[64,2048]{1,0:T(8,128)(2,1)}, u32[]{:S(2)}, u32[]{:S(2)}) collective-permute-start(bf16[64,2048]{1,0:T(8,128)(2,1)} %get-tuple-element.275), channel_id=1, source_target_pairs={{0,24},{8,16},{16,8},{24,0},{1,25},{9,17},{17,9},{25,1},{2,26},{10... | collective-permute-start | bytes 786440 | tf_op jit(solution)/shard_map/ppermute | solution.py:518
  648.7 40.6 %collective-permute-start.79 = (bf16[6,64,2048]{2,1,0:T(8,128)(2,1)}, bf16[6,64,2048]{2,1,0:T(8,128)(2,1)}, u32[]{:S(2)}, u32[]{:S(2)}) collective-permute-start(bf16[6,64,2048]{2,1,0:T(8,128)(2,1)} %get-tuple-element.287), channel_id=1, source_target_pairs={{0,4},{4,0},{1,5},{5,1},{2,6},{6,2},{3,7},{7,3},{8,12},{12,8},{9,1... | collective-permute-start | bytes 4718600 | tf_op jit(solution)/shard_map/ppermute | solution.py:514
  649.9 39.4 %collective-permute-start.78 = (bf16[6,64,2048]{2,1,0:T(8,128)(2,1)}, bf16[6,64,2048]{2,1,0:T(8,128)(2,1)}, u32[]{:S(2)}, u32[]{:S(2)}) collective-permute-start(bf16[6,64,2048]{2,1,0:T(8,128)(2,1)} %get-tuple-element.277.refs_10_), channel_id=1, source_target_pairs={{0,1},{1,0},{2,3},{3,2},{4,5},{5,4},{6,7},{7,6},{8,9},{9,8},{10,11... | collective-permute-start | bytes 4718600 | tf_op jit(solution)/shard_map/ppermute | solution.py:514
  662.2 22.2 %collective-permute-start.80 = (bf16[64,2048]{1,0:T(8,128)(2,1)}, bf16[64,2048]{1,0:T(8,128)(2,1)S(1)}, u32[]{:S(2)}, u32[]{:S(2)}) collective-permute-start(bf16[64,2048]{1,0:T(8,128)(2,1)} %get-tuple-element.289), channel_id=1, source_target_pairs={{0,8},{8,0},{16,24},{24,16},{1,9},{9,1},{17,25},{25,17},{2,10},{10... | collective-permute-start | bytes 786440 | tf_op jit(solution)/shard_map/ppermute | solution.py:518
  663.9 20.5 %collective-permute-start.81 = (bf16[64,2048]{1,0:T(8,128)(2,1)}, bf16[64,2048]{1,0:T(8,128)(2,1)S(1)}, u32[]{:S(2)}, u32[]{:S(2)}) collective-permute-start(bf16[64,2048]{1,0:T(8,128)(2,1)} %get-tuple-element.290), channel_id=1, source_target_pairs={{0,16},{8,24},{16,0},{24,8},{1,17},{9,25},{17,1},{25,9},{2,18},{10... | collective-permute-start | bytes 786440 | tf_op jit(solution)/shard_map/ppermute | solution.py:518
  665.4 23.9 %collective-permute-start.82 = (bf16[64,2048]{1,0:T(8,128)(2,1)}, bf16[64,2048]{1,0:T(8,128)(2,1)S(1)}, u32[]{:S(2)}, u32[]{:S(2)}) collective-permute-start(bf16[64,2048]{1,0:T(8,128)(2,1)} %get-tuple-element.291), channel_id=1, source_target_pairs={{0,24},{8,16},{16,8},{24,0},{1,25},{9,17},{17,9},{25,1},{2,26},{10... | collective-permute-start | bytes 786440 | tf_op jit(solution)/shard_map/ppermute | solution.py:518
  695.4 45.0 %collective-permute-start.86 = (bf16[6,64,2048]{2,1,0:T(8,128)(2,1)}, bf16[6,64,2048]{2,1,0:T(8,128)(2,1)}, u32[]{:S(2)}, u32[]{:S(2)}) collective-permute-start(bf16[6,64,2048]{2,1,0:T(8,128)(2,1)} %get-tuple-element.301), channel_id=1, source_target_pairs={{0,4},{4,0},{1,5},{5,1},{2,6},{6,2},{3,7},{7,3},{8,12},{12,8},{9,1... | collective-permute-start | bytes 4718600 | tf_op jit(solution)/shard_map/ppermute | solution.py:514
  695.8 44.5 %collective-permute-start.85 = (bf16[6,64,2048]{2,1,0:T(8,128)(2,1)}, bf16[6,64,2048]{2,1,0:T(8,128)(2,1)}, u32[]{:S(2)}, u32[]{:S(2)}) collective-permute-start(bf16[6,64,2048]{2,1,0:T(8,128)(2,1)} %get-tuple-element.292.refs_4_), channel_id=1, source_target_pairs={{0,1},{1,0},{2,3},{3,2},{4,5},{5,4},{6,7},{7,6},{8,9},{9,8},{10,11... | collective-permute-start | bytes 4718600 | tf_op jit(solution)/shard_map/ppermute | solution.py:514
  696.3 44.0 %collective-permute-start.87 = (bf16[64,2048]{1,0:T(8,128)(2,1)S(1)}, bf16[64,2048]{1,0:T(8,128)(2,1)S(1)}, u32[]{:S(2)}, u32[]{:S(2)}) collective-permute-start(bf16[64,2048]{1,0:T(8,128)(2,1)S(1)} %get-tuple-element.303), channel_id=1, source_target_pairs={{0,8},{8,0},{16,24},{24,16},{1,9},{9,1},{17,25},{25,17},{2,10},{10... | collective-permute-start | bytes 786440 | tf_op jit(solution)/shard_map/ppermute | solution.py:518
  696.3 44.0 %collective-permute-start.88 = (bf16[64,2048]{1,0:T(8,128)(2,1)S(1)}, bf16[64,2048]{1,0:T(8,128)(2,1)S(1)}, u32[]{:S(2)}, u32[]{:S(2)}) collective-permute-start(bf16[64,2048]{1,0:T(8,128)(2,1)S(1)} %get-tuple-element.304), channel_id=1, source_target_pairs={{0,16},{8,24},{16,0},{24,8},{1,17},{9,25},{17,1},{25,9},{2,18},{10... | collective-permute-start | bytes 786440 | tf_op jit(solution)/shard_map/ppermute | solution.py:518
  698.3 42.0 %collective-permute-start.89 = (bf16[64,2048]{1,0:T(8,128)(2,1)S(1)}, bf16[64,2048]{1,0:T(8,128)(2,1)S(1)}, u32[]{:S(2)}, u32[]{:S(2)}) collective-permute-start(bf16[64,2048]{1,0:T(8,128)(2,1)S(1)} %get-tuple-element.305), channel_id=1, source_target_pairs={{0,24},{8,16},{16,8},{24,0},{1,25},{9,17},{17,9},{25,1},{2,26},{10... | collective-permute-start | bytes 786440 | tf_op jit(solution)/shard_map/ppermute | solution.py:518
  750.0 47.2 %collective-permute-start.93 = (bf16[6,64,2048]{2,1,0:T(8,128)(2,1)}, bf16[6,64,2048]{2,1,0:T(8,128)(2,1)}, u32[]{:S(2)}, u32[]{:S(2)}) collective-permute-start(bf16[6,64,2048]{2,1,0:T(8,128)(2,1)} %get-tuple-element.316), channel_id=1, source_target_pairs={{0,4},{4,0},{1,5},{5,1},{2,6},{6,2},{3,7},{7,3},{8,12},{12,8},{9,1... | collective-permute-start | bytes 4718600 | tf_op jit(solution)/shard_map/ppermute | solution.py:514
  751.2 46.1 %collective-permute-start.92 = (bf16[6,64,2048]{2,1,0:T(8,128)(2,1)}, bf16[6,64,2048]{2,1,0:T(8,128)(2,1)}, u32[]{:S(2)}, u32[]{:S(2)}) collective-permute-start(bf16[6,64,2048]{2,1,0:T(8,128)(2,1)} %get-tuple-element.307.refs_9_), channel_id=1, source_target_pairs={{0,1},{1,0},{2,3},{3,2},{4,5},{5,4},{6,7},{7,6},{8,9},{9,8},{10,11... | collective-permute-start | bytes 4718600 | tf_op jit(solution)/shard_map/ppermute | solution.py:514
  767.7 40.7 %all-to-all-start.1 = ((f32[32,2,192]{2,1,0:T(2,128)}), f32[32,2,192]{2,1,0:T(2,128)S(1)}, u32[]{:S(2)}, u32[]{:S(2)}) async-start(f32[32,2,192]{2,1,0:T(2,128)} %bitcast.173), calls=%async_computation.1 | async-start | bytes 131072 | tf_op jit(solution)/shard_map/all_to_all | solution.py:1538
  773.5 23.7 %collective-permute-start.96 = (bf16[64,2048]{1,0:T(8,128)(2,1)}, bf16[64,2048]{1,0:T(8,128)(2,1)S(1)}, u32[]{:S(2)}, u32[]{:S(2)}) collective-permute-start(bf16[64,2048]{1,0:T(8,128)(2,1)} %copy-done.156), channel_id=1, source_target_pairs={{0,24},{8,16},{16,8},{24,0},{1,25},{9,17},{17,9},{25,1},{2,26},{10... | collective-permute-start | bytes 786440 | tf_op jit(solution)/shard_map/ppermute | solution.py:518
  783.2 80.7 %collective-permute-start.90 = (bf16[640,1024]{1,0:T(8,128)(2,1)S(1)}, bf16[640,1024]{1,0:T(8,128)(2,1)}, u32[]{:S(2)}, u32[]{:S(2)}) collective-permute-start(bf16[640,1024]{1,0:T(8,128)(2,1)S(1)} %get-tuple-element.308.refs_10_), channel_id=1, source_target_pairs={{0,0},{1,2},{2,1},{3,3},{4,4},{5,6},{6,5},{7,7},{8,8},{9,10},{10,9... | collective-permute-start | bytes 3932168 | tf_op jit(solution)/shard_map/ppermute | solution.py:522
  805.9 46.1 %collective-permute-start.99 = (bf16[4,64,2048]{2,1,0:T(8,128)(2,1)}, bf16[4,64,2048]{2,1,0:T(8,128)(2,1)S(1)}, u32[]{:S(2)}, u32[]{:S(2)}) collective-permute-start(bf16[4,64,2048]{2,1,0:T(8,128)(2,1)} %get-tuple-element.322), channel_id=1, source_target_pairs={{0,4},{4,0},{1,5},{5,1},{2,6},{6,2},{3,7},{7,3},{8,12},{12,8},{9,1... | collective-permute-start | bytes 3145736 | tf_op jit(solution)/shard_map/ppermute | solution.py:514
  807.1 44.9 %collective-permute-start.98 = (bf16[4,64,2048]{2,1,0:T(8,128)(2,1)}, bf16[4,64,2048]{2,1,0:T(8,128)(2,1)}, u32[]{:S(2)}, u32[]{:S(2)}) collective-permute-start(bf16[4,64,2048]{2,1,0:T(8,128)(2,1)} %get-tuple-element.321.refs_2_), channel_id=1, source_target_pairs={{0,1},{1,0},{2,3},{3,2},{4,5},{5,4},{6,7},{7,6},{8,9},{9,8},{10,11... | collective-permute-start | bytes 3145736 | tf_op jit(solution)/shard_map/ppermute | solution.py:514
  824.5 24.0 %collective-permute-start.102 = (bf16[64,2048]{1,0:T(8,128)(2,1)}, bf16[64,2048]{1,0:T(8,128)(2,1)}, u32[]{:S(2)}, u32[]{:S(2)}) collective-permute-start(bf16[64,2048]{1,0:T(8,128)(2,1)} %copy-done.160), channel_id=1, source_target_pairs={{0,24},{8,16},{16,8},{24,0},{1,25},{9,17},{17,9},{25,1},{2,26},{10... | collective-permute-start | bytes 786440 | tf_op jit(solution)/shard_map/ppermute | solution.py:518
  859.9 20.6 %collective-permute-start.109 = (bf16[64,2048]{1,0:T(8,128)(2,1)S(1)}, bf16[64,2048]{1,0:T(8,128)(2,1)S(1)}, u32[]{:S(2)}, u32[]{:S(2)}) collective-permute-start(bf16[64,2048]{1,0:T(8,128)(2,1)S(1)} %get-tuple-element.336), channel_id=1, source_target_pairs={{0,16},{8,24},{16,0},{24,8},{1,17},{9,25},{17,1},{25,9},{2,18},{10... | collective-permute-start | bytes 786440 | tf_op jit(solution)/shard_map/ppermute | solution.py:518
  862.7 24.8 %collective-permute-start.110 = (bf16[64,2048]{1,0:T(8,128)(2,1)S(1)}, bf16[64,2048]{1,0:T(8,128)(2,1)S(1)}, u32[]{:S(2)}, u32[]{:S(2)}) collective-permute-start(bf16[64,2048]{1,0:T(8,128)(2,1)S(1)} %get-tuple-element.337), channel_id=1, source_target_pairs={{0,24},{8,16},{16,8},{24,0},{1,25},{9,17},{17,9},{25,1},{2,26},{10... | collective-permute-start | bytes 786440 | tf_op jit(solution)/shard_map/ppermute | solution.py:518
  863.9 25.5 %collective-permute-start.107 = (f32[16,1024]{1,0:T(8,128)S(1)}, f32[16,1024]{1,0:T(8,128)S(1)}, u32[]{:S(2)}, u32[]{:S(2)}) collective-permute-start(f32[16,1024]{1,0:T(8,128)S(1)} %add_all.12.refs_3_.refs_1_), channel_id=1, source_target_pairs={{0,24},{8,16},{16,8},{24,0},{1,25},{9,17},{17,9},{25,1},{2,26},{10... | collective-permute-start | bytes 196616 | tf_op jit(solution)/shard_map/ppermute | solution.py:518
  864.9 28.1 %collective-permute-start.106 = (f32[16,1024]{1,0:T(8,128)S(1)}, f32[16,1024]{1,0:T(8,128)S(1)}, u32[]{:S(2)}, u32[]{:S(2)}) collective-permute-start(f32[16,1024]{1,0:T(8,128)S(1)} %add_all.12.refs_3_.refs_1_), channel_id=1, source_target_pairs={{0,16},{8,24},{16,0},{24,8},{1,17},{9,25},{17,1},{25,9},{2,18},{10... | collective-permute-start | bytes 196616 | tf_op jit(solution)/shard_map/ppermute | solution.py:518
  866.9 26.0 %collective-permute-start.105 = (f32[16,1024]{1,0:T(8,128)S(1)}, f32[16,1024]{1,0:T(8,128)S(1)}, u32[]{:S(2)}, u32[]{:S(2)}) collective-permute-start(f32[16,1024]{1,0:T(8,128)S(1)} %add_all.12.refs_3_.refs_1_), channel_id=1, source_target_pairs={{0,8},{8,0},{16,24},{24,16},{1,9},{9,1},{17,25},{25,17},{2,10},{10... | collective-permute-start | bytes 196616 | tf_op jit(solution)/shard_map/ppermute | solution.py:518
  880.5 31.5 %collective-permute-start.113 = (bf16[64,10240]{1,0:T(8,128)(2,1)S(1)}, bf16[64,10240]{1,0:T(8,128)(2,1)}, u32[]{:S(2)}, u32[]{:S(2)}) collective-permute-start(bf16[64,10240]{1,0:T(8,128)(2,1)S(1)} %join_pieces.1.refs_3_), channel_id=1, source_target_pairs={{0,0},{1,2},{2,1},{3,3},{4,4},{5,6},{6,5},{7,7},{8,8},{9,10},{10,9... | collective-permute-start | bytes 3932168 | tf_op jit(solution)/shard_map/ppermute | solution.py:522
  (243 other events, 2978.3 us)

commit v3 on v2

--- a/solution.py
+++ b/solution.py
@@ -518,8 +518,12 @@
     return lax.ppermute(values, "z", [(place, place ^ step) for place in range(4)])
 
 
+def swap_only(values):
+    return lax.ppermute(values, ("c", "x"), [(1, 2), (2, 1)])
+
+
 def swap(values):
-    return lax.ppermute(values, ("c", "x"), [(0, 0), (1, 2), (2, 1), (3, 3)])
+    return jnp.where(lax.axis_index("c") == lax.axis_index("x"), values, swap_only(values))
 
 
 def shape_of(dims, dtype=low):
@@ -529,6 +533,31 @@
 def whole(array):
     zeros = (0,) * len(array.shape)
     return pl.BlockSpec(tuple(array.shape), lambda *at: zeros)
+
+
+def whole_once(array):
+    zeros = (0,) * len(array.shape)
+    return pl.BlockSpec(
+        tuple(array.shape), lambda *at: zeros, pipeline_mode=pl.Buffered(1)
+    )
+
+
+def space_of(dims, dtype):
+    dims = [1] * (2 - len(dims)) + list(dims)
+    size = jnp.dtype(dtype).itemsize
+    rows = 32 // size
+    dims[-1] = -(-dims[-1] // 128) * 128
+    dims[-2] = -(-dims[-2] // rows) * rows
+    return int(np.prod(dims)) * size
+
+
+def room_for(specs, arrays, scratch):
+    total = 0
+    for spec, array in zip(specs, arrays):
+        if spec.block_shape is not None:
+            once = spec.pipeline_mode is not None
+            total += space_of(spec.block_shape, array.dtype) * (1 if once else 2)
+    return total + sum(space_of(held.shape, held.dtype) for held in scratch)
 
 
 class Chain:
@@ -540,11 +569,13 @@
     def wait(self, *values):
         self.pending += values
 
-    def run(self, name, kernel, args, in_specs, outs, out_specs, grid=(1,), scratch=(), mib=48, waits=()):
+    def run(self, name, kernel, args, in_specs, outs, out_specs, grid=(1,), scratch=(), extra=4, waits=()):
         count = len(args)
         unread = self.last + self.pending + list(waits)
         self.pending = []
         held = len(unread)
+
+        limit = room_for(list(in_specs) + list(out_specs), list(args) + list(outs), scratch)
 
         def body(*refs):
             kernel(*refs[: 1 + count], *refs[1 + count + held :])
@@ -559,7 +590,7 @@
                 scratch_shapes=list(scratch),
             ),
             out_shape=list(outs),
-            compiler_params=pltpu.CompilerParams(vmem_limit_bytes=mib * MIB),
+            compiler_params=pltpu.CompilerParams(vmem_limit_bytes=limit + extra * MIB),
             cost_estimate=pl.CostEstimate(flops=1, bytes_accessed=1, transcendentals=0),
             name=name,
         )(self.info, *args, *unread)
@@ -567,11 +598,35 @@
         return results
 
 
-def cut_kernel(info, packed, *outs):
+def pack_arguments(chain, rows_in, up, down, qkv, out):
+    def kernel(info, rows_from, up_in, down_in, qkv_in, out_in, rows_to, packed):
+        rows_to[...] = rows_from[...]
+        start = 0
+        for part in (up_in[0], down_in[0], qkv_in[1], out_in[1], up_in[1], down_in[1]):
+            packed[:, start : start + part.shape[1]] = part
+            start += part.shape[1]
+
+    args = [rows_in, up, down, qkv, out]
+    outs = [shape_of(rows_in.shape), shape_of((up.shape[1], 5 * PIECE))]
+    return chain.run(
+        "pack_arguments", kernel, args, [whole(v) for v in args], outs, [whole(v) for v in outs]
+    )
+
+
+def cut_kernel(info, packed, traded, *outs):
     start = 0
     for out in outs:
         width = out.shape[1]
-        out[...] = packed[:, start : start + width]
+        cols = slice(start, start + width)
+
+        @pl.when(info[4] == 1)
+        def _():
+            out[...] = packed[:, cols]
+
+        @pl.when(info[4] == 0)
+        def _():
+            out[...] = traded[:, cols]
+
         start += width
 
 
@@ -611,9 +666,12 @@
         start = 0
         if far:
             got_x, got_y = self.got[at - 1]
-            start = got_x.shape[0] - 4
+            start = (got_x.shape[0] - 4) // 2
             args += [got_x, got_y]
-            specs += [tile_spec(got_x.shape[0])] * 2
+            specs += [
+                pl.BlockSpec((2, 64, PIECE_TILE), lambda j, info: (start + 1, 0, j)),
+                pl.BlockSpec((2, 64, PIECE_TILE), lambda j, info: (start, 0, j)),
+            ]
 
         def kernel(info, *refs):
             to_x, to_y = refs[-2:]
@@ -623,8 +681,8 @@
                     to_y[(2 if far else 0) + k] = refs[k][...]
             if far:
                 from_x, from_y = refs[-4:-2]
-                to_x[0:2] = from_y[start : start + 2]
-                to_y[0:2] = from_x[start + 2 : start + 4]
+                to_x[0:2] = from_y[...]
+                to_y[0:2] = from_x[...]
 
         count = (2 if far else 0) + (4 if own else 0)
         outs = [shape_of((count, 64, PIECE))] * 2
@@ -686,40 +744,48 @@
         return [a.reshape(16 * 64, a.shape[3]) for a in results]
 
 
-def weight_grad_kernel(info, *refs, pairs, widths):
+GRAD_TILE = 512
+
+
+def weight_grad_kernel(info, *refs, pairs, tiles):
     lhs = refs[: 4 * pairs]
     rhs = refs[4 * pairs : 5 * pairs]
-    near, to_x, to_y, far_lo, far_hi, held = refs[5 * pairs :]
-    z = pl.program_id(0)
+    near, to_x, to_y, far_lo, far_hi = refs[5 * pairs : 5 * pairs + 5]
+    held = refs[5 * pairs + 5]
+    across = refs[5 * pairs + 6 :]
+    j = pl.program_id(0)
     place = info[1] * 2 + info[2]
-    start = 0
+    begin = 0
     for at in range(pairs):
-        halves = []
-        for half in range(2):
-            spot = 4 * at + 2 * half
-            halves.append(jnp.concatenate([lhs[spot][...].T, lhs[spot + 1][...].T], axis=1))
-        for begin in range(0, widths[at], 512):
-            cols = slice(begin, begin + 512)
-            block = jnp.dot(
-                halves[0], rhs[at][0, :, cols], preferred_element_type=full
-            ) + jnp.dot(halves[1], rhs[at][1, :, cols], preferred_element_type=full)
-            held[:, start + begin : start + begin + 512] = block.astype(low)
-        start += widths[at]
-
-    def part(rel):
-        return held[pl.ds(pl.multiple_of((place ^ rel) * 64, 64), 64), :]
-
-    near[0] = part(0)
-    to_x[0] = part(1)
-    to_y[0] = part(2)
-
-    @pl.when(z < 2)
-    def _():
-        far_lo[0] = part(3)
-
-    @pl.when(z >= 2)
-    def _():
-        far_hi[0] = part(3)
+
+        @pl.when(j == begin)
+        def _():
+            for part in range(4):
+                cols = slice(part * ROW_TILE, (part + 1) * ROW_TILE)
+                across[at][:, cols] = lhs[4 * at + part][...].T
+
+        @pl.when((j >= begin) & (j < begin + tiles[at]))
+        def _():
+            tokens = rhs[at][...].reshape(4 * ROW_TILE, GRAD_TILE)
+            for rows in range(0, held.shape[0], 256):
+                block = jnp.dot(
+                    across[at][rows : rows + 256], tokens, preferred_element_type=full
+                )
+                held[rows : rows + 256] = block.astype(low)
+
+        begin += tiles[at]
+
+    def part(z, rel):
+        return held[pl.ds(pl.multiple_of(z * 256 + (place ^ rel) * 64, 64), 64), :]
+
+    for z in range(4):
+        near[z] = part(z, 0)
+        to_x[z] = part(z, 1)
+        to_y[z] = part(z, 2)
+        if z < 2:
+            far_lo[z] = part(z, 3)
+        else:
+            far_hi[z - 2] = part(z, 3)
 
 
 class Scatter:
@@ -735,28 +801,32 @@
         pairs = len(items)
         widths = tuple(item[2].shape[2] for item in items)
         rows, features = items[0][0][0].shape
-        tile = features // 4
+        tiles = [w // GRAD_TILE for w in widths]
         quads = shape_of((4, 64, PIECE))
         twos = shape_of((2, 64, PIECE))
-        lhs_spec = pl.BlockSpec((rows, tile), lambda z, info: (0, z))
-        block = (1, 64, PIECE)
+
+        def rhs_spec(at):
+            first, last = sum(tiles[:at]), tiles[at] - 1
+            return pl.BlockSpec(
+                (2, 2 * rows, GRAD_TILE),
+                lambda j, info: (0, 0, jnp.clip(j - first, 0, last)),
+            )
+
+        quad_spec = pl.BlockSpec((4, 64, GRAD_TILE), lambda j, info: (0, 0, j))
+        two_spec = pl.BlockSpec((2, 64, GRAD_TILE), lambda j, info: (0, 0, j))
+        lhs = [part for item in items for pair in item[:2] for part in pair]
         self.parts.append(
             self.chain.run(
                 "weight_grad",
-                lambda *refs: weight_grad_kernel(*refs, pairs=pairs, widths=widths),
-                [part for item in items for pair in item[:2] for part in pair]
-                + [item[2] for item in items],
-                [lhs_spec] * (4 * pairs)
-                + [pl.BlockSpec((2, 2 * rows, w), lambda z, info: (0, 0, 0)) for w in widths],
+                lambda *refs: weight_grad_kernel(*refs, pairs=pairs, tiles=tiles),
+                lhs + [item[2] for item in items],
+                [whole_once(v) for v in lhs] + [rhs_spec(at) for at in range(pairs)],
                 [quads, quads, quads, twos, twos],
-                [pl.BlockSpec(block, lambda z, info: (z, 0, 0))] * 3
-                + [
-                    pl.BlockSpec(block, lambda z, info: (jnp.minimum(z, 1), 0, 0)),
-                    pl.BlockSpec(block, lambda z, info: (jnp.maximum(z - 2, 0), 0, 0)),
-                ],
-                grid=(4,),
-                scratch=[pltpu.VMEM((tile, PIECE), low)],
-                mib=56,
+                [quad_spec] * 3 + [two_spec] * 2,
+                grid=(PIECE // GRAD_TILE,),
+                scratch=[pltpu.VMEM((features, GRAD_TILE), low)]
+                + [pltpu.VMEM((features, 4 * rows), low)] * pairs,
+                extra=4,
             )
         )
         if len(self.parts) == 1:
@@ -857,6 +927,20 @@
             self.done.append(results[0])
 
 
+def collect_sums(chain, sums):
+    spots = [(4, 0), (4, 1), (3, 2), (3, 0), (3, 1), (2, 2), (2, 0), (2, 1), (1, 2), (1, 0), (1, 1), (0, 0)]
+
+    def kernel(info, *refs):
+        for row, (at, spot) in enumerate(spots):
+            refs[-1][row : row + 1] = refs[at][spot : spot + 1]
+
+    out = shape_of((len(spots), sums[0].shape[1]), full)
+    (result,) = chain.run(
+        "collect_sums", kernel, list(sums), [whole(v) for v in sums], [out], [whole(out)]
+    )
+    return result
+
+
 def add_all(chain, *values):
     def kernel(info, *refs):
         total = refs[0][...]
@@ -871,16 +955,21 @@
     return result
 
 
-def join_pieces(chain, pieces):
+def join_pieces(chain, pieces, *copied):
+    count = len(pieces)
+
     def kernel(info, *refs):
-        for at, piece in enumerate(refs[:-1]):
-            refs[-1][:, at * PIECE : (at + 1) * PIECE] = piece[...]
-
-    out = shape_of((64, PIECE * len(pieces)))
-    (result,) = chain.run(
-        "join_pieces", kernel, pieces, [whole(a) for a in pieces], [out], [whole(out)]
-    )
-    return result
+        out = refs[count + len(copied)]
+        for at in range(count):
+            out[:, at * PIECE : (at + 1) * PIECE] = refs[at][...]
+        for at in range(len(copied)):
+            refs[count + len(copied) + 1 + at][...] = refs[count + at][...]
+
+    args = list(pieces) + list(copied)
+    outs = [shape_of((64, PIECE * count))] + [shape_of(v.shape) for v in copied]
+    return chain.run(
+        "join_pieces", kernel, args, [whole(v) for v in args], outs, [whole(v) for v in outs]
+    )
 
 
 def gelu_and_slope(values):
@@ -930,7 +1019,7 @@
         "both_" + kind,
         lambda *refs: both_kernel(*refs, kind=kind),
         [*own, *other, weight] + extra,
-        [whole(part) for part in (*own, *other)]
+        [whole_once(part) for part in (*own, *other)]
         + [pl.BlockSpec((depth, tile), lambda j, info: (0, j))]
         + [out_spec] * len(extra),
         [shape_of((2, rows, width))] * count,
@@ -962,7 +1051,9 @@
         kernel,
         [values, weight],
         [
-            pl.BlockSpec((1, rows, depth), lambda j, info: (1, 0, 0)),
+            pl.BlockSpec(
+                (1, rows, depth), lambda j, info: (1, 0, 0), pipeline_mode=pl.Buffered(1)
+            ),
             pl.BlockSpec((tile, depth), lambda j, info: (j, 0)),
         ],
         [shape_of((ROW_TILE, width))] * 2,
@@ -1006,27 +1097,27 @@
     return tall, thin
 
 
-def first_norm(chain, current, rows_of):
+def first_norm(chain, current, traded, rows_of):
     rows, model_width = current.shape
     tall, thin = row_specs(model_width)
 
-    def kernel(info, values, given, normed, inverse, *moved):
-        normed[...], inverse[...], result = norm_and_move(
-            values[...].astype(full), given[0:1], given[1:2]
-        )
+    def kernel(info, ours, theirs, given, kept, normed, inverse, *moved):
+        values = jnp.where(info[4] == 1, ours[...].astype(full), theirs[...].astype(full))
+        kept[...] = values.astype(low)
+        normed[...], inverse[...], result = norm_and_move(values, given[0:1], given[1:2])
         put_half(moved, result)
 
     half = shape_of((ROW_TILE, model_width))
-    normed, inverse, *moved = chain.run(
+    kept, normed, inverse, *moved = chain.run(
         "first_norm",
         kernel,
-        [current, rows_of],
-        [tall, whole(rows_of)],
-        [shape_of(current.shape), shape_of((rows, 1), full), half, half],
-        [tall, thin, whole(half), whole(half)],
+        [current, traded, rows_of],
+        [tall, tall, whole_once(rows_of)],
+        [shape_of(current.shape)] * 2 + [shape_of((rows, 1), full), half, half],
+        [tall, tall, thin, whole(half), whole(half)],
         grid=(rows // ROW_TILE,),
     )
-    return normed, inverse, moved
+    return kept, normed, inverse, moved
 
 
 def forward_step(chain, values, weight, away, current, rows_of, last, waits=()):
@@ -1056,11 +1147,11 @@
         [values, weight, *away, current, rows_of],
         [
             pl.BlockSpec((1, ROW_TILE, depth), lambda i, info: (0, i, 0)),
-            whole(weight),
-            whole(away[0]),
-            whole(away[1]),
+            whole_once(weight),
+            whole_once(away[0]),
+            whole_once(away[1]),
             tall,
-            whole(rows_of),
+            whole_once(rows_of),
         ],
         outs,
         specs,
@@ -1097,7 +1188,7 @@
         "first_back",
         kernel,
         [state, branch, gate],
-        [tall, tall, whole(gate)],
+        [tall, tall, whole_once(gate)],
         [half, half, sums],
         [whole(half), whole(half), whole(sums)],
         grid=(rows // ROW_TILE,),
@@ -1148,13 +1239,13 @@
         [values, weight, *away, normed, inverse, state, rows_of] + extra,
         [
             pl.BlockSpec((1, ROW_TILE, depth), lambda i, info: (0, i, 0)),
-            whole(weight),
-            whole(away[0]),
-            whole(away[1]),
+            whole_once(weight),
+            whole_once(away[0]),
+            whole_once(away[1]),
             tall,
             thin,
             tall,
-            whole(rows_of),
+            whole_once(rows_of),
         ]
         + [tall] * len(extra),
         outs,
@@ -1291,7 +1382,7 @@
             *refs, heads=heads, cells=cells, masked=is_joint, sides=sides
         ),
         [blocks, joined],
-        [whole(blocks), window_specs(is_joint, frames, 3 * width)],
+        [whole_once(blocks), window_specs(is_joint, frames, 3 * width)],
         [shape_of(joined.shape[:4] + (width,)), shape_of((number, heads, cells, cells))],
         [window_specs(is_joint, frames, width), pl.BlockSpec((1, heads, cells, cells), fetch)],
         grid=grid,
@@ -1320,7 +1411,7 @@
         [window_specs(is_joint, frames, 3 * width), whole(sums)],
         grid=grid,
         scratch=[pltpu.VMEM((heads, cells, cells), full)],
-        mib=56,
+        extra=6,
     )
 
 
@@ -1357,8 +1448,12 @@
     col_width = ada_weight.shape[2]
     rows = frames * 128
     z, y, c, x = (lax.axis_index(name) for name in ("z", "y", "c", "x"))
-    count = swap(frame_counts.astype(full)).astype(jnp.int32)
-    chain = Chain(jnp.concatenate([jnp.stack([z, y, x]).astype(jnp.int32), count]))
+    counts = frame_counts.astype(full)
+    count = jnp.where(c == x, counts, flip(counts, "c")).astype(jnp.int32)
+    same = (c == x).astype(jnp.int32)
+    chain = Chain(
+        jnp.concatenate([jnp.stack([z, y, x]).astype(jnp.int32), count, same.reshape(1)])
+    )
 
     def rearranged(values):
         shaped = values.reshape(frames, 8, 2, 8, model_width).transpose(0, 2, 1, 3, 4)
@@ -1368,14 +1463,6 @@
     out_rows = out_weight.transpose(0, 2, 1)
     down_rows = down_weight.transpose(0, 2, 1)
     first_shard = swap(jnp.concatenate([qkv_rows[0], out_rows[0]], axis=1))
-    traded_latents = swap(latents)
-    packed = swap(
-        jnp.concatenate(
-            [up_weight[0], down_rows[0], qkv_rows[1], out_rows[1], up_weight[1], down_rows[1]],
-            axis=1,
-        )
-    )
-
     band_hot = (band_ids[:, None] == jnp.arange(BANDS)[None, :]).astype(low)
     class_hot = (class_ids[:, None] == jnp.arange(CLASSES)[None, :]).astype(low)
     condition = jnp.dot(band_hot, time_table, preferred_element_type=full) + jnp.dot(
@@ -1415,16 +1502,28 @@
 
     windowed = lambda values: values.reshape(2, frames, 2, 64, values.shape[-1])
 
-    latent_rows = rearranged(traded_latents)
-    cuts = [shape_of((64, PIECE))] * 5
-    shards = chain.run(
-        "cut_shards", cut_kernel, [packed], [whole(packed)], cuts, [whole(a) for a in cuts]
-    )
-    gather = Gather(chain, [first_shard] + list(shards))
+    chain.wait(own_mod, parts)
+    latent_rows, packed = pack_arguments(
+        chain, rearranged(latents), up_weight, down_rows, qkv_rows, out_rows
+    )
+    traded_rows, traded = swap_only(latent_rows), swap_only(packed)
+    gather = Gather(chain, [first_shard] + [None] * 5)
     gather.over_z(0)
     gather.step()
+    cuts = [shape_of((64, PIECE))] * 5
+    gather.shards[1:] = chain.run(
+        "cut_shards",
+        cut_kernel,
+        [packed, traded],
+        [whole(packed)] * 2,
+        cuts,
+        [whole(a) for a in cuts],
+    )
     gather.over_z(1)
-    normed_0, inverse_0, moved_0 = first_norm(chain, latent_rows, rows_of((0, 0), (0, 1)))
+    chain.wait(*bias_blocks)
+    latent_rows, normed_0, inverse_0, moved_0 = first_norm(
+        chain, latent_rows, traded_rows, rows_of((0, 0), (0, 1))
+    )
     other_0 = flip_rows(moved_0)
     gather.step()
     gather.over_z(2)
@@ -1466,7 +1565,7 @@
         chain, mixed_1, out_1, away, current_1, rows_of((1, 2), (1, 3), (1, 4)), False
     )
     other_3 = flip_rows(moved_3)
-    traded_cotangent = swap(cotangent)
+    traded_cotangent = swap(rearranged(cotangent))
     act_1, slope_1 = both_times(chain, "gelu", moved_3, other_3, up_1)
     (down_1,) = gather.place(5, [hidden])
     away = other_rows(chain, act_1, down_1)
@@ -1480,7 +1579,13 @@
 
     traded_final = swap(final)
 
-    state = rearranged(traded_cotangent)
+    exact = lax.Precision.HIGHEST
+    hot_wide = jnp.pad(hot.astype(full), ((0, 256 - wide * wide), (0, 0)))
+    table_sums = lambda sums: jnp.dot(
+        sums.reshape(heads * 9, 64 * 64), hot_wide.T, precision=exact
+    )
+
+    state = traded_cotangent
     own_g, sums_a = first_back(chain, state, branch_two_1, rows_of((1, 5)))
     other_g = flip_rows(own_g)
     scatter = Scatter(chain)
@@ -1496,6 +1601,7 @@
     scatter.step(6)
     (mixed_g,) = both_times(chain, "plain", own_g, other_g, out_1)
     back, joint_sums = attend_back(chain, joined_1, windowed(mixed_g), probs_1, True)
+    joint_tables = table_sums(joint_sums)
     back = back.reshape(2, rows, 3 * width)
     away = other_rows(chain, back, qkv_1)
     scatter.weight_grad((moved_2, other_2, back), (own_g, other_g, mixed_1))
@@ -1508,6 +1614,7 @@
     (hidden_g,) = both_times(chain, "slope", own_g, other_g, down_0, slope_0)
     away = other_rows(chain, hidden_g, up_0)
     scatter.weight_grad((own_g, other_g, act_0))
+    chain.wait(joint_tables)
     scatter.step(6)
     state, sums_d, own_g = backward_step(
         chain, hidden_g, up_0, away, normed_1, inverse_1, state, rows_of((0, 4), (0, 2)), branch_one_0
@@ -1516,24 +1623,20 @@
     scatter.weight_grad((moved_1, other_1, hidden_g))
     (mixed_g,) = both_times(chain, "plain", own_g, other_g, out_0)
     scatter.step(6)
+    first_done = swap(join_pieces(chain, scatter.done[:2])[0])
     back, spatial_sums = attend_back(chain, joined_0, windowed(mixed_g), probs_0, False)
     back = back.reshape(2, rows, 3 * width)
     away = other_rows(chain, back, qkv_0)
     scatter.weight_grad((moved_0, other_0, back), (own_g, other_g, mixed_0))
+    chain.wait(first_done)
     scatter.step(6)
     state, sums_e = backward_step(
         chain, back, qkv_0, away, normed_0, inverse_0, state, rows_of((0, 1)), None
     )
-    traded_state = swap(state)
     output = restored(traded_final)
 
-    exact = lax.Precision.HIGHEST
-    grad_mod = jnp.stack(
-        [
-            sums_e[0], sums_e[1], sums_d[2], sums_d[0], sums_d[1], sums_c[2],
-            sums_c[0], sums_c[1], sums_b[2], sums_b[0], sums_b[1], sums_a[0],
-        ]
-    )
+    chain.wait(*scatter.held[1:])
+    grad_mod = collect_sums(chain, [sums_a, sums_b, sums_c, sums_d, sums_e])
     ordered = grad_mod.reshape(2, 32, col_width).transpose(1, 0, 2)
     cols = lax.all_to_all(ordered, everyone, split_axis=0, concat_axis=0, tiled=True)
     cols = cols.reshape(8, 2, 2, 2, col_width)
@@ -1541,41 +1644,38 @@
     grad_ada_weight = jnp.einsum("cd,cbe->bde", activity.astype(full), cols, precision=exact)
     grad_ada_bias = jnp.sum(cols, axis=0)
     grad_activity = jnp.einsum("cbe,bde->cd", cols, ada_weight.astype(full), precision=exact)
-    grad_activity = grad_activity + flip(grad_activity, "c")
 
     near = spatial_sums.reshape(heads, 3, 3, 64, 64)
     near = jnp.where(c == 0, near, near[:, ::-1]).reshape(heads, 9, 64, 64)
-    tables = jnp.dot(
-        jnp.stack([near, joint_sums]).reshape(heads * 18, 64 * 64),
-        hot.astype(full).T,
-        precision=exact,
-    )
-
+    tables = jnp.concatenate([table_sums(near), joint_tables])
+
+    shared = jnp.concatenate([grad_activity.reshape(-1, 256), tables])
+    chain.wait(shared)
     scatter.step(6)
-    shared = add_all(chain, grad_activity)
-    shared_tables = add_all(chain, tables)
     scatter.step(6)
-    sent = flip(shared, "x"), flip(shared_tables, "x")
-    shared = add_all(chain, shared, sent[0])
-    shared_tables = add_all(chain, shared_tables, sent[1])
-    sent = flip(shared, "y"), flip(shared_tables, "y")
-    early = swap(join_pieces(chain, scatter.done))
-    shared = add_all(chain, shared, sent[0])
-    shared_tables = add_all(chain, shared_tables, sent[1])
-    sent = [[z_trade(values, k) for k in (1, 2, 3)] for values in (shared, shared_tables)]
+    sent = flip(shared, "x")
+    early, state_copy = join_pieces(chain, scatter.done[2:], state)
+    early = swap(early)
+    traded_state = swap(state_copy)
+    shared = add_all(chain, shared, sent)
+    shared = add_all(chain, shared, flip(shared, "y"))
+    sent = [z_trade(shared, k) for k in (1, 2, 3)]
     scatter.step(6)
     late = swap(scatter.done[5]).astype(full)
-    grad_activity = add_all(chain, shared, *sent[0])
-    tables = add_all(chain, shared_tables, *sent[1])
+    shared = add_all(chain, shared, *sent)
+    tables = shared[-heads * 18 :]
+    across = flip(shared, "c")
+    grad_activity = (shared + across)[: -heads * 18].reshape(16, model_width)
+    tables = jnp.where(c == x, tables, across[-heads * 18 :])[:, : wide * wide]
     grad_latents = restored(traded_state)
-    early = early.astype(full)
-    piece = lambda at: early[:, at * PIECE : (at + 1) * PIECE]
+    done = jnp.concatenate([first_done, early], axis=1).astype(full)
+    piece = lambda at: done[:, at * PIECE : (at + 1) * PIECE]
     grad_down = jnp.stack([piece(3).T, piece(0).T])
     grad_up = jnp.stack([piece(4), piece(1)])
     grad_qkv = jnp.stack([late[:, : 3 * width], piece(2)[:, : 3 * width]])
     grad_out = jnp.stack([late[:, 3 * width :].T, piece(2)[:, 3 * width :].T])
 
-    tables = jnp.where(c == x, tables, flip(tables, "c")).reshape(2, heads, 9, wide, wide)
+    tables = tables.reshape(2, heads, 9, wide, wide)
     grad_joint = tables[1].reshape(heads, 9 * wide * wide)
     near = tables[0].reshape(heads, 3, 3, wide, wide)
     long = 2 * WIN_S - 1

time: 934 us -> 757 us (0.81)
  Pallas kernels: 448 us -> 316 us
  waiting for transfers between devices: 130 us -> 176 us
  starting transfers between devices: 172 us -> 136 us
  blocking collectives: 25.2 us -> 0 us
  local copies, waits for them, and re-layouts: 104 us -> 80.4 us
    pallas_call x67 -> x65, Pallas kernels: 448 us -> 316 us  [run(): pl.pallas_call(body, grid_spec=pltpu.PrefetchScalarGridSpec(num_scalar_pr...]
    ppermute x42 -> x39, waiting for transfers between devices: 77.1 us -> 115 us  [z_trade(): lax.ppermute(values, 'z', [(place, place ^ step) for place in range(4)])]
    all_to_all x1 -> x0, blocking collectives: 25.2 us -> none  [fast_local(): lax.all_to_all(mod_part, everyone, split_axis=0, concat_axis=0, tiled=True)]
    ppermute x10, starting transfers between devices: 68 us -> 43.7 us  [swap_only(): return lax.ppermute(values, ('c', 'x'), [(1, 2), (2, 1)])]
    ppermute x66 -> x64, waiting for transfers between devices: 22.3 us -> 42.7 us  [flip(): return lax.ppermute(values, axis, [(0, 1), (1, 0)])]
    ppermute x10, waiting for transfers between devices: 30.1 us -> 15.6 us  [swap_only(): return lax.ppermute(values, ('c', 'x'), [(1, 2), (2, 1)])]
    ppermute x42 -> x39, starting transfers between devices: 52.4 us -> 39 us  [z_trade(): lax.ppermute(values, 'z', [(place, place ^ step) for place in range(4)])]
    unnamed x392 -> x332, local copies, waits for them, and re-layouts: 68.8 us -> 56.4 us
  transfers between devices with their start and end apart: 119 -> 115, of which waited for: 26 -> 39; matrix products, arithmetic and copies ran while one was open for 8% -> 7% of each run, Pallas kernels for 44% -> 39%
where the time goes in v3:
time: 757 us; the launch traced here: 749 us
  Pallas kernels  316 us (42%)
  waiting for transfers between devices  176 us (23%)
  starting transfers between devices  136 us (18%)
  local copies, waits for them, and re-layouts  80.4 us (11%)
  other arithmetic  23.7 us (3%)
  matrix products  11.7 us (2%)
    pallas_call x65, Pallas kernels, run(): pl.pallas_call(body, grid_spec=pltpu.PrefetchScalarGridSpec(num_scalar_pr...  316 us
    ppermute x39, waiting for transfers between devices, z_trade(): lax.ppermute(values, 'z', [(place, place ^ step) for place in range(4)])  115 us
    unnamed x332, local copies, waits for them, and re-layouts  56.4 us
    ppermute x10, starting transfers between devices, swap_only(): return lax.ppermute(values, ('c', 'x'), [(1, 2), (2, 1)])  43.7 us
    ppermute x64, waiting for transfers between devices, flip(): return lax.ppermute(values, axis, [(0, 1), (1, 0)])  42.7 us
    ppermute x64, starting transfers between devices, flip(): return lax.ppermute(values, axis, [(0, 1), (1, 0)])  41.5 us
    ppermute x39, starting transfers between devices, z_trade(): lax.ppermute(values, 'z', [(place, place ^ step) for place in range(4)])  39 us
    ppermute x10, waiting for transfers between devices, swap_only(): return lax.ppermute(values, ('c', 'x'), [(1, 2), (2, 1)])  15.6 us
  transfers between devices with their start and end apart: 115, of which 39 were waited for; matrix products, arithmetic and copies ran while one was open for 7% of the time, Pallas kernels for 39%

profile of v3, /device:TPU:9, one launch (start us, length us, event | category | flops | bytes accessed | tf_op | source)
XLA Modules:
  0.0 749.3 jit_solution(2704701179696257754)
XLA Ops:
  4.5 3.7 collective-permute-start.1
  15.5 6.4 all-to-all-start
  34.4 4.2 collective-permute-start.3
  41.5 9.0 %collective-permute-done.7.refs_4_ = bf16[64,2048]{1,0:T(8,128)(2,1)} collective-permute-done((bf16[64,2048]{1,0:T(8,128)(2,1)S(1)}, bf16[64,2048]{1,0:T(8,128)(2,1)}, u32[]{:S(2)}, u32[]{:S(2)}) %collective-permute-start.7) | collective-permute-done | bytes 262176 | tf_op jit(solution)/shard_map/ppermute | solution.py:518
  50.6 4.0 gather_step.7
  69.3 10.0 %collective-permute-done.2.refs_2_ = bf16[640,1024]{1,0:T(8,128)(2,1)} collective-permute-done((bf16[640,1024]{1,0:T(8,128)(2,1)}, bf16[640,1024]{1,0:T(8,128)(2,1)}, u32[]{:S(2)}, u32[]{:S(2)}) %collective-permute-start.2) | collective-permute-done | bytes 1310752 | tf_op jit(solution)/shard_map/ppermute | solution.py:522
  80.6 3.1 first_norm.1
  83.8 6.2 collective-permute-done.10.refs_5_.refs_2_
  90.0 3.2 collective-permute-done.14.refs_4_
  99.3 6.8 collective-permute-done.17.refs_2_
  106.1 3.5 collective-permute-done.18.refs_3_
  109.6 11.3 %collective-permute-done.19.refs_4_ = bf16[64,2048]{1,0:T(8,128)(2,1)S(1)} collective-permute-done((bf16[64,2048]{1,0:T(8,128)(2,1)S(1)}, bf16[64,2048]{1,0:T(8,128)(2,1)S(1)}, u32[]{:S(2)}, u32[]{:S(2)}) %collective-permute-start.19) | collective-permute-done | bytes 262176 | tf_op jit(solution)/shard_map/ppermute | solution.py:518
  120.9 10.7 %collective-permute-done.15.refs_5_.refs_4_.refs_2_ = bf16[6,64,2048]{2,1,0:T(8,128)(2,1)S(1)} collective-permute-done((bf16[6,64,2048]{2,1,0:T(8,128)(2,1)S(1)}, bf16[6,64,2048]{2,1,0:T(8,128)(2,1)S(1)}, u32[]{:S(2)}, u32[]{:S(2)}) %collective-permute-start.15) | collective-permute-done | bytes 1572896 | tf_op jit(solution)/shard_map/ppermute | solution.py:514
  142.6 5.6 both_plain.4.refs_3_
  148.2 14.6 %attend_spatial.1 = (bf16[2,5,2,64,512]{4,3,2,1,0:T(8,128)(2,1)S(1)}, bf16[5,8,256,256]{3,2,1,0:T(8,128)(2,1)S(1)}) custom-call(s32[5]{0:T(128)S(1)} %concatenate.16.refs_0_, bf16[8,9,64,64]{3,2,1,0:T(8,128)(2,1)S(1)} %bitcast.198, bf16[2,5,2,64,1536]{4,3,2,1,0:T(8,128)(2,1)S(1)} %bitcast.174, bf16[2,640,1536]{2,1,0:T(8,128)(2,1)S(1)} %both_plain.4.refs_3_), custom_call_target="tpu_custom_call" | custom-call | flops 1 | bytes 1 | tf_op jit(solution)/shard_map/attend_spatial/pallas_call | solution.py:583
  181.1 3.5 collective-permute-start.32
  184.7 17.3 %both_gelu.2 = (bf16[2,640,2048]{2,1,0:T(8,128)(2,1)S(1)}, bf16[2,640,2048]{2,1,0:T(8,128)(2,1)S(1)}) custom-call(s32[5]{0:T(128)S(1)} %concatenate.16.refs_0_, bf16[320,1024]{1,0:T(8,128)(2,1)S(1)} %get-tuple-element.200.refs_1_, bf16[320,1024]{1,0:T(8,128)(2,1)S(1)} %get-tuple-element.201.refs_2_, bf16[320,1024]{1,0:T(8,128)(2,1)S(1)} %collective-permute-done.27.refs_3_, ...), custom_call_target="tpu_custom_call" | custom-call | flops 1 | bytes 1 | tf_op jit(solution)/shard_map/both_gelu/pallas_call | solution.py:583
  210.2 4.6 other_rows.9
  222.0 5.0 forward_step.5
  227.5 10.1 %collective-permute-done.41.refs_3_ = bf16[64,2048]{1,0:T(8,128)(2,1)S(1)} collective-permute-done((bf16[64,2048]{1,0:T(8,128)(2,1)S(1)}, bf16[64,2048]{1,0:T(8,128)(2,1)S(1)}, u32[]{:S(2)}, u32[]{:S(2)}) %collective-permute-start.41) | collective-permute-done | bytes 262176 | tf_op jit(solution)/shard_map/ppermute | solution.py:518
  237.7 7.3 collective-permute-done.42.refs_4_
  251.9 5.6 both_plain.5.refs_3_
  257.5 16.0 %attend_joint.1 = (bf16[2,5,2,64,512]{4,3,2,1,0:T(8,128)(2,1)S(1)}, bf16[4,8,320,320]{3,2,1,0:T(8,128)(2,1)S(1)}) custom-call(s32[5]{0:T(128)S(1)} %concatenate.16.refs_0_, bf16[8,9,64,64]{3,2,1,0:T(8,128)(2,1)S(1)} %squeeze.38.refs_6_.refs_1_, bf16[2,5,2,64,1536]{4,3,2,1,0:T(8,128)(2,1)S(1)} %bitcast.172, bf16[2,640,1536]{2,1,0:T(8,128)(2,1)S(1)} %both_plain.5.refs_3_), custom_call_target="tpu_custom_call" | custom-call | flops 1 | bytes 1 | tf_op jit(solution)/shard_map/attend_joint/pallas_call | solution.py:583
  273.5 3.2 copy-done.27
  288.1 3.6 collective-permute-start.54
  292.2 17.3 %both_gelu.3 = (bf16[2,640,2048]{2,1,0:T(8,128)(2,1)S(1)}, bf16[2,640,2048]{2,1,0:T(8,128)(2,1)S(1)}) custom-call(s32[5]{0:T(128)S(1)} %concatenate.16.refs_0_, bf16[320,1024]{1,0:T(8,128)(2,1)S(1)} %get-tuple-element.222.refs_1_, bf16[320,1024]{1,0:T(8,128)(2,1)S(1)} %get-tuple-element.223.refs_2_, bf16[320,1024]{1,0:T(8,128)(2,1)S(1)} %collective-permute-done.47.refs_3_, ...), custom_call_target="tpu_custom_call" | custom-call | flops 1 | bytes 1 | tf_op jit(solution)/shard_map/both_gelu/pallas_call | solution.py:583
  309.6 7.9 %collective-permute-done.49.refs_4_ = bf16[2,64,2048]{2,1,0:T(8,128)(2,1)S(1)} collective-permute-done((bf16[2,64,2048]{2,1,0:T(8,128)(2,1)S(1)}, bf16[2,64,2048]{2,1,0:T(8,128)(2,1)S(1)}, u32[]{:S(2)}, u32[]{:S(2)}) %collective-permute-start.49) | collective-permute-done | bytes 524320 | tf_op jit(solution)/shard_map/ppermute | solution.py:514
  318.5 4.2 other_rows.11
  326.9 4.1 forward_step.7
  341.5 7.8 %both_slope.2.refs_1_.refs_3_.refs_5_ = bf16[2,640,2048]{2,1,0:T(8,128)(2,1)S(1)} custom-call(s32[5]{0:T(128)S(1)} %concatenate.16.refs_0_, bf16[320,1024]{1,0:T(8,128)(2,1)S(1)} %get-tuple-element.231.refs_1_.refs_7_, bf16[320,1024]{1,0:T(8,128)(2,1)S(1)} %get-tuple-element.232.refs_2_, bf16[320,1024]{1,0:T(8,128)(2,1)S(1)} %collective-permute-done.55.refs_3_, ...), custom_call_target="tpu_custom_call" | custom-call | flops 1 | bytes 1 | tf_op jit(solution)/shard_map/both_slope/pallas_call | solution.py:583
  349.3 4.2 other_rows.12
  354.1 9.8 %weight_grad.6 = (bf16[4,64,2048]{2,1,0:T(8,128)(2,1)S(1)}, bf16[4,64,2048]{2,1,0:T(8,128)(2,1)S(1)}, bf16[4,64,2048]{2,1,0:T(8,128)(2,1)S(1)}, bf16[2,64,2048]{2,1,0:T(8,128)(2,1)}, bf16[2,64,2048]{2,1,0:T(8,128)(2,1)}) custom-call(s32[5]{0:T(128)S(1)} %concatenate.16.refs_0_, bf16[320,1024]{1,0:T(8,128)(2,1)S(1)} %get-tuple-element.231.refs_1_.refs_7_, ...), custom_call_target="tpu_custom_call" | custom-call | flops 1 | bytes 1 | tf_op jit(solution)/shard_map/weight_grad/pallas_call | solution.py:583
  367.2 6.3 backward_step.4
  374.1 9.2 %weight_grad.7 = (bf16[4,64,2048]{2,1,0:T(8,128)(2,1)S(1)}, bf16[4,64,2048]{2,1,0:T(8,128)(2,1)S(1)}, bf16[4,64,2048]{2,1,0:T(8,128)(2,1)S(1)}, bf16[2,64,2048]{2,1,0:T(8,128)(2,1)S(1)}, bf16[2,64,2048]{2,1,0:T(8,128)(2,1)S(1)}) custom-call(s32[5]{0:T(128)S(1)} %concatenate.16.refs_0_, bf16[320,1024]{1,0:T(8,128)(2,1)S(1)} %copy-done.84, ...), custom_call_target="tpu_custom_call" | custom-call | flops 1 | bytes 1 | tf_op jit(solution)/shard_map/weight_grad/pallas_call | solution.py:583
  395.4 18.7 %attend_back_joint.1 = (bf16[2,5,2,64,1536]{4,3,2,1,0:T(8,128)(2,1)S(1)}, f32[8,9,64,64]{3,2,1,0:T(8,128)S(1)}) custom-call(s32[5]{0:T(128)S(1)} %concatenate.16.refs_0_, bf16[2,5,2,64,1536]{4,3,2,1,0:T(8,128)(2,1)S(1)} %bitcast.173, bf16[2,5,2,64,512]{4,3,2,1,0:T(8,128)(2,1)S(1)} %bitcast.196, bf16[4,8,320,320]{3,2,1,0:T(8,128)(2,1)S(1)} %bitcast.206, ...), custom_call_target="tpu_custom_call" | custom-call | flops 1 | bytes 1 | tf_op jit(solution)/shard_map/attend_back_joint/pallas_call | solution.py:583
  414.2 3.5 other_rows.13
  418.4 10.5 %weight_grad.8 = (bf16[4,64,2048]{2,1,0:T(8,128)(2,1)S(1)}, bf16[4,64,2048]{2,1,0:T(8,128)(2,1)S(1)}, bf16[4,64,2048]{2,1,0:T(8,128)(2,1)S(1)}, bf16[2,64,2048]{2,1,0:T(8,128)(2,1)S(1)}, bf16[2,64,2048]{2,1,0:T(8,128)(2,1)S(1)}) custom-call(s32[5]{0:T(128)S(1)} %concatenate.16.refs_0_, bf16[320,1024]{1,0:T(8,128)(2,1)S(1)} %copy-done.56, ...), custom_call_target="tpu_custom_call" | custom-call | flops 1 | bytes 1 | tf_op jit(solution)/shard_map/weight_grad/pallas_call | solution.py:583
  429.0 3.5 scatter_step.9
  433.3 5.8 backward_step.5
  463.9 7.8 %both_slope.3.refs_1_.refs_3_.refs_5_ = bf16[2,640,2048]{2,1,0:T(8,128)(2,1)S(1)} custom-call(s32[5]{0:T(128)S(1)} %concatenate.16.refs_0_, bf16[320,1024]{1,0:T(8,128)(2,1)S(1)} %copy-done.64, bf16[320,1024]{1,0:T(8,128)(2,1)S(1)} %copy-done.67, bf16[320,1024]{1,0:T(8,128)(2,1)S(1)} %copy-done.70, bf16[320,1024]{1,0:T(8,128)(2,1)S(1)} %copy-done.73, ...), custom_call_target="tpu_custom_call" | custom-call | flops 1 | bytes 1 | tf_op jit(solution)/shard_map/both_slope/pallas_call | solution.py:583
  473.7 4.2 other_rows.14
  480.4 9.2 %weight_grad.9 = (bf16[4,64,2048]{2,1,0:T(8,128)(2,1)S(1)}, bf16[4,64,2048]{2,1,0:T(8,128)(2,1)S(1)}, bf16[4,64,2048]{2,1,0:T(8,128)(2,1)S(1)}, bf16[2,64,2048]{2,1,0:T(8,128)(2,1)S(1)}, bf16[2,64,2048]{2,1,0:T(8,128)(2,1)S(1)}) custom-call(s32[5]{0:T(128)S(1)} %concatenate.16.refs_0_, bf16[320,1024]{1,0:T(8,128)(2,1)S(1)} %copy-done.65, ...), custom_call_target="tpu_custom_call" | custom-call | flops 1 | bytes 1 | tf_op jit(solution)/shard_map/weight_grad/pallas_call | solution.py:583
  491.5 4.5 scatter_step.10
  498.4 6.4 backward_step.6
  509.5 9.2 %weight_grad.10 = (bf16[4,64,2048]{2,1,0:T(8,128)(2,1)S(1)}, bf16[4,64,2048]{2,1,0:T(8,128)(2,1)S(1)}, bf16[4,64,2048]{2,1,0:T(8,128)(2,1)S(1)}, bf16[2,64,2048]...) custom-call(s32[5]{0:T(128)S(1)} %concatenate.16.refs_0_, bf16[320,1024]{1,0:T(8,128)(2,1)S(1)} %copy-done.76, ...), custom_call_target="tpu_custom_call" | custom-call | flops 1 | bytes 1 | tf_op jit(solution)/shard_map/weight_grad/pallas_call | solution.py:583
  520.8 4.4 collective-permute-done.81.refs_10_
  525.2 7.2 collective-permute-done.82.refs_11_
  537.1 5.0 collective-permute-start.88
  544.2 18.1 %attend_back_spatial.1 = (bf16[2,5,2,64,1536]{4,3,2,1,0:T(8,128)(2,1)S(1)}, f32[8,9,64,64]{3,2,1,0:T(8,128)S(1)}) custom-call(s32[5]{0:T(128)S(1)} %concatenate.16.refs_0_, bf16[2,5,2,64,1536]{4,3,2,1,0:T(8,128)(2,1)S(1)} %bitcast.175, bf16[2,5,2,64,512]{4,3,2,1,0:T(8,128)(2,1)S(1)} %bitcast.195, bf16[5,8,256,256]{3,2,1,0:T(8,128)(2,1)S(1)} %bitcast.209, ...), custom_call_target="tpu_custom_call" | custom-call | flops 1 | bytes 1 | tf_op jit(solution)/shard_map/attend_back_spatial/pallas_call | solution.py:583
  562.3 3.5 other_rows.15
  565.9 10.5 %weight_grad.11 = (bf16[4,64,2048]{2,1,0:T(8,128)(2,1)S(1)}, bf16[4,64,2048]{2,1,0:T(8,128)(2,1)S(1)}, bf16[4,64,2048]{2,1,0:T(8,128)(2,1)S(1)}, bf16[2,64,2048]...) custom-call(s32[5]{0:T(128)S(1)} %concatenate.16.refs_0_, bf16[320,1024]{1,0:T(8,128)(2,1)S(1)} %copy-done.48, ...), custom_call_target="tpu_custom_call" | custom-call | flops 1 | bytes 1 | tf_op jit(solution)/shard_map/weight_grad/pallas_call | solution.py:583
  578.1 11.6 %collective-permute-done.87.refs_11_ = bf16[64,2048]{1,0:T(8,128)(2,1)S(1)} collective-permute-done((bf16[64,2048]{1,0:T(8,128)(2,1)S(1)}, bf16[64,2048]{1,0:T(8,128)(2,1)S(1)}, u32[]{:S(2)}, u32[]{:S(2)}) %collective-permute-start.87) | collective-permute-done | bytes 262176 | tf_op jit(solution)/shard_map/ppermute | solution.py:518
  589.7 3.6 scatter_step.12
  602.2 3.0 reshape_reshape.3
  614.4 4.6 backward_step.7
  624.0 5.7 all-to-all-start.1
  629.7 3.5 fusion.2
  640.6 3.9 scatter_step.13
  648.7 9.1 %collective-permute-done.100.refs_7_ = bf16[64,2048]{1,0:T(8,128)(2,1)S(1)} collective-permute-done((bf16[64,2048]{1,0:T(8,128)(2,1)S(1)}, bf16[64,2048]{1,0:T(8,128)(2,1)S(1)}, u32[]{:S(2)}, u32[]{:S(2)}) %collective-permute-start.100) | collective-permute-done | bytes 262176 | tf_op jit(solution)/shard_map/ppermute | solution.py:518
  660.0 7.3 collective-permute-done.99.refs_6_
  686.4 13.8 %collective-permute-done.109.refs_4_ = bf16[64,2048]{1,0:T(8,128)(2,1)S(1)} collective-permute-done((bf16[64,2048]{1,0:T(8,128)(2,1)S(1)}, bf16[64,2048]{1,0:T(8,128)(2,1)S(1)}, u32[]{:S(2)}, u32[]{:S(2)}) %collective-permute-start.109) | collective-permute-done | bytes 262176 | tf_op jit(solution)/shard_map/ppermute | solution.py:518
  701.1 15.1 %collective-permute-start.111 = (bf16[64,2048]{1,0:T(8,128)(2,1)S(1)}, bf16[64,2048]{1,0:T(8,128)(2,1)S(1)}, u32[]{:S(2)}, u32[]{:S(2)}) collective-permute-start(bf16[64,2048]{1,0:T(8,128)(2,1)S(1)} %scatter_step.15.refs_5_), channel_id=1, source_target_pairs={{1,2},{2,1},{5,6},{6,5},{9,10},{10,9},{13,14},{14,13},{17,18},{18,... | collective-permute-start | bytes 786440 | tf_op jit(solution)/shard_map/ppermute | solution.py:522
  720.2 3.6 collective-permute-start.101
  740.2 5.5 collective-permute-done.101
  (655 shorter events, 272.1 us)
Async XLA Ops:
  4.5 23.2 %collective-permute-start.1 = (bf16[16,9,225]{2,1,0:T(8,128)(2,1)}, bf16[16,9,225]{2,1,0:T(8,128)(2,1)}, u32[]{:S(2)}, u32[]{:S(2)}) collective-permute-start(bf16[16,9,225]{2,1,0:T(8,128)(2,1)} %pad_maximum_fusion.7), channel_id=1, source_target_pairs={{1,2},{2,1},{5,6},{6,5},{9,10},{10,9},{13,14},{14,13},{17,18},{18,... | collective-permute-start | bytes 194408 | tf_op jit(solution)/shard_map/ppermute | solution.py:522
  27.4 23.2 %collective-permute-start.7 = (bf16[64,2048]{1,0:T(8,128)(2,1)S(1)}, bf16[64,2048]{1,0:T(8,128)(2,1)}, u32[]{:S(2)}, u32[]{:S(2)}) collective-permute-start(bf16[64,2048]{1,0:T(8,128)(2,1)S(1)} %broadcast_select_fusion.5.refs_1_), channel_id=1, source_target_pairs={{0,24},{8,16},{16,8},{24,0},{1,25},{9,17},{17,9},{25,1},{2,26},{10... | collective-permute-start | bytes 786440 | tf_op jit(solution)/shard_map/ppermute | solution.py:518
  34.4 29.9 %collective-permute-start.3 = (bf16[64,10240]{1,0:T(8,128)(2,1)}, bf16[64,10240]{1,0:T(8,128)(2,1)}, u32[]{:S(2)}, u32[]{:S(2)}) collective-permute-start(bf16[64,10240]{1,0:T(8,128)(2,1)} %get-tuple-element.181.refs_1_), channel_id=1, source_target_pairs={{1,2},{2,1},{5,6},{6,5},{9,10},{10,9},{13,14},{14,13},{17,18},{18,... | collective-permute-start | bytes 3932168 | tf_op jit(solution)/shard_map/ppermute | solution.py:522
  38.6 40.8 %collective-permute-start.2 = (bf16[640,1024]{1,0:T(8,128)(2,1)}, bf16[640,1024]{1,0:T(8,128)(2,1)}, u32[]{:S(2)}, u32[]{:S(2)}) collective-permute-start(bf16[640,1024]{1,0:T(8,128)(2,1)} %get-tuple-element.180.refs_5_.refs_1_), channel_id=1, source_target_pairs={{1,2},{2,1},{5,6},{6,5},{9,10},{10,9},{13,14},{14,13},{17,18},{18,... | collective-permute-start | bytes 3932168 | tf_op jit(solution)/shard_map/ppermute | solution.py:522
  54.6 35.4 %collective-permute-start.10 = (bf16[4,64,2048]{2,1,0:T(8,128)(2,1)}, bf16[4,64,2048]{2,1,0:T(8,128)(2,1)S(1)}, u32[]{:S(2)}, u32[]{:S(2)}) collective-permute-start(bf16[4,64,2048]{2,1,0:T(8,128)(2,1)} %get-tuple-element.182.refs_3_.refs_1_), channel_id=1, source_target_pairs={{0,1},{1,0},{2,3},{3,2},{4,5},{5,4},{6,7},{7,6},{8,9},{9,8},{10,11... | collective-permute-start | bytes 3145736 | tf_op jit(solution)/shard_map/ppermute | solution.py:514
  55.6 34.4 %collective-permute-start.11 = (bf16[4,64,2048]{2,1,0:T(8,128)(2,1)}, bf16[4,64,2048]{2,1,0:T(8,128)(2,1)}, u32[]{:S(2)}, u32[]{:S(2)}) collective-permute-start(bf16[4,64,2048]{2,1,0:T(8,128)(2,1)} %get-tuple-element.186), channel_id=1, source_target_pairs={{0,4},{4,0},{1,5},{5,1},{2,6},{6,2},{3,7},{7,3},{8,12},{12,8},{9,1... | collective-permute-start | bytes 3145736 | tf_op jit(solution)/shard_map/ppermute | solution.py:514
  66.9 23.1 %collective-permute-start.12 = (bf16[64,2048]{1,0:T(8,128)(2,1)S(1)}, bf16[64,2048]{1,0:T(8,128)(2,1)S(1)}, u32[]{:S(2)}, u32[]{:S(2)}) collective-permute-start(bf16[64,2048]{1,0:T(8,128)(2,1)S(1)} %get-tuple-element.183.refs_4_.refs_1_), channel_id=1, source_target_pairs={{0,8},{8,0},{16,24},{24,16},{1,9},{9,1},{17,25},{25,17},{2,10},{10... | collective-permute-start | bytes 786440 | tf_op jit(solution)/shard_map/ppermute | solution.py:518
  67.0 23.0 %collective-permute-start.13 = (bf16[64,2048]{1,0:T(8,128)(2,1)S(1)}, bf16[64,2048]{1,0:T(8,128)(2,1)S(1)}, u32[]{:S(2)}, u32[]{:S(2)}) collective-permute-start(bf16[64,2048]{1,0:T(8,128)(2,1)S(1)} %get-tuple-element.183.refs_4_.refs_1_), channel_id=1, source_target_pairs={{0,16},{8,24},{16,0},{24,8},{1,17},{9,25},{17,1},{25,9},{2,18},{10... | collective-permute-start | bytes 786440 | tf_op jit(solution)/shard_map/ppermute | solution.py:518
  96.1 35.5 %collective-permute-start.15 = (bf16[6,64,2048]{2,1,0:T(8,128)(2,1)S(1)}, bf16[6,64,2048]{2,1,0:T(8,128)(2,1)S(1)}, u32[]{:S(2)}, u32[]{:S(2)}) collective-permute-start(bf16[6,64,2048]{2,1,0:T(8,128)(2,1)S(1)} %get-tuple-element.188.refs_7_.refs_1_), channel_id=1, source_target_pairs={{0,1},{1,0},{2,3},{3,2},{4,5},{5,4},{6,7},{7,6},{8,9},{9,8},{10,11... | collective-permute-start | bytes 4718600 | tf_op jit(solution)/shard_map/ppermute | solution.py:514
  96.2 35.4 %collective-permute-start.16 = (bf16[6,64,2048]{2,1,0:T(8,128)(2,1)S(1)}, bf16[6,64,2048]{2,1,0:T(8,128)(2,1)S(1)}, u32[]{:S(2)}, u32[]{:S(2)}) collective-permute-start(bf16[6,64,2048]{2,1,0:T(8,128)(2,1)S(1)} %get-tuple-element.189), channel_id=1, source_target_pairs={{0,4},{4,0},{1,5},{5,1},{2,6},{6,2},{3,7},{7,3},{8,12},{12,8},{9,1... | collective-permute-start | bytes 4718600 | tf_op jit(solution)/shard_map/ppermute | solution.py:514
  99.0 21.9 %collective-permute-start.19 = (bf16[64,2048]{1,0:T(8,128)(2,1)S(1)}, bf16[64,2048]{1,0:T(8,128)(2,1)S(1)}, u32[]{:S(2)}, u32[]{:S(2)}) collective-permute-start(bf16[64,2048]{1,0:T(8,128)(2,1)S(1)} %get-tuple-element.190.refs_1_), channel_id=1, source_target_pairs={{0,24},{8,16},{16,8},{24,0},{1,25},{9,17},{17,9},{25,1},{2,26},{10... | collective-permute-start | bytes 786440 | tf_op jit(solution)/shard_map/ppermute | solution.py:518
  132.8 35.7 %collective-permute-start.22 = (bf16[6,64,2048]{2,1,0:T(8,128)(2,1)S(1)}, bf16[6,64,2048]{2,1,0:T(8,128)(2,1)S(1)}, u32[]{:S(2)}, u32[]{:S(2)}) collective-permute-start(bf16[6,64,2048]{2,1,0:T(8,128)(2,1)S(1)} %get-tuple-element.191.refs_6_.refs_1_), channel_id=1, source_target_pairs={{0,1},{1,0},{2,3},{3,2},{4,5},{5,4},{6,7},{7,6},{8,9},{9,8},{10,11... | collective-permute-start | bytes 4718600 | tf_op jit(solution)/shard_map/ppermute | solution.py:514
  134.0 34.5 %collective-permute-start.23 = (bf16[6,64,2048]{2,1,0:T(8,128)(2,1)S(1)}, bf16[6,64,2048]{2,1,0:T(8,128)(2,1)S(1)}, u32[]{:S(2)}, u32[]{:S(2)}) collective-permute-start(bf16[6,64,2048]{2,1,0:T(8,128)(2,1)S(1)} %get-tuple-element.197), channel_id=1, source_target_pairs={{0,4},{4,0},{1,5},{5,1},{2,6},{6,2},{3,7},{7,3},{8,12},{12,8},{9,1... | collective-permute-start | bytes 4718600 | tf_op jit(solution)/shard_map/ppermute | solution.py:514
  136.6 30.7 %collective-permute-start.24 = (bf16[64,2048]{1,0:T(8,128)(2,1)S(1)}, bf16[64,2048]{1,0:T(8,128)(2,1)S(1)}, u32[]{:S(2)}, u32[]{:S(2)}) collective-permute-start(bf16[64,2048]{1,0:T(8,128)(2,1)S(1)} %get-tuple-element.198.refs_1_), channel_id=1, source_target_pairs={{0,8},{8,0},{16,24},{24,16},{1,9},{9,1},{17,25},{25,17},{2,10},{10... | collective-permute-start | bytes 786440 | tf_op jit(solution)/shard_map/ppermute | solution.py:518
  138.3 30.1 %collective-permute-start.25 = (bf16[64,2048]{1,0:T(8,128)(2,1)S(1)}, bf16[64,2048]{1,0:T(8,128)(2,1)S(1)}, u32[]{:S(2)}, u32[]{:S(2)}) collective-permute-start(bf16[64,2048]{1,0:T(8,128)(2,1)S(1)} %get-tuple-element.198.refs_1_), channel_id=1, source_target_pairs={{0,16},{8,24},{16,0},{24,8},{1,17},{9,25},{17,1},{25,9},{2,18},{10... | collective-permute-start | bytes 786440 | tf_op jit(solution)/shard_map/ppermute | solution.py:518
  139.5 29.0 %collective-permute-start.26 = (bf16[64,2048]{1,0:T(8,128)(2,1)S(1)}, bf16[64,2048]{1,0:T(8,128)(2,1)S(1)}, u32[]{:S(2)}, u32[]{:S(2)}) collective-permute-start(bf16[64,2048]{1,0:T(8,128)(2,1)S(1)} %get-tuple-element.198.refs_1_), channel_id=1, source_target_pairs={{0,24},{8,16},{16,8},{24,0},{1,25},{9,17},{17,9},{25,1},{2,26},{10... | collective-permute-start | bytes 786440 | tf_op jit(solution)/shard_map/ppermute | solution.py:518
  169.8 37.1 %collective-permute-start.29 = (bf16[6,64,2048]{2,1,0:T(8,128)(2,1)S(1)}, bf16[6,64,2048]{2,1,0:T(8,128)(2,1)S(1)}, u32[]{:S(2)}, u32[]{:S(2)}) collective-permute-start(bf16[6,64,2048]{2,1,0:T(8,128)(2,1)S(1)} %get-tuple-element.199.refs_6_.refs_1_), channel_id=1, source_target_pairs={{0,1},{1,0},{2,3},{3,2},{4,5},{5,4},{6,7},{7,6},{8,9},{9,8},{10,11... | collective-permute-start | bytes 4718600 | tf_op jit(solution)/shard_map/ppermute | solution.py:514
  170.8 36.1 %collective-permute-start.30 = (bf16[6,64,2048]{2,1,0:T(8,128)(2,1)S(1)}, bf16[6,64,2048]{2,1,0:T(8,128)(2,1)S(1)}, u32[]{:S(2)}, u32[]{:S(2)}) collective-permute-start(bf16[6,64,2048]{2,1,0:T(8,128)(2,1)S(1)} %get-tuple-element.204), channel_id=1, source_target_pairs={{0,4},{4,0},{1,5},{5,1},{2,6},{6,2},{3,7},{7,3},{8,12},{12,8},{9,1... | collective-permute-start | bytes 4718600 | tf_op jit(solution)/shard_map/ppermute | solution.py:514
  179.4 24.9 %collective-permute-start.31 = (bf16[64,2048]{1,0:T(8,128)(2,1)S(1)}, bf16[64,2048]{1,0:T(8,128)(2,1)S(1)}, u32[]{:S(2)}, u32[]{:S(2)}) collective-permute-start(bf16[64,2048]{1,0:T(8,128)(2,1)S(1)} %get-tuple-element.205.refs_1_), channel_id=1, source_target_pairs={{0,8},{8,0},{16,24},{24,16},{1,9},{9,1},{17,25},{25,17},{2,10},{10... | collective-permute-start | bytes 786440 | tf_op jit(solution)/shard_map/ppermute | solution.py:518
  181.1 23.3 %collective-permute-start.32 = (bf16[64,2048]{1,0:T(8,128)(2,1)S(1)}, bf16[64,2048]{1,0:T(8,128)(2,1)S(1)}, u32[]{:S(2)}, u32[]{:S(2)}) collective-permute-start(bf16[64,2048]{1,0:T(8,128)(2,1)S(1)} %get-tuple-element.205.refs_1_), channel_id=1, source_target_pairs={{0,16},{8,24},{16,0},{24,8},{1,17},{9,25},{17,1},{25,9},{2,18},{10... | collective-permute-start | bytes 786440 | tf_op jit(solution)/shard_map/ppermute | solution.py:518
  184.6 22.2 %collective-permute-start.33 = (bf16[64,2048]{1,0:T(8,128)(2,1)S(1)}, bf16[64,2048]{1,0:T(8,128)(2,1)S(1)}, u32[]{:S(2)}, u32[]{:S(2)}) collective-permute-start(bf16[64,2048]{1,0:T(8,128)(2,1)S(1)} %get-tuple-element.205.refs_1_), channel_id=1, source_target_pairs={{0,24},{8,16},{16,8},{24,0},{1,25},{9,17},{17,9},{25,1},{2,26},{10... | collective-permute-start | bytes 786440 | tf_op jit(solution)/shard_map/ppermute | solution.py:518
  208.1 36.8 %collective-permute-start.38 = (bf16[6,64,2048]{2,1,0:T(8,128)(2,1)S(1)}, bf16[6,64,2048]{2,1,0:T(8,128)(2,1)S(1)}, u32[]{:S(2)}, u32[]{:S(2)}) collective-permute-start(bf16[6,64,2048]{2,1,0:T(8,128)(2,1)S(1)} %get-tuple-element.206.refs_6_.refs_1_), channel_id=1, source_target_pairs={{0,1},{1,0},{2,3},{3,2},{4,5},{5,4},{6,7},{7,6},{8,9},{9,8},{10,11... | collective-permute-start | bytes 4718600 | tf_op jit(solution)/shard_map/ppermute | solution.py:514
  209.0 36.0 %collective-permute-start.39 = (bf16[6,64,2048]{2,1,0:T(8,128)(2,1)S(1)}, bf16[6,64,2048]{2,1,0:T(8,128)(2,1)S(1)}, u32[]{:S(2)}, u32[]{:S(2)}) collective-permute-start(bf16[6,64,2048]{2,1,0:T(8,128)(2,1)S(1)} %get-tuple-element.211), channel_id=1, source_target_pairs={{0,4},{4,0},{1,5},{5,1},{2,6},{6,2},{3,7},{7,3},{8,12},{12,8},{9,1... | collective-permute-start | bytes 4718600 | tf_op jit(solution)/shard_map/ppermute | solution.py:514
  219.2 18.5 %collective-permute-start.41 = (bf16[64,2048]{1,0:T(8,128)(2,1)S(1)}, bf16[64,2048]{1,0:T(8,128)(2,1)S(1)}, u32[]{:S(2)}, u32[]{:S(2)}) collective-permute-start(bf16[64,2048]{1,0:T(8,128)(2,1)S(1)} %get-tuple-element.212.refs_1_), channel_id=1, source_target_pairs={{0,16},{8,24},{16,0},{24,8},{1,17},{9,25},{17,1},{25,9},{2,18},{10... | collective-permute-start | bytes 786440 | tf_op jit(solution)/shard_map/ppermute | solution.py:518
  221.1 23.9 %collective-permute-start.42 = (bf16[64,2048]{1,0:T(8,128)(2,1)S(1)}, bf16[64,2048]{1,0:T(8,128)(2,1)S(1)}, u32[]{:S(2)}, u32[]{:S(2)}) collective-permute-start(bf16[64,2048]{1,0:T(8,128)(2,1)S(1)} %get-tuple-element.212.refs_1_), channel_id=1, source_target_pairs={{0,24},{8,16},{16,8},{24,0},{1,25},{9,17},{17,9},{25,1},{2,26},{10... | collective-permute-start | bytes 786440 | tf_op jit(solution)/shard_map/ppermute | solution.py:518
  246.2 34.8 %collective-permute-start.45 = (bf16[6,64,2048]{2,1,0:T(8,128)(2,1)S(1)}, bf16[6,64,2048]{2,1,0:T(8,128)(2,1)S(1)}, u32[]{:S(2)}, u32[]{:S(2)}) collective-permute-start(bf16[6,64,2048]{2,1,0:T(8,128)(2,1)S(1)} %get-tuple-element.214.refs_6_.refs_1_), channel_id=1, source_target_pairs={{0,1},{1,0},{2,3},{3,2},{4,5},{5,4},{6,7},{7,6},{8,9},{9,8},{10,11... | collective-permute-start | bytes 4718600 | tf_op jit(solution)/shard_map/ppermute | solution.py:514
  246.4 34.6 %collective-permute-start.46 = (bf16[6,64,2048]{2,1,0:T(8,128)(2,1)S(1)}, bf16[6,64,2048]{2,1,0:T(8,128)(2,1)S(1)}, u32[]{:S(2)}, u32[]{:S(2)}) collective-permute-start(bf16[6,64,2048]{2,1,0:T(8,128)(2,1)S(1)} %get-tuple-element.220), channel_id=1, source_target_pairs={{0,4},{4,0},{1,5},{5,1},{2,6},{6,2},{3,7},{7,3},{8,12},{12,8},{9,1... | collective-permute-start | bytes 4718600 | tf_op jit(solution)/shard_map/ppermute | solution.py:514
  288.1 45.6 %collective-permute-start.54 = (bf16[640,1024]{1,0:T(8,128)(2,1)S(1)}, bf16[640,1024]{1,0:T(8,128)(2,1)S(1)}, u32[]{:S(2)}, u32[]{:S(2)}) collective-permute-start(bf16[640,1024]{1,0:T(8,128)(2,1)S(1)} %bitcast.215), channel_id=1, source_target_pairs={{1,2},{2,1},{5,6},{6,5},{9,10},{10,9},{13,14},{14,13},{17,18},{18,... | collective-permute-start | bytes 3932168 | tf_op jit(solution)/shard_map/ppermute | solution.py:522
  291.8 25.8 %collective-permute-start.49 = (bf16[2,64,2048]{2,1,0:T(8,128)(2,1)S(1)}, bf16[2,64,2048]{2,1,0:T(8,128)(2,1)S(1)}, u32[]{:S(2)}, u32[]{:S(2)}) collective-permute-start(bf16[2,64,2048]{2,1,0:T(8,128)(2,1)S(1)} %get-tuple-element.221.refs_6_), channel_id=1, source_target_pairs={{0,1},{1,0},{2,3},{3,2},{4,5},{5,4},{6,7},{7,6},{8,9},{9,8},{10,11... | collective-permute-start | bytes 1572872 | tf_op jit(solution)/shard_map/ppermute | solution.py:514
  291.8 25.7 %collective-permute-start.50 = (bf16[2,64,2048]{2,1,0:T(8,128)(2,1)S(1)}, bf16[2,64,2048]{2,1,0:T(8,128)(2,1)S(1)}, u32[]{:S(2)}, u32[]{:S(2)}) collective-permute-start(bf16[2,64,2048]{2,1,0:T(8,128)(2,1)S(1)} %get-tuple-element.226), channel_id=1, source_target_pairs={{0,4},{4,0},{1,5},{5,1},{2,6},{6,2},{3,7},{7,3},{8,12},{12,8},{9,1... | collective-permute-start | bytes 1572872 | tf_op jit(solution)/shard_map/ppermute | solution.py:514
  331.0 34.7 %collective-permute-start.53 = (bf16[640,1024]{1,0:T(8,128)(2,1)S(1)}, bf16[640,1024]{1,0:T(8,128)(2,1)}, u32[]{:S(2)}, u32[]{:S(2)}) collective-permute-start(bf16[640,1024]{1,0:T(8,128)(2,1)S(1)} %get-tuple-element.229.refs_4_), channel_id=1, source_target_pairs={{1,2},{2,1},{5,6},{6,5},{9,10},{10,9},{13,14},{14,13},{17,18},{18,... | collective-permute-start | bytes 3932168 | tf_op jit(solution)/shard_map/ppermute | solution.py:522
  363.9 19.4 %collective-permute-start.61 = (bf16[2,64,2048]{2,1,0:T(8,128)(2,1)}, bf16[2,64,2048]{2,1,0:T(8,128)(2,1)S(1)}, u32[]{:S(2)}, u32[]{:S(2)}) collective-permute-start(bf16[2,64,2048]{2,1,0:T(8,128)(2,1)} %get-tuple-element.247), channel_id=1, source_target_pairs={{0,1},{1,0},{2,3},{3,2},{4,5},{5,4},{6,7},{7,6},{8,9},{9,8},{10,11... | collective-permute-start | bytes 1572872 | tf_op jit(solution)/shard_map/ppermute | solution.py:514
  364.6 18.8 %collective-permute-start.62 = (bf16[2,64,2048]{2,1,0:T(8,128)(2,1)}, bf16[2,64,2048]{2,1,0:T(8,128)(2,1)S(1)}, u32[]{:S(2)}, u32[]{:S(2)}) collective-permute-start(bf16[2,64,2048]{2,1,0:T(8,128)(2,1)} %get-tuple-element.248), channel_id=1, source_target_pairs={{0,4},{4,0},{1,5},{5,1},{2,6},{6,2},{3,7},{7,3},{8,12},{12,8},{9,1... | collective-permute-start | bytes 1572872 | tf_op jit(solution)/shard_map/ppermute | solution.py:514
  388.1 40.9 %collective-permute-start.65 = (bf16[6,64,2048]{2,1,0:T(8,128)(2,1)S(1)}, bf16[6,64,2048]{2,1,0:T(8,128)(2,1)S(1)}, u32[]{:S(2)}, u32[]{:S(2)}) collective-permute-start(bf16[6,64,2048]{2,1,0:T(8,128)(2,1)S(1)} %get-tuple-element.250.refs_6_), channel_id=1, source_target_pairs={{0,1},{1,0},{2,3},{3,2},{4,5},{5,4},{6,7},{7,6},{8,9},{9,8},{10,11... | collective-permute-start | bytes 4718600 | tf_op jit(solution)/shard_map/ppermute | solution.py:514
  388.2 40.8 %collective-permute-start.66 = (bf16[6,64,2048]{2,1,0:T(8,128)(2,1)}, bf16[6,64,2048]{2,1,0:T(8,128)(2,1)S(1)}, u32[]{:S(2)}, u32[]{:S(2)}) collective-permute-start(bf16[6,64,2048]{2,1,0:T(8,128)(2,1)} %get-tuple-element.262), channel_id=1, source_target_pairs={{0,4},{4,0},{1,5},{5,1},{2,6},{6,2},{3,7},{7,3},{8,12},{12,8},{9,1... | collective-permute-start | bytes 4718600 | tf_op jit(solution)/shard_map/ppermute | solution.py:514
  443.4 48.0 %collective-permute-start.71 = (bf16[6,64,2048]{2,1,0:T(8,128)(2,1)}, bf16[6,64,2048]{2,1,0:T(8,128)(2,1)}, u32[]{:S(2)}, u32[]{:S(2)}) collective-permute-start(bf16[6,64,2048]{2,1,0:T(8,128)(2,1)} %get-tuple-element.264.refs_10_), channel_id=1, source_target_pairs={{0,1},{1,0},{2,3},{3,2},{4,5},{5,4},{6,7},{7,6},{8,9},{9,8},{10,11... | collective-permute-start | bytes 4718600 | tf_op jit(solution)/shard_map/ppermute | solution.py:514
  443.4 48.0 %collective-permute-start.72 = (bf16[6,64,2048]{2,1,0:T(8,128)(2,1)}, bf16[6,64,2048]{2,1,0:T(8,128)(2,1)}, u32[]{:S(2)}, u32[]{:S(2)}) collective-permute-start(bf16[6,64,2048]{2,1,0:T(8,128)(2,1)} %get-tuple-element.278), channel_id=1, source_target_pairs={{0,4},{4,0},{1,5},{5,1},{2,6},{6,2},{3,7},{7,3},{8,12},{12,8},{9,1... | collective-permute-start | bytes 4718600 | tf_op jit(solution)/shard_map/ppermute | solution.py:514
  444.2 45.4 %collective-permute-start.73 = (bf16[64,2048]{1,0:T(8,128)(2,1)}, bf16[64,2048]{1,0:T(8,128)(2,1)}, u32[]{:S(2)}, u32[]{:S(2)}) collective-permute-start(bf16[64,2048]{1,0:T(8,128)(2,1)} %get-tuple-element.280), channel_id=1, source_target_pairs={{0,8},{8,0},{16,24},{24,16},{1,9},{9,1},{17,25},{25,17},{2,10},{10... | collective-permute-start | bytes 786440 | tf_op jit(solution)/shard_map/ppermute | solution.py:518
  445.1 46.2 %collective-permute-start.74 = (bf16[64,2048]{1,0:T(8,128)(2,1)}, bf16[64,2048]{1,0:T(8,128)(2,1)}, u32[]{:S(2)}, u32[]{:S(2)}) collective-permute-start(bf16[64,2048]{1,0:T(8,128)(2,1)} %get-tuple-element.281), channel_id=1, source_target_pairs={{0,16},{8,24},{16,0},{24,8},{1,17},{9,25},{17,1},{25,9},{2,18},{10... | collective-permute-start | bytes 786440 | tf_op jit(solution)/shard_map/ppermute | solution.py:518
  447.9 43.4 %collective-permute-start.75 = (bf16[64,2048]{1,0:T(8,128)(2,1)}, bf16[64,2048]{1,0:T(8,128)(2,1)}, u32[]{:S(2)}, u32[]{:S(2)}) collective-permute-start(bf16[64,2048]{1,0:T(8,128)(2,1)} %get-tuple-element.282), channel_id=1, source_target_pairs={{0,24},{8,16},{16,8},{24,0},{1,25},{9,17},{17,9},{25,1},{2,26},{10... | collective-permute-start | bytes 786440 | tf_op jit(solution)/shard_map/ppermute | solution.py:518
  495.9 36.5 %collective-permute-start.78 = (bf16[6,64,2048]{2,1,0:T(8,128)(2,1)S(1)}, bf16[6,64,2048]{2,1,0:T(8,128)(2,1)S(1)}, u32[]{:S(2)}, u32[]{:S(2)}) collective-permute-start(bf16[6,64,2048]{2,1,0:T(8,128)(2,1)S(1)} %get-tuple-element.285.refs_10_), channel_id=1, source_target_pairs={{0,1},{1,0},{2,3},{3,2},{4,5},{5,4},{6,7},{7,6},{8,9},{9,8},{10,11... | collective-permute-start | bytes 4718600 | tf_op jit(solution)/shard_map/ppermute | solution.py:514
  497.1 35.3 %collective-permute-start.79 = (bf16[6,64,2048]{2,1,0:T(8,128)(2,1)S(1)}, bf16[6,64,2048]{2,1,0:T(8,128)(2,1)S(1)}, u32[]{:S(2)}, u32[]{:S(2)}) collective-permute-start(bf16[6,64,2048]{2,1,0:T(8,128)(2,1)S(1)} %get-tuple-element.296), channel_id=1, source_target_pairs={{0,4},{4,0},{1,5},{5,1},{2,6},{6,2},{3,7},{7,3},{8,12},{12,8},{9,1... | collective-permute-start | bytes 4718600 | tf_op jit(solution)/shard_map/ppermute | solution.py:514
  508.8 23.6 %collective-permute-start.82 = (bf16[64,2048]{1,0:T(8,128)(2,1)S(1)}, bf16[64,2048]{1,0:T(8,128)(2,1)S(1)}, u32[]{:S(2)}, u32[]{:S(2)}) collective-permute-start(bf16[64,2048]{1,0:T(8,128)(2,1)S(1)} %get-tuple-element.300), channel_id=1, source_target_pairs={{0,24},{8,16},{16,8},{24,0},{1,25},{9,17},{17,9},{25,1},{2,26},{10... | collective-permute-start | bytes 786440 | tf_op jit(solution)/shard_map/ppermute | solution.py:518
  534.9 54.7 %collective-permute-start.83 = (bf16[6,64,2048]{2,1,0:T(8,128)(2,1)S(1)}, bf16[6,64,2048]{2,1,0:T(8,128)(2,1)S(1)}, u32[]{:S(2)}, u32[]{:S(2)}) collective-permute-start(bf16[6,64,2048]{2,1,0:T(8,128)(2,1)S(1)} %get-tuple-element.302.refs_3_), channel_id=1, source_target_pairs={{0,1},{1,0},{2,3},{3,2},{4,5},{5,4},{6,7},{7,6},{8,9},{9,8},{10,11... | collective-permute-start | bytes 4718600 | tf_op jit(solution)/shard_map/ppermute | solution.py:514
  535.3 54.4 %collective-permute-start.84 = (bf16[6,64,2048]{2,1,0:T(8,128)(2,1)S(1)}, bf16[6,64,2048]{2,1,0:T(8,128)(2,1)S(1)}, u32[]{:S(2)}, u32[]{:S(2)}) collective-permute-start(bf16[6,64,2048]{2,1,0:T(8,128)(2,1)S(1)} %get-tuple-element.309), channel_id=1, source_target_pairs={{0,4},{4,0},{1,5},{5,1},{2,6},{6,2},{3,7},{7,3},{8,12},{12,8},{9,1... | collective-permute-start | bytes 4718600 | tf_op jit(solution)/shard_map/ppermute | solution.py:514
  537.1 40.2 %collective-permute-start.88 = (bf16[64,4096]{1,0:T(8,128)(2,1)S(1)}, bf16[64,4096]{1,0:T(8,128)(2,1)S(1)}, u32[]{:S(2)}, u32[]{:S(2)}) collective-permute-start(bf16[64,4096]{1,0:T(8,128)(2,1)S(1)} %join_pieces.2.refs_4_), channel_id=1, source_target_pairs={{1,2},{2,1},{5,6},{6,5},{9,10},{10,9},{13,14},{14,13},{17,18},{18,... | collective-permute-start | bytes 1572872 | tf_op jit(solution)/shard_map/ppermute | solution.py:522
  542.1 34.4 %collective-permute-start.85 = (bf16[64,2048]{1,0:T(8,128)(2,1)S(1)}, bf16[64,2048]{1,0:T(8,128)(2,1)S(1)}, u32[]{:S(2)}, u32[]{:S(2)}) collective-permute-start(bf16[64,2048]{1,0:T(8,128)(2,1)S(1)} %get-tuple-element.311), channel_id=1, source_target_pairs={{0,8},{8,0},{16,24},{24,16},{1,9},{9,1},{17,25},{25,17},{2,10},{10... | collective-permute-start | bytes 786440 | tf_op jit(solution)/shard_map/ppermute | solution.py:518
  542.8 33.8 %collective-permute-start.86 = (bf16[64,2048]{1,0:T(8,128)(2,1)S(1)}, bf16[64,2048]{1,0:T(8,128)(2,1)S(1)}, u32[]{:S(2)}, u32[]{:S(2)}) collective-permute-start(bf16[64,2048]{1,0:T(8,128)(2,1)S(1)} %get-tuple-element.312), channel_id=1, source_target_pairs={{0,16},{8,24},{16,0},{24,8},{1,17},{9,25},{17,1},{25,9},{2,18},{10... | collective-permute-start | bytes 786440 | tf_op jit(solution)/shard_map/ppermute | solution.py:518
  576.5 19.7 %collective-permute-start.94 = (bf16[320,1024]{1,0:T(8,128)(2,1)S(1)}, bf16[320,1024]{1,0:T(8,128)(2,1)S(1)}, u32[]{:S(2)}, u32[]{:S(2)}) collective-permute-start(bf16[320,1024]{1,0:T(8,128)(2,1)S(1)} %get-tuple-element.304.refs_11_), channel_id=1, source_target_pairs={{0,2},{2,0},{1,3},{3,1},{4,6},{6,4},{5,7},{7,5},{8,10},{10,8},{9,1... | collective-permute-start | bytes 1966088 | tf_op jit(solution)/shard_map/ppermute | solution.py:514
  577.3 21.5 %collective-permute-start.95 = (bf16[320,1024]{1,0:T(8,128)(2,1)S(1)}, bf16[320,1024]{1,0:T(8,128)(2,1)S(1)}, u32[]{:S(2)}, u32[]{:S(2)}) collective-permute-start(bf16[320,1024]{1,0:T(8,128)(2,1)S(1)} %get-tuple-element.328), channel_id=1, source_target_pairs={{0,2},{2,0},{1,3},{3,1},{4,6},{6,4},{5,7},{7,5},{8,10},{10,8},{9,1... | collective-permute-start | bytes 1966088 | tf_op jit(solution)/shard_map/ppermute | solution.py:514
  594.8 42.0 %collective-permute-start.89 = (bf16[6,64,2048]{2,1,0:T(8,128)(2,1)}, bf16[6,64,2048]{2,1,0:T(8,128)(2,1)}, u32[]{:S(2)}, u32[]{:S(2)}) collective-permute-start(bf16[6,64,2048]{2,1,0:T(8,128)(2,1)} %get-tuple-element.318.refs_9_), channel_id=1, source_target_pairs={{0,1},{1,0},{2,3},{3,2},{4,5},{5,4},{6,7},{7,6},{8,9},{9,8},{10,11... | collective-permute-start | bytes 4718600 | tf_op jit(solution)/shard_map/ppermute | solution.py:514
  595.9 41.0 %collective-permute-start.90 = (bf16[6,64,2048]{2,1,0:T(8,128)(2,1)}, bf16[6,64,2048]{2,1,0:T(8,128)(2,1)}, u32[]{:S(2)}, u32[]{:S(2)}) collective-permute-start(bf16[6,64,2048]{2,1,0:T(8,128)(2,1)} %get-tuple-element.319), channel_id=1, source_target_pairs={{0,4},{4,0},{1,5},{5,1},{2,6},{6,2},{3,7},{7,3},{8,12},{12,8},{9,1... | collective-permute-start | bytes 4718600 | tf_op jit(solution)/shard_map/ppermute | solution.py:514
  596.1 22.9 %collective-permute-start.91 = (bf16[64,2048]{1,0:T(8,128)(2,1)}, bf16[64,2048]{1,0:T(8,128)(2,1)}, u32[]{:S(2)}, u32[]{:S(2)}) collective-permute-start(bf16[64,2048]{1,0:T(8,128)(2,1)} %get-tuple-element.321), channel_id=1, source_target_pairs={{0,8},{8,0},{16,24},{24,16},{1,9},{9,1},{17,25},{25,17},{2,10},{10... | collective-permute-start | bytes 786440 | tf_op jit(solution)/shard_map/ppermute | solution.py:518
  597.0 22.0 %collective-permute-start.92 = (bf16[64,2048]{1,0:T(8,128)(2,1)}, bf16[64,2048]{1,0:T(8,128)(2,1)}, u32[]{:S(2)}, u32[]{:S(2)}) collective-permute-start(bf16[64,2048]{1,0:T(8,128)(2,1)} %get-tuple-element.322), channel_id=1, source_target_pairs={{0,16},{8,24},{16,0},{24,8},{1,17},{9,25},{17,1},{25,9},{2,18},{10... | collective-permute-start | bytes 786440 | tf_op jit(solution)/shard_map/ppermute | solution.py:518
  599.7 21.9 %collective-permute-start.93 = (bf16[64,2048]{1,0:T(8,128)(2,1)}, bf16[64,2048]{1,0:T(8,128)(2,1)}, u32[]{:S(2)}, u32[]{:S(2)}) collective-permute-start(bf16[64,2048]{1,0:T(8,128)(2,1)} %get-tuple-element.323), channel_id=1, source_target_pairs={{0,24},{8,16},{16,8},{24,0},{1,25},{9,17},{17,9},{25,1},{2,26},{10... | collective-permute-start | bytes 786440 | tf_op jit(solution)/shard_map/ppermute | solution.py:518
  644.6 24.5 %collective-permute-start.96 = (bf16[4,64,2048]{2,1,0:T(8,128)(2,1)S(1)}, bf16[4,64,2048]{2,1,0:T(8,128)(2,1)S(1)}, u32[]{:S(2)}, u32[]{:S(2)}) collective-permute-start(bf16[4,64,2048]{2,1,0:T(8,128)(2,1)S(1)} %get-tuple-element.335.refs_8_), channel_id=1, source_target_pairs={{0,1},{1,0},{2,3},{3,2},{4,5},{5,4},{6,7},{7,6},{8,9},{9,8},{10,11... | collective-permute-start | bytes 3145736 | tf_op jit(solution)/shard_map/ppermute | solution.py:514
  644.9 24.2 %collective-permute-start.97 = (bf16[4,64,2048]{2,1,0:T(8,128)(2,1)S(1)}, bf16[4,64,2048]{2,1,0:T(8,128)(2,1)S(1)}, u32[]{:S(2)}, u32[]{:S(2)}) collective-permute-start(bf16[4,64,2048]{2,1,0:T(8,128)(2,1)S(1)} %get-tuple-element.336), channel_id=1, source_target_pairs={{0,4},{4,0},{1,5},{5,1},{2,6},{6,2},{3,7},{7,3},{8,12},{12,8},{9,1... | collective-permute-start | bytes 3145736 | tf_op jit(solution)/shard_map/ppermute | solution.py:514
  647.9 19.4 %collective-permute-start.99 = (bf16[64,2048]{1,0:T(8,128)(2,1)S(1)}, bf16[64,2048]{1,0:T(8,128)(2,1)S(1)}, u32[]{:S(2)}, u32[]{:S(2)}) collective-permute-start(bf16[64,2048]{1,0:T(8,128)(2,1)S(1)} %get-tuple-element.339), channel_id=1, source_target_pairs={{0,16},{8,24},{16,0},{24,8},{1,17},{9,25},{17,1},{25,9},{2,18},{10... | collective-permute-start | bytes 786440 | tf_op jit(solution)/shard_map/ppermute | solution.py:518
  675.9 24.3 %collective-permute-start.109 = (bf16[64,2048]{1,0:T(8,128)(2,1)S(1)}, bf16[64,2048]{1,0:T(8,128)(2,1)S(1)}, u32[]{:S(2)}, u32[]{:S(2)}) collective-permute-start(bf16[64,2048]{1,0:T(8,128)(2,1)S(1)} %get-tuple-element.347), channel_id=1, source_target_pairs={{0,24},{8,16},{16,8},{24,0},{1,25},{9,17},{17,9},{25,1},{2,26},{10... | collective-permute-start | bytes 786440 | tf_op jit(solution)/shard_map/ppermute | solution.py:518
  680.5 39.7 %collective-permute-start.104 = (f32[208,256]{1,0:T(8,128)S(1)}, f32[208,256]{1,0:T(8,128)S(1)}, u32[]{:S(2)}, u32[]{:S(2)}) collective-permute-start(f32[208,256]{1,0:T(8,128)S(1)} %add_all.4.refs_5_.refs_1_), channel_id=1, source_target_pairs={{0,8},{8,0},{16,24},{24,16},{1,9},{9,1},{17,25},{25,17},{2,10},{10... | collective-permute-start | bytes 638984 | tf_op jit(solution)/shard_map/ppermute | solution.py:518
  681.5 42.4 %collective-permute-start.105 = (f32[208,256]{1,0:T(8,128)S(1)}, f32[208,256]{1,0:T(8,128)S(1)}, u32[]{:S(2)}, u32[]{:S(2)}) collective-permute-start(f32[208,256]{1,0:T(8,128)S(1)} %add_all.4.refs_5_.refs_1_), channel_id=1, source_target_pairs={{0,16},{8,24},{16,0},{24,8},{1,17},{9,25},{17,1},{25,9},{2,18},{10... | collective-permute-start | bytes 638984 | tf_op jit(solution)/shard_map/ppermute | solution.py:518
  683.8 40.1 %collective-permute-start.106 = (f32[208,256]{1,0:T(8,128)S(1)}, f32[208,256]{1,0:T(8,128)S(1)}, u32[]{:S(2)}, u32[]{:S(2)}) collective-permute-start(f32[208,256]{1,0:T(8,128)S(1)} %add_all.4.refs_5_.refs_1_), channel_id=1, source_target_pairs={{0,24},{8,16},{16,8},{24,0},{1,25},{9,17},{17,9},{25,1},{2,26},{10... | collective-permute-start | bytes 638984 | tf_op jit(solution)/shard_map/ppermute | solution.py:518
  701.1 23.4 %collective-permute-start.111 = (bf16[64,2048]{1,0:T(8,128)(2,1)S(1)}, bf16[64,2048]{1,0:T(8,128)(2,1)S(1)}, u32[]{:S(2)}, u32[]{:S(2)}) collective-permute-start(bf16[64,2048]{1,0:T(8,128)(2,1)S(1)} %scatter_step.15.refs_5_), channel_id=1, source_target_pairs={{1,2},{2,1},{5,6},{6,5},{9,10},{10,9},{13,14},{14,13},{17,18},{18,... | collective-permute-start | bytes 786440 | tf_op jit(solution)/shard_map/ppermute | solution.py:522
  720.2 25.5 %collective-permute-start.101 = (bf16[640,1024]{1,0:T(8,128)(2,1)}, bf16[640,1024]{1,0:T(8,128)(2,1)}, u32[]{:S(2)}, u32[]{:S(2)}) collective-permute-start(bf16[640,1024]{1,0:T(8,128)(2,1)} %get-tuple-element.343), channel_id=1, source_target_pairs={{1,2},{2,1},{5,6},{6,5},{9,10},{10,9},{13,14},{14,13},{17,18},{18,... | collective-permute-start | bytes 3932168 | tf_op jit(solution)/shard_map/ppermute | solution.py:522
  (217 other events, 1926.9 us)

commit v4 on v3

--- a/solution.py
+++ b/solution.py
@@ -569,7 +569,7 @@
     def wait(self, *values):
         self.pending += values
 
-    def run(self, name, kernel, args, in_specs, outs, out_specs, grid=(1,), scratch=(), extra=4, waits=()):
+    def run(self, name, kernel, args, in_specs, outs, out_specs, grid=(1,), scratch=(), extra=3, waits=()):
         count = len(args)
         unread = self.last + self.pending + list(waits)
         self.pending = []
@@ -598,19 +598,30 @@
         return results
 
 
-def pack_arguments(chain, rows_in, up, down, qkv, out):
-    def kernel(info, rows_from, up_in, down_in, qkv_in, out_in, rows_to, packed):
-        rows_to[...] = rows_from[...]
+def pack_arguments(chain, up, down, qkv, out):
+    def kernel(info, up_in, down_in, qkv_in, out_in, packed):
         start = 0
         for part in (up_in[0], down_in[0], qkv_in[1], out_in[1], up_in[1], down_in[1]):
             packed[:, start : start + part.shape[1]] = part
             start += part.shape[1]
 
-    args = [rows_in, up, down, qkv, out]
-    outs = [shape_of(rows_in.shape), shape_of((up.shape[1], 5 * PIECE))]
-    return chain.run(
-        "pack_arguments", kernel, args, [whole(v) for v in args], outs, [whole(v) for v in outs]
-    )
+    args = [up, down, qkv, out]
+    result = shape_of((up.shape[1], 5 * PIECE))
+    (packed,) = chain.run(
+        "pack_arguments", kernel, args, [whole(v) for v in args], [result], [whole(result)]
+    )
+    return packed
+
+
+def copy_rows(chain, values):
+    def kernel(info, source, result):
+        result[...] = source[...]
+
+    spec = pl.BlockSpec((ROW_TILE, values.shape[1]), lambda i, info: (i, 0))
+    (result,) = chain.run(
+        "copy_rows", kernel, [values], [spec], [shape_of(values.shape)], [spec], grid=(2,)
+    )
+    return result
 
 
 def cut_kernel(info, packed, traded, *outs):
@@ -826,7 +837,7 @@
                 grid=(PIECE // GRAD_TILE,),
                 scratch=[pltpu.VMEM((features, GRAD_TILE), low)]
                 + [pltpu.VMEM((features, 4 * rows), low)] * pairs,
-                extra=4,
+                extra=3,
             )
         )
         if len(self.parts) == 1:
@@ -1411,7 +1422,7 @@
         [window_specs(is_joint, frames, 3 * width), whole(sums)],
         grid=grid,
         scratch=[pltpu.VMEM((heads, cells, cells), full)],
-        extra=6,
+        extra=5,
     )
 
 
@@ -1503,10 +1514,8 @@
     windowed = lambda values: values.reshape(2, frames, 2, 64, values.shape[-1])
 
     chain.wait(own_mod, parts)
-    latent_rows, packed = pack_arguments(
-        chain, rearranged(latents), up_weight, down_rows, qkv_rows, out_rows
-    )
-    traded_rows, traded = swap_only(latent_rows), swap_only(packed)
+    packed = pack_arguments(chain, up_weight, down_rows, qkv_rows, out_rows)
+    traded = swap_only(packed)
     gather = Gather(chain, [first_shard] + [None] * 5)
     gather.over_z(0)
     gather.step()
@@ -1520,13 +1529,15 @@
         [whole(a) for a in cuts],
     )
     gather.over_z(1)
+    latent_rows = copy_rows(chain, rearranged(latents))
+    traded_rows = swap_only(latent_rows)
+    gather.step()
+    gather.over_z(2)
     chain.wait(*bias_blocks)
     latent_rows, normed_0, inverse_0, moved_0 = first_norm(
         chain, latent_rows, traded_rows, rows_of((0, 0), (0, 1))
     )
     other_0 = flip_rows(moved_0)
-    gather.step()
-    gather.over_z(2)
     gather.step()
     gather.over_z(3)
     qkv_0, out_0 = gather.place(0, [3 * width, width])
@@ -1565,9 +1576,9 @@
         chain, mixed_1, out_1, away, current_1, rows_of((1, 2), (1, 3), (1, 4)), False
     )
     other_3 = flip_rows(moved_3)
-    traded_cotangent = swap(rearranged(cotangent))
     act_1, slope_1 = both_times(chain, "gelu", moved_3, other_3, up_1)
     (down_1,) = gather.place(5, [hidden])
+    traded_cotangent = swap(copy_rows(chain, rearranged(cotangent)))
     away = other_rows(chain, act_1, down_1)
     final, branch_two_1 = forward_step(
         chain, act_1, down_1, away, after_1, rows_of((1, 5)), True
@@ -1614,7 +1625,6 @@
     (hidden_g,) = both_times(chain, "slope", own_g, other_g, down_0, slope_0)
     away = other_rows(chain, hidden_g, up_0)
     scatter.weight_grad((own_g, other_g, act_0))
-    chain.wait(joint_tables)
     scatter.step(6)
     state, sums_d, own_g = backward_step(
         chain, hidden_g, up_0, away, normed_1, inverse_1, state, rows_of((0, 4), (0, 2)), branch_one_0
@@ -1623,12 +1633,10 @@
     scatter.weight_grad((moved_1, other_1, hidden_g))
     (mixed_g,) = both_times(chain, "plain", own_g, other_g, out_0)
     scatter.step(6)
-    first_done = swap(join_pieces(chain, scatter.done[:2])[0])
     back, spatial_sums = attend_back(chain, joined_0, windowed(mixed_g), probs_0, False)
     back = back.reshape(2, rows, 3 * width)
     away = other_rows(chain, back, qkv_0)
     scatter.weight_grad((moved_0, other_0, back), (own_g, other_g, mixed_0))
-    chain.wait(first_done)
     scatter.step(6)
     state, sums_e = backward_step(
         chain, back, qkv_0, away, normed_0, inverse_0, state, rows_of((0, 1)), None
@@ -1653,22 +1661,26 @@
     chain.wait(shared)
     scatter.step(6)
     scatter.step(6)
-    sent = flip(shared, "x")
-    early, state_copy = join_pieces(chain, scatter.done[2:], state)
+    shared = add_all(chain, shared)
+    sent = flip(shared, "y")
+    traded_state = swap(copy_rows(chain, state))
+    (early,) = join_pieces(chain, scatter.done)
     early = swap(early)
-    traded_state = swap(state_copy)
     shared = add_all(chain, shared, sent)
-    shared = add_all(chain, shared, flip(shared, "y"))
     sent = [z_trade(shared, k) for k in (1, 2, 3)]
+    chain.wait(traded_state)
     scatter.step(6)
     late = swap(scatter.done[5]).astype(full)
     shared = add_all(chain, shared, *sent)
+    sent = flip(shared, "x")
+    chain.wait(early)
+    shared = add_all(chain, shared, sent)
     tables = shared[-heads * 18 :]
     across = flip(shared, "c")
     grad_activity = (shared + across)[: -heads * 18].reshape(16, model_width)
     tables = jnp.where(c == x, tables, across[-heads * 18 :])[:, : wide * wide]
     grad_latents = restored(traded_state)
-    done = jnp.concatenate([first_done, early], axis=1).astype(full)
+    done = early.astype(full)
     piece = lambda at: done[:, at * PIECE : (at + 1) * PIECE]
     grad_down = jnp.stack([piece(3).T, piece(0).T])
     grad_up = jnp.stack([piece(4), piece(1)])

time: 757 us -> 732 us (0.967)
  starting transfers between devices: 136 us -> 119 us
  local copies, waits for them, and re-layouts: 80.4 us -> 66.7 us
  Pallas kernels: 316 us -> 325 us
    ppermute x10 -> x9, starting transfers between devices: 43.7 us -> 25.8 us  [swap_only(): return lax.ppermute(values, ('c', 'x'), [(1, 2), (2, 1)])]
    unnamed x332 -> x336, local copies, waits for them, and re-layouts: 56.4 us -> 42.1 us
    pallas_call x65 -> x68, Pallas kernels: 316 us -> 325 us  [run(): pl.pallas_call(body, grid_spec=pltpu.PrefetchScalarGridSpec(num_scalar_pr...]
    ppermute x10 -> x9, waiting for transfers between devices: 15.6 us -> 10.5 us  [swap_only(): return lax.ppermute(values, ('c', 'x'), [(1, 2), (2, 1)])]
  transfers between devices with their start and end apart: 115 -> 114, of which waited for: 39 -> 47; matrix products, arithmetic and copies ran while one was open for 7% -> 8% of each run, Pallas kernels for 39% -> 42%
where the time goes in v4:
time: 732 us; the launch traced here: 727 us
  Pallas kernels  325 us (44%)
  waiting for transfers between devices  172 us (23%)
  starting transfers between devices  119 us (16%)
  local copies, waits for them, and re-layouts  66.7 us (9%)
  other arithmetic  24.2 us (3%)
  matrix products  15.1 us (2%)
    pallas_call x68, Pallas kernels, run(): pl.pallas_call(body, grid_spec=pltpu.PrefetchScalarGridSpec(num_scalar_pr...  325 us
    ppermute x39, waiting for transfers between devices, z_trade(): lax.ppermute(values, 'z', [(place, place ^ step) for place in range(4)])  112 us
    ppermute x64, waiting for transfers between devices, flip(): return lax.ppermute(values, axis, [(0, 1), (1, 0)])  43.3 us
    unnamed x336, local copies, waits for them, and re-layouts  42.1 us
    ppermute x64, starting transfers between devices, flip(): return lax.ppermute(values, axis, [(0, 1), (1, 0)])  40.6 us
    ppermute x39, starting transfers between devices, z_trade(): lax.ppermute(values, 'z', [(place, place ^ step) for place in range(4)])  39.8 us
    ppermute x9, starting transfers between devices, swap_only(): return lax.ppermute(values, ('c', 'x'), [(1, 2), (2, 1)])  25.8 us
  transfers between devices with their start and end apart: 114, of which 47 were waited for; matrix products, arithmetic and copies ran while one was open for 8% of the time, Pallas kernels for 42%

profile of v4, /device:TPU:9, one launch (start us, length us, event | category | flops | bytes accessed | tf_op | source)
XLA Modules:
  0.0 726.8 jit_solution(17469692039497301403)
XLA Ops:
  4.5 3.7 collective-permute-start.1
  14.1 6.3 all-to-all-start
  22.2 4.2 all-to-all-done
  33.7 7.7 %collective-permute-done.4.refs_2_ = bf16[64,2048]{1,0:T(8,128)(2,1)S(1)} collective-permute-done((bf16[64,2048]{1,0:T(8,128)(2,1)S(1)}, bf16[64,2048]{1,0:T(8,128)(2,1)S(1)}, u32[]{:S(2)}, u32[]{:S(2)}) %collective-permute-start.4) | collective-permute-done | bytes 262176 | tf_op jit(solution)/shard_map/ppermute | solution.py:518
  41.4 8.6 %collective-permute-done.5.refs_3_ = bf16[64,2048]{1,0:T(8,128)(2,1)S(1)} collective-permute-done((bf16[64,2048]{1,0:T(8,128)(2,1)S(1)}, bf16[64,2048]{1,0:T(8,128)(2,1)S(1)}, u32[]{:S(2)}, u32[]{:S(2)}) %collective-permute-start.5) | collective-permute-done | bytes 262176 | tf_op jit(solution)/shard_map/ppermute | solution.py:518
  50.1 5.2 collective-permute-done.6.refs_4_
  67.0 15.4 %collective-permute-done.11.refs_5_.refs_2_ = bf16[4,64,2048]{2,1,0:T(8,128)(2,1)S(1)} collective-permute-done((bf16[4,64,2048]{2,1,0:T(8,128)(2,1)}, bf16[4,64,2048]{2,1,0:T(8,128)(2,1)S(1)}, u32[]{:S(2)}, u32[]{:S(2)}) %collective-permute-start.11) | collective-permute-done | bytes 1048608 | tf_op jit(solution)/shard_map/ppermute | solution.py:514
  85.5 4.5 gather_step.8
  102.0 8.7 %collective-permute-done.7.refs_2_ = bf16[640,1024]{1,0:T(8,128)(2,1)} collective-permute-done((bf16[640,1024]{1,0:T(8,128)(2,1)}, bf16[640,1024]{1,0:T(8,128)(2,1)}, u32[]{:S(2)}, u32[]{:S(2)}) %collective-permute-start.7) | collective-permute-done | bytes 1310752 | tf_op jit(solution)/shard_map/ppermute | solution.py:522
  116.7 9.2 %collective-permute-done.19.refs_4_ = bf16[64,2048]{1,0:T(8,128)(2,1)S(1)} collective-permute-done((bf16[64,2048]{1,0:T(8,128)(2,1)S(1)}, bf16[64,2048]{1,0:T(8,128)(2,1)S(1)}, u32[]{:S(2)}, u32[]{:S(2)}) %collective-permute-start.19) | collective-permute-done | bytes 262176 | tf_op jit(solution)/shard_map/ppermute | solution.py:518
  125.9 7.9 %collective-permute-done.15.refs_5_.refs_4_.refs_2_ = bf16[6,64,2048]{2,1,0:T(8,128)(2,1)S(1)} collective-permute-done((bf16[6,64,2048]{2,1,0:T(8,128)(2,1)}, bf16[6,64,2048]{2,1,0:T(8,128)(2,1)S(1)}, u32[]{:S(2)}, u32[]{:S(2)}) %collective-permute-start.15) | collective-permute-done | bytes 1572896 | tf_op jit(solution)/shard_map/ppermute | solution.py:514
  133.9 3.2 gather_step.9
  143.6 3.2 place_weights.6
  146.8 5.8 both_plain.4.refs_3_
  152.6 14.6 %attend_spatial.1 = (bf16[2,5,2,64,512]{4,3,2,1,0:T(8,128)(2,1)S(1)}, bf16[5,8,256,256]{3,2,1,0:T(8,128)(2,1)S(1)}) custom-call(s32[5]{0:T(128)S(1)} %concatenate.13.refs_0_, bf16[8,9,64,64]{3,2,1,0:T(8,128)(2,1)S(1)} %bitcast.200, bf16[2,5,2,64,1536]{4,3,2,1,0:T(8,128)(2,1)S(1)} %bitcast.173, bf16[2,640,1536]{2,1,0:T(8,128)(2,1)S(1)} %both_plain.4.refs_3_), custom_call_target="tpu_custom_call" | custom-call | flops 1 | bytes 1 | tf_op jit(solution)/shard_map/attend_spatial/pallas_call | solution.py:583
  179.8 3.4 forward_step.4
  189.6 17.3 %both_gelu.2 = (bf16[2,640,2048]{2,1,0:T(8,128)(2,1)S(1)}, bf16[2,640,2048]{2,1,0:T(8,128)(2,1)S(1)}) custom-call(s32[5]{0:T(128)S(1)} %concatenate.13.refs_0_, bf16[320,1024]{1,0:T(8,128)(2,1)S(1)} %get-tuple-element.194.refs_1_, bf16[320,1024]{1,0:T(8,128)(2,1)S(1)} %get-tuple-element.195.refs_2_, bf16[320,1024]{1,0:T(8,128)(2,1)S(1)} %collective-permute-done.27.refs_3_, ...), custom_call_target="tpu_custom_call" | custom-call | flops 1 | bytes 1 | tf_op jit(solution)/shard_map/both_gelu/pallas_call | solution.py:583
  209.4 3.2 collective-permute-done.33.refs_4_
  215.7 4.2 other_rows.9
  225.6 5.1 forward_step.5
  231.6 9.2 %collective-permute-done.41.refs_3_ = bf16[64,2048]{1,0:T(8,128)(2,1)S(1)} collective-permute-done((bf16[64,2048]{1,0:T(8,128)(2,1)S(1)}, bf16[64,2048]{1,0:T(8,128)(2,1)S(1)}, u32[]{:S(2)}, u32[]{:S(2)}) %collective-permute-start.41) | collective-permute-done | bytes 262176 | tf_op jit(solution)/shard_map/ppermute | solution.py:518
  240.8 7.6 %collective-permute-done.42.refs_4_ = bf16[64,2048]{1,0:T(8,128)(2,1)S(1)} collective-permute-done((bf16[64,2048]{1,0:T(8,128)(2,1)S(1)}, bf16[64,2048]{1,0:T(8,128)(2,1)S(1)}, u32[]{:S(2)}, u32[]{:S(2)}) %collective-permute-start.42) | collective-permute-done | bytes 262176 | tf_op jit(solution)/shard_map/ppermute | solution.py:518
  257.5 5.8 both_plain.5.refs_3_
  263.3 16.0 %attend_joint.1 = (bf16[2,5,2,64,512]{4,3,2,1,0:T(8,128)(2,1)S(1)}, bf16[4,8,320,320]{3,2,1,0:T(8,128)(2,1)S(1)}) custom-call(s32[5]{0:T(128)S(1)} %concatenate.13.refs_0_, bf16[8,9,64,64]{3,2,1,0:T(8,128)(2,1)S(1)} %squeeze.38.refs_6_.refs_1_, bf16[2,5,2,64,1536]{4,3,2,1,0:T(8,128)(2,1)S(1)} %bitcast.175, bf16[2,640,1536]{2,1,0:T(8,128)(2,1)S(1)} %both_plain.5.refs_3_), custom_call_target="tpu_custom_call" | custom-call | flops 1 | bytes 1 | tf_op jit(solution)/shard_map/attend_joint/pallas_call | solution.py:583
  279.4 3.2 copy-done.27
  296.3 17.3 %both_gelu.3 = (bf16[2,640,2048]{2,1,0:T(8,128)(2,1)S(1)}, bf16[2,640,2048]{2,1,0:T(8,128)(2,1)S(1)}) custom-call(s32[5]{0:T(128)S(1)} %concatenate.13.refs_0_, bf16[320,1024]{1,0:T(8,128)(2,1)S(1)} %get-tuple-element.216.refs_1_, bf16[320,1024]{1,0:T(8,128)(2,1)S(1)} %get-tuple-element.217.refs_2_, bf16[320,1024]{1,0:T(8,128)(2,1)S(1)} %collective-permute-done.47.refs_3_, ...), custom_call_target="tpu_custom_call" | custom-call | flops 1 | bytes 1 | tf_op jit(solution)/shard_map/both_gelu/pallas_call | solution.py:583
  319.3 4.2 other_rows.11
  326.6 4.2 forward_step.7
  343.0 8.1 %both_slope.2.refs_1_.refs_3_.refs_5_ = bf16[2,640,2048]{2,1,0:T(8,128)(2,1)S(1)} custom-call(s32[5]{0:T(128)S(1)} %concatenate.13.refs_0_, bf16[320,1024]{1,0:T(8,128)(2,1)S(1)} %get-tuple-element.225.refs_1_.refs_7_, bf16[320,1024]{1,0:T(8,128)(2,1)S(1)} %get-tuple-element.226.refs_2_, bf16[320,1024]{1,0:T(8,128)(2,1)S(1)} %collective-permute-done.55.refs_3_, ...), custom_call_target="tpu_custom_call" | custom-call | flops 1 | bytes 1 | tf_op jit(solution)/shard_map/both_slope/pallas_call | solution.py:583
  351.1 4.8 other_rows.12
  356.4 9.8 %weight_grad.6 = (bf16[4,64,2048]{2,1,0:T(8,128)(2,1)S(1)}, bf16[4,64,2048]{2,1,0:T(8,128)(2,1)S(1)}, bf16[4,64,2048]{2,1,0:T(8,128)(2,1)S(1)}, bf16[2,64,2048]{2,1,0:T(8,128)(2,1)}, bf16[2,64,2048]{2,1,0:T(8,128)(2,1)}) custom-call(s32[5]{0:T(128)S(1)} %concatenate.13.refs_0_, bf16[320,1024]{1,0:T(8,128)(2,1)S(1)} %get-tuple-element.225.refs_1_.refs_7_, ...), custom_call_target="tpu_custom_call" | custom-call | flops 1 | bytes 1 | tf_op jit(solution)/shard_map/weight_grad/pallas_call | solution.py:583
  369.1 7.7 %backward_step.4 = (f32[640,1024]{1,0:T(8,128)S(1)}, f32[8,1024]{1,0:T(8,128)S(1)}, bf16[320,1024]{1,0:T(8,128)(2,1)S(1)}, bf16[320,1024]{1,0:T(8,128)(2,1)S(1)}) custom-call(s32[5]{0:T(128)S(1)} %concatenate.13.refs_0_, bf16[2,640,2048]{2,1,0:T(8,128)(2,1)S(1)} %both_slope.2.refs_1_.refs_3_.refs_5_, bf16[1024,2048]{1,0:T(8,128)(2,1)S(1)} %bitcast.164, ...), custom_call_target="tpu_custom_call" | custom-call | flops 1 | bytes 1 | tf_op jit(solution)/shard_map/backward_step/pallas_call | solution.py:583
  376.8 9.2 %weight_grad.7 = (bf16[4,64,2048]{2,1,0:T(8,128)(2,1)S(1)}, bf16[4,64,2048]{2,1,0:T(8,128)(2,1)S(1)}, bf16[4,64,2048]{2,1,0:T(8,128)(2,1)S(1)}, bf16[2,64,2048]{2,1,0:T(8,128)(2,1)S(1)}, bf16[2,64,2048]{2,1,0:T(8,128)(2,1)S(1)}) custom-call(s32[5]{0:T(128)S(1)} %concatenate.13.refs_0_, bf16[320,1024]{1,0:T(8,128)(2,1)S(1)} %copy-done.70, ...), custom_call_target="tpu_custom_call" | custom-call | flops 1 | bytes 1 | tf_op jit(solution)/shard_map/weight_grad/pallas_call | solution.py:583
  398.1 18.8 %attend_back_joint.1 = (bf16[2,5,2,64,1536]{4,3,2,1,0:T(8,128)(2,1)S(1)}, f32[8,9,64,64]{3,2,1,0:T(8,128)S(1)}) custom-call(s32[5]{0:T(128)S(1)} %concatenate.13.refs_0_, bf16[2,5,2,64,1536]{4,3,2,1,0:T(8,128)(2,1)S(1)} %bitcast.176, bf16[2,5,2,64,512]{4,3,2,1,0:T(8,128)(2,1)S(1)} %bitcast.198, bf16[4,8,320,320]{3,2,1,0:T(8,128)(2,1)S(1)} %bitcast.208, ...), custom_call_target="tpu_custom_call" | custom-call | flops 1 | bytes 1 | tf_op jit(solution)/shard_map/attend_back_joint/pallas_call | solution.py:583
  416.9 4.1 other_rows.13
  421.6 10.5 %weight_grad.8 = (bf16[4,64,2048]{2,1,0:T(8,128)(2,1)S(1)}, bf16[4,64,2048]{2,1,0:T(8,128)(2,1)S(1)}, bf16[4,64,2048]{2,1,0:T(8,128)(2,1)S(1)}, bf16[2,64,2048]{2,1,0:T(8,128)(2,1)S(1)}, bf16[2,64,2048]{2,1,0:T(8,128)(2,1)S(1)}) custom-call(s32[5]{0:T(128)S(1)} %concatenate.13.refs_0_, bf16[320,1024]{1,0:T(8,128)(2,1)S(1)} %copy-done.54, ...), custom_call_target="tpu_custom_call" | custom-call | flops 1 | bytes 1 | tf_op jit(solution)/shard_map/weight_grad/pallas_call | solution.py:583
  432.2 3.4 scatter_step.9
  436.7 7.1 backward_step.5
  451.0 8.1 %both_slope.3.refs_1_.refs_3_.refs_5_ = bf16[2,640,2048]{2,1,0:T(8,128)(2,1)S(1)} custom-call(s32[5]{0:T(128)S(1)} %concatenate.13.refs_0_, bf16[320,1024]{1,0:T(8,128)(2,1)S(1)} %get-tuple-element.259.refs_1_, bf16[320,1024]{1,0:T(8,128)(2,1)S(1)} %get-tuple-element.260.refs_2_, bf16[320,1024]{1,0:T(8,128)(2,1)S(1)} %collective-permute-done.67.refs_3_, ...), custom_call_target="tpu_custom_call" | custom-call | flops 1 | bytes 1 | tf_op jit(solution)/shard_map/both_slope/pallas_call | solution.py:583
  459.1 4.2 other_rows.14
  463.4 9.2 %weight_grad.9 = (bf16[4,64,2048]{2,1,0:T(8,128)(2,1)S(1)}, bf16[4,64,2048]{2,1,0:T(8,128)(2,1)S(1)}, bf16[4,64,2048]{2,1,0:T(8,128)(2,1)S(1)}, bf16[2,64,2048]{2,1,0:T(8,128)(2,1)S(1)}, bf16[2,64,2048]{2,1,0:T(8,128)(2,1)S(1)}) custom-call(s32[5]{0:T(128)S(1)} %concatenate.13.refs_0_, bf16[320,1024]{1,0:T(8,128)(2,1)S(1)} %get-tuple-element.259.refs_1_, ...), custom_call_target="tpu_custom_call" | custom-call | flops 1 | bytes 1 | tf_op jit(solution)/shard_map/weight_grad/pallas_call | solution.py:583
  473.7 3.5 scatter_step.10
  480.0 6.3 backward_step.6
  493.1 9.4 %weight_grad.10 = (bf16[4,64,2048]{2,1,0:T(8,128)(2,1)S(1)}, bf16[4,64,2048]{2,1,0:T(8,128)(2,1)S(1)}, bf16[4,64,2048]{2,1,0:T(8,128)(2,1)S(1)}, bf16[2,64,2048]...) custom-call(s32[5]{0:T(128)S(1)} %concatenate.13.refs_0_, bf16[320,1024]{1,0:T(8,128)(2,1)S(1)} %copy-done.62, ...), custom_call_target="tpu_custom_call" | custom-call | flops 1 | bytes 1 | tf_op jit(solution)/shard_map/weight_grad/pallas_call | solution.py:583
  504.6 3.9 collective-permute-done.81.refs_10_
  508.6 7.5 %collective-permute-done.82.refs_11_ = bf16[64,2048]{1,0:T(8,128)(2,1)S(1)} collective-permute-done((bf16[64,2048]{1,0:T(8,128)(2,1)S(1)}, bf16[64,2048]{1,0:T(8,128)(2,1)S(1)}, u32[]{:S(2)}, u32[]{:S(2)}) %collective-permute-start.82) | collective-permute-done | bytes 262176 | tf_op jit(solution)/shard_map/ppermute | solution.py:518
  522.7 17.9 %attend_back_spatial.1 = (bf16[2,5,2,64,1536]{4,3,2,1,0:T(8,128)(2,1)S(1)}, f32[8,9,64,64]{3,2,1,0:T(8,128)S(1)}) custom-call(s32[5]{0:T(128)S(1)} %concatenate.13.refs_0_, bf16[2,5,2,64,1536]{4,3,2,1,0:T(8,128)(2,1)S(1)} %bitcast.174, bf16[2,5,2,64,512]{4,3,2,1,0:T(8,128)(2,1)S(1)} %bitcast.195, bf16[5,8,256,256]{3,2,1,0:T(8,128)(2,1)S(1)} %bitcast.210, ...), custom_call_target="tpu_custom_call" | custom-call | flops 1 | bytes 1 | tf_op jit(solution)/shard_map/attend_back_spatial/pallas_call | solution.py:583
  540.7 4.4 other_rows.15
  545.1 10.9 %weight_grad.11 = (bf16[4,64,2048]{2,1,0:T(8,128)(2,1)S(1)}, bf16[4,64,2048]{2,1,0:T(8,128)(2,1)S(1)}, bf16[4,64,2048]{2,1,0:T(8,128)(2,1)S(1)}, bf16[2,64,2048]...) custom-call(s32[5]{0:T(128)S(1)} %concatenate.13.refs_0_, bf16[320,1024]{1,0:T(8,128)(2,1)S(1)} %copy-done.46, ...), custom_call_target="tpu_custom_call" | custom-call | flops 1 | bytes 1 | tf_op jit(solution)/shard_map/weight_grad/pallas_call | solution.py:583
  558.8 3.6 scatter_step.12
  570.6 4.1 fusion.2
  578.1 4.4 reverse_select_fusion
  594.6 5.6 backward_step.7
  602.0 6.2 all-to-all-start.1
  608.2 4.1 fusion
  624.4 3.9 scatter_step.13
  631.9 7.5 %collective-permute-done.97.refs_5_ = bf16[64,2048]{1,0:T(8,128)(2,1)S(1)} collective-permute-done((bf16[64,2048]{1,0:T(8,128)(2,1)S(1)}, bf16[64,2048]{1,0:T(8,128)(2,1)S(1)}, u32[]{:S(2)}, u32[]{:S(2)}) %collective-permute-start.97) | collective-permute-done | bytes 262176 | tf_op jit(solution)/shard_map/ppermute | solution.py:518
  642.5 11.3 %collective-permute-done.99.refs_7_ = bf16[64,2048]{1,0:T(8,128)(2,1)S(1)} collective-permute-done((bf16[64,2048]{1,0:T(8,128)(2,1)S(1)}, bf16[64,2048]{1,0:T(8,128)(2,1)S(1)}, u32[]{:S(2)}, u32[]{:S(2)}) %collective-permute-start.99) | collective-permute-done | bytes 262176 | tf_op jit(solution)/shard_map/ppermute | solution.py:518
  656.7 5.0 collective-permute-start.100
  672.4 4.0 collective-permute-done.105.refs_2_
  679.2 7.6 %collective-permute-done.106.refs_3_ = bf16[64,2048]{1,0:T(8,128)(2,1)S(1)} collective-permute-done((bf16[64,2048]{1,0:T(8,128)(2,1)S(1)}, bf16[64,2048]{1,0:T(8,128)(2,1)S(1)}, u32[]{:S(2)}, u32[]{:S(2)}) %collective-permute-start.106) | collective-permute-done | bytes 262176 | tf_op jit(solution)/shard_map/ppermute | solution.py:518
  686.8 3.3 collective-permute-start.103
  691.3 10.7 %collective-permute-done.107.refs_4_ = bf16[64,2048]{1,0:T(8,128)(2,1)S(1)} collective-permute-done((bf16[64,2048]{1,0:T(8,128)(2,1)S(1)}, bf16[64,2048]{1,0:T(8,128)(2,1)S(1)}, u32[]{:S(2)}, u32[]{:S(2)}) %collective-permute-start.107) | collective-permute-done | bytes 262176 | tf_op jit(solution)/shard_map/ppermute | solution.py:518
  705.4 3.7 collective-permute-done.104.refs_4_
  (660 shorter events, 258.8 us)
Async XLA Ops:
  10.7 19.3 %collective-permute-start.3 = (bf16[64,2048]{1,0:T(8,128)(2,1)}, bf16[64,2048]{1,0:T(8,128)(2,1)}, u32[]{:S(2)}, u32[]{:S(2)}) collective-permute-start(bf16[64,2048]{1,0:T(8,128)(2,1)} %pad_maximum_fusion.3), channel_id=1, source_target_pairs={{1,2},{2,1},{5,6},{6,5},{9,10},{10,9},{13,14},{14,13},{17,18},{18,... | collective-permute-start | bytes 786440 | tf_op jit(solution)/shard_map/ppermute | solution.py:522
  27.2 31.1 %collective-permute-start.2 = (bf16[64,10240]{1,0:T(8,128)(2,1)S(1)}, bf16[64,10240]{1,0:T(8,128)(2,1)S(1)}, u32[]{:S(2)}, u32[]{:S(2)}) collective-permute-start(bf16[64,10240]{1,0:T(8,128)(2,1)S(1)} %pack_arguments.1.refs_5_.refs_1_), channel_id=1, source_target_pairs={{1,2},{2,1},{5,6},{6,5},{9,10},{10,9},{13,14},{14,13},{17,18},{18,... | collective-permute-start | bytes 3932168 | tf_op jit(solution)/shard_map/ppermute | solution.py:522
  32.6 22.6 %collective-permute-start.6 = (bf16[64,2048]{1,0:T(8,128)(2,1)S(1)}, bf16[64,2048]{1,0:T(8,128)(2,1)S(1)}, u32[]{:S(2)}, u32[]{:S(2)}) collective-permute-start(bf16[64,2048]{1,0:T(8,128)(2,1)S(1)} %broadcast_select_fusion.4.refs_1_), channel_id=1, source_target_pairs={{0,24},{8,16},{16,8},{24,0},{1,25},{9,17},{17,9},{25,1},{2,26},{10... | collective-permute-start | bytes 786440 | tf_op jit(solution)/shard_map/ppermute | solution.py:518
  57.7 24.7 %collective-permute-start.11 = (bf16[4,64,2048]{2,1,0:T(8,128)(2,1)}, bf16[4,64,2048]{2,1,0:T(8,128)(2,1)S(1)}, u32[]{:S(2)}, u32[]{:S(2)}) collective-permute-start(bf16[4,64,2048]{2,1,0:T(8,128)(2,1)} %get-tuple-element.176.refs_3_.refs_1_), channel_id=1, source_target_pairs={{0,1},{1,0},{2,3},{3,2},{4,5},{5,4},{6,7},{7,6},{8,9},{9,8},{10,11... | collective-permute-start | bytes 3145736 | tf_op jit(solution)/shard_map/ppermute | solution.py:514
  57.7 27.8 %collective-permute-start.12 = (bf16[4,64,2048]{2,1,0:T(8,128)(2,1)}, bf16[4,64,2048]{2,1,0:T(8,128)(2,1)}, u32[]{:S(2)}, u32[]{:S(2)}) collective-permute-start(bf16[4,64,2048]{2,1,0:T(8,128)(2,1)} %get-tuple-element.178), channel_id=1, source_target_pairs={{0,4},{4,0},{1,5},{5,1},{2,6},{6,2},{3,7},{7,3},{8,12},{12,8},{9,1... | collective-permute-start | bytes 3145736 | tf_op jit(solution)/shard_map/ppermute | solution.py:514
  61.8 23.7 %collective-permute-start.10 = (bf16[64,2048]{1,0:T(8,128)(2,1)S(1)}, bf16[64,2048]{1,0:T(8,128)(2,1)}, u32[]{:S(2)}, u32[]{:S(2)}) collective-permute-start(bf16[64,2048]{1,0:T(8,128)(2,1)S(1)} %get-tuple-element.177.refs_2_.refs_1_), channel_id=1, source_target_pairs={{0,24},{8,16},{16,8},{24,0},{1,25},{9,17},{17,9},{25,1},{2,26},{10... | collective-permute-start | bytes 786440 | tf_op jit(solution)/shard_map/ppermute | solution.py:518
  62.2 23.4 %collective-permute-start.8 = (bf16[64,2048]{1,0:T(8,128)(2,1)S(1)}, bf16[64,2048]{1,0:T(8,128)(2,1)}, u32[]{:S(2)}, u32[]{:S(2)}) collective-permute-start(bf16[64,2048]{1,0:T(8,128)(2,1)S(1)} %get-tuple-element.177.refs_2_.refs_1_), channel_id=1, source_target_pairs={{0,8},{8,0},{16,24},{24,16},{1,9},{9,1},{17,25},{25,17},{2,10},{10... | collective-permute-start | bytes 786440 | tf_op jit(solution)/shard_map/ppermute | solution.py:518
  62.2 23.4 %collective-permute-start.9 = (bf16[64,2048]{1,0:T(8,128)(2,1)S(1)}, bf16[64,2048]{1,0:T(8,128)(2,1)}, u32[]{:S(2)}, u32[]{:S(2)}) collective-permute-start(bf16[64,2048]{1,0:T(8,128)(2,1)S(1)} %get-tuple-element.177.refs_2_.refs_1_), channel_id=1, source_target_pairs={{0,16},{8,24},{16,0},{24,8},{1,17},{9,25},{17,1},{25,9},{2,18},{10... | collective-permute-start | bytes 786440 | tf_op jit(solution)/shard_map/ppermute | solution.py:518
  82.4 28.3 %collective-permute-start.7 = (bf16[640,1024]{1,0:T(8,128)(2,1)}, bf16[640,1024]{1,0:T(8,128)(2,1)}, u32[]{:S(2)}, u32[]{:S(2)}) collective-permute-start(bf16[640,1024]{1,0:T(8,128)(2,1)} %copy_rows.3.refs_7_.refs_1_), channel_id=1, source_target_pairs={{1,2},{2,1},{5,6},{6,5},{9,10},{10,9},{13,14},{14,13},{17,18},{18,... | collective-permute-start | bytes 3932168 | tf_op jit(solution)/shard_map/ppermute | solution.py:522
  90.0 43.8 %collective-permute-start.15 = (bf16[6,64,2048]{2,1,0:T(8,128)(2,1)}, bf16[6,64,2048]{2,1,0:T(8,128)(2,1)S(1)}, u32[]{:S(2)}, u32[]{:S(2)}) collective-permute-start(bf16[6,64,2048]{2,1,0:T(8,128)(2,1)} %get-tuple-element.179.refs_4_.refs_1_), channel_id=1, source_target_pairs={{0,1},{1,0},{2,3},{3,2},{4,5},{5,4},{6,7},{7,6},{8,9},{9,8},{10,11... | collective-permute-start | bytes 4718600 | tf_op jit(solution)/shard_map/ppermute | solution.py:514
  90.1 43.8 %collective-permute-start.16 = (bf16[6,64,2048]{2,1,0:T(8,128)(2,1)}, bf16[6,64,2048]{2,1,0:T(8,128)(2,1)}, u32[]{:S(2)}, u32[]{:S(2)}) collective-permute-start(bf16[6,64,2048]{2,1,0:T(8,128)(2,1)} %get-tuple-element.182), channel_id=1, source_target_pairs={{0,4},{4,0},{1,5},{5,1},{2,6},{6,2},{3,7},{7,3},{8,12},{12,8},{9,1... | collective-permute-start | bytes 4718600 | tf_op jit(solution)/shard_map/ppermute | solution.py:514
  137.1 35.7 %collective-permute-start.22 = (bf16[6,64,2048]{2,1,0:T(8,128)(2,1)S(1)}, bf16[6,64,2048]{2,1,0:T(8,128)(2,1)S(1)}, u32[]{:S(2)}, u32[]{:S(2)}) collective-permute-start(bf16[6,64,2048]{2,1,0:T(8,128)(2,1)S(1)} %get-tuple-element.185.refs_6_.refs_1_), channel_id=1, source_target_pairs={{0,1},{1,0},{2,3},{3,2},{4,5},{5,4},{6,7},{7,6},{8,9},{9,8},{10,11... | collective-permute-start | bytes 4718600 | tf_op jit(solution)/shard_map/ppermute | solution.py:514
  139.0 35.6 %collective-permute-start.23 = (bf16[6,64,2048]{2,1,0:T(8,128)(2,1)S(1)}, bf16[6,64,2048]{2,1,0:T(8,128)(2,1)S(1)}, u32[]{:S(2)}, u32[]{:S(2)}) collective-permute-start(bf16[6,64,2048]{2,1,0:T(8,128)(2,1)S(1)} %get-tuple-element.191), channel_id=1, source_target_pairs={{0,4},{4,0},{1,5},{5,1},{2,6},{6,2},{3,7},{7,3},{8,12},{12,8},{9,1... | collective-permute-start | bytes 4718600 | tf_op jit(solution)/shard_map/ppermute | solution.py:514
  140.4 31.3 %collective-permute-start.24 = (bf16[64,2048]{1,0:T(8,128)(2,1)S(1)}, bf16[64,2048]{1,0:T(8,128)(2,1)S(1)}, u32[]{:S(2)}, u32[]{:S(2)}) collective-permute-start(bf16[64,2048]{1,0:T(8,128)(2,1)S(1)} %copy-done.125), channel_id=1, source_target_pairs={{0,8},{8,0},{16,24},{24,16},{1,9},{9,1},{17,25},{25,17},{2,10},{10... | collective-permute-start | bytes 786440 | tf_op jit(solution)/shard_map/ppermute | solution.py:518
  142.1 30.4 %collective-permute-start.25 = (bf16[64,2048]{1,0:T(8,128)(2,1)S(1)}, bf16[64,2048]{1,0:T(8,128)(2,1)S(1)}, u32[]{:S(2)}, u32[]{:S(2)}) collective-permute-start(bf16[64,2048]{1,0:T(8,128)(2,1)S(1)} %copy-done.125), channel_id=1, source_target_pairs={{0,16},{8,24},{16,0},{24,8},{1,17},{9,25},{17,1},{25,9},{2,18},{10... | collective-permute-start | bytes 786440 | tf_op jit(solution)/shard_map/ppermute | solution.py:518
  143.0 29.6 %collective-permute-start.26 = (bf16[64,2048]{1,0:T(8,128)(2,1)S(1)}, bf16[64,2048]{1,0:T(8,128)(2,1)S(1)}, u32[]{:S(2)}, u32[]{:S(2)}) collective-permute-start(bf16[64,2048]{1,0:T(8,128)(2,1)S(1)} %copy-done.125), channel_id=1, source_target_pairs={{0,24},{8,16},{16,8},{24,0},{1,25},{9,17},{17,9},{25,1},{2,26},{10... | collective-permute-start | bytes 786440 | tf_op jit(solution)/shard_map/ppermute | solution.py:518
  175.9 36.7 %collective-permute-start.29 = (bf16[6,64,2048]{2,1,0:T(8,128)(2,1)S(1)}, bf16[6,64,2048]{2,1,0:T(8,128)(2,1)S(1)}, u32[]{:S(2)}, u32[]{:S(2)}) collective-permute-start(bf16[6,64,2048]{2,1,0:T(8,128)(2,1)S(1)} %get-tuple-element.193.refs_6_.refs_1_), channel_id=1, source_target_pairs={{0,1},{1,0},{2,3},{3,2},{4,5},{5,4},{6,7},{7,6},{8,9},{9,8},{10,11... | collective-permute-start | bytes 4718600 | tf_op jit(solution)/shard_map/ppermute | solution.py:514
  176.3 36.2 %collective-permute-start.30 = (bf16[6,64,2048]{2,1,0:T(8,128)(2,1)S(1)}, bf16[6,64,2048]{2,1,0:T(8,128)(2,1)S(1)}, u32[]{:S(2)}, u32[]{:S(2)}) collective-permute-start(bf16[6,64,2048]{2,1,0:T(8,128)(2,1)S(1)} %get-tuple-element.198), channel_id=1, source_target_pairs={{0,4},{4,0},{1,5},{5,1},{2,6},{6,2},{3,7},{7,3},{8,12},{12,8},{9,1... | collective-permute-start | bytes 4718600 | tf_op jit(solution)/shard_map/ppermute | solution.py:514
  185.6 23.8 %collective-permute-start.31 = (bf16[64,2048]{1,0:T(8,128)(2,1)S(1)}, bf16[64,2048]{1,0:T(8,128)(2,1)S(1)}, u32[]{:S(2)}, u32[]{:S(2)}) collective-permute-start(bf16[64,2048]{1,0:T(8,128)(2,1)S(1)} %copy-done.123), channel_id=1, source_target_pairs={{0,8},{8,0},{16,24},{24,16},{1,9},{9,1},{17,25},{25,17},{2,10},{10... | collective-permute-start | bytes 786440 | tf_op jit(solution)/shard_map/ppermute | solution.py:518
  187.2 22.2 %collective-permute-start.32 = (bf16[64,2048]{1,0:T(8,128)(2,1)S(1)}, bf16[64,2048]{1,0:T(8,128)(2,1)S(1)}, u32[]{:S(2)}, u32[]{:S(2)}) collective-permute-start(bf16[64,2048]{1,0:T(8,128)(2,1)S(1)} %copy-done.123), channel_id=1, source_target_pairs={{0,16},{8,24},{16,0},{24,8},{1,17},{9,25},{17,1},{25,9},{2,18},{10... | collective-permute-start | bytes 786440 | tf_op jit(solution)/shard_map/ppermute | solution.py:518
  188.5 24.1 %collective-permute-start.33 = (bf16[64,2048]{1,0:T(8,128)(2,1)S(1)}, bf16[64,2048]{1,0:T(8,128)(2,1)S(1)}, u32[]{:S(2)}, u32[]{:S(2)}) collective-permute-start(bf16[64,2048]{1,0:T(8,128)(2,1)S(1)} %copy-done.123), channel_id=1, source_target_pairs={{0,24},{8,16},{16,8},{24,0},{1,25},{9,17},{17,9},{25,1},{2,26},{10... | collective-permute-start | bytes 786440 | tf_op jit(solution)/shard_map/ppermute | solution.py:518
  213.8 34.8 %collective-permute-start.38 = (bf16[6,64,2048]{2,1,0:T(8,128)(2,1)S(1)}, bf16[6,64,2048]{2,1,0:T(8,128)(2,1)S(1)}, u32[]{:S(2)}, u32[]{:S(2)}) collective-permute-start(bf16[6,64,2048]{2,1,0:T(8,128)(2,1)S(1)} %get-tuple-element.200.refs_6_.refs_1_), channel_id=1, source_target_pairs={{0,1},{1,0},{2,3},{3,2},{4,5},{5,4},{6,7},{7,6},{8,9},{9,8},{10,11... | collective-permute-start | bytes 4718600 | tf_op jit(solution)/shard_map/ppermute | solution.py:514
  213.9 34.7 %collective-permute-start.39 = (bf16[6,64,2048]{2,1,0:T(8,128)(2,1)S(1)}, bf16[6,64,2048]{2,1,0:T(8,128)(2,1)S(1)}, u32[]{:S(2)}, u32[]{:S(2)}) collective-permute-start(bf16[6,64,2048]{2,1,0:T(8,128)(2,1)S(1)} %get-tuple-element.205), channel_id=1, source_target_pairs={{0,4},{4,0},{1,5},{5,1},{2,6},{6,2},{3,7},{7,3},{8,12},{12,8},{9,1... | collective-permute-start | bytes 4718600 | tf_op jit(solution)/shard_map/ppermute | solution.py:514
  224.5 24.0 %collective-permute-start.42 = (bf16[64,2048]{1,0:T(8,128)(2,1)S(1)}, bf16[64,2048]{1,0:T(8,128)(2,1)S(1)}, u32[]{:S(2)}, u32[]{:S(2)}) collective-permute-start(bf16[64,2048]{1,0:T(8,128)(2,1)S(1)} %copy-done.119), channel_id=1, source_target_pairs={{0,24},{8,16},{16,8},{24,0},{1,25},{9,17},{17,9},{25,1},{2,26},{10... | collective-permute-start | bytes 786440 | tf_op jit(solution)/shard_map/ppermute | solution.py:518
  249.8 35.4 %collective-permute-start.45 = (bf16[6,64,2048]{2,1,0:T(8,128)(2,1)S(1)}, bf16[6,64,2048]{2,1,0:T(8,128)(2,1)S(1)}, u32[]{:S(2)}, u32[]{:S(2)}) collective-permute-start(bf16[6,64,2048]{2,1,0:T(8,128)(2,1)S(1)} %get-tuple-element.208.refs_6_.refs_1_), channel_id=1, source_target_pairs={{0,1},{1,0},{2,3},{3,2},{4,5},{5,4},{6,7},{7,6},{8,9},{9,8},{10,11... | collective-permute-start | bytes 4718600 | tf_op jit(solution)/shard_map/ppermute | solution.py:514
  251.2 34.1 %collective-permute-start.46 = (bf16[6,64,2048]{2,1,0:T(8,128)(2,1)S(1)}, bf16[6,64,2048]{2,1,0:T(8,128)(2,1)S(1)}, u32[]{:S(2)}, u32[]{:S(2)}) collective-permute-start(bf16[6,64,2048]{2,1,0:T(8,128)(2,1)S(1)} %get-tuple-element.214), channel_id=1, source_target_pairs={{0,4},{4,0},{1,5},{5,1},{2,6},{6,2},{3,7},{7,3},{8,12},{12,8},{9,1... | collective-permute-start | bytes 4718600 | tf_op jit(solution)/shard_map/ppermute | solution.py:514
  293.7 20.1 %collective-permute-start.49 = (bf16[2,64,2048]{2,1,0:T(8,128)(2,1)S(1)}, bf16[2,64,2048]{2,1,0:T(8,128)(2,1)S(1)}, u32[]{:S(2)}, u32[]{:S(2)}) collective-permute-start(bf16[2,64,2048]{2,1,0:T(8,128)(2,1)S(1)} %get-tuple-element.215.refs_6_), channel_id=1, source_target_pairs={{0,1},{1,0},{2,3},{3,2},{4,5},{5,4},{6,7},{7,6},{8,9},{9,8},{10,11... | collective-permute-start | bytes 1572872 | tf_op jit(solution)/shard_map/ppermute | solution.py:514
  293.9 19.9 %collective-permute-start.50 = (bf16[2,64,2048]{2,1,0:T(8,128)(2,1)S(1)}, bf16[2,64,2048]{2,1,0:T(8,128)(2,1)S(1)}, u32[]{:S(2)}, u32[]{:S(2)}) collective-permute-start(bf16[2,64,2048]{2,1,0:T(8,128)(2,1)S(1)} %get-tuple-element.220), channel_id=1, source_target_pairs={{0,4},{4,0},{1,5},{5,1},{2,6},{6,2},{3,7},{7,3},{8,12},{12,8},{9,1... | collective-permute-start | bytes 1572872 | tf_op jit(solution)/shard_map/ppermute | solution.py:514
  316.6 18.9 %collective-permute-start.54 = (bf16[640,1024]{1,0:T(8,128)(2,1)S(1)}, bf16[640,1024]{1,0:T(8,128)(2,1)S(1)}, u32[]{:S(2)}, u32[]{:S(2)}) collective-permute-start(bf16[640,1024]{1,0:T(8,128)(2,1)S(1)} %copy_rows.4.refs_3_), channel_id=1, source_target_pairs={{1,2},{2,1},{5,6},{6,5},{9,10},{10,9},{13,14},{14,13},{17,18},{18,... | collective-permute-start | bytes 3932168 | tf_op jit(solution)/shard_map/ppermute | solution.py:522
  330.8 36.6 %collective-permute-start.53 = (bf16[640,1024]{1,0:T(8,128)(2,1)S(1)}, bf16[640,1024]{1,0:T(8,128)(2,1)}, u32[]{:S(2)}, u32[]{:S(2)}) collective-permute-start(bf16[640,1024]{1,0:T(8,128)(2,1)S(1)} %get-tuple-element.223.refs_4_), channel_id=1, source_target_pairs={{1,2},{2,1},{5,6},{6,5},{9,10},{10,9},{13,14},{14,13},{17,18},{18,... | collective-permute-start | bytes 3932168 | tf_op jit(solution)/shard_map/ppermute | solution.py:522
  366.3 20.8 %collective-permute-start.61 = (bf16[2,64,2048]{2,1,0:T(8,128)(2,1)}, bf16[2,64,2048]{2,1,0:T(8,128)(2,1)S(1)}, u32[]{:S(2)}, u32[]{:S(2)}) collective-permute-start(bf16[2,64,2048]{2,1,0:T(8,128)(2,1)} %get-tuple-element.241), channel_id=1, source_target_pairs={{0,1},{1,0},{2,3},{3,2},{4,5},{5,4},{6,7},{7,6},{8,9},{9,8},{10,11... | collective-permute-start | bytes 1572872 | tf_op jit(solution)/shard_map/ppermute | solution.py:514
  366.7 20.4 %collective-permute-start.62 = (bf16[2,64,2048]{2,1,0:T(8,128)(2,1)}, bf16[2,64,2048]{2,1,0:T(8,128)(2,1)S(1)}, u32[]{:S(2)}, u32[]{:S(2)}) collective-permute-start(bf16[2,64,2048]{2,1,0:T(8,128)(2,1)} %get-tuple-element.242), channel_id=1, source_target_pairs={{0,4},{4,0},{1,5},{5,1},{2,6},{6,2},{3,7},{7,3},{8,12},{12,8},{9,1... | collective-permute-start | bytes 1572872 | tf_op jit(solution)/shard_map/ppermute | solution.py:514
  390.2 41.9 %collective-permute-start.65 = (bf16[6,64,2048]{2,1,0:T(8,128)(2,1)S(1)}, bf16[6,64,2048]{2,1,0:T(8,128)(2,1)S(1)}, u32[]{:S(2)}, u32[]{:S(2)}) collective-permute-start(bf16[6,64,2048]{2,1,0:T(8,128)(2,1)S(1)} %get-tuple-element.244.refs_6_), channel_id=1, source_target_pairs={{0,1},{1,0},{2,3},{3,2},{4,5},{5,4},{6,7},{7,6},{8,9},{9,8},{10,11... | collective-permute-start | bytes 4718600 | tf_op jit(solution)/shard_map/ppermute | solution.py:514
  390.7 41.4 %collective-permute-start.66 = (bf16[6,64,2048]{2,1,0:T(8,128)(2,1)}, bf16[6,64,2048]{2,1,0:T(8,128)(2,1)S(1)}, u32[]{:S(2)}, u32[]{:S(2)}) collective-permute-start(bf16[6,64,2048]{2,1,0:T(8,128)(2,1)} %get-tuple-element.256), channel_id=1, source_target_pairs={{0,4},{4,0},{1,5},{5,1},{2,6},{6,2},{3,7},{7,3},{8,12},{12,8},{9,1... | collective-permute-start | bytes 4718600 | tf_op jit(solution)/shard_map/ppermute | solution.py:514
  435.7 38.0 %collective-permute-start.71 = (bf16[6,64,2048]{2,1,0:T(8,128)(2,1)S(1)}, bf16[6,64,2048]{2,1,0:T(8,128)(2,1)S(1)}, u32[]{:S(2)}, u32[]{:S(2)}) collective-permute-start(bf16[6,64,2048]{2,1,0:T(8,128)(2,1)S(1)} %get-tuple-element.258.refs_10_), channel_id=1, source_target_pairs={{0,1},{1,0},{2,3},{3,2},{4,5},{5,4},{6,7},{7,6},{8,9},{9,8},{10,11... | collective-permute-start | bytes 4718600 | tf_op jit(solution)/shard_map/ppermute | solution.py:514
  435.8 37.9 %collective-permute-start.72 = (bf16[6,64,2048]{2,1,0:T(8,128)(2,1)}, bf16[6,64,2048]{2,1,0:T(8,128)(2,1)S(1)}, u32[]{:S(2)}, u32[]{:S(2)}) collective-permute-start(bf16[6,64,2048]{2,1,0:T(8,128)(2,1)} %get-tuple-element.272), channel_id=1, source_target_pairs={{0,4},{4,0},{1,5},{5,1},{2,6},{6,2},{3,7},{7,3},{8,12},{12,8},{9,1... | collective-permute-start | bytes 4718600 | tf_op jit(solution)/shard_map/ppermute | solution.py:514
  445.2 27.3 %collective-permute-start.73 = (bf16[64,2048]{1,0:T(8,128)(2,1)}, bf16[64,2048]{1,0:T(8,128)(2,1)S(1)}, u32[]{:S(2)}, u32[]{:S(2)}) collective-permute-start(bf16[64,2048]{1,0:T(8,128)(2,1)} %get-tuple-element.274), channel_id=1, source_target_pairs={{0,8},{8,0},{16,24},{24,16},{1,9},{9,1},{17,25},{25,17},{2,10},{10... | collective-permute-start | bytes 786440 | tf_op jit(solution)/shard_map/ppermute | solution.py:518
  447.0 26.6 %collective-permute-start.74 = (bf16[64,2048]{1,0:T(8,128)(2,1)}, bf16[64,2048]{1,0:T(8,128)(2,1)S(1)}, u32[]{:S(2)}, u32[]{:S(2)}) collective-permute-start(bf16[64,2048]{1,0:T(8,128)(2,1)} %get-tuple-element.275), channel_id=1, source_target_pairs={{0,16},{8,24},{16,0},{24,8},{1,17},{9,25},{17,1},{25,9},{2,18},{10... | collective-permute-start | bytes 786440 | tf_op jit(solution)/shard_map/ppermute | solution.py:518
  447.9 25.8 %collective-permute-start.75 = (bf16[64,2048]{1,0:T(8,128)(2,1)}, bf16[64,2048]{1,0:T(8,128)(2,1)S(1)}, u32[]{:S(2)}, u32[]{:S(2)}) collective-permute-start(bf16[64,2048]{1,0:T(8,128)(2,1)} %get-tuple-element.276), channel_id=1, source_target_pairs={{0,24},{8,16},{16,8},{24,0},{1,25},{9,17},{17,9},{25,1},{2,26},{10... | collective-permute-start | bytes 786440 | tf_op jit(solution)/shard_map/ppermute | solution.py:518
  477.9 38.1 %collective-permute-start.78 = (bf16[6,64,2048]{2,1,0:T(8,128)(2,1)S(1)}, bf16[6,64,2048]{2,1,0:T(8,128)(2,1)S(1)}, u32[]{:S(2)}, u32[]{:S(2)}) collective-permute-start(bf16[6,64,2048]{2,1,0:T(8,128)(2,1)S(1)} %get-tuple-element.278.refs_10_), channel_id=1, source_target_pairs={{0,1},{1,0},{2,3},{3,2},{4,5},{5,4},{6,7},{7,6},{8,9},{9,8},{10,11... | collective-permute-start | bytes 4718600 | tf_op jit(solution)/shard_map/ppermute | solution.py:514
  479.2 36.8 %collective-permute-start.79 = (bf16[6,64,2048]{2,1,0:T(8,128)(2,1)}, bf16[6,64,2048]{2,1,0:T(8,128)(2,1)S(1)}, u32[]{:S(2)}, u32[]{:S(2)}) collective-permute-start(bf16[6,64,2048]{2,1,0:T(8,128)(2,1)} %get-tuple-element.288), channel_id=1, source_target_pairs={{0,4},{4,0},{1,5},{5,1},{2,6},{6,2},{3,7},{7,3},{8,12},{12,8},{9,1... | collective-permute-start | bytes 4718600 | tf_op jit(solution)/shard_map/ppermute | solution.py:514
  492.0 24.1 %collective-permute-start.82 = (bf16[64,2048]{1,0:T(8,128)(2,1)S(1)}, bf16[64,2048]{1,0:T(8,128)(2,1)S(1)}, u32[]{:S(2)}, u32[]{:S(2)}) collective-permute-start(bf16[64,2048]{1,0:T(8,128)(2,1)S(1)} %get-tuple-element.292), channel_id=1, source_target_pairs={{0,24},{8,16},{16,8},{24,0},{1,25},{9,17},{17,9},{25,1},{2,26},{10... | collective-permute-start | bytes 786440 | tf_op jit(solution)/shard_map/ppermute | solution.py:518
  519.2 39.5 %collective-permute-start.85 = (bf16[6,64,2048]{2,1,0:T(8,128)(2,1)S(1)}, bf16[6,64,2048]{2,1,0:T(8,128)(2,1)S(1)}, u32[]{:S(2)}, u32[]{:S(2)}) collective-permute-start(bf16[6,64,2048]{2,1,0:T(8,128)(2,1)S(1)} %get-tuple-element.293.refs_4_), channel_id=1, source_target_pairs={{0,1},{1,0},{2,3},{3,2},{4,5},{5,4},{6,7},{7,6},{8,9},{9,8},{10,11... | collective-permute-start | bytes 4718600 | tf_op jit(solution)/shard_map/ppermute | solution.py:514
  519.3 39.5 %collective-permute-start.86 = (bf16[6,64,2048]{2,1,0:T(8,128)(2,1)S(1)}, bf16[6,64,2048]{2,1,0:T(8,128)(2,1)S(1)}, u32[]{:S(2)}, u32[]{:S(2)}) collective-permute-start(bf16[6,64,2048]{2,1,0:T(8,128)(2,1)S(1)} %get-tuple-element.303), channel_id=1, source_target_pairs={{0,4},{4,0},{1,5},{5,1},{2,6},{6,2},{3,7},{7,3},{8,12},{12,8},{9,1... | collective-permute-start | bytes 4718600 | tf_op jit(solution)/shard_map/ppermute | solution.py:514
  520.0 36.0 %collective-permute-start.87 = (bf16[64,2048]{1,0:T(8,128)(2,1)S(1)}, bf16[64,2048]{1,0:T(8,128)(2,1)S(1)}, u32[]{:S(2)}, u32[]{:S(2)}) collective-permute-start(bf16[64,2048]{1,0:T(8,128)(2,1)S(1)} %get-tuple-element.305), channel_id=1, source_target_pairs={{0,8},{8,0},{16,24},{24,16},{1,9},{9,1},{17,25},{25,17},{2,10},{10... | collective-permute-start | bytes 786440 | tf_op jit(solution)/shard_map/ppermute | solution.py:518
  520.9 37.8 %collective-permute-start.88 = (bf16[64,2048]{1,0:T(8,128)(2,1)S(1)}, bf16[64,2048]{1,0:T(8,128)(2,1)S(1)}, u32[]{:S(2)}, u32[]{:S(2)}) collective-permute-start(bf16[64,2048]{1,0:T(8,128)(2,1)S(1)} %get-tuple-element.306), channel_id=1, source_target_pairs={{0,16},{8,24},{16,0},{24,8},{1,17},{9,25},{17,1},{25,9},{2,18},{10... | collective-permute-start | bytes 786440 | tf_op jit(solution)/shard_map/ppermute | solution.py:518
  521.8 37.0 %collective-permute-start.89 = (bf16[64,2048]{1,0:T(8,128)(2,1)S(1)}, bf16[64,2048]{1,0:T(8,128)(2,1)S(1)}, u32[]{:S(2)}, u32[]{:S(2)}) collective-permute-start(bf16[64,2048]{1,0:T(8,128)(2,1)S(1)} %get-tuple-element.307), channel_id=1, source_target_pairs={{0,24},{8,16},{16,8},{24,0},{1,25},{9,17},{17,9},{25,1},{2,26},{10... | collective-permute-start | bytes 786440 | tf_op jit(solution)/shard_map/ppermute | solution.py:518
  556.1 20.7 %collective-permute-start.83 = (bf16[320,1024]{1,0:T(8,128)(2,1)S(1)}, bf16[320,1024]{1,0:T(8,128)(2,1)S(1)}, u32[]{:S(2)}, u32[]{:S(2)}) collective-permute-start(bf16[320,1024]{1,0:T(8,128)(2,1)S(1)} %get-tuple-element.295.refs_11_), channel_id=1, source_target_pairs={{0,2},{2,0},{1,3},{3,1},{4,6},{6,4},{5,7},{7,5},{8,10},{10,8},{9,1... | collective-permute-start | bytes 1966088 | tf_op jit(solution)/shard_map/ppermute | solution.py:514
  558.7 18.5 %collective-permute-start.84 = (bf16[320,1024]{1,0:T(8,128)(2,1)}, bf16[320,1024]{1,0:T(8,128)(2,1)}, u32[]{:S(2)}, u32[]{:S(2)}) collective-permute-start(bf16[320,1024]{1,0:T(8,128)(2,1)} %get-tuple-element.296), channel_id=1, source_target_pairs={{0,2},{2,0},{1,3},{3,1},{4,6},{6,4},{5,7},{7,5},{8,10},{10,8},{9,1... | collective-permute-start | bytes 1966088 | tf_op jit(solution)/shard_map/ppermute | solution.py:514
  563.9 55.8 %collective-permute-start.93 = (bf16[6,64,2048]{2,1,0:T(8,128)(2,1)}, bf16[6,64,2048]{2,1,0:T(8,128)(2,1)}, u32[]{:S(2)}, u32[]{:S(2)}) collective-permute-start(bf16[6,64,2048]{2,1,0:T(8,128)(2,1)} %get-tuple-element.309.refs_9_), channel_id=1, source_target_pairs={{0,1},{1,0},{2,3},{3,2},{4,5},{5,4},{6,7},{7,6},{8,9},{9,8},{10,11... | collective-permute-start | bytes 4718600 | tf_op jit(solution)/shard_map/ppermute | solution.py:514
  565.4 54.3 %collective-permute-start.94 = (bf16[6,64,2048]{2,1,0:T(8,128)(2,1)}, bf16[6,64,2048]{2,1,0:T(8,128)(2,1)}, u32[]{:S(2)}, u32[]{:S(2)}) collective-permute-start(bf16[6,64,2048]{2,1,0:T(8,128)(2,1)} %get-tuple-element.323), channel_id=1, source_target_pairs={{0,4},{4,0},{1,5},{5,1},{2,6},{6,2},{3,7},{7,3},{8,12},{12,8},{9,1... | collective-permute-start | bytes 4718600 | tf_op jit(solution)/shard_map/ppermute | solution.py:514
  574.7 25.6 %collective-permute-start.90 = (bf16[64,2048]{1,0:T(8,128)(2,1)}, bf16[64,2048]{1,0:T(8,128)(2,1)}, u32[]{:S(2)}, u32[]{:S(2)}) collective-permute-start(bf16[64,2048]{1,0:T(8,128)(2,1)} %get-tuple-element.316), channel_id=1, source_target_pairs={{0,8},{8,0},{16,24},{24,16},{1,9},{9,1},{17,25},{25,17},{2,10},{10... | collective-permute-start | bytes 786440 | tf_op jit(solution)/shard_map/ppermute | solution.py:518
  576.8 23.5 %collective-permute-start.91 = (bf16[64,2048]{1,0:T(8,128)(2,1)}, bf16[64,2048]{1,0:T(8,128)(2,1)}, u32[]{:S(2)}, u32[]{:S(2)}) collective-permute-start(bf16[64,2048]{1,0:T(8,128)(2,1)} %get-tuple-element.317), channel_id=1, source_target_pairs={{0,16},{8,24},{16,0},{24,8},{1,17},{9,25},{17,1},{25,9},{2,18},{10... | collective-permute-start | bytes 786440 | tf_op jit(solution)/shard_map/ppermute | solution.py:518
  577.1 23.5 %collective-permute-start.92 = (bf16[64,2048]{1,0:T(8,128)(2,1)}, bf16[64,2048]{1,0:T(8,128)(2,1)}, u32[]{:S(2)}, u32[]{:S(2)}) collective-permute-start(bf16[64,2048]{1,0:T(8,128)(2,1)} %get-tuple-element.318), channel_id=1, source_target_pairs={{0,24},{8,16},{16,8},{24,0},{1,25},{9,17},{17,9},{25,1},{2,26},{10... | collective-permute-start | bytes 786440 | tf_op jit(solution)/shard_map/ppermute | solution.py:518
  628.4 25.5 %collective-permute-start.95 = (bf16[4,64,2048]{2,1,0:T(8,128)(2,1)S(1)}, bf16[4,64,2048]{2,1,0:T(8,128)(2,1)S(1)}, u32[]{:S(2)}, u32[]{:S(2)}) collective-permute-start(bf16[4,64,2048]{2,1,0:T(8,128)(2,1)S(1)} %get-tuple-element.325.refs_8_), channel_id=1, source_target_pairs={{0,1},{1,0},{2,3},{3,2},{4,5},{5,4},{6,7},{7,6},{8,9},{9,8},{10,11... | collective-permute-start | bytes 3145736 | tf_op jit(solution)/shard_map/ppermute | solution.py:514
  628.7 25.1 %collective-permute-start.96 = (bf16[4,64,2048]{2,1,0:T(8,128)(2,1)S(1)}, bf16[4,64,2048]{2,1,0:T(8,128)(2,1)S(1)}, u32[]{:S(2)}, u32[]{:S(2)}) collective-permute-start(bf16[4,64,2048]{2,1,0:T(8,128)(2,1)S(1)} %get-tuple-element.326), channel_id=1, source_target_pairs={{0,4},{4,0},{1,5},{5,1},{2,6},{6,2},{3,7},{7,3},{8,12},{12,8},{9,1... | collective-permute-start | bytes 3145736 | tf_op jit(solution)/shard_map/ppermute | solution.py:514
  631.4 22.4 %collective-permute-start.99 = (bf16[64,2048]{1,0:T(8,128)(2,1)S(1)}, bf16[64,2048]{1,0:T(8,128)(2,1)S(1)}, u32[]{:S(2)}, u32[]{:S(2)}) collective-permute-start(bf16[64,2048]{1,0:T(8,128)(2,1)S(1)} %get-tuple-element.330), channel_id=1, source_target_pairs={{0,24},{8,16},{16,8},{24,0},{1,25},{9,17},{17,9},{25,1},{2,26},{10... | collective-permute-start | bytes 786440 | tf_op jit(solution)/shard_map/ppermute | solution.py:518
  656.7 33.4 %collective-permute-start.100 = (bf16[640,1024]{1,0:T(8,128)(2,1)S(1)}, bf16[640,1024]{1,0:T(8,128)(2,1)S(1)}, u32[]{:S(2)}, u32[]{:S(2)}) collective-permute-start(bf16[640,1024]{1,0:T(8,128)(2,1)S(1)} %copy_rows.5.refs_6_), channel_id=1, source_target_pairs={{1,2},{2,1},{5,6},{6,5},{9,10},{10,9},{13,14},{14,13},{17,18},{18,... | collective-permute-start | bytes 3932168 | tf_op jit(solution)/shard_map/ppermute | solution.py:522
  662.4 47.5 %collective-permute-start.109 = (bf16[64,10240]{1,0:T(8,128)(2,1)S(1)}, bf16[64,10240]{1,0:T(8,128)(2,1)S(1)}, u32[]{:S(2)}, u32[]{:S(2)}) collective-permute-start(bf16[64,10240]{1,0:T(8,128)(2,1)S(1)} %join_pieces.1.refs_3_), channel_id=1, source_target_pairs={{1,2},{2,1},{5,6},{6,5},{9,10},{10,9},{13,14},{14,13},{17,18},{18,... | collective-permute-start | bytes 3932168 | tf_op jit(solution)/shard_map/ppermute | solution.py:522
  667.2 19.5 %collective-permute-start.106 = (bf16[64,2048]{1,0:T(8,128)(2,1)S(1)}, bf16[64,2048]{1,0:T(8,128)(2,1)S(1)}, u32[]{:S(2)}, u32[]{:S(2)}) collective-permute-start(bf16[64,2048]{1,0:T(8,128)(2,1)S(1)} %get-tuple-element.338), channel_id=1, source_target_pairs={{0,16},{8,24},{16,0},{24,8},{1,17},{9,25},{17,1},{25,9},{2,18},{10... | collective-permute-start | bytes 786440 | tf_op jit(solution)/shard_map/ppermute | solution.py:518
  671.1 30.9 %collective-permute-start.107 = (bf16[64,2048]{1,0:T(8,128)(2,1)S(1)}, bf16[64,2048]{1,0:T(8,128)(2,1)S(1)}, u32[]{:S(2)}, u32[]{:S(2)}) collective-permute-start(bf16[64,2048]{1,0:T(8,128)(2,1)S(1)} %get-tuple-element.339), channel_id=1, source_target_pairs={{0,24},{8,16},{16,8},{24,0},{1,25},{9,17},{17,9},{25,1},{2,26},{10... | collective-permute-start | bytes 786440 | tf_op jit(solution)/shard_map/ppermute | solution.py:518
  676.5 28.4 %collective-permute-start.102 = (f32[208,256]{1,0:T(8,128)S(1)}, f32[208,256]{1,0:T(8,128)S(1)}, u32[]{:S(2)}, u32[]{:S(2)}) collective-permute-start(f32[208,256]{1,0:T(8,128)S(1)} %add_all.5.refs_5_.refs_1_), channel_id=1, source_target_pairs={{0,8},{8,0},{16,24},{24,16},{1,9},{9,1},{17,25},{25,17},{2,10},{10... | collective-permute-start | bytes 638984 | tf_op jit(solution)/shard_map/ppermute | solution.py:518
  686.8 18.7 %collective-permute-start.103 = (f32[208,256]{1,0:T(8,128)S(1)}, f32[208,256]{1,0:T(8,128)S(1)}, u32[]{:S(2)}, u32[]{:S(2)}) collective-permute-start(f32[208,256]{1,0:T(8,128)S(1)} %add_all.5.refs_5_.refs_1_), channel_id=1, source_target_pairs={{0,16},{8,24},{16,0},{24,8},{1,17},{9,25},{17,1},{25,9},{2,18},{10... | collective-permute-start | bytes 638984 | tf_op jit(solution)/shard_map/ppermute | solution.py:518
  690.1 19.1 %collective-permute-start.104 = (f32[208,256]{1,0:T(8,128)S(1)}, f32[208,256]{1,0:T(8,128)S(1)}, u32[]{:S(2)}, u32[]{:S(2)}) collective-permute-start(f32[208,256]{1,0:T(8,128)S(1)} %add_all.5.refs_5_.refs_1_), channel_id=1, source_target_pairs={{0,24},{8,16},{16,8},{24,0},{1,25},{9,17},{17,9},{25,1},{2,26},{10... | collective-permute-start | bytes 638984 | tf_op jit(solution)/shard_map/ppermute | solution.py:518
  (218 other events, 2325.1 us)

commit v5 on v4

--- a/solution.py
+++ b/solution.py
@@ -938,6 +938,44 @@
             self.done.append(results[0])
 
 
+def offset_columns():
+    cells = np.arange(WIN_T * WIN_T)
+    spots = 119 - (cells // WIN_T * 16 + cells % WIN_T)
+    hot = (spots[:, None] == np.arange(256)[None, :]).astype(np.float32)
+    return jnp.asarray(np.concatenate([hot] * 3), low)
+
+
+def bias_tables(chain, sums):
+    heads, sides = sums[0].shape[:2]
+
+    def kernel(info, *refs):
+        hot = refs[len(sums)][...]
+        for at, out in enumerate(refs[len(sums) + 1 :]):
+            for h in range(heads):
+                values = refs[at][h].reshape(sides * 64, 64)
+                first = values.astype(low)
+                rest = values - first.astype(full)
+                second = rest.astype(low)
+                third = (rest - second.astype(full)).astype(low)
+                parts = jnp.concatenate([first, second, third], axis=1)
+                spread = jnp.dot(parts, hot, preferred_element_type=full)
+                spread = spread.reshape(sides, 8, 8, 256)
+                by_row = spread[:, 0]
+                for row in range(1, 8):
+                    by_row = by_row + pltpu.roll(spread[:, row], 16 * row, 2)
+                total = by_row[:, 0]
+                for col in range(1, 8):
+                    total = total + pltpu.roll(by_row[:, col], col, 1)
+                out[h] = total
+
+    hot = offset_columns()
+    args = list(sums) + [hot]
+    outs = [shape_of((heads, sides, 256), full)] * len(sums)
+    return chain.run(
+        "bias_tables", kernel, args, [whole(v) for v in args], outs, [whole(v) for v in outs], extra=8
+    )
+
+
 def collect_sums(chain, sums):
     spots = [(4, 0), (4, 1), (3, 2), (3, 0), (3, 1), (2, 2), (2, 0), (2, 1), (1, 2), (1, 0), (1, 1), (0, 0)]
 
@@ -955,15 +993,20 @@
 def add_all(chain, *values):
     def kernel(info, *refs):
         total = refs[0][...]
-        for other in refs[1:-1]:
-            total = total + other[...]
-        refs[-1][...] = total
-
-    out = shape_of(values[0].shape, full)
-    (result,) = chain.run(
-        "add_all", kernel, list(values), [whole(a) for a in values], [out], [whole(out)]
-    )
-    return result
+        for other in refs[1:-2]:
+            total = total + other[...].astype(full)
+        refs[-2][...] = total
+        refs[-1][...] = total.astype(low)
+
+    outs = [shape_of(values[0].shape, full), shape_of(values[0].shape)]
+    return chain.run(
+        "add_all",
+        kernel,
+        list(values),
+        [whole(v) for v in values],
+        outs,
+        [whole(v) for v in outs],
+    )
 
 
 def join_pieces(chain, pieces, *copied):
@@ -1022,7 +1065,7 @@
     depth = weight.shape[0]
     rows = 2 * ROW_TILE
     width = weight.shape[1]
-    tile = 256 if kind == "gelu" else 512
+    tile = 512
     out_spec = pl.BlockSpec((2, rows, tile), lambda j, info: (0, 0, j))
     extra = [] if slope is None else [slope]
     count = 2 if kind == "gelu" else 1
@@ -1591,10 +1634,6 @@
     traded_final = swap(final)
 
     exact = lax.Precision.HIGHEST
-    hot_wide = jnp.pad(hot.astype(full), ((0, 256 - wide * wide), (0, 0)))
-    table_sums = lambda sums: jnp.dot(
-        sums.reshape(heads * 9, 64 * 64), hot_wide.T, precision=exact
-    )
 
     state = traded_cotangent
     own_g, sums_a = first_back(chain, state, branch_two_1, rows_of((1, 5)))
@@ -1612,7 +1651,6 @@
     scatter.step(6)
     (mixed_g,) = both_times(chain, "plain", own_g, other_g, out_1)
     back, joint_sums = attend_back(chain, joined_1, windowed(mixed_g), probs_1, True)
-    joint_tables = table_sums(joint_sums)
     back = back.reshape(2, rows, 3 * width)
     away = other_rows(chain, back, qkv_1)
     scatter.weight_grad((moved_2, other_2, back), (own_g, other_g, mixed_1))
@@ -1638,6 +1676,7 @@
     away = other_rows(chain, back, qkv_0)
     scatter.weight_grad((moved_0, other_0, back), (own_g, other_g, mixed_0))
     scatter.step(6)
+    spatial_tables, joint_tables = bias_tables(chain, [spatial_sums, joint_sums])
     state, sums_e = backward_step(
         chain, back, qkv_0, away, normed_0, inverse_0, state, rows_of((0, 1)), None
     )
@@ -1653,32 +1692,36 @@
     grad_ada_bias = jnp.sum(cols, axis=0)
     grad_activity = jnp.einsum("cbe,bde->cd", cols, ada_weight.astype(full), precision=exact)
 
-    near = spatial_sums.reshape(heads, 3, 3, 64, 64)
-    near = jnp.where(c == 0, near, near[:, ::-1]).reshape(heads, 9, 64, 64)
-    tables = jnp.concatenate([table_sums(near), joint_tables])
+    near = spatial_tables.reshape(heads, 3, 3, 256)
+    near = jnp.where(c == 0, near, near[:, ::-1])
+    tables = jnp.concatenate(
+        [near.reshape(heads * 9, 256), joint_tables.reshape(heads * 9, 256)]
+    )
 
     shared = jnp.concatenate([grad_activity.reshape(-1, 256), tables])
-    chain.wait(shared)
+    chain.wait(cols)
     scatter.step(6)
     scatter.step(6)
-    shared = add_all(chain, shared)
-    sent = flip(shared, "y")
+    shared, sent = add_all(chain, shared)
+    sent = flip(sent, "y")
     traded_state = swap(copy_rows(chain, state))
     (early,) = join_pieces(chain, scatter.done)
     early = swap(early)
-    shared = add_all(chain, shared, sent)
-    sent = [z_trade(shared, k) for k in (1, 2, 3)]
+    shared, sent = add_all(chain, shared, sent)
+    sent = [z_trade(sent, k) for k in (1, 2, 3)]
     chain.wait(traded_state)
     scatter.step(6)
-    late = swap(scatter.done[5]).astype(full)
-    shared = add_all(chain, shared, *sent)
-    sent = flip(shared, "x")
-    chain.wait(early)
-    shared = add_all(chain, shared, sent)
-    tables = shared[-heads * 18 :]
-    across = flip(shared, "c")
+    traded_late = swap_only(scatter.done[5])
+    late = jnp.where(c == x, scatter.done[5], traded_late).astype(full)
+    chain.wait(early, traded_late)
+    shared, sent = add_all(chain, shared, *sent)
+    over_x = flip(sent, "x").astype(full)
+    over_c = flip(sent, "c").astype(full)
+    over_both = lax.ppermute(sent, ("c", "x"), [(0, 3), (1, 2), (2, 1), (3, 0)]).astype(full)
+    shared = shared + over_x
+    across = over_c + over_both
     grad_activity = (shared + across)[: -heads * 18].reshape(16, model_width)
-    tables = jnp.where(c == x, tables, across[-heads * 18 :])[:, : wide * wide]
+    tables = jnp.where(c == x, shared[-heads * 18 :], across[-heads * 18 :])
     grad_latents = restored(traded_state)
     done = early.astype(full)
     piece = lambda at: done[:, at * PIECE : (at + 1) * PIECE]
@@ -1687,7 +1730,7 @@
     grad_qkv = jnp.stack([late[:, : 3 * width], piece(2)[:, : 3 * width]])
     grad_out = jnp.stack([late[:, 3 * width :].T, piece(2)[:, 3 * width :].T])
 
-    tables = tables.reshape(2, heads, 9, wide, wide)
+    tables = tables.reshape(2, heads, 9, 16, 16)[..., :wide, :wide]
     grad_joint = tables[1].reshape(heads, 9 * wide * wide)
     near = tables[0].reshape(heads, 3, 3, wide, wide)
     long = 2 * WIN_S - 1

time: 732 us -> 726 us (level)
  waiting for transfers between devices: 172 us -> 157 us
  blocking collectives: 0 us -> 9.58 us
  starting transfers between devices: 119 us -> 128 us
  matrix products: 15.1 us -> 6.25 us
    ppermute x39, waiting for transfers between devices: 112 us -> 85.4 us  [z_trade(): lax.ppermute(values, 'z', [(place, place ^ step) for place in range(4)])]
    ppermute x9, waiting for transfers between devices: 10.5 us -> 26.6 us  [swap_only(): return lax.ppermute(values, ('c', 'x'), [(1, 2), (2, 1)])]
    all_to_all x0 -> x1, blocking collectives: none -> 9.58 us  [fast_local(): lax.all_to_all(ordered, everyone, split_axis=0, concat_axis=0, tiled=True)]
    ppermute x64, starting transfers between devices: 40.6 us -> 49.1 us  [flip(): return lax.ppermute(values, axis, [(0, 1), (1, 0)])]
    ppermute x39, starting transfers between devices: 39.8 us -> 48.2 us  [z_trade(): lax.ppermute(values, 'z', [(place, place ^ step) for place in range(4)])]
    dot_general x2 -> x0, matrix products: 8.18 us -> none  [fast_local(): jnp.dot(sums.reshape(heads * 9, 64 * 64), hot_wide.T, precision=exact)]
    unnamed x336 -> x350, local copies, waits for them, and re-layouts: 42.1 us -> 43.7 us
  transfers between devices with their start and end apart: 114 -> 114, of which waited for: 47 -> 43; matrix products, arithmetic and copies ran while one was open for 8% -> 6% of each run, Pallas kernels for 42% -> 41%
where the time goes in v5:
time: 726 us; the launch traced here: 721 us
  Pallas kernels  330 us (45%)
  waiting for transfers between devices  157 us (22%)
  starting transfers between devices  128 us (18%)
  local copies, waits for them, and re-layouts  65.8 us (9%)
  other arithmetic  19.4 us (3%)
  blocking collectives  9.58 us (1%)
    pallas_call x68, Pallas kernels, run(): pl.pallas_call(body, grid_spec=pltpu.PrefetchScalarGridSpec(num_scalar_pr...  330 us
    ppermute x39, waiting for transfers between devices, z_trade(): lax.ppermute(values, 'z', [(place, place ^ step) for place in range(4)])  85.4 us
    ppermute x64, starting transfers between devices, flip(): return lax.ppermute(values, axis, [(0, 1), (1, 0)])  49.1 us
    ppermute x39, starting transfers between devices, z_trade(): lax.ppermute(values, 'z', [(place, place ^ step) for place in range(4)])  48.2 us
    unnamed x350, local copies, waits for them, and re-layouts  43.7 us
    ppermute x64, waiting for transfers between devices, flip(): return lax.ppermute(values, axis, [(0, 1), (1, 0)])  40.4 us
    ppermute x9, waiting for transfers between devices, swap_only(): return lax.ppermute(values, ('c', 'x'), [(1, 2), (2, 1)])  26.6 us
    ppermute x9, starting transfers between devices, swap_only(): return lax.ppermute(values, ('c', 'x'), [(1, 2), (2, 1)])  25.4 us
  transfers between devices with their start and end apart: 114, of which 43 were waited for; matrix products, arithmetic and copies ran while one was open for 6% of the time, Pallas kernels for 41%

profile of v5, /device:TPU:9, one launch (start us, length us, event | category | flops | bytes accessed | tf_op | source)
XLA Modules:
  0.0 721.0 jit_solution(11931585891543005230)
XLA Ops:
  14.2 5.7 all-to-all-start
  21.6 4.3 all-to-all-done
  33.8 16.1 %collective-permute-done.6.refs_4_ = bf16[64,2048]{1,0:T(8,128)(2,1)S(1)} collective-permute-done((bf16[64,2048]{1,0:T(8,128)(2,1)S(1)}, bf16[64,2048]{1,0:T(8,128)(2,1)S(1)}, u32[]{:S(2)}, u32[]{:S(2)}) %collective-permute-start.6) | collective-permute-done | bytes 262176 | tf_op jit(solution)/shard_map/ppermute | solution.py:518
  59.4 3.7 collective-permute-start.9
  66.9 12.3 %collective-permute-done.12.refs_6_.refs_3_ = bf16[4,64,2048]{2,1,0:T(8,128)(2,1)S(1)} collective-permute-done((bf16[4,64,2048]{2,1,0:T(8,128)(2,1)}, bf16[4,64,2048]{2,1,0:T(8,128)(2,1)S(1)}, u32[]{:S(2)}, u32[]{:S(2)}) %collective-permute-start.12) | collective-permute-done | bytes 1048608 | tf_op jit(solution)/shard_map/ppermute | solution.py:514
  81.5 4.5 gather_step.8
  98.0 4.1 collective-permute-start.18
  102.1 5.2 collective-permute-done.7.refs_2_
  111.6 3.4 collective-permute-done.19.refs_4_
  115.0 4.4 collective-permute-done.18.refs_3_
  120.9 8.8 %collective-permute-done.15.refs_5_.refs_4_.refs_2_ = bf16[6,64,2048]{2,1,0:T(8,128)(2,1)} collective-permute-done((bf16[6,64,2048]{2,1,0:T(8,128)(2,1)}, bf16[6,64,2048]{2,1,0:T(8,128)(2,1)}, u32[]{:S(2)}, u32[]{:S(2)}) %collective-permute-start.15) | collective-permute-done | bytes 1572896 | tf_op jit(solution)/shard_map/ppermute | solution.py:514
  141.7 3.2 place_weights.6
  145.0 5.8 both_plain.4.refs_3_
  150.7 14.6 %attend_spatial.1 = (bf16[2,5,2,64,512]{4,3,2,1,0:T(8,128)(2,1)S(1)}, bf16[5,8,256,256]{3,2,1,0:T(8,128)(2,1)S(1)}) custom-call(s32[5]{0:T(128)S(1)} %concatenate.13.refs_0_, bf16[8,9,64,64]{3,2,1,0:T(8,128)(2,1)S(1)} %bitcast.197, bf16[2,5,2,64,1536]{4,3,2,1,0:T(8,128)(2,1)S(1)} %bitcast.170, bf16[2,640,1536]{2,1,0:T(8,128)(2,1)S(1)} %both_plain.4.refs_3_), custom_call_target="tpu_custom_call" | custom-call | flops 1 | bytes 1 | tf_op jit(solution)/shard_map/attend_spatial/pallas_call | solution.py:583
  177.5 3.5 forward_step.4
  188.5 16.0 %both_gelu.2 = (bf16[2,640,2048]{2,1,0:T(8,128)(2,1)S(1)}, bf16[2,640,2048]{2,1,0:T(8,128)(2,1)S(1)}) custom-call(s32[5]{0:T(128)S(1)} %concatenate.13.refs_0_, bf16[320,1024]{1,0:T(8,128)(2,1)S(1)} %get-tuple-element.202.refs_1_, bf16[320,1024]{1,0:T(8,128)(2,1)S(1)} %get-tuple-element.203.refs_2_, bf16[320,1024]{1,0:T(8,128)(2,1)S(1)} %collective-permute-done.27.refs_3_, ...), custom_call_target="tpu_custom_call" | custom-call | flops 1 | bytes 1 | tf_op jit(solution)/shard_map/both_gelu/pallas_call | solution.py:583
  212.7 4.2 other_rows.9
  223.5 5.1 forward_step.5
  229.6 8.3 %collective-permute-done.42.refs_4_ = bf16[64,2048]{1,0:T(8,128)(2,1)S(1)} collective-permute-done((bf16[64,2048]{1,0:T(8,128)(2,1)S(1)}, bf16[64,2048]{1,0:T(8,128)(2,1)S(1)}, u32[]{:S(2)}, u32[]{:S(2)}) %collective-permute-start.42) | collective-permute-done | bytes 262176 | tf_op jit(solution)/shard_map/ppermute | solution.py:518
  237.9 4.3 collective-permute-done.41.refs_3_
  247.8 3.3 collective-permute-start.36
  253.8 5.7 both_plain.5.refs_3_
  259.5 16.2 %attend_joint.1 = (bf16[2,5,2,64,512]{4,3,2,1,0:T(8,128)(2,1)S(1)}, bf16[4,8,320,320]{3,2,1,0:T(8,128)(2,1)S(1)}) custom-call(s32[5]{0:T(128)S(1)} %concatenate.13.refs_0_, bf16[8,9,64,64]{3,2,1,0:T(8,128)(2,1)S(1)} %squeeze.38.refs_6_.refs_1_, bf16[2,5,2,64,1536]{4,3,2,1,0:T(8,128)(2,1)S(1)} %bitcast.172, bf16[2,640,1536]{2,1,0:T(8,128)(2,1)S(1)} %both_plain.5.refs_3_), custom_call_target="tpu_custom_call" | custom-call | flops 1 | bytes 1 | tf_op jit(solution)/shard_map/attend_joint/pallas_call | solution.py:583
  275.8 3.1 copy-done.22
  293.0 16.0 %both_gelu.3 = (bf16[2,640,2048]{2,1,0:T(8,128)(2,1)S(1)}, bf16[2,640,2048]{2,1,0:T(8,128)(2,1)S(1)}) custom-call(s32[5]{0:T(128)S(1)} %concatenate.13.refs_0_, bf16[320,1024]{1,0:T(8,128)(2,1)S(1)} %get-tuple-element.224.refs_1_, bf16[320,1024]{1,0:T(8,128)(2,1)S(1)} %get-tuple-element.225.refs_2_, bf16[320,1024]{1,0:T(8,128)(2,1)S(1)} %collective-permute-done.47.refs_3_, ...), custom_call_target="tpu_custom_call" | custom-call | flops 1 | bytes 1 | tf_op jit(solution)/shard_map/both_gelu/pallas_call | solution.py:583
  315.1 4.2 other_rows.11
  322.4 4.2 forward_step.7
  338.7 8.1 %both_slope.2.refs_1_.refs_3_.refs_5_ = bf16[2,640,2048]{2,1,0:T(8,128)(2,1)S(1)} custom-call(s32[5]{0:T(128)S(1)} %concatenate.13.refs_0_, bf16[320,1024]{1,0:T(8,128)(2,1)S(1)} %get-tuple-element.233.refs_1_.refs_7_, bf16[320,1024]{1,0:T(8,128)(2,1)S(1)} %get-tuple-element.234.refs_2_, bf16[320,1024]{1,0:T(8,128)(2,1)S(1)} %collective-permute-done.55.refs_3_, ...), custom_call_target="tpu_custom_call" | custom-call | flops 1 | bytes 1 | tf_op jit(solution)/shard_map/both_slope/pallas_call | solution.py:583
  346.8 4.2 other_rows.12
  351.6 9.2 %weight_grad.6 = (bf16[4,64,2048]{2,1,0:T(8,128)(2,1)S(1)}, bf16[4,64,2048]{2,1,0:T(8,128)(2,1)S(1)}, bf16[4,64,2048]{2,1,0:T(8,128)(2,1)S(1)}, bf16[2,64,2048]{2,1,0:T(8,128)(2,1)S(1)}, bf16[2,64,2048]{2,1,0:T(8,128)(2,1)S(1)}) custom-call(s32[5]{0:T(128)S(1)} %concatenate.13.refs_0_, bf16[320,1024]{1,0:T(8,128)(2,1)S(1)} %get-tuple-element.233.refs_1_.refs_7_, ...), custom_call_target="tpu_custom_call" | custom-call | flops 1 | bytes 1 | tf_op jit(solution)/shard_map/weight_grad/pallas_call | solution.py:583
  364.6 6.3 backward_step.4
  371.6 9.2 %weight_grad.7 = (bf16[4,64,2048]{2,1,0:T(8,128)(2,1)S(1)}, bf16[4,64,2048]{2,1,0:T(8,128)(2,1)S(1)}, bf16[4,64,2048]{2,1,0:T(8,128)(2,1)S(1)}, bf16[2,64,2048]{2,1,0:T(8,128)(2,1)S(1)}, bf16[2,64,2048]{2,1,0:T(8,128)(2,1)S(1)}) custom-call(s32[5]{0:T(128)S(1)} %concatenate.13.refs_0_, bf16[320,1024]{1,0:T(8,128)(2,1)S(1)} %copy-done.63, ...), custom_call_target="tpu_custom_call" | custom-call | flops 1 | bytes 1 | tf_op jit(solution)/shard_map/weight_grad/pallas_call | solution.py:583
  381.8 3.3 scatter_step.8
  392.6 18.8 %attend_back_joint.1 = (bf16[2,5,2,64,1536]{4,3,2,1,0:T(8,128)(2,1)S(1)}, f32[8,9,64,64]{3,2,1,0:T(8,128)S(1)}) custom-call(s32[5]{0:T(128)S(1)} %concatenate.13.refs_0_, bf16[2,5,2,64,1536]{4,3,2,1,0:T(8,128)(2,1)S(1)} %bitcast.173, bf16[2,5,2,64,512]{4,3,2,1,0:T(8,128)(2,1)S(1)} %bitcast.195, bf16[4,8,320,320]{3,2,1,0:T(8,128)(2,1)S(1)} %bitcast.205, ...), custom_call_target="tpu_custom_call" | custom-call | flops 1 | bytes 1 | tf_op jit(solution)/shard_map/attend_back_joint/pallas_call | solution.py:583
  411.4 3.5 other_rows.13
  415.5 10.5 %weight_grad.8 = (bf16[4,64,2048]{2,1,0:T(8,128)(2,1)S(1)}, bf16[4,64,2048]{2,1,0:T(8,128)(2,1)S(1)}, bf16[4,64,2048]{2,1,0:T(8,128)(2,1)S(1)}, bf16[2,64,2048]{2,1,0:T(8,128)(2,1)S(1)}, bf16[2,64,2048]{2,1,0:T(8,128)(2,1)S(1)}) custom-call(s32[5]{0:T(128)S(1)} %concatenate.13.refs_0_, bf16[320,1024]{1,0:T(8,128)(2,1)S(1)} %copy-done.47, ...), custom_call_target="tpu_custom_call" | custom-call | flops 1 | bytes 1 | tf_op jit(solution)/shard_map/weight_grad/pallas_call | solution.py:583
  426.2 3.5 scatter_step.9
  431.2 5.5 backward_step.5
  445.3 8.1 %both_slope.3.refs_1_.refs_3_.refs_5_ = bf16[2,640,2048]{2,1,0:T(8,128)(2,1)S(1)} custom-call(s32[5]{0:T(128)S(1)} %concatenate.13.refs_0_, bf16[320,1024]{1,0:T(8,128)(2,1)S(1)} %get-tuple-element.267.refs_1_, bf16[320,1024]{1,0:T(8,128)(2,1)S(1)} %get-tuple-element.268.refs_2_, bf16[320,1024]{1,0:T(8,128)(2,1)S(1)} %collective-permute-done.67.refs_3_, ...), custom_call_target="tpu_custom_call" | custom-call | flops 1 | bytes 1 | tf_op jit(solution)/shard_map/both_slope/pallas_call | solution.py:583
  453.4 4.2 other_rows.14
  457.6 9.2 %weight_grad.9 = (bf16[4,64,2048]{2,1,0:T(8,128)(2,1)S(1)}, bf16[4,64,2048]{2,1,0:T(8,128)(2,1)S(1)}, bf16[4,64,2048]{2,1,0:T(8,128)(2,1)S(1)}, bf16[2,64,2048]{2,1,0:T(8,128)(2,1)S(1)}, bf16[2,64,2048]{2,1,0:T(8,128)(2,1)S(1)}) custom-call(s32[5]{0:T(128)S(1)} %concatenate.13.refs_0_, bf16[320,1024]{1,0:T(8,128)(2,1)S(1)} %get-tuple-element.267.refs_1_, ...), custom_call_target="tpu_custom_call" | custom-call | flops 1 | bytes 1 | tf_op jit(solution)/shard_map/weight_grad/pallas_call | solution.py:583
  468.0 4.2 scatter_step.10
  474.0 6.3 backward_step.6
  485.4 9.4 %weight_grad.10 = (bf16[4,64,2048]{2,1,0:T(8,128)(2,1)S(1)}, bf16[4,64,2048]{2,1,0:T(8,128)(2,1)S(1)}, bf16[4,64,2048]{2,1,0:T(8,128)(2,1)S(1)}, bf16[2,64,2048]...) custom-call(s32[5]{0:T(128)S(1)} %concatenate.13.refs_0_, bf16[320,1024]{1,0:T(8,128)(2,1)S(1)} %copy-done.55, ...), custom_call_target="tpu_custom_call" | custom-call | flops 1 | bytes 1 | tf_op jit(solution)/shard_map/weight_grad/pallas_call | solution.py:583
  497.9 3.4 collective-permute-done.81.refs_10_
  501.3 7.0 collective-permute-done.82.refs_11_
  508.4 3.5 scatter_step.11
  516.1 17.9 %attend_back_spatial.1 = (bf16[2,5,2,64,1536]{4,3,2,1,0:T(8,128)(2,1)S(1)}, f32[8,9,64,64]{3,2,1,0:T(8,128)S(1)}) custom-call(s32[5]{0:T(128)S(1)} %concatenate.13.refs_0_, bf16[2,5,2,64,1536]{4,3,2,1,0:T(8,128)(2,1)S(1)} %bitcast.171, bf16[2,5,2,64,512]{4,3,2,1,0:T(8,128)(2,1)S(1)} %bitcast.192, bf16[5,8,256,256]{3,2,1,0:T(8,128)(2,1)S(1)} %bitcast.207, ...), custom_call_target="tpu_custom_call" | custom-call | flops 1 | bytes 1 | tf_op jit(solution)/shard_map/attend_back_spatial/pallas_call | solution.py:583
  534.0 3.5 other_rows.15
  537.6 10.5 %weight_grad.11 = (bf16[4,64,2048]{2,1,0:T(8,128)(2,1)S(1)}, bf16[4,64,2048]{2,1,0:T(8,128)(2,1)S(1)}, bf16[4,64,2048]{2,1,0:T(8,128)(2,1)S(1)}, bf16[2,64,2048]...) custom-call(s32[5]{0:T(128)S(1)} %concatenate.13.refs_0_, bf16[320,1024]{1,0:T(8,128)(2,1)S(1)} %copy-done.39, ...), custom_call_target="tpu_custom_call" | custom-call | flops 1 | bytes 1 | tf_op jit(solution)/shard_map/weight_grad/pallas_call | solution.py:583
  550.2 3.8 scatter_step.12
  556.1 3.4 collective-permute-start.84
  564.8 8.7 %bias_tables.1 = (f32[8,9,256]{2,1,0:T(8,128)S(1)}, f32[8,9,256]{2,1,0:T(8,128)S(1)}) custom-call(s32[5]{0:T(128)S(1)} %concatenate.13.refs_0_, f32[8,9,64,64]{3,2,1,0:T(8,128)S(1)} %get-tuple-element.307.refs_1_, f32[8,9,64,64]{3,2,1,0:T(8,128)S(1)} %copy-done.71, bf16[192,256]{1,0:T(8,128)(2,1)S(1)} %copy-done.142, ...), custom_call_target="tpu_custom_call" | custom-call | flops 1 | bytes 1 | tf_op jit(solution)/shard_map/bias_tables/pallas_call | solution.py:583
  573.6 4.5 backward_step.7
  580.6 7.2 %collective-permute-done.92.refs_9_ = bf16[64,2048]{1,0:T(8,128)(2,1)S(1)} collective-permute-done((bf16[64,2048]{1,0:T(8,128)(2,1)S(1)}, bf16[64,2048]{1,0:T(8,128)(2,1)S(1)}, u32[]{:S(2)}, u32[]{:S(2)}) %collective-permute-start.92) | collective-permute-done | bytes 262176 | tf_op jit(solution)/shard_map/ppermute | solution.py:518
  592.1 9.6 %all_to_all.10 = f32[32,2,192]{2,1,0:T(2,128)S(1)} all-to-all(f32[32,2,192]{2,1,0:T(2,128)S(1)} %bitcast.227), channel_id=1, replica_groups=mesh['z'=4,'y'=2,'c'=2,'x'=2] {'z','y','c','x'}, dimensions={0} | all-to-all | bytes 98304 | tf_op jit(solution)/shard_map/all_to_all | solution.py:1688
  609.9 4.8 scatter_step.13
  627.2 5.5 collective-permute-done.97.refs_5_
  635.2 12.1 %collective-permute-done.99.refs_7_ = bf16[64,2048]{1,0:T(8,128)(2,1)} collective-permute-done((bf16[64,2048]{1,0:T(8,128)(2,1)}, bf16[64,2048]{1,0:T(8,128)(2,1)}, u32[]{:S(2)}, u32[]{:S(2)}) %collective-permute-start.99) | collective-permute-done | bytes 262176 | tf_op jit(solution)/shard_map/ppermute | solution.py:518
  649.6 3.3 scatter_step.14
  655.3 5.2 collective-permute-start.108
  671.6 4.4 collective-permute-done.108
  676.6 13.4 %collective-permute-done.100 = bf16[640,1024]{1,0:T(8,128)(2,1)S(1)} collective-permute-done((bf16[640,1024]{1,0:T(8,128)(2,1)S(1)}, bf16[640,1024]{1,0:T(8,128)(2,1)S(1)}, u32[]{:S(2)}, u32[]{:S(2)}) %collective-permute-start.100) | collective-permute-done | bytes 1310752 | tf_op jit(solution)/shard_map/ppermute | solution.py:522
  691.6 6.1 collective-permute-done.107.refs_4_
  (676 shorter events, 264.4 us)
Async XLA Ops:
  1.4 18.6 %collective-permute-start = (f32[1]{0:T(128)}, f32[1]{0:T(128)}, u32[]{:S(2)}, u32[]{:S(2)}) collective-permute-start(f32[1]{0:T(128)} %convert_element_type.71), channel_id=1, source_target_pairs={{0,2},{2,0},{1,3},{3,1},{4,6},{6,4},{5,7},{7,5},{8,10},{10,8},{9,1... | collective-permute-start | bytes 20 | tf_op jit(solution)/shard_map/ppermute | solution.py:514
  10.2 19.3 %collective-permute-start.3 = (bf16[64,2048]{1,0:T(8,128)(2,1)S(1)}, bf16[64,2048]{1,0:T(8,128)(2,1)}, u32[]{:S(2)}, u32[]{:S(2)}) collective-permute-start(bf16[64,2048]{1,0:T(8,128)(2,1)S(1)} %pad_maximum_fusion.3), channel_id=1, source_target_pairs={{1,2},{2,1},{5,6},{6,5},{9,10},{10,9},{13,14},{14,13},{17,18},{18,... | collective-permute-start | bytes 786440 | tf_op jit(solution)/shard_map/ppermute | solution.py:522
  26.7 28.0 %collective-permute-start.2 = (bf16[64,10240]{1,0:T(8,128)(2,1)S(1)}, bf16[64,10240]{1,0:T(8,128)(2,1)S(1)}, u32[]{:S(2)}, u32[]{:S(2)}) collective-permute-start(bf16[64,10240]{1,0:T(8,128)(2,1)S(1)} %pack_arguments.1.refs_5_.refs_1_), channel_id=1, source_target_pairs={{1,2},{2,1},{5,6},{6,5},{9,10},{10,9},{13,14},{14,13},{17,18},{18,... | collective-permute-start | bytes 3932168 | tf_op jit(solution)/shard_map/ppermute | solution.py:522
  30.5 19.4 %collective-permute-start.6 = (bf16[64,2048]{1,0:T(8,128)(2,1)S(1)}, bf16[64,2048]{1,0:T(8,128)(2,1)S(1)}, u32[]{:S(2)}, u32[]{:S(2)}) collective-permute-start(bf16[64,2048]{1,0:T(8,128)(2,1)S(1)} %broadcast_select_fusion.4.refs_1_), channel_id=1, source_target_pairs={{0,24},{8,16},{16,8},{24,0},{1,25},{9,17},{17,9},{25,1},{2,26},{10... | collective-permute-start | bytes 786440 | tf_op jit(solution)/shard_map/ppermute | solution.py:518
  30.9 20.8 %collective-permute-start.5 = (bf16[64,2048]{1,0:T(8,128)(2,1)S(1)}, bf16[64,2048]{1,0:T(8,128)(2,1)S(1)}, u32[]{:S(2)}, u32[]{:S(2)}) collective-permute-start(bf16[64,2048]{1,0:T(8,128)(2,1)S(1)} %broadcast_select_fusion.4.refs_1_), channel_id=1, source_target_pairs={{0,16},{8,24},{16,0},{24,8},{1,17},{9,25},{17,1},{25,9},{2,18},{10... | collective-permute-start | bytes 786440 | tf_op jit(solution)/shard_map/ppermute | solution.py:518
  54.1 25.1 %collective-permute-start.12 = (bf16[4,64,2048]{2,1,0:T(8,128)(2,1)}, bf16[4,64,2048]{2,1,0:T(8,128)(2,1)S(1)}, u32[]{:S(2)}, u32[]{:S(2)}) collective-permute-start(bf16[4,64,2048]{2,1,0:T(8,128)(2,1)} %get-tuple-element.186), channel_id=1, source_target_pairs={{0,4},{4,0},{1,5},{5,1},{2,6},{6,2},{3,7},{7,3},{8,12},{12,8},{9,1... | collective-permute-start | bytes 3145736 | tf_op jit(solution)/shard_map/ppermute | solution.py:514
  54.7 26.7 %collective-permute-start.11 = (bf16[4,64,2048]{2,1,0:T(8,128)(2,1)}, bf16[4,64,2048]{2,1,0:T(8,128)(2,1)}, u32[]{:S(2)}, u32[]{:S(2)}) collective-permute-start(bf16[4,64,2048]{2,1,0:T(8,128)(2,1)} %get-tuple-element.184.refs_3_.refs_1_), channel_id=1, source_target_pairs={{0,1},{1,0},{2,3},{3,2},{4,5},{5,4},{6,7},{7,6},{8,9},{9,8},{10,11... | collective-permute-start | bytes 3145736 | tf_op jit(solution)/shard_map/ppermute | solution.py:514
  58.2 23.2 %collective-permute-start.10 = (bf16[64,2048]{1,0:T(8,128)(2,1)S(1)}, bf16[64,2048]{1,0:T(8,128)(2,1)}, u32[]{:S(2)}, u32[]{:S(2)}) collective-permute-start(bf16[64,2048]{1,0:T(8,128)(2,1)S(1)} %get-tuple-element.185.refs_2_.refs_1_), channel_id=1, source_target_pairs={{0,24},{8,16},{16,8},{24,0},{1,25},{9,17},{17,9},{25,1},{2,26},{10... | collective-permute-start | bytes 786440 | tf_op jit(solution)/shard_map/ppermute | solution.py:518
  59.4 22.1 %collective-permute-start.9 = (bf16[64,2048]{1,0:T(8,128)(2,1)S(1)}, bf16[64,2048]{1,0:T(8,128)(2,1)}, u32[]{:S(2)}, u32[]{:S(2)}) collective-permute-start(bf16[64,2048]{1,0:T(8,128)(2,1)S(1)} %get-tuple-element.185.refs_2_.refs_1_), channel_id=1, source_target_pairs={{0,16},{8,24},{16,0},{24,8},{1,17},{9,25},{17,1},{25,9},{2,18},{10... | collective-permute-start | bytes 786440 | tf_op jit(solution)/shard_map/ppermute | solution.py:518
  79.2 28.1 %collective-permute-start.7 = (bf16[640,1024]{1,0:T(8,128)(2,1)}, bf16[640,1024]{1,0:T(8,128)(2,1)}, u32[]{:S(2)}, u32[]{:S(2)}) collective-permute-start(bf16[640,1024]{1,0:T(8,128)(2,1)} %copy_rows.3.refs_7_.refs_1_), channel_id=1, source_target_pairs={{1,2},{2,1},{5,6},{6,5},{9,10},{10,9},{13,14},{14,13},{17,18},{18,... | collective-permute-start | bytes 3932168 | tf_op jit(solution)/shard_map/ppermute | solution.py:522
  85.9 35.0 %collective-permute-start.16 = (bf16[6,64,2048]{2,1,0:T(8,128)(2,1)}, bf16[6,64,2048]{2,1,0:T(8,128)(2,1)S(1)}, u32[]{:S(2)}, u32[]{:S(2)}) collective-permute-start(bf16[6,64,2048]{2,1,0:T(8,128)(2,1)} %get-tuple-element.190), channel_id=1, source_target_pairs={{0,4},{4,0},{1,5},{5,1},{2,6},{6,2},{3,7},{7,3},{8,12},{12,8},{9,1... | collective-permute-start | bytes 4718600 | tf_op jit(solution)/shard_map/ppermute | solution.py:514
  86.8 42.9 %collective-permute-start.15 = (bf16[6,64,2048]{2,1,0:T(8,128)(2,1)}, bf16[6,64,2048]{2,1,0:T(8,128)(2,1)}, u32[]{:S(2)}, u32[]{:S(2)}) collective-permute-start(bf16[6,64,2048]{2,1,0:T(8,128)(2,1)} %get-tuple-element.187.refs_4_.refs_1_), channel_id=1, source_target_pairs={{0,1},{1,0},{2,3},{3,2},{4,5},{5,4},{6,7},{7,6},{8,9},{9,8},{10,11... | collective-permute-start | bytes 4718600 | tf_op jit(solution)/shard_map/ppermute | solution.py:514
  98.0 21.4 %collective-permute-start.18 = (bf16[64,2048]{1,0:T(8,128)(2,1)S(1)}, bf16[64,2048]{1,0:T(8,128)(2,1)S(1)}, u32[]{:S(2)}, u32[]{:S(2)}) collective-permute-start(bf16[64,2048]{1,0:T(8,128)(2,1)S(1)} %copy-done.138), channel_id=1, source_target_pairs={{0,16},{8,24},{16,0},{24,8},{1,17},{9,25},{17,1},{25,9},{2,18},{10... | collective-permute-start | bytes 786440 | tf_op jit(solution)/shard_map/ppermute | solution.py:518
  132.6 38.1 %collective-permute-start.23 = (bf16[6,64,2048]{2,1,0:T(8,128)(2,1)S(1)}, bf16[6,64,2048]{2,1,0:T(8,128)(2,1)S(1)}, u32[]{:S(2)}, u32[]{:S(2)}) collective-permute-start(bf16[6,64,2048]{2,1,0:T(8,128)(2,1)S(1)} %get-tuple-element.199), channel_id=1, source_target_pairs={{0,4},{4,0},{1,5},{5,1},{2,6},{6,2},{3,7},{7,3},{8,12},{12,8},{9,1... | collective-permute-start | bytes 4718600 | tf_op jit(solution)/shard_map/ppermute | solution.py:514
  133.2 37.5 %collective-permute-start.22 = (bf16[6,64,2048]{2,1,0:T(8,128)(2,1)S(1)}, bf16[6,64,2048]{2,1,0:T(8,128)(2,1)S(1)}, u32[]{:S(2)}, u32[]{:S(2)}) collective-permute-start(bf16[6,64,2048]{2,1,0:T(8,128)(2,1)S(1)} %get-tuple-element.193.refs_6_.refs_1_), channel_id=1, source_target_pairs={{0,1},{1,0},{2,3},{3,2},{4,5},{5,4},{6,7},{7,6},{8,9},{9,8},{10,11... | collective-permute-start | bytes 4718600 | tf_op jit(solution)/shard_map/ppermute | solution.py:514
  136.6 33.2 %collective-permute-start.26 = (bf16[64,2048]{1,0:T(8,128)(2,1)S(1)}, bf16[64,2048]{1,0:T(8,128)(2,1)S(1)}, u32[]{:S(2)}, u32[]{:S(2)}) collective-permute-start(bf16[64,2048]{1,0:T(8,128)(2,1)S(1)} %copy-done.134), channel_id=1, source_target_pairs={{0,24},{8,16},{16,8},{24,0},{1,25},{9,17},{17,9},{25,1},{2,26},{10... | collective-permute-start | bytes 786440 | tf_op jit(solution)/shard_map/ppermute | solution.py:518
  138.3 32.2 %collective-permute-start.25 = (bf16[64,2048]{1,0:T(8,128)(2,1)S(1)}, bf16[64,2048]{1,0:T(8,128)(2,1)S(1)}, u32[]{:S(2)}, u32[]{:S(2)}) collective-permute-start(bf16[64,2048]{1,0:T(8,128)(2,1)S(1)} %copy-done.134), channel_id=1, source_target_pairs={{0,16},{8,24},{16,0},{24,8},{1,17},{9,25},{17,1},{25,9},{2,18},{10... | collective-permute-start | bytes 786440 | tf_op jit(solution)/shard_map/ppermute | solution.py:518
  141.4 29.2 %collective-permute-start.24 = (bf16[64,2048]{1,0:T(8,128)(2,1)S(1)}, bf16[64,2048]{1,0:T(8,128)(2,1)S(1)}, u32[]{:S(2)}, u32[]{:S(2)}) collective-permute-start(bf16[64,2048]{1,0:T(8,128)(2,1)S(1)} %copy-done.134), channel_id=1, source_target_pairs={{0,8},{8,0},{16,24},{24,16},{1,9},{9,1},{17,25},{25,17},{2,10},{10... | collective-permute-start | bytes 786440 | tf_op jit(solution)/shard_map/ppermute | solution.py:518
  171.9 35.6 %collective-permute-start.30 = (bf16[6,64,2048]{2,1,0:T(8,128)(2,1)S(1)}, bf16[6,64,2048]{2,1,0:T(8,128)(2,1)S(1)}, u32[]{:S(2)}, u32[]{:S(2)}) collective-permute-start(bf16[6,64,2048]{2,1,0:T(8,128)(2,1)S(1)} %get-tuple-element.206), channel_id=1, source_target_pairs={{0,4},{4,0},{1,5},{5,1},{2,6},{6,2},{3,7},{7,3},{8,12},{12,8},{9,1... | collective-permute-start | bytes 4718600 | tf_op jit(solution)/shard_map/ppermute | solution.py:514
  172.7 35.8 %collective-permute-start.29 = (bf16[6,64,2048]{2,1,0:T(8,128)(2,1)S(1)}, bf16[6,64,2048]{2,1,0:T(8,128)(2,1)S(1)}, u32[]{:S(2)}, u32[]{:S(2)}) collective-permute-start(bf16[6,64,2048]{2,1,0:T(8,128)(2,1)S(1)} %get-tuple-element.201.refs_6_.refs_1_), channel_id=1, source_target_pairs={{0,1},{1,0},{2,3},{3,2},{4,5},{5,4},{6,7},{7,6},{8,9},{9,8},{10,11... | collective-permute-start | bytes 4718600 | tf_op jit(solution)/shard_map/ppermute | solution.py:514
  184.2 22.7 %collective-permute-start.33 = (bf16[64,2048]{1,0:T(8,128)(2,1)S(1)}, bf16[64,2048]{1,0:T(8,128)(2,1)S(1)}, u32[]{:S(2)}, u32[]{:S(2)}) collective-permute-start(bf16[64,2048]{1,0:T(8,128)(2,1)S(1)} %copy-done.130), channel_id=1, source_target_pairs={{0,24},{8,16},{16,8},{24,0},{1,25},{9,17},{17,9},{25,1},{2,26},{10... | collective-permute-start | bytes 786440 | tf_op jit(solution)/shard_map/ppermute | solution.py:518
  185.8 21.6 %collective-permute-start.32 = (bf16[64,2048]{1,0:T(8,128)(2,1)S(1)}, bf16[64,2048]{1,0:T(8,128)(2,1)S(1)}, u32[]{:S(2)}, u32[]{:S(2)}) collective-permute-start(bf16[64,2048]{1,0:T(8,128)(2,1)S(1)} %copy-done.130), channel_id=1, source_target_pairs={{0,16},{8,24},{16,0},{24,8},{1,17},{9,25},{17,1},{25,9},{2,18},{10... | collective-permute-start | bytes 786440 | tf_op jit(solution)/shard_map/ppermute | solution.py:518
  188.3 19.1 %collective-permute-start.31 = (bf16[64,2048]{1,0:T(8,128)(2,1)S(1)}, bf16[64,2048]{1,0:T(8,128)(2,1)S(1)}, u32[]{:S(2)}, u32[]{:S(2)}) collective-permute-start(bf16[64,2048]{1,0:T(8,128)(2,1)S(1)} %copy-done.130), channel_id=1, source_target_pairs={{0,8},{8,0},{16,24},{24,16},{1,9},{9,1},{17,25},{25,17},{2,10},{10... | collective-permute-start | bytes 786440 | tf_op jit(solution)/shard_map/ppermute | solution.py:518
  209.8 34.7 %collective-permute-start.39 = (bf16[6,64,2048]{2,1,0:T(8,128)(2,1)S(1)}, bf16[6,64,2048]{2,1,0:T(8,128)(2,1)S(1)}, u32[]{:S(2)}, u32[]{:S(2)}) collective-permute-start(bf16[6,64,2048]{2,1,0:T(8,128)(2,1)S(1)} %get-tuple-element.213), channel_id=1, source_target_pairs={{0,4},{4,0},{1,5},{5,1},{2,6},{6,2},{3,7},{7,3},{8,12},{12,8},{9,1... | collective-permute-start | bytes 4718600 | tf_op jit(solution)/shard_map/ppermute | solution.py:514
  210.6 34.4 %collective-permute-start.38 = (bf16[6,64,2048]{2,1,0:T(8,128)(2,1)S(1)}, bf16[6,64,2048]{2,1,0:T(8,128)(2,1)S(1)}, u32[]{:S(2)}, u32[]{:S(2)}) collective-permute-start(bf16[6,64,2048]{2,1,0:T(8,128)(2,1)S(1)} %get-tuple-element.208.refs_6_.refs_1_), channel_id=1, source_target_pairs={{0,1},{1,0},{2,3},{3,2},{4,5},{5,4},{6,7},{7,6},{8,9},{9,8},{10,11... | collective-permute-start | bytes 4718600 | tf_op jit(solution)/shard_map/ppermute | solution.py:514
  219.2 18.7 %collective-permute-start.42 = (bf16[64,2048]{1,0:T(8,128)(2,1)S(1)}, bf16[64,2048]{1,0:T(8,128)(2,1)S(1)}, u32[]{:S(2)}, u32[]{:S(2)}) collective-permute-start(bf16[64,2048]{1,0:T(8,128)(2,1)S(1)} %copy-done.128), channel_id=1, source_target_pairs={{0,24},{8,16},{16,8},{24,0},{1,25},{9,17},{17,9},{25,1},{2,26},{10... | collective-permute-start | bytes 786440 | tf_op jit(solution)/shard_map/ppermute | solution.py:518
  220.9 21.4 %collective-permute-start.41 = (bf16[64,2048]{1,0:T(8,128)(2,1)S(1)}, bf16[64,2048]{1,0:T(8,128)(2,1)S(1)}, u32[]{:S(2)}, u32[]{:S(2)}) collective-permute-start(bf16[64,2048]{1,0:T(8,128)(2,1)S(1)} %copy-done.128), channel_id=1, source_target_pairs={{0,16},{8,24},{16,0},{24,8},{1,17},{9,25},{17,1},{25,9},{2,18},{10... | collective-permute-start | bytes 786440 | tf_op jit(solution)/shard_map/ppermute | solution.py:518
  223.1 19.1 %collective-permute-start.40 = (bf16[64,2048]{1,0:T(8,128)(2,1)S(1)}, bf16[64,2048]{1,0:T(8,128)(2,1)S(1)}, u32[]{:S(2)}, u32[]{:S(2)}) collective-permute-start(bf16[64,2048]{1,0:T(8,128)(2,1)S(1)} %copy-done.128), channel_id=1, source_target_pairs={{0,8},{8,0},{16,24},{24,16},{1,9},{9,1},{17,25},{25,17},{2,10},{10... | collective-permute-start | bytes 786440 | tf_op jit(solution)/shard_map/ppermute | solution.py:518
  246.2 35.4 %collective-permute-start.46 = (bf16[6,64,2048]{2,1,0:T(8,128)(2,1)S(1)}, bf16[6,64,2048]{2,1,0:T(8,128)(2,1)S(1)}, u32[]{:S(2)}, u32[]{:S(2)}) collective-permute-start(bf16[6,64,2048]{2,1,0:T(8,128)(2,1)S(1)} %get-tuple-element.222), channel_id=1, source_target_pairs={{0,4},{4,0},{1,5},{5,1},{2,6},{6,2},{3,7},{7,3},{8,12},{12,8},{9,1... | collective-permute-start | bytes 4718600 | tf_op jit(solution)/shard_map/ppermute | solution.py:514
  247.0 34.7 %collective-permute-start.45 = (bf16[6,64,2048]{2,1,0:T(8,128)(2,1)S(1)}, bf16[6,64,2048]{2,1,0:T(8,128)(2,1)S(1)}, u32[]{:S(2)}, u32[]{:S(2)}) collective-permute-start(bf16[6,64,2048]{2,1,0:T(8,128)(2,1)S(1)} %get-tuple-element.216.refs_6_.refs_1_), channel_id=1, source_target_pairs={{0,1},{1,0},{2,3},{3,2},{4,5},{5,4},{6,7},{7,6},{8,9},{9,8},{10,11... | collective-permute-start | bytes 4718600 | tf_op jit(solution)/shard_map/ppermute | solution.py:514
  290.5 18.7 %collective-permute-start.50 = (bf16[2,64,2048]{2,1,0:T(8,128)(2,1)S(1)}, bf16[2,64,2048]{2,1,0:T(8,128)(2,1)S(1)}, u32[]{:S(2)}, u32[]{:S(2)}) collective-permute-start(bf16[2,64,2048]{2,1,0:T(8,128)(2,1)S(1)} %get-tuple-element.228), channel_id=1, source_target_pairs={{0,4},{4,0},{1,5},{5,1},{2,6},{6,2},{3,7},{7,3},{8,12},{12,8},{9,1... | collective-permute-start | bytes 1572872 | tf_op jit(solution)/shard_map/ppermute | solution.py:514
  312.1 18.9 %collective-permute-start.54 = (bf16[640,1024]{1,0:T(8,128)(2,1)S(1)}, bf16[640,1024]{1,0:T(8,128)(2,1)S(1)}, u32[]{:S(2)}, u32[]{:S(2)}) collective-permute-start(bf16[640,1024]{1,0:T(8,128)(2,1)S(1)} %copy_rows.4.refs_3_), channel_id=1, source_target_pairs={{1,2},{2,1},{5,6},{6,5},{9,10},{10,9},{13,14},{14,13},{17,18},{18,... | collective-permute-start | bytes 3932168 | tf_op jit(solution)/shard_map/ppermute | solution.py:522
  326.6 35.8 %collective-permute-start.53 = (bf16[640,1024]{1,0:T(8,128)(2,1)S(1)}, bf16[640,1024]{1,0:T(8,128)(2,1)}, u32[]{:S(2)}, u32[]{:S(2)}) collective-permute-start(bf16[640,1024]{1,0:T(8,128)(2,1)S(1)} %get-tuple-element.231.refs_4_), channel_id=1, source_target_pairs={{1,2},{2,1},{5,6},{6,5},{9,10},{10,9},{13,14},{14,13},{17,18},{18,... | collective-permute-start | bytes 3932168 | tf_op jit(solution)/shard_map/ppermute | solution.py:522
  360.8 21.0 %collective-permute-start.61 = (bf16[2,64,2048]{2,1,0:T(8,128)(2,1)S(1)}, bf16[2,64,2048]{2,1,0:T(8,128)(2,1)S(1)}, u32[]{:S(2)}, u32[]{:S(2)}) collective-permute-start(bf16[2,64,2048]{2,1,0:T(8,128)(2,1)S(1)} %get-tuple-element.249), channel_id=1, source_target_pairs={{0,1},{1,0},{2,3},{3,2},{4,5},{5,4},{6,7},{7,6},{8,9},{9,8},{10,11... | collective-permute-start | bytes 1572872 | tf_op jit(solution)/shard_map/ppermute | solution.py:514
  361.6 20.2 %collective-permute-start.62 = (bf16[2,64,2048]{2,1,0:T(8,128)(2,1)S(1)}, bf16[2,64,2048]{2,1,0:T(8,128)(2,1)S(1)}, u32[]{:S(2)}, u32[]{:S(2)}) collective-permute-start(bf16[2,64,2048]{2,1,0:T(8,128)(2,1)S(1)} %get-tuple-element.250), channel_id=1, source_target_pairs={{0,4},{4,0},{1,5},{5,1},{2,6},{6,2},{3,7},{7,3},{8,12},{12,8},{9,1... | collective-permute-start | bytes 1572872 | tf_op jit(solution)/shard_map/ppermute | solution.py:514
  385.2 40.9 %collective-permute-start.66 = (bf16[6,64,2048]{2,1,0:T(8,128)(2,1)}, bf16[6,64,2048]{2,1,0:T(8,128)(2,1)S(1)}, u32[]{:S(2)}, u32[]{:S(2)}) collective-permute-start(bf16[6,64,2048]{2,1,0:T(8,128)(2,1)} %get-tuple-element.264), channel_id=1, source_target_pairs={{0,4},{4,0},{1,5},{5,1},{2,6},{6,2},{3,7},{7,3},{8,12},{12,8},{9,1... | collective-permute-start | bytes 4718600 | tf_op jit(solution)/shard_map/ppermute | solution.py:514
  385.9 40.2 %collective-permute-start.65 = (bf16[6,64,2048]{2,1,0:T(8,128)(2,1)}, bf16[6,64,2048]{2,1,0:T(8,128)(2,1)S(1)}, u32[]{:S(2)}, u32[]{:S(2)}) collective-permute-start(bf16[6,64,2048]{2,1,0:T(8,128)(2,1)} %get-tuple-element.252.refs_6_), channel_id=1, source_target_pairs={{0,1},{1,0},{2,3},{3,2},{4,5},{5,4},{6,7},{7,6},{8,9},{9,8},{10,11... | collective-permute-start | bytes 4718600 | tf_op jit(solution)/shard_map/ppermute | solution.py:514
  429.7 38.2 %collective-permute-start.72 = (bf16[6,64,2048]{2,1,0:T(8,128)(2,1)}, bf16[6,64,2048]{2,1,0:T(8,128)(2,1)S(1)}, u32[]{:S(2)}, u32[]{:S(2)}) collective-permute-start(bf16[6,64,2048]{2,1,0:T(8,128)(2,1)} %get-tuple-element.280), channel_id=1, source_target_pairs={{0,4},{4,0},{1,5},{5,1},{2,6},{6,2},{3,7},{7,3},{8,12},{12,8},{9,1... | collective-permute-start | bytes 4718600 | tf_op jit(solution)/shard_map/ppermute | solution.py:514
  430.5 37.4 %collective-permute-start.71 = (bf16[6,64,2048]{2,1,0:T(8,128)(2,1)}, bf16[6,64,2048]{2,1,0:T(8,128)(2,1)}, u32[]{:S(2)}, u32[]{:S(2)}) collective-permute-start(bf16[6,64,2048]{2,1,0:T(8,128)(2,1)} %get-tuple-element.266.refs_10_), channel_id=1, source_target_pairs={{0,1},{1,0},{2,3},{3,2},{4,5},{5,4},{6,7},{7,6},{8,9},{9,8},{10,11... | collective-permute-start | bytes 4718600 | tf_op jit(solution)/shard_map/ppermute | solution.py:514
  438.3 28.6 %collective-permute-start.73 = (bf16[64,2048]{1,0:T(8,128)(2,1)S(1)}, bf16[64,2048]{1,0:T(8,128)(2,1)S(1)}, u32[]{:S(2)}, u32[]{:S(2)}) collective-permute-start(bf16[64,2048]{1,0:T(8,128)(2,1)S(1)} %get-tuple-element.282), channel_id=1, source_target_pairs={{0,8},{8,0},{16,24},{24,16},{1,9},{9,1},{17,25},{25,17},{2,10},{10... | collective-permute-start | bytes 786440 | tf_op jit(solution)/shard_map/ppermute | solution.py:518
  440.0 27.9 %collective-permute-start.74 = (bf16[64,2048]{1,0:T(8,128)(2,1)S(1)}, bf16[64,2048]{1,0:T(8,128)(2,1)S(1)}, u32[]{:S(2)}, u32[]{:S(2)}) collective-permute-start(bf16[64,2048]{1,0:T(8,128)(2,1)S(1)} %get-tuple-element.283), channel_id=1, source_target_pairs={{0,16},{8,24},{16,0},{24,8},{1,17},{9,25},{17,1},{25,9},{2,18},{10... | collective-permute-start | bytes 786440 | tf_op jit(solution)/shard_map/ppermute | solution.py:518
  442.2 25.7 %collective-permute-start.75 = (bf16[64,2048]{1,0:T(8,128)(2,1)S(1)}, bf16[64,2048]{1,0:T(8,128)(2,1)S(1)}, u32[]{:S(2)}, u32[]{:S(2)}) collective-permute-start(bf16[64,2048]{1,0:T(8,128)(2,1)S(1)} %get-tuple-element.284), channel_id=1, source_target_pairs={{0,24},{8,16},{16,8},{24,0},{1,25},{9,17},{17,9},{25,1},{2,26},{10... | collective-permute-start | bytes 786440 | tf_op jit(solution)/shard_map/ppermute | solution.py:518
  472.2 36.1 %collective-permute-start.79 = (bf16[6,64,2048]{2,1,0:T(8,128)(2,1)S(1)}, bf16[6,64,2048]{2,1,0:T(8,128)(2,1)S(1)}, u32[]{:S(2)}, u32[]{:S(2)}) collective-permute-start(bf16[6,64,2048]{2,1,0:T(8,128)(2,1)S(1)} %get-tuple-element.296), channel_id=1, source_target_pairs={{0,4},{4,0},{1,5},{5,1},{2,6},{6,2},{3,7},{7,3},{8,12},{12,8},{9,1... | collective-permute-start | bytes 4718600 | tf_op jit(solution)/shard_map/ppermute | solution.py:514
  473.1 35.3 %collective-permute-start.78 = (bf16[6,64,2048]{2,1,0:T(8,128)(2,1)S(1)}, bf16[6,64,2048]{2,1,0:T(8,128)(2,1)S(1)}, u32[]{:S(2)}, u32[]{:S(2)}) collective-permute-start(bf16[6,64,2048]{2,1,0:T(8,128)(2,1)S(1)} %get-tuple-element.286.refs_10_), channel_id=1, source_target_pairs={{0,1},{1,0},{2,3},{3,2},{4,5},{5,4},{6,7},{7,6},{8,9},{9,8},{10,11... | collective-permute-start | bytes 4718600 | tf_op jit(solution)/shard_map/ppermute | solution.py:514
  484.7 23.6 %collective-permute-start.82 = (bf16[64,2048]{1,0:T(8,128)(2,1)S(1)}, bf16[64,2048]{1,0:T(8,128)(2,1)S(1)}, u32[]{:S(2)}, u32[]{:S(2)}) collective-permute-start(bf16[64,2048]{1,0:T(8,128)(2,1)S(1)} %get-tuple-element.300), channel_id=1, source_target_pairs={{0,24},{8,16},{16,8},{24,0},{1,25},{9,17},{17,9},{25,1},{2,26},{10... | collective-permute-start | bytes 786440 | tf_op jit(solution)/shard_map/ppermute | solution.py:518
  511.9 38.3 %collective-permute-start.86 = (bf16[6,64,2048]{2,1,0:T(8,128)(2,1)}, bf16[6,64,2048]{2,1,0:T(8,128)(2,1)S(1)}, u32[]{:S(2)}, u32[]{:S(2)}) collective-permute-start(bf16[6,64,2048]{2,1,0:T(8,128)(2,1)} %get-tuple-element.313), channel_id=1, source_target_pairs={{0,4},{4,0},{1,5},{5,1},{2,6},{6,2},{3,7},{7,3},{8,12},{12,8},{9,1... | collective-permute-start | bytes 4718600 | tf_op jit(solution)/shard_map/ppermute | solution.py:514
  512.5 37.7 %collective-permute-start.85 = (bf16[6,64,2048]{2,1,0:T(8,128)(2,1)S(1)}, bf16[6,64,2048]{2,1,0:T(8,128)(2,1)S(1)}, u32[]{:S(2)}, u32[]{:S(2)}) collective-permute-start(bf16[6,64,2048]{2,1,0:T(8,128)(2,1)S(1)} %get-tuple-element.301.refs_4_), channel_id=1, source_target_pairs={{0,1},{1,0},{2,3},{3,2},{4,5},{5,4},{6,7},{7,6},{8,9},{9,8},{10,11... | collective-permute-start | bytes 4718600 | tf_op jit(solution)/shard_map/ppermute | solution.py:514
  513.4 36.7 %collective-permute-start.87 = (bf16[64,2048]{1,0:T(8,128)(2,1)}, bf16[64,2048]{1,0:T(8,128)(2,1)S(1)}, u32[]{:S(2)}, u32[]{:S(2)}) collective-permute-start(bf16[64,2048]{1,0:T(8,128)(2,1)} %get-tuple-element.315), channel_id=1, source_target_pairs={{0,8},{8,0},{16,24},{24,16},{1,9},{9,1},{17,25},{25,17},{2,10},{10... | collective-permute-start | bytes 786440 | tf_op jit(solution)/shard_map/ppermute | solution.py:518
  514.2 36.0 %collective-permute-start.88 = (bf16[64,2048]{1,0:T(8,128)(2,1)}, bf16[64,2048]{1,0:T(8,128)(2,1)S(1)}, u32[]{:S(2)}, u32[]{:S(2)}) collective-permute-start(bf16[64,2048]{1,0:T(8,128)(2,1)} %get-tuple-element.316), channel_id=1, source_target_pairs={{0,16},{8,24},{16,0},{24,8},{1,17},{9,25},{17,1},{25,9},{2,18},{10... | collective-permute-start | bytes 786440 | tf_op jit(solution)/shard_map/ppermute | solution.py:518
  515.3 34.8 %collective-permute-start.89 = (bf16[64,2048]{1,0:T(8,128)(2,1)S(1)}, bf16[64,2048]{1,0:T(8,128)(2,1)S(1)}, u32[]{:S(2)}, u32[]{:S(2)}) collective-permute-start(bf16[64,2048]{1,0:T(8,128)(2,1)S(1)} %get-tuple-element.317), channel_id=1, source_target_pairs={{0,24},{8,16},{16,8},{24,0},{1,25},{9,17},{17,9},{25,1},{2,26},{10... | collective-permute-start | bytes 786440 | tf_op jit(solution)/shard_map/ppermute | solution.py:518
  554.7 47.6 %collective-permute-start.94 = (bf16[6,64,2048]{2,1,0:T(8,128)(2,1)}, bf16[6,64,2048]{2,1,0:T(8,128)(2,1)}, u32[]{:S(2)}, u32[]{:S(2)}) collective-permute-start(bf16[6,64,2048]{2,1,0:T(8,128)(2,1)} %get-tuple-element.333), channel_id=1, source_target_pairs={{0,4},{4,0},{1,5},{5,1},{2,6},{6,2},{3,7},{7,3},{8,12},{12,8},{9,1... | collective-permute-start | bytes 4718600 | tf_op jit(solution)/shard_map/ppermute | solution.py:514
  555.6 46.7 %collective-permute-start.93 = (bf16[6,64,2048]{2,1,0:T(8,128)(2,1)}, bf16[6,64,2048]{2,1,0:T(8,128)(2,1)}, u32[]{:S(2)}, u32[]{:S(2)}) collective-permute-start(bf16[6,64,2048]{2,1,0:T(8,128)(2,1)} %get-tuple-element.319.refs_4_), channel_id=1, source_target_pairs={{0,1},{1,0},{2,3},{3,2},{4,5},{5,4},{6,7},{7,6},{8,9},{9,8},{10,11... | collective-permute-start | bytes 4718600 | tf_op jit(solution)/shard_map/ppermute | solution.py:514
  559.6 18.6 %collective-permute-start.90 = (bf16[64,2048]{1,0:T(8,128)(2,1)S(1)}, bf16[64,2048]{1,0:T(8,128)(2,1)S(1)}, u32[]{:S(2)}, u32[]{:S(2)}) collective-permute-start(bf16[64,2048]{1,0:T(8,128)(2,1)S(1)} %get-tuple-element.327), channel_id=1, source_target_pairs={{0,8},{8,0},{16,24},{24,16},{1,9},{9,1},{17,25},{25,17},{2,10},{10... | collective-permute-start | bytes 786440 | tf_op jit(solution)/shard_map/ppermute | solution.py:518
  561.9 18.7 %collective-permute-start.91 = (bf16[64,2048]{1,0:T(8,128)(2,1)S(1)}, bf16[64,2048]{1,0:T(8,128)(2,1)S(1)}, u32[]{:S(2)}, u32[]{:S(2)}) collective-permute-start(bf16[64,2048]{1,0:T(8,128)(2,1)S(1)} %get-tuple-element.328), channel_id=1, source_target_pairs={{0,16},{8,24},{16,0},{24,8},{1,17},{9,25},{17,1},{25,9},{2,18},{10... | collective-permute-start | bytes 786440 | tf_op jit(solution)/shard_map/ppermute | solution.py:518
  564.0 23.8 %collective-permute-start.92 = (bf16[64,2048]{1,0:T(8,128)(2,1)S(1)}, bf16[64,2048]{1,0:T(8,128)(2,1)S(1)}, u32[]{:S(2)}, u32[]{:S(2)}) collective-permute-start(bf16[64,2048]{1,0:T(8,128)(2,1)S(1)} %get-tuple-element.329), channel_id=1, source_target_pairs={{0,24},{8,16},{16,8},{24,0},{1,25},{9,17},{17,9},{25,1},{2,26},{10... | collective-permute-start | bytes 786440 | tf_op jit(solution)/shard_map/ppermute | solution.py:518
  616.2 31.2 %collective-permute-start.96 = (bf16[4,64,2048]{2,1,0:T(8,128)(2,1)}, bf16[4,64,2048]{2,1,0:T(8,128)(2,1)}, u32[]{:S(2)}, u32[]{:S(2)}) collective-permute-start(bf16[4,64,2048]{2,1,0:T(8,128)(2,1)} %get-tuple-element.336), channel_id=1, source_target_pairs={{0,4},{4,0},{1,5},{5,1},{2,6},{6,2},{3,7},{7,3},{8,12},{12,8},{9,1... | collective-permute-start | bytes 3145736 | tf_op jit(solution)/shard_map/ppermute | solution.py:514
  616.5 30.8 %collective-permute-start.95 = (bf16[4,64,2048]{2,1,0:T(8,128)(2,1)}, bf16[4,64,2048]{2,1,0:T(8,128)(2,1)}, u32[]{:S(2)}, u32[]{:S(2)}) collective-permute-start(bf16[4,64,2048]{2,1,0:T(8,128)(2,1)} %get-tuple-element.335.refs_8_), channel_id=1, source_target_pairs={{0,1},{1,0},{2,3},{3,2},{4,5},{5,4},{6,7},{7,6},{8,9},{9,8},{10,11... | collective-permute-start | bytes 3145736 | tf_op jit(solution)/shard_map/ppermute | solution.py:514
  623.9 23.5 %collective-permute-start.99 = (bf16[64,2048]{1,0:T(8,128)(2,1)}, bf16[64,2048]{1,0:T(8,128)(2,1)}, u32[]{:S(2)}, u32[]{:S(2)}) collective-permute-start(bf16[64,2048]{1,0:T(8,128)(2,1)} %copy-done.149), channel_id=1, source_target_pairs={{0,24},{8,16},{16,8},{24,0},{1,25},{9,17},{17,9},{25,1},{2,26},{10... | collective-permute-start | bytes 786440 | tf_op jit(solution)/shard_map/ppermute | solution.py:518
  655.3 20.6 %collective-permute-start.108 = (bf16[64,10240]{1,0:T(8,128)(2,1)S(1)}, bf16[64,10240]{1,0:T(8,128)(2,1)S(1)}, u32[]{:S(2)}, u32[]{:S(2)}) collective-permute-start(bf16[64,10240]{1,0:T(8,128)(2,1)S(1)} %join_pieces.1.refs_3_), channel_id=1, source_target_pairs={{1,2},{2,1},{5,6},{6,5},{9,10},{10,9},{13,14},{14,13},{17,18},{18,... | collective-permute-start | bytes 3932168 | tf_op jit(solution)/shard_map/ppermute | solution.py:522
  665.4 24.5 %collective-permute-start.100 = (bf16[640,1024]{1,0:T(8,128)(2,1)S(1)}, bf16[640,1024]{1,0:T(8,128)(2,1)S(1)}, u32[]{:S(2)}, u32[]{:S(2)}) collective-permute-start(bf16[640,1024]{1,0:T(8,128)(2,1)S(1)} %copy_rows.5.refs_6_), channel_id=1, source_target_pairs={{1,2},{2,1},{5,6},{6,5},{9,10},{10,9},{13,14},{14,13},{17,18},{18,... | collective-permute-start | bytes 3932168 | tf_op jit(solution)/shard_map/ppermute | solution.py:522
  667.6 22.5 %collective-permute-start.105 = (bf16[64,2048]{1,0:T(8,128)(2,1)S(1)}, bf16[64,2048]{1,0:T(8,128)(2,1)S(1)}, u32[]{:S(2)}, u32[]{:S(2)}) collective-permute-start(bf16[64,2048]{1,0:T(8,128)(2,1)S(1)} %get-tuple-element.351), channel_id=1, source_target_pairs={{0,8},{8,0},{16,24},{24,16},{1,9},{9,1},{17,25},{25,17},{2,10},{10... | collective-permute-start | bytes 786440 | tf_op jit(solution)/shard_map/ppermute | solution.py:518
  667.7 23.9 %collective-permute-start.106 = (bf16[64,2048]{1,0:T(8,128)(2,1)S(1)}, bf16[64,2048]{1,0:T(8,128)(2,1)S(1)}, u32[]{:S(2)}, u32[]{:S(2)}) collective-permute-start(bf16[64,2048]{1,0:T(8,128)(2,1)S(1)} %get-tuple-element.352), channel_id=1, source_target_pairs={{0,16},{8,24},{16,0},{24,8},{1,17},{9,25},{17,1},{25,9},{2,18},{10... | collective-permute-start | bytes 786440 | tf_op jit(solution)/shard_map/ppermute | solution.py:518
  669.2 28.4 %collective-permute-start.107 = (bf16[64,2048]{1,0:T(8,128)(2,1)S(1)}, bf16[64,2048]{1,0:T(8,128)(2,1)S(1)}, u32[]{:S(2)}, u32[]{:S(2)}) collective-permute-start(bf16[64,2048]{1,0:T(8,128)(2,1)S(1)} %get-tuple-element.353), channel_id=1, source_target_pairs={{0,24},{8,16},{16,8},{24,0},{1,25},{9,17},{17,9},{25,1},{2,26},{10... | collective-permute-start | bytes 786440 | tf_op jit(solution)/shard_map/ppermute | solution.py:518
  675.9 29.6 %collective-permute-start.104 = (bf16[208,256]{1,0:T(8,128)(2,1)}, bf16[208,256]{1,0:T(8,128)(2,1)S(1)}, u32[]{:S(2)}, u32[]{:S(2)}) collective-permute-start(bf16[208,256]{1,0:T(8,128)(2,1)} %get-tuple-element.350), channel_id=1, source_target_pairs={{0,24},{8,16},{16,8},{24,0},{1,25},{9,17},{17,9},{25,1},{2,26},{10... | collective-permute-start | bytes 319496 | tf_op jit(solution)/shard_map/ppermute | solution.py:518
  (225 other events, 1880.6 us)

commit v6 on v5

--- a/solution.py
+++ b/solution.py
@@ -1092,7 +1092,7 @@
 def other_rows(chain, values, weight):
     rows, depth = values.shape[1:]
     width = weight.shape[0]
-    tile = 256
+    tile = 512
 
     def kernel(info, rows_in, weight_in, first, second):
         result = times_back(rows_in[0], weight_in[...])

time: 726 us -> 723 us (level)
    unnamed x350 -> x334, local copies, waits for them, and re-layouts: 43.7 us -> 41.4 us
  transfers between devices with their start and end apart: 114 -> 114, of which waited for: 43 -> 45; matrix products, arithmetic and copies ran while one was open for 6% -> 6% of each run, Pallas kernels for 41% -> 41%
where the time goes in v6:
time: 723 us; the launch traced here: 717 us
  Pallas kernels  326 us (45%)
  waiting for transfers between devices  159 us (22%)
  starting transfers between devices  128 us (18%)
  local copies, waits for them, and re-layouts  63.6 us (9%)
  other arithmetic  19.4 us (3%)
  blocking collectives  10.1 us (1%)
    pallas_call x68, Pallas kernels, run(): pl.pallas_call(body, grid_spec=pltpu.PrefetchScalarGridSpec(num_scalar_pr...  326 us
    ppermute x39, waiting for transfers between devices, z_trade(): lax.ppermute(values, 'z', [(place, place ^ step) for place in range(4)])  86.6 us
    ppermute x64, starting transfers between devices, flip(): return lax.ppermute(values, axis, [(0, 1), (1, 0)])  49.8 us
    ppermute x39, starting transfers between devices, z_trade(): lax.ppermute(values, 'z', [(place, place ^ step) for place in range(4)])  47.2 us
    unnamed x334, local copies, waits for them, and re-layouts  41.4 us
    ppermute x64, waiting for transfers between devices, flip(): return lax.ppermute(values, axis, [(0, 1), (1, 0)])  41.3 us
    ppermute x9, waiting for transfers between devices, swap_only(): return lax.ppermute(values, ('c', 'x'), [(1, 2), (2, 1)])  27 us
    ppermute x9, starting transfers between devices, swap_only(): return lax.ppermute(values, ('c', 'x'), [(1, 2), (2, 1)])  25.3 us
  transfers between devices with their start and end apart: 114, of which 45 were waited for; matrix products, arithmetic and copies ran while one was open for 6% of the time, Pallas kernels for 41%

profile of v6, /device:TPU:9, one launch (start us, length us, event | category | flops | bytes accessed | tf_op | source)
XLA Modules:
  0.0 717.5 jit_solution(18038500243327367523)
XLA Ops:
  14.2 5.7 all-to-all-start
  21.6 4.3 all-to-all-done
  33.8 16.1 %collective-permute-done.6.refs_4_ = bf16[64,2048]{1,0:T(8,128)(2,1)S(1)} collective-permute-done((bf16[64,2048]{1,0:T(8,128)(2,1)S(1)}, bf16[64,2048]{1,0:T(8,128)(2,1)S(1)}, u32[]{:S(2)}, u32[]{:S(2)}) %collective-permute-start.6) | collective-permute-done | bytes 262176 | tf_op jit(solution)/shard_map/ppermute | solution.py:518
  59.4 3.7 collective-permute-start.9
  66.9 12.3 %collective-permute-done.12.refs_6_.refs_3_ = bf16[4,64,2048]{2,1,0:T(8,128)(2,1)S(1)} collective-permute-done((bf16[4,64,2048]{2,1,0:T(8,128)(2,1)}, bf16[4,64,2048]{2,1,0:T(8,128)(2,1)S(1)}, u32[]{:S(2)}, u32[]{:S(2)}) %collective-permute-start.12) | collective-permute-done | bytes 1048608 | tf_op jit(solution)/shard_map/ppermute | solution.py:514
  81.4 4.5 gather_step.8
  98.0 4.1 collective-permute-start.18
  102.1 5.2 collective-permute-done.7.refs_2_
  108.4 3.1 first_norm.1
  111.6 3.8 collective-permute-done.19.refs_4_
  115.4 4.0 collective-permute-done.18.refs_3_
  120.8 8.9 %collective-permute-done.15.refs_5_.refs_4_.refs_2_ = bf16[6,64,2048]{2,1,0:T(8,128)(2,1)} collective-permute-done((bf16[6,64,2048]{2,1,0:T(8,128)(2,1)}, bf16[6,64,2048]{2,1,0:T(8,128)(2,1)}, u32[]{:S(2)}, u32[]{:S(2)}) %collective-permute-start.15) | collective-permute-done | bytes 1572896 | tf_op jit(solution)/shard_map/ppermute | solution.py:514
  138.3 3.1 collective-permute-start.25
  141.7 3.2 place_weights.6
  145.0 5.8 both_plain.4.refs_3_
  150.7 14.6 %attend_spatial.1 = (bf16[2,5,2,64,512]{4,3,2,1,0:T(8,128)(2,1)S(1)}, bf16[5,8,256,256]{3,2,1,0:T(8,128)(2,1)S(1)}) custom-call(s32[5]{0:T(128)S(1)} %concatenate.13.refs_0_, bf16[8,9,64,64]{3,2,1,0:T(8,128)(2,1)S(1)} %bitcast.197, bf16[2,5,2,64,1536]{4,3,2,1,0:T(8,128)(2,1)S(1)} %bitcast.170, bf16[2,640,1536]{2,1,0:T(8,128)(2,1)S(1)} %both_plain.4.refs_3_), custom_call_target="tpu_custom_call" | custom-call | flops 1 | bytes 1 | tf_op jit(solution)/shard_map/attend_spatial/pallas_call | solution.py:583
  177.0 3.2 forward_step.4
  187.9 16.0 %both_gelu.2 = (bf16[2,640,2048]{2,1,0:T(8,128)(2,1)S(1)}, bf16[2,640,2048]{2,1,0:T(8,128)(2,1)S(1)}) custom-call(s32[5]{0:T(128)S(1)} %concatenate.13.refs_0_, bf16[320,1024]{1,0:T(8,128)(2,1)S(1)} %get-tuple-element.202.refs_1_, bf16[320,1024]{1,0:T(8,128)(2,1)S(1)} %get-tuple-element.203.refs_2_, bf16[320,1024]{1,0:T(8,128)(2,1)S(1)} %collective-permute-done.27.refs_3_, ...), custom_call_target="tpu_custom_call" | custom-call | flops 1 | bytes 1 | tf_op jit(solution)/shard_map/both_gelu/pallas_call | solution.py:583
  212.3 3.8 other_rows.9
  222.5 5.1 forward_step.5
  227.7 9.3 %collective-permute-done.42.refs_4_ = bf16[64,2048]{1,0:T(8,128)(2,1)S(1)} collective-permute-done((bf16[64,2048]{1,0:T(8,128)(2,1)S(1)}, bf16[64,2048]{1,0:T(8,128)(2,1)S(1)}, u32[]{:S(2)}, u32[]{:S(2)}) %collective-permute-start.42) | collective-permute-done | bytes 262176 | tf_op jit(solution)/shard_map/ppermute | solution.py:518
  237.0 4.3 collective-permute-done.41.refs_3_
  247.4 3.3 collective-permute-start.36
  253.4 5.8 both_plain.5.refs_3_
  259.2 16.4 %attend_joint.1 = (bf16[2,5,2,64,512]{4,3,2,1,0:T(8,128)(2,1)S(1)}, bf16[4,8,320,320]{3,2,1,0:T(8,128)(2,1)S(1)}) custom-call(s32[5]{0:T(128)S(1)} %concatenate.13.refs_0_, bf16[8,9,64,64]{3,2,1,0:T(8,128)(2,1)S(1)} %squeeze.38.refs_6_.refs_1_, bf16[2,5,2,64,1536]{4,3,2,1,0:T(8,128)(2,1)S(1)} %bitcast.172, bf16[2,640,1536]{2,1,0:T(8,128)(2,1)S(1)} %both_plain.5.refs_3_), custom_call_target="tpu_custom_call" | custom-call | flops 1 | bytes 1 | tf_op jit(solution)/shard_map/attend_joint/pallas_call | solution.py:583
  275.6 3.2 copy-done.22
  290.8 16.0 %both_gelu.3 = (bf16[2,640,2048]{2,1,0:T(8,128)(2,1)S(1)}, bf16[2,640,2048]{2,1,0:T(8,128)(2,1)S(1)}) custom-call(s32[5]{0:T(128)S(1)} %concatenate.13.refs_0_, bf16[320,1024]{1,0:T(8,128)(2,1)S(1)} %get-tuple-element.224.refs_1_, bf16[320,1024]{1,0:T(8,128)(2,1)S(1)} %get-tuple-element.225.refs_2_, bf16[320,1024]{1,0:T(8,128)(2,1)S(1)} %collective-permute-done.47.refs_3_, ...), custom_call_target="tpu_custom_call" | custom-call | flops 1 | bytes 1 | tf_op jit(solution)/shard_map/both_gelu/pallas_call | solution.py:583
  313.9 3.8 other_rows.11
  320.8 4.2 forward_step.7
  337.3 8.1 %both_slope.2.refs_1_.refs_3_.refs_5_ = bf16[2,640,2048]{2,1,0:T(8,128)(2,1)S(1)} custom-call(s32[5]{0:T(128)S(1)} %concatenate.13.refs_0_, bf16[320,1024]{1,0:T(8,128)(2,1)S(1)} %get-tuple-element.233.refs_1_.refs_7_, bf16[320,1024]{1,0:T(8,128)(2,1)S(1)} %get-tuple-element.234.refs_2_, bf16[320,1024]{1,0:T(8,128)(2,1)S(1)} %collective-permute-done.55.refs_3_, ...), custom_call_target="tpu_custom_call" | custom-call | flops 1 | bytes 1 | tf_op jit(solution)/shard_map/both_slope/pallas_call | solution.py:583
  345.4 3.8 other_rows.12
  349.7 9.2 %weight_grad.6 = (bf16[4,64,2048]{2,1,0:T(8,128)(2,1)S(1)}, bf16[4,64,2048]{2,1,0:T(8,128)(2,1)S(1)}, bf16[4,64,2048]{2,1,0:T(8,128)(2,1)S(1)}, bf16[2,64,2048]{2,1,0:T(8,128)(2,1)S(1)}, bf16[2,64,2048]{2,1,0:T(8,128)(2,1)S(1)}) custom-call(s32[5]{0:T(128)S(1)} %concatenate.13.refs_0_, bf16[320,1024]{1,0:T(8,128)(2,1)S(1)} %get-tuple-element.233.refs_1_.refs_7_, ...), custom_call_target="tpu_custom_call" | custom-call | flops 1 | bytes 1 | tf_op jit(solution)/shard_map/weight_grad/pallas_call | solution.py:583
  362.8 6.3 backward_step.4
  369.2 9.2 %weight_grad.7 = (bf16[4,64,2048]{2,1,0:T(8,128)(2,1)S(1)}, bf16[4,64,2048]{2,1,0:T(8,128)(2,1)S(1)}, bf16[4,64,2048]{2,1,0:T(8,128)(2,1)S(1)}, bf16[2,64,2048]{2,1,0:T(8,128)(2,1)S(1)}, bf16[2,64,2048]{2,1,0:T(8,128)(2,1)S(1)}) custom-call(s32[5]{0:T(128)S(1)} %concatenate.13.refs_0_, bf16[320,1024]{1,0:T(8,128)(2,1)S(1)} %copy-done.61, ...), custom_call_target="tpu_custom_call" | custom-call | flops 1 | bytes 1 | tf_op jit(solution)/shard_map/weight_grad/pallas_call | solution.py:583
  379.4 3.1 scatter_step.8
  390.0 18.8 %attend_back_joint.1 = (bf16[2,5,2,64,1536]{4,3,2,1,0:T(8,128)(2,1)S(1)}, f32[8,9,64,64]{3,2,1,0:T(8,128)S(1)}) custom-call(s32[5]{0:T(128)S(1)} %concatenate.13.refs_0_, bf16[2,5,2,64,1536]{4,3,2,1,0:T(8,128)(2,1)S(1)} %bitcast.173, bf16[2,5,2,64,512]{4,3,2,1,0:T(8,128)(2,1)S(1)} %bitcast.195, bf16[4,8,320,320]{3,2,1,0:T(8,128)(2,1)S(1)} %bitcast.205, ...), custom_call_target="tpu_custom_call" | custom-call | flops 1 | bytes 1 | tf_op jit(solution)/shard_map/attend_back_joint/pallas_call | solution.py:583
  412.5 10.5 %weight_grad.8 = (bf16[4,64,2048]{2,1,0:T(8,128)(2,1)S(1)}, bf16[4,64,2048]{2,1,0:T(8,128)(2,1)S(1)}, bf16[4,64,2048]{2,1,0:T(8,128)(2,1)S(1)}, bf16[2,64,2048]{2,1,0:T(8,128)(2,1)S(1)}, bf16[2,64,2048]{2,1,0:T(8,128)(2,1)S(1)}) custom-call(s32[5]{0:T(128)S(1)} %concatenate.13.refs_0_, bf16[320,1024]{1,0:T(8,128)(2,1)S(1)} %copy-done.45, ...), custom_call_target="tpu_custom_call" | custom-call | flops 1 | bytes 1 | tf_op jit(solution)/shard_map/weight_grad/pallas_call | solution.py:583
  423.1 3.8 scatter_step.9
  428.5 5.5 backward_step.5
  441.4 8.1 %both_slope.3.refs_1_.refs_3_.refs_5_ = bf16[2,640,2048]{2,1,0:T(8,128)(2,1)S(1)} custom-call(s32[5]{0:T(128)S(1)} %concatenate.13.refs_0_, bf16[320,1024]{1,0:T(8,128)(2,1)S(1)} %get-tuple-element.267.refs_1_, bf16[320,1024]{1,0:T(8,128)(2,1)S(1)} %get-tuple-element.268.refs_2_, bf16[320,1024]{1,0:T(8,128)(2,1)S(1)} %collective-permute-done.67.refs_3_, ...), custom_call_target="tpu_custom_call" | custom-call | flops 1 | bytes 1 | tf_op jit(solution)/shard_map/both_slope/pallas_call | solution.py:583
  449.5 3.7 other_rows.14
  453.3 9.2 %weight_grad.9 = (bf16[4,64,2048]{2,1,0:T(8,128)(2,1)S(1)}, bf16[4,64,2048]{2,1,0:T(8,128)(2,1)S(1)}, bf16[4,64,2048]{2,1,0:T(8,128)(2,1)S(1)}, bf16[2,64,2048]{2,1,0:T(8,128)(2,1)S(1)}, bf16[2,64,2048]{2,1,0:T(8,128)(2,1)S(1)}) custom-call(s32[5]{0:T(128)S(1)} %concatenate.13.refs_0_, bf16[320,1024]{1,0:T(8,128)(2,1)S(1)} %get-tuple-element.267.refs_1_, ...), custom_call_target="tpu_custom_call" | custom-call | flops 1 | bytes 1 | tf_op jit(solution)/shard_map/weight_grad/pallas_call | solution.py:583
  463.7 4.2 scatter_step.10
  470.2 6.5 backward_step.6
  483.0 9.2 %weight_grad.10 = (bf16[4,64,2048]{2,1,0:T(8,128)(2,1)S(1)}, bf16[4,64,2048]{2,1,0:T(8,128)(2,1)S(1)}, bf16[4,64,2048]{2,1,0:T(8,128)(2,1)S(1)}, bf16[2,64,2048]...) custom-call(s32[5]{0:T(128)S(1)} %concatenate.13.refs_0_, bf16[320,1024]{1,0:T(8,128)(2,1)S(1)} %copy-done.53, ...), custom_call_target="tpu_custom_call" | custom-call | flops 1 | bytes 1 | tf_op jit(solution)/shard_map/weight_grad/pallas_call | solution.py:583
  495.3 3.3 collective-permute-done.81.refs_10_
  498.6 7.4 %collective-permute-done.82.refs_11_ = bf16[64,2048]{1,0:T(8,128)(2,1)S(1)} collective-permute-done((bf16[64,2048]{1,0:T(8,128)(2,1)S(1)}, bf16[64,2048]{1,0:T(8,128)(2,1)S(1)}, u32[]{:S(2)}, u32[]{:S(2)}) %collective-permute-start.82) | collective-permute-done | bytes 262176 | tf_op jit(solution)/shard_map/ppermute | solution.py:518
  506.0 3.5 scatter_step.11
  512.9 17.9 %attend_back_spatial.1 = (bf16[2,5,2,64,1536]{4,3,2,1,0:T(8,128)(2,1)S(1)}, f32[8,9,64,64]{3,2,1,0:T(8,128)S(1)}) custom-call(s32[5]{0:T(128)S(1)} %concatenate.13.refs_0_, bf16[2,5,2,64,1536]{4,3,2,1,0:T(8,128)(2,1)S(1)} %bitcast.171, bf16[2,5,2,64,512]{4,3,2,1,0:T(8,128)(2,1)S(1)} %bitcast.192, bf16[5,8,256,256]{3,2,1,0:T(8,128)(2,1)S(1)} %bitcast.207, ...), custom_call_target="tpu_custom_call" | custom-call | flops 1 | bytes 1 | tf_op jit(solution)/shard_map/attend_back_spatial/pallas_call | solution.py:583
  533.9 10.5 %weight_grad.11 = (bf16[4,64,2048]{2,1,0:T(8,128)(2,1)S(1)}, bf16[4,64,2048]{2,1,0:T(8,128)(2,1)S(1)}, bf16[4,64,2048]{2,1,0:T(8,128)(2,1)S(1)}, bf16[2,64,2048]...) custom-call(s32[5]{0:T(128)S(1)} %concatenate.13.refs_0_, bf16[320,1024]{1,0:T(8,128)(2,1)S(1)} %copy-done.37, ...), custom_call_target="tpu_custom_call" | custom-call | flops 1 | bytes 1 | tf_op jit(solution)/shard_map/weight_grad/pallas_call | solution.py:583
  546.5 3.6 scatter_step.12
  553.1 3.2 collective-permute-start.84
  560.6 8.7 %bias_tables.1 = (f32[8,9,256]{2,1,0:T(8,128)S(1)}, f32[8,9,256]{2,1,0:T(8,128)S(1)}) custom-call(s32[5]{0:T(128)S(1)} %concatenate.13.refs_0_, f32[8,9,64,64]{3,2,1,0:T(8,128)S(1)} %get-tuple-element.307.refs_1_, f32[8,9,64,64]{3,2,1,0:T(8,128)S(1)} %copy-done.69, bf16[192,256]{1,0:T(8,128)(2,1)S(1)} %copy-done.140, ...), custom_call_target="tpu_custom_call" | custom-call | flops 1 | bytes 1 | tf_op jit(solution)/shard_map/bias_tables/pallas_call | solution.py:583
  569.4 4.5 backward_step.7
  576.7 7.0 collective-permute-done.92.refs_9_
  588.0 10.1 %all_to_all.10 = f32[32,2,192]{2,1,0:T(2,128)S(1)} all-to-all(f32[32,2,192]{2,1,0:T(2,128)S(1)} %bitcast.227), channel_id=1, replica_groups=mesh['z'=4,'y'=2,'c'=2,'x'=2] {'z','y','c','x'}, dimensions={0} | all-to-all | bytes 98304 | tf_op jit(solution)/shard_map/all_to_all | solution.py:1688
  606.2 4.8 scatter_step.13
  623.5 5.5 collective-permute-done.97.refs_5_
  631.5 12.1 %collective-permute-done.99.refs_7_ = bf16[64,2048]{1,0:T(8,128)(2,1)} collective-permute-done((bf16[64,2048]{1,0:T(8,128)(2,1)}, bf16[64,2048]{1,0:T(8,128)(2,1)}, u32[]{:S(2)}, u32[]{:S(2)}) %collective-permute-start.99) | collective-permute-done | bytes 262176 | tf_op jit(solution)/shard_map/ppermute | solution.py:518
  645.9 3.3 scatter_step.14
  651.6 5.3 collective-permute-start.108
  667.9 4.3 collective-permute-done.108
  672.9 13.4 %collective-permute-done.100 = bf16[640,1024]{1,0:T(8,128)(2,1)S(1)} collective-permute-done((bf16[640,1024]{1,0:T(8,128)(2,1)S(1)}, bf16[640,1024]{1,0:T(8,128)(2,1)S(1)}, u32[]{:S(2)}, u32[]{:S(2)}) %collective-permute-start.100) | collective-permute-done | bytes 1310752 | tf_op jit(solution)/shard_map/ppermute | solution.py:522
  687.9 6.1 collective-permute-done.107.refs_4_
  (660 shorter events, 262.3 us)
Async XLA Ops:
  1.4 18.6 %collective-permute-start = (f32[1]{0:T(128)}, f32[1]{0:T(128)}, u32[]{:S(2)}, u32[]{:S(2)}) collective-permute-start(f32[1]{0:T(128)} %convert_element_type.71), channel_id=1, source_target_pairs={{0,2},{2,0},{1,3},{3,1},{4,6},{6,4},{5,7},{7,5},{8,10},{10,8},{9,1... | collective-permute-start | bytes 20 | tf_op jit(solution)/shard_map/ppermute | solution.py:514
  10.2 19.3 %collective-permute-start.3 = (bf16[64,2048]{1,0:T(8,128)(2,1)S(1)}, bf16[64,2048]{1,0:T(8,128)(2,1)}, u32[]{:S(2)}, u32[]{:S(2)}) collective-permute-start(bf16[64,2048]{1,0:T(8,128)(2,1)S(1)} %pad_maximum_fusion.3), channel_id=1, source_target_pairs={{1,2},{2,1},{5,6},{6,5},{9,10},{10,9},{13,14},{14,13},{17,18},{18,... | collective-permute-start | bytes 786440 | tf_op jit(solution)/shard_map/ppermute | solution.py:522
  26.7 28.0 %collective-permute-start.2 = (bf16[64,10240]{1,0:T(8,128)(2,1)S(1)}, bf16[64,10240]{1,0:T(8,128)(2,1)S(1)}, u32[]{:S(2)}, u32[]{:S(2)}) collective-permute-start(bf16[64,10240]{1,0:T(8,128)(2,1)S(1)} %pack_arguments.1.refs_5_.refs_1_), channel_id=1, source_target_pairs={{1,2},{2,1},{5,6},{6,5},{9,10},{10,9},{13,14},{14,13},{17,18},{18,... | collective-permute-start | bytes 3932168 | tf_op jit(solution)/shard_map/ppermute | solution.py:522
  30.5 19.4 %collective-permute-start.6 = (bf16[64,2048]{1,0:T(8,128)(2,1)S(1)}, bf16[64,2048]{1,0:T(8,128)(2,1)S(1)}, u32[]{:S(2)}, u32[]{:S(2)}) collective-permute-start(bf16[64,2048]{1,0:T(8,128)(2,1)S(1)} %broadcast_select_fusion.4.refs_1_), channel_id=1, source_target_pairs={{0,24},{8,16},{16,8},{24,0},{1,25},{9,17},{17,9},{25,1},{2,26},{10... | collective-permute-start | bytes 786440 | tf_op jit(solution)/shard_map/ppermute | solution.py:518
  30.9 20.8 %collective-permute-start.5 = (bf16[64,2048]{1,0:T(8,128)(2,1)S(1)}, bf16[64,2048]{1,0:T(8,128)(2,1)S(1)}, u32[]{:S(2)}, u32[]{:S(2)}) collective-permute-start(bf16[64,2048]{1,0:T(8,128)(2,1)S(1)} %broadcast_select_fusion.4.refs_1_), channel_id=1, source_target_pairs={{0,16},{8,24},{16,0},{24,8},{1,17},{9,25},{17,1},{25,9},{2,18},{10... | collective-permute-start | bytes 786440 | tf_op jit(solution)/shard_map/ppermute | solution.py:518
  54.1 25.1 %collective-permute-start.12 = (bf16[4,64,2048]{2,1,0:T(8,128)(2,1)}, bf16[4,64,2048]{2,1,0:T(8,128)(2,1)S(1)}, u32[]{:S(2)}, u32[]{:S(2)}) collective-permute-start(bf16[4,64,2048]{2,1,0:T(8,128)(2,1)} %get-tuple-element.186), channel_id=1, source_target_pairs={{0,4},{4,0},{1,5},{5,1},{2,6},{6,2},{3,7},{7,3},{8,12},{12,8},{9,1... | collective-permute-start | bytes 3145736 | tf_op jit(solution)/shard_map/ppermute | solution.py:514
  54.7 26.6 %collective-permute-start.11 = (bf16[4,64,2048]{2,1,0:T(8,128)(2,1)}, bf16[4,64,2048]{2,1,0:T(8,128)(2,1)}, u32[]{:S(2)}, u32[]{:S(2)}) collective-permute-start(bf16[4,64,2048]{2,1,0:T(8,128)(2,1)} %get-tuple-element.184.refs_3_.refs_1_), channel_id=1, source_target_pairs={{0,1},{1,0},{2,3},{3,2},{4,5},{5,4},{6,7},{7,6},{8,9},{9,8},{10,11... | collective-permute-start | bytes 3145736 | tf_op jit(solution)/shard_map/ppermute | solution.py:514
  58.2 23.1 %collective-permute-start.10 = (bf16[64,2048]{1,0:T(8,128)(2,1)S(1)}, bf16[64,2048]{1,0:T(8,128)(2,1)}, u32[]{:S(2)}, u32[]{:S(2)}) collective-permute-start(bf16[64,2048]{1,0:T(8,128)(2,1)S(1)} %get-tuple-element.185.refs_2_.refs_1_), channel_id=1, source_target_pairs={{0,24},{8,16},{16,8},{24,0},{1,25},{9,17},{17,9},{25,1},{2,26},{10... | collective-permute-start | bytes 786440 | tf_op jit(solution)/shard_map/ppermute | solution.py:518
  59.4 22.1 %collective-permute-start.9 = (bf16[64,2048]{1,0:T(8,128)(2,1)S(1)}, bf16[64,2048]{1,0:T(8,128)(2,1)}, u32[]{:S(2)}, u32[]{:S(2)}) collective-permute-start(bf16[64,2048]{1,0:T(8,128)(2,1)S(1)} %get-tuple-element.185.refs_2_.refs_1_), channel_id=1, source_target_pairs={{0,16},{8,24},{16,0},{24,8},{1,17},{9,25},{17,1},{25,9},{2,18},{10... | collective-permute-start | bytes 786440 | tf_op jit(solution)/shard_map/ppermute | solution.py:518
  79.2 28.1 %collective-permute-start.7 = (bf16[640,1024]{1,0:T(8,128)(2,1)}, bf16[640,1024]{1,0:T(8,128)(2,1)}, u32[]{:S(2)}, u32[]{:S(2)}) collective-permute-start(bf16[640,1024]{1,0:T(8,128)(2,1)} %copy_rows.3.refs_7_.refs_1_), channel_id=1, source_target_pairs={{1,2},{2,1},{5,6},{6,5},{9,10},{10,9},{13,14},{14,13},{17,18},{18,... | collective-permute-start | bytes 3932168 | tf_op jit(solution)/shard_map/ppermute | solution.py:522
  85.9 34.9 %collective-permute-start.16 = (bf16[6,64,2048]{2,1,0:T(8,128)(2,1)}, bf16[6,64,2048]{2,1,0:T(8,128)(2,1)S(1)}, u32[]{:S(2)}, u32[]{:S(2)}) collective-permute-start(bf16[6,64,2048]{2,1,0:T(8,128)(2,1)} %get-tuple-element.190), channel_id=1, source_target_pairs={{0,4},{4,0},{1,5},{5,1},{2,6},{6,2},{3,7},{7,3},{8,12},{12,8},{9,1... | collective-permute-start | bytes 4718600 | tf_op jit(solution)/shard_map/ppermute | solution.py:514
  86.8 42.8 %collective-permute-start.15 = (bf16[6,64,2048]{2,1,0:T(8,128)(2,1)}, bf16[6,64,2048]{2,1,0:T(8,128)(2,1)}, u32[]{:S(2)}, u32[]{:S(2)}) collective-permute-start(bf16[6,64,2048]{2,1,0:T(8,128)(2,1)} %get-tuple-element.187.refs_4_.refs_1_), channel_id=1, source_target_pairs={{0,1},{1,0},{2,3},{3,2},{4,5},{5,4},{6,7},{7,6},{8,9},{9,8},{10,11... | collective-permute-start | bytes 4718600 | tf_op jit(solution)/shard_map/ppermute | solution.py:514
  98.0 21.4 %collective-permute-start.18 = (bf16[64,2048]{1,0:T(8,128)(2,1)S(1)}, bf16[64,2048]{1,0:T(8,128)(2,1)S(1)}, u32[]{:S(2)}, u32[]{:S(2)}) collective-permute-start(bf16[64,2048]{1,0:T(8,128)(2,1)S(1)} %copy-done.136), channel_id=1, source_target_pairs={{0,16},{8,24},{16,0},{24,8},{1,17},{9,25},{17,1},{25,9},{2,18},{10... | collective-permute-start | bytes 786440 | tf_op jit(solution)/shard_map/ppermute | solution.py:518
  132.6 37.6 %collective-permute-start.23 = (bf16[6,64,2048]{2,1,0:T(8,128)(2,1)S(1)}, bf16[6,64,2048]{2,1,0:T(8,128)(2,1)S(1)}, u32[]{:S(2)}, u32[]{:S(2)}) collective-permute-start(bf16[6,64,2048]{2,1,0:T(8,128)(2,1)S(1)} %get-tuple-element.199), channel_id=1, source_target_pairs={{0,4},{4,0},{1,5},{5,1},{2,6},{6,2},{3,7},{7,3},{8,12},{12,8},{9,1... | collective-permute-start | bytes 4718600 | tf_op jit(solution)/shard_map/ppermute | solution.py:514
  133.2 37.1 %collective-permute-start.22 = (bf16[6,64,2048]{2,1,0:T(8,128)(2,1)S(1)}, bf16[6,64,2048]{2,1,0:T(8,128)(2,1)S(1)}, u32[]{:S(2)}, u32[]{:S(2)}) collective-permute-start(bf16[6,64,2048]{2,1,0:T(8,128)(2,1)S(1)} %get-tuple-element.193.refs_6_.refs_1_), channel_id=1, source_target_pairs={{0,1},{1,0},{2,3},{3,2},{4,5},{5,4},{6,7},{7,6},{8,9},{9,8},{10,11... | collective-permute-start | bytes 4718600 | tf_op jit(solution)/shard_map/ppermute | solution.py:514
  136.6 32.8 %collective-permute-start.26 = (bf16[64,2048]{1,0:T(8,128)(2,1)S(1)}, bf16[64,2048]{1,0:T(8,128)(2,1)S(1)}, u32[]{:S(2)}, u32[]{:S(2)}) collective-permute-start(bf16[64,2048]{1,0:T(8,128)(2,1)S(1)} %copy-done.132), channel_id=1, source_target_pairs={{0,24},{8,16},{16,8},{24,0},{1,25},{9,17},{17,9},{25,1},{2,26},{10... | collective-permute-start | bytes 786440 | tf_op jit(solution)/shard_map/ppermute | solution.py:518
  138.3 31.8 %collective-permute-start.25 = (bf16[64,2048]{1,0:T(8,128)(2,1)S(1)}, bf16[64,2048]{1,0:T(8,128)(2,1)S(1)}, u32[]{:S(2)}, u32[]{:S(2)}) collective-permute-start(bf16[64,2048]{1,0:T(8,128)(2,1)S(1)} %copy-done.132), channel_id=1, source_target_pairs={{0,16},{8,24},{16,0},{24,8},{1,17},{9,25},{17,1},{25,9},{2,18},{10... | collective-permute-start | bytes 786440 | tf_op jit(solution)/shard_map/ppermute | solution.py:518
  141.4 28.8 %collective-permute-start.24 = (bf16[64,2048]{1,0:T(8,128)(2,1)S(1)}, bf16[64,2048]{1,0:T(8,128)(2,1)S(1)}, u32[]{:S(2)}, u32[]{:S(2)}) collective-permute-start(bf16[64,2048]{1,0:T(8,128)(2,1)S(1)} %copy-done.132), channel_id=1, source_target_pairs={{0,8},{8,0},{16,24},{24,16},{1,9},{9,1},{17,25},{25,17},{2,10},{10... | collective-permute-start | bytes 786440 | tf_op jit(solution)/shard_map/ppermute | solution.py:518
  171.5 35.6 %collective-permute-start.30 = (bf16[6,64,2048]{2,1,0:T(8,128)(2,1)S(1)}, bf16[6,64,2048]{2,1,0:T(8,128)(2,1)S(1)}, u32[]{:S(2)}, u32[]{:S(2)}) collective-permute-start(bf16[6,64,2048]{2,1,0:T(8,128)(2,1)S(1)} %get-tuple-element.206), channel_id=1, source_target_pairs={{0,4},{4,0},{1,5},{5,1},{2,6},{6,2},{3,7},{7,3},{8,12},{12,8},{9,1... | collective-permute-start | bytes 4718600 | tf_op jit(solution)/shard_map/ppermute | solution.py:514
  172.2 35.8 %collective-permute-start.29 = (bf16[6,64,2048]{2,1,0:T(8,128)(2,1)S(1)}, bf16[6,64,2048]{2,1,0:T(8,128)(2,1)S(1)}, u32[]{:S(2)}, u32[]{:S(2)}) collective-permute-start(bf16[6,64,2048]{2,1,0:T(8,128)(2,1)S(1)} %get-tuple-element.201.refs_6_.refs_1_), channel_id=1, source_target_pairs={{0,1},{1,0},{2,3},{3,2},{4,5},{5,4},{6,7},{7,6},{8,9},{9,8},{10,11... | collective-permute-start | bytes 4718600 | tf_op jit(solution)/shard_map/ppermute | solution.py:514
  183.4 23.0 %collective-permute-start.33 = (bf16[64,2048]{1,0:T(8,128)(2,1)S(1)}, bf16[64,2048]{1,0:T(8,128)(2,1)S(1)}, u32[]{:S(2)}, u32[]{:S(2)}) collective-permute-start(bf16[64,2048]{1,0:T(8,128)(2,1)S(1)} %copy-done.128), channel_id=1, source_target_pairs={{0,24},{8,16},{16,8},{24,0},{1,25},{9,17},{17,9},{25,1},{2,26},{10... | collective-permute-start | bytes 786440 | tf_op jit(solution)/shard_map/ppermute | solution.py:518
  185.0 21.6 %collective-permute-start.32 = (bf16[64,2048]{1,0:T(8,128)(2,1)S(1)}, bf16[64,2048]{1,0:T(8,128)(2,1)S(1)}, u32[]{:S(2)}, u32[]{:S(2)}) collective-permute-start(bf16[64,2048]{1,0:T(8,128)(2,1)S(1)} %copy-done.128), channel_id=1, source_target_pairs={{0,16},{8,24},{16,0},{24,8},{1,17},{9,25},{17,1},{25,9},{2,18},{10... | collective-permute-start | bytes 786440 | tf_op jit(solution)/shard_map/ppermute | solution.py:518
  187.9 18.8 %collective-permute-start.31 = (bf16[64,2048]{1,0:T(8,128)(2,1)S(1)}, bf16[64,2048]{1,0:T(8,128)(2,1)S(1)}, u32[]{:S(2)}, u32[]{:S(2)}) collective-permute-start(bf16[64,2048]{1,0:T(8,128)(2,1)S(1)} %copy-done.128), channel_id=1, source_target_pairs={{0,8},{8,0},{16,24},{24,16},{1,9},{9,1},{17,25},{25,17},{2,10},{10... | collective-permute-start | bytes 786440 | tf_op jit(solution)/shard_map/ppermute | solution.py:518
  209.3 34.7 %collective-permute-start.39 = (bf16[6,64,2048]{2,1,0:T(8,128)(2,1)S(1)}, bf16[6,64,2048]{2,1,0:T(8,128)(2,1)S(1)}, u32[]{:S(2)}, u32[]{:S(2)}) collective-permute-start(bf16[6,64,2048]{2,1,0:T(8,128)(2,1)S(1)} %get-tuple-element.213), channel_id=1, source_target_pairs={{0,4},{4,0},{1,5},{5,1},{2,6},{6,2},{3,7},{7,3},{8,12},{12,8},{9,1... | collective-permute-start | bytes 4718600 | tf_op jit(solution)/shard_map/ppermute | solution.py:514
  210.2 34.4 %collective-permute-start.38 = (bf16[6,64,2048]{2,1,0:T(8,128)(2,1)S(1)}, bf16[6,64,2048]{2,1,0:T(8,128)(2,1)S(1)}, u32[]{:S(2)}, u32[]{:S(2)}) collective-permute-start(bf16[6,64,2048]{2,1,0:T(8,128)(2,1)S(1)} %get-tuple-element.208.refs_6_.refs_1_), channel_id=1, source_target_pairs={{0,1},{1,0},{2,3},{3,2},{4,5},{5,4},{6,7},{7,6},{8,9},{9,8},{10,11... | collective-permute-start | bytes 4718600 | tf_op jit(solution)/shard_map/ppermute | solution.py:514
  218.3 18.7 %collective-permute-start.42 = (bf16[64,2048]{1,0:T(8,128)(2,1)S(1)}, bf16[64,2048]{1,0:T(8,128)(2,1)S(1)}, u32[]{:S(2)}, u32[]{:S(2)}) collective-permute-start(bf16[64,2048]{1,0:T(8,128)(2,1)S(1)} %copy-done.126), channel_id=1, source_target_pairs={{0,24},{8,16},{16,8},{24,0},{1,25},{9,17},{17,9},{25,1},{2,26},{10... | collective-permute-start | bytes 786440 | tf_op jit(solution)/shard_map/ppermute | solution.py:518
  220.0 21.4 %collective-permute-start.41 = (bf16[64,2048]{1,0:T(8,128)(2,1)S(1)}, bf16[64,2048]{1,0:T(8,128)(2,1)S(1)}, u32[]{:S(2)}, u32[]{:S(2)}) collective-permute-start(bf16[64,2048]{1,0:T(8,128)(2,1)S(1)} %copy-done.126), channel_id=1, source_target_pairs={{0,16},{8,24},{16,0},{24,8},{1,17},{9,25},{17,1},{25,9},{2,18},{10... | collective-permute-start | bytes 786440 | tf_op jit(solution)/shard_map/ppermute | solution.py:518
  222.2 19.1 %collective-permute-start.40 = (bf16[64,2048]{1,0:T(8,128)(2,1)S(1)}, bf16[64,2048]{1,0:T(8,128)(2,1)S(1)}, u32[]{:S(2)}, u32[]{:S(2)}) collective-permute-start(bf16[64,2048]{1,0:T(8,128)(2,1)S(1)} %copy-done.126), channel_id=1, source_target_pairs={{0,8},{8,0},{16,24},{24,16},{1,9},{9,1},{17,25},{25,17},{2,10},{10... | collective-permute-start | bytes 786440 | tf_op jit(solution)/shard_map/ppermute | solution.py:518
  245.8 35.3 %collective-permute-start.46 = (bf16[6,64,2048]{2,1,0:T(8,128)(2,1)S(1)}, bf16[6,64,2048]{2,1,0:T(8,128)(2,1)S(1)}, u32[]{:S(2)}, u32[]{:S(2)}) collective-permute-start(bf16[6,64,2048]{2,1,0:T(8,128)(2,1)S(1)} %get-tuple-element.222), channel_id=1, source_target_pairs={{0,4},{4,0},{1,5},{5,1},{2,6},{6,2},{3,7},{7,3},{8,12},{12,8},{9,1... | collective-permute-start | bytes 4718600 | tf_op jit(solution)/shard_map/ppermute | solution.py:514
  246.4 34.7 %collective-permute-start.45 = (bf16[6,64,2048]{2,1,0:T(8,128)(2,1)S(1)}, bf16[6,64,2048]{2,1,0:T(8,128)(2,1)S(1)}, u32[]{:S(2)}, u32[]{:S(2)}) collective-permute-start(bf16[6,64,2048]{2,1,0:T(8,128)(2,1)S(1)} %get-tuple-element.216.refs_6_.refs_1_), channel_id=1, source_target_pairs={{0,1},{1,0},{2,3},{3,2},{4,5},{5,4},{6,7},{7,6},{8,9},{9,8},{10,11... | collective-permute-start | bytes 4718600 | tf_op jit(solution)/shard_map/ppermute | solution.py:514
  288.2 20.9 %collective-permute-start.50 = (bf16[2,64,2048]{2,1,0:T(8,128)(2,1)S(1)}, bf16[2,64,2048]{2,1,0:T(8,128)(2,1)S(1)}, u32[]{:S(2)}, u32[]{:S(2)}) collective-permute-start(bf16[2,64,2048]{2,1,0:T(8,128)(2,1)S(1)} %get-tuple-element.228), channel_id=1, source_target_pairs={{0,4},{4,0},{1,5},{5,1},{2,6},{6,2},{3,7},{7,3},{8,12},{12,8},{9,1... | collective-permute-start | bytes 1572872 | tf_op jit(solution)/shard_map/ppermute | solution.py:514
  289.1 20.1 %collective-permute-start.49 = (bf16[2,64,2048]{2,1,0:T(8,128)(2,1)S(1)}, bf16[2,64,2048]{2,1,0:T(8,128)(2,1)S(1)}, u32[]{:S(2)}, u32[]{:S(2)}) collective-permute-start(bf16[2,64,2048]{2,1,0:T(8,128)(2,1)S(1)} %get-tuple-element.223.refs_6_), channel_id=1, source_target_pairs={{0,1},{1,0},{2,3},{3,2},{4,5},{5,4},{6,7},{7,6},{8,9},{9,8},{10,11... | collective-permute-start | bytes 1572872 | tf_op jit(solution)/shard_map/ppermute | solution.py:514
  310.8 18.9 %collective-permute-start.54 = (bf16[640,1024]{1,0:T(8,128)(2,1)S(1)}, bf16[640,1024]{1,0:T(8,128)(2,1)S(1)}, u32[]{:S(2)}, u32[]{:S(2)}) collective-permute-start(bf16[640,1024]{1,0:T(8,128)(2,1)S(1)} %copy_rows.4.refs_3_), channel_id=1, source_target_pairs={{1,2},{2,1},{5,6},{6,5},{9,10},{10,9},{13,14},{14,13},{17,18},{18,... | collective-permute-start | bytes 3932168 | tf_op jit(solution)/shard_map/ppermute | solution.py:522
  325.0 35.7 %collective-permute-start.53 = (bf16[640,1024]{1,0:T(8,128)(2,1)S(1)}, bf16[640,1024]{1,0:T(8,128)(2,1)}, u32[]{:S(2)}, u32[]{:S(2)}) collective-permute-start(bf16[640,1024]{1,0:T(8,128)(2,1)S(1)} %get-tuple-element.231.refs_4_), channel_id=1, source_target_pairs={{1,2},{2,1},{5,6},{6,5},{9,10},{10,9},{13,14},{14,13},{17,18},{18,... | collective-permute-start | bytes 3932168 | tf_op jit(solution)/shard_map/ppermute | solution.py:522
  358.9 20.5 %collective-permute-start.61 = (bf16[2,64,2048]{2,1,0:T(8,128)(2,1)S(1)}, bf16[2,64,2048]{2,1,0:T(8,128)(2,1)S(1)}, u32[]{:S(2)}, u32[]{:S(2)}) collective-permute-start(bf16[2,64,2048]{2,1,0:T(8,128)(2,1)S(1)} %get-tuple-element.249), channel_id=1, source_target_pairs={{0,1},{1,0},{2,3},{3,2},{4,5},{5,4},{6,7},{7,6},{8,9},{9,8},{10,11... | collective-permute-start | bytes 1572872 | tf_op jit(solution)/shard_map/ppermute | solution.py:514
  359.9 19.5 %collective-permute-start.62 = (bf16[2,64,2048]{2,1,0:T(8,128)(2,1)S(1)}, bf16[2,64,2048]{2,1,0:T(8,128)(2,1)S(1)}, u32[]{:S(2)}, u32[]{:S(2)}) collective-permute-start(bf16[2,64,2048]{2,1,0:T(8,128)(2,1)S(1)} %get-tuple-element.250), channel_id=1, source_target_pairs={{0,4},{4,0},{1,5},{5,1},{2,6},{6,2},{3,7},{7,3},{8,12},{12,8},{9,1... | collective-permute-start | bytes 1572872 | tf_op jit(solution)/shard_map/ppermute | solution.py:514
  382.6 40.4 %collective-permute-start.66 = (bf16[6,64,2048]{2,1,0:T(8,128)(2,1)}, bf16[6,64,2048]{2,1,0:T(8,128)(2,1)S(1)}, u32[]{:S(2)}, u32[]{:S(2)}) collective-permute-start(bf16[6,64,2048]{2,1,0:T(8,128)(2,1)} %get-tuple-element.264), channel_id=1, source_target_pairs={{0,4},{4,0},{1,5},{5,1},{2,6},{6,2},{3,7},{7,3},{8,12},{12,8},{9,1... | collective-permute-start | bytes 4718600 | tf_op jit(solution)/shard_map/ppermute | solution.py:514
  383.3 39.7 %collective-permute-start.65 = (bf16[6,64,2048]{2,1,0:T(8,128)(2,1)}, bf16[6,64,2048]{2,1,0:T(8,128)(2,1)S(1)}, u32[]{:S(2)}, u32[]{:S(2)}) collective-permute-start(bf16[6,64,2048]{2,1,0:T(8,128)(2,1)} %get-tuple-element.252.refs_6_), channel_id=1, source_target_pairs={{0,1},{1,0},{2,3},{3,2},{4,5},{5,4},{6,7},{7,6},{8,9},{9,8},{10,11... | collective-permute-start | bytes 4718600 | tf_op jit(solution)/shard_map/ppermute | solution.py:514
  426.9 36.7 %collective-permute-start.72 = (bf16[6,64,2048]{2,1,0:T(8,128)(2,1)}, bf16[6,64,2048]{2,1,0:T(8,128)(2,1)S(1)}, u32[]{:S(2)}, u32[]{:S(2)}) collective-permute-start(bf16[6,64,2048]{2,1,0:T(8,128)(2,1)} %get-tuple-element.280), channel_id=1, source_target_pairs={{0,4},{4,0},{1,5},{5,1},{2,6},{6,2},{3,7},{7,3},{8,12},{12,8},{9,1... | collective-permute-start | bytes 4718600 | tf_op jit(solution)/shard_map/ppermute | solution.py:514
  427.8 35.9 %collective-permute-start.71 = (bf16[6,64,2048]{2,1,0:T(8,128)(2,1)}, bf16[6,64,2048]{2,1,0:T(8,128)(2,1)}, u32[]{:S(2)}, u32[]{:S(2)}) collective-permute-start(bf16[6,64,2048]{2,1,0:T(8,128)(2,1)} %get-tuple-element.266.refs_10_), channel_id=1, source_target_pairs={{0,1},{1,0},{2,3},{3,2},{4,5},{5,4},{6,7},{7,6},{8,9},{9,8},{10,11... | collective-permute-start | bytes 4718600 | tf_op jit(solution)/shard_map/ppermute | solution.py:514
  435.1 27.5 %collective-permute-start.73 = (bf16[64,2048]{1,0:T(8,128)(2,1)S(1)}, bf16[64,2048]{1,0:T(8,128)(2,1)S(1)}, u32[]{:S(2)}, u32[]{:S(2)}) collective-permute-start(bf16[64,2048]{1,0:T(8,128)(2,1)S(1)} %get-tuple-element.282), channel_id=1, source_target_pairs={{0,8},{8,0},{16,24},{24,16},{1,9},{9,1},{17,25},{25,17},{2,10},{10... | collective-permute-start | bytes 786440 | tf_op jit(solution)/shard_map/ppermute | solution.py:518
  436.7 26.8 %collective-permute-start.74 = (bf16[64,2048]{1,0:T(8,128)(2,1)S(1)}, bf16[64,2048]{1,0:T(8,128)(2,1)S(1)}, u32[]{:S(2)}, u32[]{:S(2)}) collective-permute-start(bf16[64,2048]{1,0:T(8,128)(2,1)S(1)} %get-tuple-element.283), channel_id=1, source_target_pairs={{0,16},{8,24},{16,0},{24,8},{1,17},{9,25},{17,1},{25,9},{2,18},{10... | collective-permute-start | bytes 786440 | tf_op jit(solution)/shard_map/ppermute | solution.py:518
  438.2 25.4 %collective-permute-start.75 = (bf16[64,2048]{1,0:T(8,128)(2,1)S(1)}, bf16[64,2048]{1,0:T(8,128)(2,1)S(1)}, u32[]{:S(2)}, u32[]{:S(2)}) collective-permute-start(bf16[64,2048]{1,0:T(8,128)(2,1)S(1)} %get-tuple-element.284), channel_id=1, source_target_pairs={{0,24},{8,16},{16,8},{24,0},{1,25},{9,17},{17,9},{25,1},{2,26},{10... | collective-permute-start | bytes 786440 | tf_op jit(solution)/shard_map/ppermute | solution.py:518
  468.7 37.3 %collective-permute-start.79 = (bf16[6,64,2048]{2,1,0:T(8,128)(2,1)S(1)}, bf16[6,64,2048]{2,1,0:T(8,128)(2,1)S(1)}, u32[]{:S(2)}, u32[]{:S(2)}) collective-permute-start(bf16[6,64,2048]{2,1,0:T(8,128)(2,1)S(1)} %get-tuple-element.296), channel_id=1, source_target_pairs={{0,4},{4,0},{1,5},{5,1},{2,6},{6,2},{3,7},{7,3},{8,12},{12,8},{9,1... | collective-permute-start | bytes 4718600 | tf_op jit(solution)/shard_map/ppermute | solution.py:514
  469.9 36.1 %collective-permute-start.78 = (bf16[6,64,2048]{2,1,0:T(8,128)(2,1)S(1)}, bf16[6,64,2048]{2,1,0:T(8,128)(2,1)S(1)}, u32[]{:S(2)}, u32[]{:S(2)}) collective-permute-start(bf16[6,64,2048]{2,1,0:T(8,128)(2,1)S(1)} %get-tuple-element.286.refs_10_), channel_id=1, source_target_pairs={{0,1},{1,0},{2,3},{3,2},{4,5},{5,4},{6,7},{7,6},{8,9},{9,8},{10,11... | collective-permute-start | bytes 4718600 | tf_op jit(solution)/shard_map/ppermute | solution.py:514
  482.0 24.0 %collective-permute-start.82 = (bf16[64,2048]{1,0:T(8,128)(2,1)S(1)}, bf16[64,2048]{1,0:T(8,128)(2,1)S(1)}, u32[]{:S(2)}, u32[]{:S(2)}) collective-permute-start(bf16[64,2048]{1,0:T(8,128)(2,1)S(1)} %get-tuple-element.300), channel_id=1, source_target_pairs={{0,24},{8,16},{16,8},{24,0},{1,25},{9,17},{17,9},{25,1},{2,26},{10... | collective-permute-start | bytes 786440 | tf_op jit(solution)/shard_map/ppermute | solution.py:518
  509.5 37.0 %collective-permute-start.86 = (bf16[6,64,2048]{2,1,0:T(8,128)(2,1)}, bf16[6,64,2048]{2,1,0:T(8,128)(2,1)S(1)}, u32[]{:S(2)}, u32[]{:S(2)}) collective-permute-start(bf16[6,64,2048]{2,1,0:T(8,128)(2,1)} %get-tuple-element.313), channel_id=1, source_target_pairs={{0,4},{4,0},{1,5},{5,1},{2,6},{6,2},{3,7},{7,3},{8,12},{12,8},{9,1... | collective-permute-start | bytes 4718600 | tf_op jit(solution)/shard_map/ppermute | solution.py:514
  509.8 36.7 %collective-permute-start.85 = (bf16[6,64,2048]{2,1,0:T(8,128)(2,1)S(1)}, bf16[6,64,2048]{2,1,0:T(8,128)(2,1)S(1)}, u32[]{:S(2)}, u32[]{:S(2)}) collective-permute-start(bf16[6,64,2048]{2,1,0:T(8,128)(2,1)S(1)} %get-tuple-element.301.refs_4_), channel_id=1, source_target_pairs={{0,1},{1,0},{2,3},{3,2},{4,5},{5,4},{6,7},{7,6},{8,9},{9,8},{10,11... | collective-permute-start | bytes 4718600 | tf_op jit(solution)/shard_map/ppermute | solution.py:514
  510.2 36.2 %collective-permute-start.87 = (bf16[64,2048]{1,0:T(8,128)(2,1)}, bf16[64,2048]{1,0:T(8,128)(2,1)S(1)}, u32[]{:S(2)}, u32[]{:S(2)}) collective-permute-start(bf16[64,2048]{1,0:T(8,128)(2,1)} %get-tuple-element.315), channel_id=1, source_target_pairs={{0,8},{8,0},{16,24},{24,16},{1,9},{9,1},{17,25},{25,17},{2,10},{10... | collective-permute-start | bytes 786440 | tf_op jit(solution)/shard_map/ppermute | solution.py:518
  510.6 35.8 %collective-permute-start.88 = (bf16[64,2048]{1,0:T(8,128)(2,1)}, bf16[64,2048]{1,0:T(8,128)(2,1)S(1)}, u32[]{:S(2)}, u32[]{:S(2)}) collective-permute-start(bf16[64,2048]{1,0:T(8,128)(2,1)} %get-tuple-element.316), channel_id=1, source_target_pairs={{0,16},{8,24},{16,0},{24,8},{1,17},{9,25},{17,1},{25,9},{2,18},{10... | collective-permute-start | bytes 786440 | tf_op jit(solution)/shard_map/ppermute | solution.py:518
  512.2 34.3 %collective-permute-start.89 = (bf16[64,2048]{1,0:T(8,128)(2,1)S(1)}, bf16[64,2048]{1,0:T(8,128)(2,1)S(1)}, u32[]{:S(2)}, u32[]{:S(2)}) collective-permute-start(bf16[64,2048]{1,0:T(8,128)(2,1)S(1)} %get-tuple-element.317), channel_id=1, source_target_pairs={{0,24},{8,16},{16,8},{24,0},{1,25},{9,17},{17,9},{25,1},{2,26},{10... | collective-permute-start | bytes 786440 | tf_op jit(solution)/shard_map/ppermute | solution.py:518
  550.8 47.8 %collective-permute-start.94 = (bf16[6,64,2048]{2,1,0:T(8,128)(2,1)}, bf16[6,64,2048]{2,1,0:T(8,128)(2,1)}, u32[]{:S(2)}, u32[]{:S(2)}) collective-permute-start(bf16[6,64,2048]{2,1,0:T(8,128)(2,1)} %get-tuple-element.333), channel_id=1, source_target_pairs={{0,4},{4,0},{1,5},{5,1},{2,6},{6,2},{3,7},{7,3},{8,12},{12,8},{9,1... | collective-permute-start | bytes 4718600 | tf_op jit(solution)/shard_map/ppermute | solution.py:514
  551.8 46.9 %collective-permute-start.93 = (bf16[6,64,2048]{2,1,0:T(8,128)(2,1)}, bf16[6,64,2048]{2,1,0:T(8,128)(2,1)}, u32[]{:S(2)}, u32[]{:S(2)}) collective-permute-start(bf16[6,64,2048]{2,1,0:T(8,128)(2,1)} %get-tuple-element.319.refs_4_), channel_id=1, source_target_pairs={{0,1},{1,0},{2,3},{3,2},{4,5},{5,4},{6,7},{7,6},{8,9},{9,8},{10,11... | collective-permute-start | bytes 4718600 | tf_op jit(solution)/shard_map/ppermute | solution.py:514
  558.0 18.8 %collective-permute-start.91 = (bf16[64,2048]{1,0:T(8,128)(2,1)S(1)}, bf16[64,2048]{1,0:T(8,128)(2,1)S(1)}, u32[]{:S(2)}, u32[]{:S(2)}) collective-permute-start(bf16[64,2048]{1,0:T(8,128)(2,1)S(1)} %get-tuple-element.328), channel_id=1, source_target_pairs={{0,16},{8,24},{16,0},{24,8},{1,17},{9,25},{17,1},{25,9},{2,18},{10... | collective-permute-start | bytes 786440 | tf_op jit(solution)/shard_map/ppermute | solution.py:518
  560.1 23.6 %collective-permute-start.92 = (bf16[64,2048]{1,0:T(8,128)(2,1)S(1)}, bf16[64,2048]{1,0:T(8,128)(2,1)S(1)}, u32[]{:S(2)}, u32[]{:S(2)}) collective-permute-start(bf16[64,2048]{1,0:T(8,128)(2,1)S(1)} %get-tuple-element.329), channel_id=1, source_target_pairs={{0,24},{8,16},{16,8},{24,0},{1,25},{9,17},{17,9},{25,1},{2,26},{10... | collective-permute-start | bytes 786440 | tf_op jit(solution)/shard_map/ppermute | solution.py:518
  612.5 31.1 %collective-permute-start.96 = (bf16[4,64,2048]{2,1,0:T(8,128)(2,1)}, bf16[4,64,2048]{2,1,0:T(8,128)(2,1)}, u32[]{:S(2)}, u32[]{:S(2)}) collective-permute-start(bf16[4,64,2048]{2,1,0:T(8,128)(2,1)} %get-tuple-element.336), channel_id=1, source_target_pairs={{0,4},{4,0},{1,5},{5,1},{2,6},{6,2},{3,7},{7,3},{8,12},{12,8},{9,1... | collective-permute-start | bytes 3145736 | tf_op jit(solution)/shard_map/ppermute | solution.py:514
  612.9 30.8 %collective-permute-start.95 = (bf16[4,64,2048]{2,1,0:T(8,128)(2,1)}, bf16[4,64,2048]{2,1,0:T(8,128)(2,1)}, u32[]{:S(2)}, u32[]{:S(2)}) collective-permute-start(bf16[4,64,2048]{2,1,0:T(8,128)(2,1)} %get-tuple-element.335.refs_8_), channel_id=1, source_target_pairs={{0,1},{1,0},{2,3},{3,2},{4,5},{5,4},{6,7},{7,6},{8,9},{9,8},{10,11... | collective-permute-start | bytes 3145736 | tf_op jit(solution)/shard_map/ppermute | solution.py:514
  620.2 23.5 %collective-permute-start.99 = (bf16[64,2048]{1,0:T(8,128)(2,1)}, bf16[64,2048]{1,0:T(8,128)(2,1)}, u32[]{:S(2)}, u32[]{:S(2)}) collective-permute-start(bf16[64,2048]{1,0:T(8,128)(2,1)} %copy-done.141), channel_id=1, source_target_pairs={{0,24},{8,16},{16,8},{24,0},{1,25},{9,17},{17,9},{25,1},{2,26},{10... | collective-permute-start | bytes 786440 | tf_op jit(solution)/shard_map/ppermute | solution.py:518
  651.6 20.6 %collective-permute-start.108 = (bf16[64,10240]{1,0:T(8,128)(2,1)S(1)}, bf16[64,10240]{1,0:T(8,128)(2,1)S(1)}, u32[]{:S(2)}, u32[]{:S(2)}) collective-permute-start(bf16[64,10240]{1,0:T(8,128)(2,1)S(1)} %join_pieces.1.refs_3_), channel_id=1, source_target_pairs={{1,2},{2,1},{5,6},{6,5},{9,10},{10,9},{13,14},{14,13},{17,18},{18,... | collective-permute-start | bytes 3932168 | tf_op jit(solution)/shard_map/ppermute | solution.py:522
  661.8 24.4 %collective-permute-start.100 = (bf16[640,1024]{1,0:T(8,128)(2,1)S(1)}, bf16[640,1024]{1,0:T(8,128)(2,1)S(1)}, u32[]{:S(2)}, u32[]{:S(2)}) collective-permute-start(bf16[640,1024]{1,0:T(8,128)(2,1)S(1)} %copy_rows.5.refs_6_), channel_id=1, source_target_pairs={{1,2},{2,1},{5,6},{6,5},{9,10},{10,9},{13,14},{14,13},{17,18},{18,... | collective-permute-start | bytes 3932168 | tf_op jit(solution)/shard_map/ppermute | solution.py:522
  664.0 22.4 %collective-permute-start.105 = (bf16[64,2048]{1,0:T(8,128)(2,1)S(1)}, bf16[64,2048]{1,0:T(8,128)(2,1)S(1)}, u32[]{:S(2)}, u32[]{:S(2)}) collective-permute-start(bf16[64,2048]{1,0:T(8,128)(2,1)S(1)} %get-tuple-element.351), channel_id=1, source_target_pairs={{0,8},{8,0},{16,24},{24,16},{1,9},{9,1},{17,25},{25,17},{2,10},{10... | collective-permute-start | bytes 786440 | tf_op jit(solution)/shard_map/ppermute | solution.py:518
  664.1 23.8 %collective-permute-start.106 = (bf16[64,2048]{1,0:T(8,128)(2,1)S(1)}, bf16[64,2048]{1,0:T(8,128)(2,1)S(1)}, u32[]{:S(2)}, u32[]{:S(2)}) collective-permute-start(bf16[64,2048]{1,0:T(8,128)(2,1)S(1)} %get-tuple-element.352), channel_id=1, source_target_pairs={{0,16},{8,24},{16,0},{24,8},{1,17},{9,25},{17,1},{25,9},{2,18},{10... | collective-permute-start | bytes 786440 | tf_op jit(solution)/shard_map/ppermute | solution.py:518
  665.6 28.4 %collective-permute-start.107 = (bf16[64,2048]{1,0:T(8,128)(2,1)S(1)}, bf16[64,2048]{1,0:T(8,128)(2,1)S(1)}, u32[]{:S(2)}, u32[]{:S(2)}) collective-permute-start(bf16[64,2048]{1,0:T(8,128)(2,1)S(1)} %get-tuple-element.353), channel_id=1, source_target_pairs={{0,24},{8,16},{16,8},{24,0},{1,25},{9,17},{17,9},{25,1},{2,26},{10... | collective-permute-start | bytes 786440 | tf_op jit(solution)/shard_map/ppermute | solution.py:518
  672.2 29.6 %collective-permute-start.104 = (bf16[208,256]{1,0:T(8,128)(2,1)}, bf16[208,256]{1,0:T(8,128)(2,1)S(1)}, u32[]{:S(2)}, u32[]{:S(2)}) collective-permute-start(bf16[208,256]{1,0:T(8,128)(2,1)} %get-tuple-element.350), channel_id=1, source_target_pairs={{0,24},{8,16},{16,8},{24,0},{1,25},{9,17},{17,9},{25,1},{2,26},{10... | collective-permute-start | bytes 319496 | tf_op jit(solution)/shard_map/ppermute | solution.py:518
  (217 other events, 1862.3 us)
